TPU v7x, 1024 devices: a whole 4x8x16 slice. The times are simulated.
1024 devices in a mesh: fsdp: 256 (over z, x_lo, y), tp: 4 (over x_hi, core).
Axes of the slice: x: 4 (x_hi: 2, x_lo: 2; x = x_hi * 2 + x_lo), y: 8, z: 16, core: 2. Of those that a mesh axis runs over, the one named last changes fastest.
Arguments:
- inputs: bfloat16 [65536, 4096], P('fsdp'), may hold values from -24 to 24
- value_grad: bfloat16 [65536, 1024], P('fsdp', 'tp'), may hold values from -24 to 24
- value_weight: bfloat16 [4096, 1024], P('tp', 'fsdp'), may hold values from -0.09375 to 0.09375
- counts: int32 [256, 4], P('fsdp'), may hold values from 1 to 232, as said below
- offsets: int32 [256, 4], P('fsdp'), may hold values from 0 to 248, as said below
Outputs:
- input_grad: bfloat16 [65536, 4096], P('fsdp', 'tp')
- weight_grad: float32 [4096, 1024], P('fsdp', 'tp')
Inputs may be any that keep to these rules, and one draw needn't show every extreme that they name: `offsets`: on each index of fsdp the 4 samples lie in order; each starts at a multiple of 8, at or after the 8-row-aligned end of the previous one, and all lie within the 256 rows; on some index the aligned blocks of its samples fill all 256 rows. `counts`: how many rows the samples of a row group fill varies widely between indices of fsdp.
All inputs are finite; a program needn't handle non-finite values.
Results may differ from a plain program's by a relative error of at most 0.0046.
Values may be sent and summed in bfloat16 or wider, within the bound.
No kernel may reach another device: no remote copies, remote signals or barrier semaphores. Data moves between devices by JAX's collectives and lax.ppermute only.
A program may use at most 32 MiB of HBM per device.

v0:
```python
import math

import jax
import jax.numpy as jnp
from jax import lax
from jax.sharding import Mesh
from jax.sharding import PartitionSpec as P

FSDP = ("fsdp_0", "fsdp_1", "fsdp_2")


def sent_to_all(shard, axis):
    copies = jnp.broadcast_to(shard, (lax.axis_size(axis), *shard.shape))
    return lax.all_to_all(copies, axis, split_axis=0, concat_axis=0, tiled=True)


def in_order(parts, dim):
    parts = jnp.moveaxis(parts, 0, dim)
    dims = parts.shape
    return parts.reshape(*dims[:dim], dims[dim] * dims[dim + 1], *dims[dim + 2 :])


def gather_directly(shard, axis, dim):
    parts = sent_to_all(shard, axis)
    return in_order(parts, dim)


def stacked_from(shard, axes, sequence):
    parts = shard[None]
    for k in sequence:
        parts = lax.all_gather(parts, axes[k], axis=0, tiled=True)
    carried = [lax.axis_size(axes[k]) for k in reversed(sequence)]
    parts = parts.reshape(*carried, *shard.shape)
    turned = sorted(range(len(sequence)), key=lambda place: sequence[len(sequence) - 1 - place])
    return parts.transpose(*turned, *range(len(sequence), parts.ndim)).reshape(-1, *shard.shape)


def gathered_by_axis(shard, axes, sequence, dim):
    return in_order(stacked_from(shard, axes, sequence), dim)


def own_block(parts, axes, sequence):
    dims = [lax.axis_size(a) for a in axes]
    parts = parts.reshape(*dims, *parts.shape[1:])
    parts = parts.transpose(*sequence, *range(len(axes), parts.ndim))
    parts = parts.reshape(-1, *parts.shape[len(axes) :])
    for k in sequence:
        parts = lax.psum_scatter(parts, axes[k], scatter_dimension=0, tiled=True)
    return parts[0]


def split_up(shard, dim, peers):
    before, after = (shard.shape[:dim], shard.shape[dim + 1 :])
    return jnp.moveaxis(shard.reshape(*before, peers, -1, *after), dim, 0)


def summed_rows(shard, axes, sequence, dim):
    peers = lax.axis_size(axes)
    return own_block(split_up(shard, dim, peers), axes, sequence)


def local(inputs, value_grad, value_weight, counts, offsets):
    tok_rows = inputs.shape[0]
    positions = jnp.arange(tok_rows, dtype=jnp.int32)[:, None]
    starts = offsets[0][None, :]
    lengths = counts[0][None, :]
    inside = (positions >= starts) & (positions < starts + lengths)
    inverse_root = lax.rsqrt(lengths.astype(jnp.float32))
    row_factor = jnp.sum(jnp.where(inside, inverse_root, jnp.zeros_like(inverse_root)), axis=1)
    scaled = (value_grad.astype(jnp.float32) * row_factor[:, None]).astype(jnp.bfloat16)
    scaled_all = gather_directly(scaled, "tp", 1)
    result = lax.dot_general(
        scaled_all,
        gathered_by_axis(value_weight, FSDP, (1, 0, 2), 1),
        (((1,), (1,)), ((), ())),
        preferred_element_type=jnp.float32,
    )
    input_grad = result.astype(jnp.bfloat16)
    normalizer = 1.0 / math.sqrt(counts.shape[1] * lax.axis_size(FSDP))
    result = lax.dot_general(
        inputs, scaled, (((0,), (0,)), ((), ())), preferred_element_type=jnp.float32
    )
    summed = summed_rows(result, FSDP, (0, 2, 1), 0)
    return (input_grad, summed * normalizer)


def solution(mesh):
    split = Mesh(
        mesh.devices.reshape(16, 2, 8, mesh.shape["tp"]), ("fsdp_0", "fsdp_1", "fsdp_2", "tp")
    )
    in_specs = (P(FSDP, None), P(FSDP, "tp"), P("tp", FSDP), P(FSDP, None), P(FSDP, None))
    out_specs = (P(FSDP, "tp"), P(FSDP, "tp"))
    return jax.shard_map(local, mesh=split, in_specs=in_specs, out_specs=out_specs, check_vma=False)
```

profile of v0, /device:TPU:6, one launch (start us, length us, event | category | flops | bytes accessed | tf_op | source)
XLA Modules:
  0.0 199.2 jit_solution(5318661733422751152)
XLA Ops:
  8.0 0.0 copy-start
  8.0 0.0 reduce-scatter.4.cloned.1.call-start
  8.1 0.8 rsqrt_bitcast_fusion
  8.9 0.7 add_bitcast_fusion
  9.5 0.7 select_reduce_fusion
  10.3 1.0 multiply_convert_fusion
  11.3 0.0 copy-done
  11.3 2.7 %convolution_bitcast_fusion = f32[4096,256]{0,1:T(8,128)} fusion(bf16[256,256]{1,0:T(8,128)(2,1)S(1)} %multiply_convert_fusion, bf16[256,4096]{1,0:T(8,128)(2,1)S(1)} %copy-done), kind=kOutput, calls=%fused_computation | convolution fusion | flops 536870912 | bytes 6422528 | tf_op jit(solution)/shard_map/dot_general | solution.py:80
  14.0 5.6 %copy.25 = f32[4096,256]{1,0:T(8,128)} copy(f32[4096,256]{0,1:T(8,128)} %convolution_bitcast_fusion) | data formatting | bytes 8388608 | tf_op jit(solution)/shard_map/dot_general | solution.py:80
  19.6 4.8 %copy.26 = f32[16,8,2,16,256]{4,3,2,1,0:T(8,128)} copy(f32[16,8,2,16,256]{4,3,1,2,0:T(8,128)} %bitcast.30) | data formatting | bytes 8388608 | tf_op jit(solution)/shard_map/transpose | solution.py:45
  24.4 0.0 copy-start.1
  24.4 0.0 reduce-scatter.4.cloned.1.call-update
  24.4 0.0 all-gather.3.cloned.1.call-start
  24.4 0.6 copy-done.1
  25.1 4.4 %all-gather = bf16[2048,4]{0,1:T(4,128)(2,1)S(1)} all-gather(bf16[1024,4]{0,1:T(4,128)(2,1)S(1)} %copy-done.1), channel_id=2, replica_groups=mesh['fsdp_0'=16,'fsdp_1'=2,'fsdp_2'=8,'tp'=4] {'fsdp_1'}, dimensions={0}, use_global_device_ids=true | all-gather | bytes 24576 | tf_op jit(solution)/shard_map/all_gather | solution.py:31
  29.4 46.8 %all_gather.10 = bf16[32,1024,4]{1,2,0:T(4,128)(2,1)} all-gather(bf16[2,1024,4]{1,2,0:T(4,128)(2,1)S(1)} %bitcast.34), channel_id=1, replica_groups=mesh['fsdp_0'=16,'fsdp_1'=2,'fsdp_2'=8,'tp'=4] {'fsdp_0'}, dimensions={0}, use_global_device_ids=true | all-gather | bytes 278528 | tf_op jit(solution)/shard_map/all_gather | solution.py:31
  76.2 0.0 all-gather.3.cloned.1.call-update
  76.3 0.0 reduce-scatter.6.cloned.1.call-start
  76.3 40.1 %reduce-scatter.4.cloned.1.call-done = f32[16,16,256]{2,1,0:T(8,128)} async-done(((f32[256,16,256]{2,1,0:T(8,128)}), f32[16,16,256]{2,1,0:T(8,128)}) %reduce-scatter.4.cloned.1.call-update) | async-done | bytes 262160 | tf_op jit(solution)/shard_map/reduce_scatter | solution.py:48
  116.4 0.0 reduce-scatter.6.cloned.1.call-update
  116.5 0.1 copy.22
  116.6 0.8 broadcast_in_dim.29
  117.4 5.3 %all-to-all-start = ((bf16[4,256,256]{1,2,0:T(8,128)(2,1)}), bf16[4,256,256]{1,2,0:T(8,128)(2,1)S(1)}, u32[]{:S(2)}, u32[]{:S(2)}) async-start(bf16[4,256,256]{1,2,0:T(8,128)(2,1)} %broadcast_in_dim.29), calls=%async_computation | async-start | bytes 1048576 | tf_op jit(solution)/shard_map/all_to_all | solution.py:14
  122.7 0.0 reduce-scatter.8.cloned.1.call-start
  122.7 0.0 all-gather.3.cloned.1.call-done
  122.7 2.7 %copy.23 = bf16[16,2,8,1024,4]{3,2,1,0,4:T(8,128)(2,1)S(1)} copy(bf16[16,2,8,1024,4]{3,4,1,0,2:T(4,128)(2,1)} %bitcast.32) | data formatting | bytes 4194304 | tf_op jit(solution)/shard_map/transpose | solution.py:35
  125.4 2.9 %copy.24 = bf16[1024,256,4]{0,2,1:T(4,128)(2,1)} copy(bf16[1024,256,4]{0,1,2:T(8,128)(2,1)S(1)} %bitcast.31) | data formatting | bytes 4194304 | tf_op jit(solution)/shard_map/transpose | solution.py:18
  128.3 3.9 %reshape.25 = bf16[1024,1024]{0,1:T(8,128)(2,1)} reshape(bf16[1024,256,4]{0,2,1:T(4,128)(2,1)} %copy.24) | data formatting | bytes 4194304 | tf_op jit(solution)/shard_map/reshape | solution.py:20
  132.3 32.7 %reduce-scatter.6.cloned.1.call-done = f32[2,16,256]{2,1,0:T(8,128)} async-done(((f32[16,16,256]{2,1,0:T(8,128)}), f32[2,16,256]{2,1,0:T(8,128)}) %reduce-scatter.6.cloned.1.call-update) | async-done | bytes 32784 | tf_op jit(solution)/shard_map/reduce_scatter | solution.py:48
  165.0 0.0 reduce-scatter.8.cloned.1.call-update
  165.0 0.0 all-to-all-done
  165.0 3.1 %convolution_convert_fusion = bf16[256,1024]{1,0:T(8,128)(2,1)} fusion(bf16[256,1024]{0,1:T(8,128)(2,1)S(1)} %bitcast.33, bf16[1024,1024]{0,1:T(8,128)(2,1)} %reshape.25), kind=kOutput, calls=%fused_computation.1 | convolution fusion | flops 537133056 | bytes 3145728 | tf_op jit(solution)/shard_map/dot_general | solution.py:72
  168.1 22.1 %reduce-scatter.8.cloned.1.call-done = f32[1,16,256]{2,1,0:T(8,128)} async-done(((f32[2,16,256]{2,1,0:T(8,128)}), f32[1,16,256]{2,1,0:T(8,128)}) %reduce-scatter.8.cloned.1.call-update) | async-done | bytes 16400 | tf_op jit(solution)/shard_map/reduce_scatter | solution.py:48
  190.3 1.3 multiply_bitcast_fusion
Async XLA Ops:
  8.0 3.3 %copy-start = (bf16[256,4096]{1,0:T(8,128)(2,1)S(1)}, bf16[256,4096]{1,0:T(8,128)(2,1)}, u32[]{:S(2)}) copy-start(bf16[256,4096]{1,0:T(8,128)(2,1)} %param.5) | copy-start | bytes 6291460
  8.0 108.4 %reduce-scatter.4.cloned.1.call-start = ((), (), s32[]{:S(2)}) async-start(), calls=%async_computation.5 | async-start | bytes 4456448 | tf_op jit(solution)/shard_map/reduce_scatter | solution.py:48
  24.4 0.7 copy-start.1
  24.4 98.3 %all-gather.3.cloned.1.call-start = ((), (), s32[]{:S(2)}) async-start(), calls=%async_computation.4 | async-start | bytes 2359296 | tf_op jit(solution)/shard_map/all_gather | solution.py:31
  76.3 88.7 %reduce-scatter.6.cloned.1.call-start = ((), (), s32[]{:S(2)}) async-start(), calls=%async_computation.6 | async-start | bytes 294912 | tf_op jit(solution)/shard_map/reduce_scatter | solution.py:48
  117.4 47.6 %all-to-all-start = ((bf16[4,256,256]{1,2,0:T(8,128)(2,1)}), bf16[4,256,256]{1,2,0:T(8,128)(2,1)S(1)}, u32[]{:S(2)}, u32[]{:S(2)}) async-start(bf16[4,256,256]{1,2,0:T(8,128)(2,1)} %broadcast_in_dim.29), calls=%async_computation | async-start | bytes 1048576 | tf_op jit(solution)/shard_map/all_to_all | solution.py:14
  122.7 67.6 %reduce-scatter.8.cloned.1.call-start = ((), (), s32[]{:S(2)}) async-start(), calls=%async_computation.7 | async-start | bytes 49152 | tf_op jit(solution)/shard_map/reduce_scatter | solution.py:48
Sparse Core Ops, SparseCore 0:
  24.5 91.8 reduce-scatter.3
Sparse Core Ops, SparseCore 1:
  76.3 42.0 all-gather.2
  121.6 43.3 reduce-scatter.5
  168.5 21.7 reduce-scatter.7
where the time goes:
time: 202 us; the launch traced here: 199 us
  waiting for transfers between devices  95 us (47%)
  blocking collectives  51.2 us (25%)
  local copies, waits for them, and re-layouts  21.6 us (11%)
  between operations  15.7 us (8%)
  matrix products  5.79 us (3%)
  starting transfers between devices  5.39 us (3%)
  other arithmetic  4.54 us (2%)
    reduce_scatter x3, waiting for transfers between devices, own_block(): parts = lax.psum_scatter(parts, axes[k], scatter_dimension=0, tiled=True)  95 us
    all_gather x2, blocking collectives, stacked_from(): parts = lax.all_gather(parts, axes[k], axis=0, tiled=True)  51.2 us
    dot_general x1, local copies, waits for them, and re-layouts, local(): lax.dot_general(inputs, scaled, (((0,), (0,)), ((), ())), preferred_eleme...  5.61 us
    all_to_all x1, starting transfers between devices, sent_to_all(): return lax.all_to_all(copies, axis, split_axis=0, concat_axis=0, tiled=True)  5.27 us
    transpose x1, local copies, waits for them, and re-layouts, own_block(): parts = parts.transpose(*sequence, *range(len(axes), parts.ndim))  4.79 us
  transfers between devices with their start and end apart: 5, of which 3 were waited for; matrix products, arithmetic and copies ran while one was open for 7% of the time, Pallas kernels for 0%

commit v1 on v0

v1 whole, which is shorter than its diff:
```python
import math

import jax
import jax.numpy as jnp
from jax import lax
from jax.experimental import pallas as pl
from jax.experimental.pallas import tpu as pltpu
from jax.sharding import Mesh
from jax.sharding import PartitionSpec as P

FSDP = ("z", "xl", "y")
TP = ("xh", "c")
VMEM_LIMIT = 48 * 1024 * 1024


def prep_kernel(place_ref, counts_ref, offsets_ref, grad_ref, inputs_ref, scaled_ref, send_ref, sems):
    half = place_ref[0]
    blocks = send_ref.shape[1] // 128
    copies = []
    for z in range(blocks):
        source = pl.ds(pl.multiple_of((2 * z + 1 - half) * 128, 128), 128)
        copy = pltpu.make_async_copy(
            inputs_ref.at[:, source], send_ref.at[:, pl.ds(z * 128, 128)], sems.at[z]
        )
        copy.start()
        copies.append(copy)
    rows, columns = grad_ref.shape
    positions = lax.broadcasted_iota(jnp.int32, (rows, columns), 0)
    length = jnp.zeros((rows, columns), jnp.int32)
    for s in range(counts_ref.shape[1]):
        first = offsets_ref[0, s]
        count = counts_ref[0, s]
        length = jnp.where((positions >= first) & (positions < first + count), count, length)
    factor = jnp.where(length > 0, lax.rsqrt(jnp.maximum(length, 1).astype(jnp.float32)), 0.0)
    scaled_ref[...] = (grad_ref[...].astype(jnp.float32) * factor).astype(jnp.bfloat16)
    for copy in copies:
        copy.wait()


def weight_kernel(place_ref, inputs_ref, received_ref, own_ref, all_ref, out_ref):
    half = place_ref[0]
    peer = all_ref[place_ref[1]]
    own = own_ref[...]
    peers = out_ref.shape[0]
    for z in range(received_ref.shape[1] // 128):
        mine = inputs_ref[:, pl.ds(pl.multiple_of((2 * z + half) * 128, 128), 128)]
        other = received_ref[:, z * 128 : (z + 1) * 128]
        dims = (((0,), (0,)), ((), ()))
        term = lax.dot_general(mine, own, dims, preferred_element_type=jnp.float32)
        term += lax.dot_general(other, peer, dims, preferred_element_type=jnp.float32)
        each = 128 // peers
        out_ref[:, z * each : (z + 1) * each, :] = term.reshape(peers, each, -1).astype(jnp.bfloat16)


def input_kernel(all_ref, weight_ref, out_ref):
    groups = out_ref.shape[0]
    parts = all_ref.shape[0] // groups
    wide = all_ref.shape[2]
    for g in range(groups):
        total = None
        for t in range(parts):
            term = jnp.dot(
                all_ref[g * parts + t],
                weight_ref[t * wide : (t + 1) * wide, :],
                preferred_element_type=jnp.float32,
            )
            total = term if total is None else total + term
        out_ref[g] = total.astype(jnp.bfloat16)


def in_vmem():
    return pl.BlockSpec(memory_space=pltpu.VMEM)


def in_smem():
    return pl.BlockSpec(memory_space=pltpu.SMEM)


def anywhere():
    return pl.BlockSpec(memory_space=pl.ANY)


PARAMS = pltpu.CompilerParams(vmem_limit_bytes=VMEM_LIMIT)


def local(inputs, value_grad, value_weight, counts, offsets):
    rows, features = inputs.shape
    columns = value_grad.shape[1]
    quarter, own_columns = value_weight.shape
    half = lax.axis_index("xl")
    tensor = lax.axis_index(TP)
    n_tp = lax.axis_size(TP)
    n_z = lax.axis_size("z")
    n_y = lax.axis_size("y")

    mine = value_weight.T.reshape(own_columns, 2, quarter // 2).transpose(1, 0, 2)
    mine = jnp.broadcast_to(mine[:, None], (2, n_y, own_columns, quarter // 2))
    mine = mine.reshape(2 * n_y, own_columns, quarter // 2)
    block = lax.all_to_all(mine, ("xl", "y"), 0, 0, tiled=True)
    block = block.reshape(2 * n_y * own_columns, quarter // 2)
    weight = lax.all_gather(block, "z", axis=0, tiled=True)

    place = jnp.stack([half, (1 - half) * n_tp + tensor]).astype(jnp.int32)
    scaled, send = pl.pallas_call(
        prep_kernel,
        out_shape=(
            jax.ShapeDtypeStruct((rows, columns), jnp.bfloat16),
            jax.ShapeDtypeStruct((rows, features // 2), jnp.bfloat16),
        ),
        in_specs=[in_smem(), in_smem(), in_smem(), in_vmem(), anywhere()],
        out_specs=(in_vmem(), anywhere()),
        scratch_shapes=[pltpu.SemaphoreType.DMA((features // 256,))],
        compiler_params=PARAMS,
    )(place, counts, offsets, value_grad, inputs)

    received = lax.ppermute(send, "xl", [(0, 1), (1, 0)])
    copies = jnp.broadcast_to(scaled, (2 * n_tp, rows, columns))
    scaled_all = lax.all_to_all(copies, ("xl", *TP), 0, 0, tiled=True)

    term = pl.pallas_call(
        weight_kernel,
        out_shape=jax.ShapeDtypeStruct((n_y, features // 2 // n_y, columns), jnp.bfloat16),
        in_specs=[in_smem(), in_vmem(), in_vmem(), in_vmem(), in_vmem()],
        out_specs=in_vmem(),
        compiler_params=PARAMS,
    )(place, inputs, received, scaled, scaled_all)
    terms = lax.all_to_all(term, "y", 0, 0, tiled=True)
    summed = jnp.sum(terms.astype(jnp.float32), axis=0)
    summed = summed.reshape(n_z, -1, columns)
    summed = lax.all_to_all(summed, "z", 0, 0, tiled=True)
    normalizer = 1.0 / math.sqrt(counts.shape[1] * lax.axis_size(FSDP))
    weight_grad = jnp.sum(summed, axis=0) * normalizer

    halves = pl.pallas_call(
        input_kernel,
        out_shape=jax.ShapeDtypeStruct((2, rows, quarter // 2), jnp.bfloat16),
        in_specs=[in_vmem(), in_vmem()],
        out_specs=in_vmem(),
        compiler_params=PARAMS,
    )(scaled_all, weight)
    halves = lax.all_to_all(halves, "xl", 0, 0, tiled=True)
    input_grad = jnp.concatenate([halves[0], halves[1]], axis=1)
    return (input_grad, weight_grad)


def solution(mesh):
    split = Mesh(mesh.devices.reshape(16, 2, 8, 2, 2), (*FSDP, *TP))
    in_specs = (P(FSDP, None), P(FSDP, TP), P(TP, FSDP), P(FSDP, None), P(FSDP, None))
    out_specs = (P(FSDP, TP), P(FSDP, TP))
    return jax.shard_map(local, mesh=split, in_specs=in_specs, out_specs=out_specs, check_vma=False)
```

time: 202 us -> 176 us (0.87)
  blocking collectives: 51.2 us -> 25 us
  starting transfers between devices: 5.39 us -> 26.9 us
  local copies, waits for them, and re-layouts: 21.6 us -> 7.82 us
  matrix products: 5.79 us -> 0 us
  Pallas kernels: 0 us -> 5.28 us
  waiting for transfers between devices: 95 us -> 92.5 us
  other arithmetic: 4.54 us -> 2.4 us
    reduce_scatter x3 -> x0, waiting for transfers between devices: 95 us -> none  [own_block(): parts = lax.psum_scatter(parts, axes[k], scatter_dimension=0, tiled=True)]
    all_gather x1, waiting for transfers between devices: 0.01 us -> 63.3 us  [local(): weight = lax.all_gather(block, 'z', axis=0, tiled=True)]
    all_gather x2 -> x0, blocking collectives: 51.2 us -> none  [stacked_from(): parts = lax.all_gather(parts, axes[k], axis=0, tiled=True)]
    all_to_all x1 -> x4, waiting for transfers between devices: 0.01 us -> 29.2 us  [the longest x1 12.9 us: local(): summed = lax.all_to_all(summed, 'z', 0, 0, tiled=True)]
    all_to_all x0 -> x1, blocking collectives: none -> 25 us  [local(): block = lax.all_to_all(mine, ('xl', 'y'), 0, 0, tiled=True)]
    all_to_all x1 -> x4, starting transfers between devices: 5.27 us -> 24 us  [the longest x1 7.77 us: local(): summed = lax.all_to_all(summed, 'z', 0, 0, tiled=True)]
    transpose x3 -> x1, local copies, waits for them, and re-layouts: 10.5 us -> 0.01 us  [local(): value_weight.T.reshape(own_columns, 2, quarter // 2).transpose(1, 0, 2)]
    dot_general x2 -> x0, matrix products: 5.79 us -> none  [the longest x1 3.12 us: local(): lax.dot_general(scaled_all, gathered_by_axis(value_weight, FSDP, (1, 0, 2...]
  transfers between devices with their start and end apart: 5 -> 6, of which waited for: 3 -> 4; matrix products, arithmetic and copies ran while one was open for 7% -> 2% of each run, Pallas kernels for 0% -> 2%
where the time goes in v1:
time: 176 us; the launch traced here: 174 us
  waiting for transfers between devices  92.5 us (53%)
  starting transfers between devices  26.9 us (15%)
  blocking collectives  25 us (14%)
  between operations  14.1 us (8%)
  local copies, waits for them, and re-layouts  7.82 us (4%)
  Pallas kernels  5.28 us (3%)
  other arithmetic  2.4 us (1%)
    all_gather x1, waiting for transfers between devices, local(): weight = lax.all_gather(block, 'z', axis=0, tiled=True)  63.3 us
    all_to_all x1, blocking collectives, local(): block = lax.all_to_all(mine, ('xl', 'y'), 0, 0, tiled=True)  25 us
    all_to_all x1, waiting for transfers between devices, local(): summed = lax.all_to_all(summed, 'z', 0, 0, tiled=True)  12.9 us
    all_to_all x1, waiting for transfers between devices, local(): scaled_all = lax.all_to_all(copies, ('xl', *TP), 0, 0, tiled=True)  12.5 us
    all_to_all x1, starting transfers between devices, local(): summed = lax.all_to_all(summed, 'z', 0, 0, tiled=True)  7.77 us
    all_to_all x1, starting transfers between devices, local(): scaled_all = lax.all_to_all(copies, ('xl', *TP), 0, 0, tiled=True)  6.17 us
    unnamed x16, local copies, waits for them, and re-layouts  6.02 us
    all_to_all x1, starting transfers between devices, local(): terms = lax.all_to_all(term, 'y', 0, 0, tiled=True)  5.73 us
  transfers between devices with their start and end apart: 6, of which 4 were waited for; matrix products, arithmetic and copies ran while one was open for 2% of the time, Pallas kernels for 2%

profile of v1, /device:TPU:6, one launch (start us, length us, event | category | flops | bytes accessed | tf_op | source)
XLA Modules:
  0.0 174.0 jit_solution(10187679100103527349)
XLA Ops:
  7.2 0.0 copy-start.7
  7.2 0.1 pad_add_fusion.place_ref
  7.3 0.0 copy-start
  7.3 1.6 copy-done
  8.8 0.0 copy-start.4
  8.9 0.9 copy-done.4
  9.8 0.0 copy-start.5
  9.8 0.7 copy-done.5
  10.4 0.0 copy-start.6
  10.4 0.7 copy-done.6
  11.1 1.7 shard_map.68
  12.8 0.0 copy-start.1
  12.8 2.9 %collective-permute-start = (bf16[256,2048]{1,0:T(8,128)(2,1)}, bf16[256,2048]{1,0:T(8,128)(2,1)}, u32[]{:S(2)}, u32[]{:S(2)}) collective-permute-start(bf16[256,2048]{1,0:T(8,128)(2,1)} %get-tuple-element.5), channel_id=1, source_target_pairs={{0,32},{32,0},{1,33},{33,1},{2,34},{34,2},{3,35},{35,3},{4,36},{36... | collective-permute-start | bytes 3145736 | tf_op jit(solution)/shard_map/ppermute | solution.py:116
  15.7 0.0 copy-done.7
  15.8 25.0 %all_to_all.25 = bf16[16,4,512]{2,1,0:T(4,128)(2,1)S(1)} all-to-all(bf16[16,4,512]{2,1,0:T(4,128)(2,1)S(1)} %bitcast.10), channel_id=1, replica_groups=mesh['z'=16,'xl'=2,'y'=8,'xh'=2,'c'=2] {'xl','y'}, dimensions={0} | all-to-all | bytes 131072 | tf_op jit(solution)/shard_map/all_to_all | solution.py:99
  40.7 1.1 broadcast_in_dim.4
  41.8 6.2 %all-to-all-start = ((bf16[8,256,256]{2,1,0:T(8,128)(2,1)}), bf16[8,256,256]{2,1,0:T(8,128)(2,1)S(1)}, u32[]{:S(2)}, u32[]{:S(2)}) async-start(bf16[8,256,256]{2,1,0:T(8,128)(2,1)} %broadcast_in_dim.4), calls=%async_computation | async-start | bytes 2097152 | tf_op jit(solution)/shard_map/all_to_all | solution.py:118
  48.0 0.0 all-gather.2.cloned.1.call-start
  48.0 0.6 reshape.19
  48.6 0.1 all-gather.2.cloned.1.call-update
  48.7 12.5 %all-to-all-done.all_ref = bf16[8,256,256]{2,1,0:T(8,128)(2,1)S(1)} async-done(((bf16[8,256,256]{2,1,0:T(8,128)(2,1)}), bf16[8,256,256]{2,1,0:T(8,128)(2,1)S(1)}, u32[]{:S(2)}, u32[]{:S(2)}) %all-to-all-start) | async-done | bytes 1048608 | tf_op jit(solution)/shard_map/all_to_all | solution.py:118
  61.2 0.0 collective-permute-done.received_ref
  61.2 0.0 copy-done.1
  61.2 2.0 %shard_map.70 = bf16[8,256,256]{2,1,0:T(8,128)(2,1)S(1)} custom-call(s32[2]{0:T(128)S(1)} %pad_add_fusion.place_ref, bf16[256,4096]{1,0:T(8,128)(2,1)S(1)} %copy-done.1, bf16[256,2048]{1,0:T(8,128)(2,1)} %collective-permute-done.received_ref, bf16[256,256]{1,0:T(8,128)(2,1)S(1)} %get-tuple-element.4.own_ref, bf16[8,256,256]{2,1,0:T(8,128)(2,1)S(1)} %all-to-all-done.all_ref), custom_call_target="tpu_custom_call" | custom-call | tf_op jit(solution)/shard_map/pallas_call | solution.py:120
  63.3 0.0 copy-start.2
  63.3 1.0 copy-done.2
  64.3 5.7 %all-to-all-start.3 = ((bf16[8,256,256]{2,1,0:T(8,128)(2,1)}), bf16[8,256,256]{2,1,0:T(8,128)(2,1)S(1)}, u32[]{:S(2)}, u32[]{:S(2)}) async-start(bf16[8,256,256]{2,1,0:T(8,128)(2,1)} %copy-done.2), calls=%async_computation.3 | async-start | bytes 2097152 | tf_op jit(solution)/shard_map/all_to_all | solution.py:127
  70.0 63.3 %all-gather.2.cloned.1.call-done.weight_ref = bf16[1024,512]{1,0:T(8,128)(2,1)} async-done(((bf16[64,512]{1,0:T(8,128)(2,1)}), bf16[1024,512]{1,0:T(8,128)(2,1)}) %all-gather.2.cloned.1.call-update) | async-done | bytes 1048592 | tf_op jit(solution)/shard_map/all_gather | solution.py:101
  133.3 0.0 copy-start.3
  133.3 1.2 copy-done.3
  134.5 1.5 shard_map.69
  136.0 0.0 all-to-all-done.3
  136.0 4.3 %all-to-all-start.2 = ((bf16[2,256,512]{2,1,0:T(8,128)(2,1)}), bf16[2,256,512]{2,1,0:T(8,128)(2,1)S(1)}, u32[]{:S(2)}, u32[]{:S(2)}) async-start(bf16[2,256,512]{2,1,0:T(8,128)(2,1)} %shard_map.69), calls=%async_computation.2 | async-start | bytes 1048576 | tf_op jit(solution)/shard_map/all_to_all | solution.py:141
  140.3 0.8 convert_reduce_fusion
  141.2 3.7 %all-to-all-done.2 = bf16[2,256,512]{2,1,0:T(8,128)(2,1)S(1)} async-done(((bf16[2,256,512]{2,1,0:T(8,128)(2,1)}), bf16[2,256,512]{2,1,0:T(8,128)(2,1)S(1)}, u32[]{:S(2)}, u32[]{:S(2)}) %all-to-all-start.2) | async-done | bytes 524320 | tf_op jit(solution)/shard_map/all_to_all | solution.py:141
  144.9 7.8 %all-to-all-start.4 = ((f32[16,16,256]{2,1,0:T(8,128)}), f32[16,16,256]{2,1,0:T(8,128)S(1)}, u32[]{:S(2)}, u32[]{:S(2)}) async-start(f32[16,16,256]{2,1,0:T(8,128)} %bitcast.7), calls=%async_computation.4 | async-start | bytes 524288 | tf_op jit(solution)/shard_map/all_to_all | solution.py:130
  152.7 0.9 pad_maximum_fusion
  153.6 12.9 %all-to-all-done.4 = f32[16,16,256]{2,1,0:T(8,128)S(1)} async-done(((f32[16,16,256]{2,1,0:T(8,128)}), f32[16,16,256]{2,1,0:T(8,128)S(1)}, u32[]{:S(2)}, u32[]{:S(2)}) %all-to-all-start.4) | async-done | bytes 262176 | tf_op jit(solution)/shard_map/all_to_all | solution.py:130
  166.5 0.6 broadcast_multiply_fusion
  (5 shorter events, 0.1 us)
Async XLA Ops:
  7.2 8.5 %copy-start.7 = (bf16[1024,4]{0,1:T(4,128)(2,1)S(1)}, bf16[1024,4]{0,1:T(4,128)(2,1)}, u32[]{:S(2)}) copy-start(bf16[1024,4]{0,1:T(4,128)(2,1)} %param.7) | copy-start | bytes 24580
  7.3 1.6 copy-start
  8.8 0.9 copy-start.4
  9.8 0.7 copy-start.5
  10.4 0.7 copy-start.6
  12.8 48.4 %copy-start.1 = (bf16[256,4096]{1,0:T(8,128)(2,1)S(1)}, bf16[256,4096]{1,0:T(8,128)(2,1)}, u32[]{:S(2)}) copy-start(bf16[256,4096]{1,0:T(8,128)(2,1)} %inputs_ref.3) | copy-start | bytes 6291460
  12.8 48.4 %collective-permute-start = (bf16[256,2048]{1,0:T(8,128)(2,1)}, bf16[256,2048]{1,0:T(8,128)(2,1)}, u32[]{:S(2)}, u32[]{:S(2)}) collective-permute-start(bf16[256,2048]{1,0:T(8,128)(2,1)} %get-tuple-element.5), channel_id=1, source_target_pairs={{0,32},{32,0},{1,33},{33,1},{2,34},{34,2},{3,35},{35,3},{4,36},{36... | collective-permute-start | bytes 3145736 | tf_op jit(solution)/shard_map/ppermute | solution.py:116
  41.8 19.4 %all-to-all-start = ((bf16[8,256,256]{2,1,0:T(8,128)(2,1)}), bf16[8,256,256]{2,1,0:T(8,128)(2,1)S(1)}, u32[]{:S(2)}, u32[]{:S(2)}) async-start(bf16[8,256,256]{2,1,0:T(8,128)(2,1)} %broadcast_in_dim.4), calls=%async_computation | async-start | bytes 2097152 | tf_op jit(solution)/shard_map/all_to_all | solution.py:118
  48.0 85.3 %all-gather.2.cloned.1.call-start = ((), (), s32[]{:S(2)}) async-start(), calls=%async_computation.5 | async-start | bytes 1114112 | tf_op jit(solution)/shard_map/all_gather | solution.py:101
  63.3 1.0 copy-start.2
  64.3 71.7 %all-to-all-start.3 = ((bf16[8,256,256]{2,1,0:T(8,128)(2,1)}), bf16[8,256,256]{2,1,0:T(8,128)(2,1)S(1)}, u32[]{:S(2)}, u32[]{:S(2)}) async-start(bf16[8,256,256]{2,1,0:T(8,128)(2,1)} %copy-done.2), calls=%async_computation.3 | async-start | bytes 2097152 | tf_op jit(solution)/shard_map/all_to_all | solution.py:127
  133.3 1.2 copy-start.3
  136.0 8.9 %all-to-all-start.2 = ((bf16[2,256,512]{2,1,0:T(8,128)(2,1)}), bf16[2,256,512]{2,1,0:T(8,128)(2,1)S(1)}, u32[]{:S(2)}, u32[]{:S(2)}) async-start(bf16[2,256,512]{2,1,0:T(8,128)(2,1)} %shard_map.69), calls=%async_computation.2 | async-start | bytes 1048576 | tf_op jit(solution)/shard_map/all_to_all | solution.py:141
  144.9 21.6 %all-to-all-start.4 = ((f32[16,16,256]{2,1,0:T(8,128)}), f32[16,16,256]{2,1,0:T(8,128)S(1)}, u32[]{:S(2)}, u32[]{:S(2)}) async-start(f32[16,16,256]{2,1,0:T(8,128)} %bitcast.7), calls=%async_computation.4 | async-start | bytes 524288 | tf_op jit(solution)/shard_map/all_to_all | solution.py:130
Sparse Core Ops, SparseCore 0:
  52.0 81.1 all-gather.1

commit v2 on v1

v2 whole, which is shorter than its diff:
```python
import functools
import math

import jax
import jax.numpy as jnp
from jax import lax
from jax.experimental import pallas as pl
from jax.experimental.pallas import tpu as pltpu
from jax.sharding import Mesh
from jax.sharding import PartitionSpec as P

FSDP = ("z", "xl", "y")
TP = ("xh", "c")
SWAP = [(0, 1), (1, 0)]
VMEM_LIMIT = 24 * 1024 * 1024
PREP_LIMIT = 60 * 1024 * 1024


def prep_kernel(place_ref, counts_ref, offsets_ref, grad_ref, inputs_ref, scaled_ref, send_ref, sems):
    half = place_ref[0]
    rows, columns = grad_ref.shape
    wide = send_ref.shape[1] - columns
    blocks = wide // 128
    copies = []
    for z in range(blocks):
        source = pl.ds(pl.multiple_of((2 * z + 1 - half) * 128, 128), 128)
        copies.append(
            pltpu.make_async_copy(
                inputs_ref.at[:, source], send_ref.at[:, pl.ds(z * 128, 128)], sems.at[z]
            )
        )
        copies[-1].start()
    positions = lax.broadcasted_iota(jnp.int32, (rows, columns), 0)
    length = jnp.zeros((rows, columns), jnp.int32)
    for s in range(counts_ref.shape[1]):
        first = offsets_ref[0, s]
        count = counts_ref[0, s]
        length = jnp.where((positions >= first) & (positions < first + count), count, length)
    factor = jnp.where(length > 0, lax.rsqrt(jnp.maximum(length, 1).astype(jnp.float32)), 0.0)
    scaled_ref[...] = (grad_ref[...].astype(jnp.float32) * factor).astype(jnp.bfloat16)
    copies.append(
        pltpu.make_async_copy(scaled_ref, send_ref.at[:, pl.ds(wide, columns)], sems.at[blocks])
    )
    copies[-1].start()
    for copy in copies:
        copy.wait()


def weight_kernel(place_ref, inputs_ref, received_ref, own_ref, out_ref):
    half = place_ref[0]
    own = own_ref[...]
    wide = received_ref.shape[1] - own.shape[1]
    peer = received_ref[:, wide:]
    peers = out_ref.shape[0]
    for z in range(wide // 128):
        mine = inputs_ref[:, pl.ds(pl.multiple_of((2 * z + half) * 128, 128), 128)]
        other = received_ref[:, z * 128 : (z + 1) * 128]
        dims = (((0,), (0,)), ((), ()))
        term = lax.dot_general(mine, own, dims, preferred_element_type=jnp.float32)
        term += lax.dot_general(other, peer, dims, preferred_element_type=jnp.float32)
        each = 128 // peers
        out_ref[:, z * each : (z + 1) * each, :] = term.reshape(peers, each, -1).astype(jnp.bfloat16)


def order_kernel(sizes, place_ref, own_ref, core_ref, far_ref, both_ref, out_ref):
    tensor = place_ref[1]
    parts = [own_ref, core_ref, far_ref, both_ref]
    wide = own_ref.shape[1]
    n_z, n_y, n_j = sizes
    total = len(parts) * wide
    spot = lax.broadcasted_iota(jnp.int32, (1, total), 1)
    j = spot % n_j
    z = (spot // n_j) % n_z
    xl = (spot // (n_j * n_z)) % 2
    y = spot // (n_j * n_z * 2)
    source = ((z * 2 + xl) * n_y + y) * n_j + j
    for c in range(0, total, 256):
        moved = None
        for p, part in enumerate(parts):
            row = lax.broadcasted_iota(jnp.int32, (wide, 256), 0) + (tensor ^ p) * wide
            pick = (row == source[:, c : c + 256]).astype(jnp.float32).astype(jnp.bfloat16)
            term = jnp.dot(part[...], pick, preferred_element_type=jnp.float32)
            moved = term if moved is None else moved + term
        out_ref[:, c : c + 256] = moved.astype(jnp.bfloat16)


def input_kernel(scaled_ref, weight_ref, own_ref, peer_ref):
    rows = own_ref.shape[0]
    for g, out_ref in enumerate((own_ref, peer_ref)):
        out_ref[...] = jnp.dot(
            scaled_ref[g * rows : (g + 1) * rows, :],
            weight_ref[...],
            preferred_element_type=jnp.float32,
        ).astype(jnp.bfloat16)


def in_vmem():
    return pl.BlockSpec(memory_space=pltpu.VMEM)


def in_smem():
    return pl.BlockSpec(memory_space=pltpu.SMEM)


def anywhere():
    return pl.BlockSpec(memory_space=pl.ANY)


PARAMS = pltpu.CompilerParams(vmem_limit_bytes=VMEM_LIMIT)


def local(inputs, value_grad, value_weight, counts, offsets):
    rows, features = inputs.shape
    columns = value_grad.shape[1]
    quarter, own_columns = value_weight.shape
    half = lax.axis_index("xl")
    n_tp = lax.axis_size(TP)
    n_z = lax.axis_size("z")
    n_y = lax.axis_size("y")
    wide = features // 2

    place = jnp.stack([half, lax.axis_index(TP)]).astype(jnp.int32)
    scaled, send = pl.pallas_call(
        prep_kernel,
        out_shape=(
            jax.ShapeDtypeStruct((rows, columns), jnp.bfloat16),
            jax.ShapeDtypeStruct((rows, wide + columns), jnp.bfloat16),
        ),
        in_specs=[in_smem(), in_smem(), in_smem(), in_vmem(), anywhere()],
        out_specs=(in_vmem(), anywhere()),
        scratch_shapes=[pltpu.SemaphoreType.DMA((wide // 128 + 1,))],
        compiler_params=pltpu.CompilerParams(vmem_limit_bytes=PREP_LIMIT),
    )(place, counts, offsets, value_grad, inputs)
    send, value_weight = lax.optimization_barrier((send, value_weight))
    received = lax.ppermute(send, "xl", SWAP)

    mine = value_weight.T.reshape(own_columns, 2, quarter // 2).transpose(1, 0, 2)
    mine = jnp.broadcast_to(mine[:, None], (2, n_z, own_columns, quarter // 2))
    mine = mine.reshape(2 * n_z, own_columns, quarter // 2)
    block = lax.all_to_all(mine, ("xl", "z"), 0, 0, tiled=True)
    block = block.reshape(2 * n_z * own_columns, quarter // 2)
    block = jnp.broadcast_to(block, (n_y, *block.shape))
    weight = lax.all_to_all(block, "y", 0, 0, tiled=True)
    weight = weight.reshape(-1, quarter // 2)

    term = pl.pallas_call(
        weight_kernel,
        out_shape=jax.ShapeDtypeStruct((n_y, wide // n_y, columns), jnp.bfloat16),
        in_specs=[in_smem(), in_vmem(), in_vmem(), in_vmem()],
        out_specs=in_vmem(),
        compiler_params=PARAMS,
    )(place, inputs, received, scaled)
    both = jnp.concatenate([scaled, received[:, wide:]])
    term, weight, both = lax.optimization_barrier((term, weight, both))
    terms = lax.all_to_all(term, "y", 0, 0, tiled=True)
    from_core = lax.ppermute(both, "c", SWAP)
    from_far = lax.ppermute(both, "xh", SWAP)
    from_both = lax.ppermute(both, TP, [(i, i ^ 3) for i in range(n_tp)])
    ordered = pl.pallas_call(
        functools.partial(order_kernel, (n_z, n_y, own_columns)),
        out_shape=jax.ShapeDtypeStruct((2 * rows, n_tp * columns), jnp.bfloat16),
        in_specs=[in_smem(), in_vmem(), in_vmem(), in_vmem(), in_vmem()],
        out_specs=in_vmem(),
        compiler_params=PARAMS,
    )(place, both, from_core, from_far, from_both)
    kept, sent = pl.pallas_call(
        input_kernel,
        out_shape=[jax.ShapeDtypeStruct((rows, quarter // 2), jnp.bfloat16)] * 2,
        in_specs=[in_vmem(), in_vmem()],
        out_specs=[in_vmem(), in_vmem()],
        compiler_params=PARAMS,
    )(ordered, weight)
    terms, sent = lax.optimization_barrier((terms, sent))
    summed = jnp.sum(terms.astype(jnp.float32), axis=0)
    summed = summed.reshape(n_z, -1, columns)
    summed = lax.all_to_all(summed, "z", 0, 0, tiled=True)
    normalizer = 1.0 / math.sqrt(counts.shape[1] * lax.axis_size(FSDP))
    weight_grad = jnp.sum(summed, axis=0) * normalizer
    other = lax.ppermute(sent, "xl", SWAP)
    low = jnp.where(half == 0, kept, other)
    high = jnp.where(half == 0, other, kept)
    input_grad = jnp.concatenate([low, high], axis=1)
    return (input_grad, weight_grad)


def solution(mesh):
    split = Mesh(mesh.devices.reshape(16, 2, 8, 2, 2), (*FSDP, *TP))
    in_specs = (P(FSDP, None), P(FSDP, TP), P(TP, FSDP), P(FSDP, None), P(FSDP, None))
    out_specs = (P(FSDP, TP), P(FSDP, TP))
    return jax.shard_map(local, mesh=split, in_specs=in_specs, out_specs=out_specs, check_vma=False)
```

time: 176 us -> 168 us (0.955)
  waiting for transfers between devices: 92.5 us -> 49.7 us
  Pallas kernels: 5.28 us -> 39.4 us
  between operations: 14.1 us -> 0.82 us
  blocking collectives: 25 us -> 35.9 us
  starting transfers between devices: 26.9 us -> 36.8 us
  local copies, waits for them, and re-layouts: 7.82 us -> 1.19 us
    all_gather x1 -> x0, waiting for transfers between devices: 63.3 us -> none  [local(): weight = lax.all_gather(block, 'z', axis=0, tiled=True)]
    ppermute x1 -> x5, waiting for transfers between devices: 0.01 us -> 34.1 us  [the longest x1 23.6 us: local(): received = lax.ppermute(send, 'xl', SWAP)]
    pallas_call x1, Pallas kernels: 1.74 us -> 34.6 us  [local(): pl.pallas_call(prep_kernel, out_shape=(jax.ShapeDtypeStruct((rows, column...]
    all_to_all x2 -> x1, waiting for transfers between devices: 16.3 us -> 0.01 us  [local(): weight = lax.all_to_all(block, 'y', 0, 0, tiled=True)]
    ppermute x1 -> x5, starting transfers between devices: 2.87 us -> 15.7 us  [the longest x1 3.86 us: local(): from_core = lax.ppermute(both, 'c', SWAP)]
    all_to_all x1, blocking collectives: 25 us -> 35.9 us  [local(): block = lax.all_to_all(mine, ('xl', 'z'), 0, 0, tiled=True)]
    all_to_all x1, waiting for transfers between devices: 0.01 us -> 7.62 us  [local(): terms = lax.all_to_all(term, 'y', 0, 0, tiled=True)]
    unnamed x16 -> x8, local copies, waits for them, and re-layouts: 6.02 us -> 0.02 us
  transfers between devices with their start and end apart: 6 -> 8, of which waited for: 4 -> 6; matrix products, arithmetic and copies ran while one was open for 2% -> 1% of each run, Pallas kernels for 2% -> 3%
where the time goes in v2:
time: 168 us; the launch traced here: 167 us
  waiting for transfers between devices  49.7 us (30%)
  Pallas kernels  39.4 us (23%)
  starting transfers between devices  36.8 us (22%)
  blocking collectives  35.9 us (21%)
  other arithmetic  3.05 us (2%)
    all_to_all x1, blocking collectives, local(): block = lax.all_to_all(mine, ('xl', 'z'), 0, 0, tiled=True)  35.9 us
    pallas_call x1, Pallas kernels, local(): pl.pallas_call(prep_kernel, out_shape=(jax.ShapeDtypeStruct((rows, column...  34.6 us
    ppermute x1, waiting for transfers between devices, local(): received = lax.ppermute(send, 'xl', SWAP)  23.6 us
    all_to_all x1, waiting for transfers between devices, local(): summed = lax.all_to_all(summed, 'z', 0, 0, tiled=True)  8.05 us
    all_to_all x1, waiting for transfers between devices, local(): terms = lax.all_to_all(term, 'y', 0, 0, tiled=True)  7.62 us
    all_to_all x1, starting transfers between devices, local(): summed = lax.all_to_all(summed, 'z', 0, 0, tiled=True)  7.12 us
    all_to_all x1, starting transfers between devices, local(): weight = lax.all_to_all(block, 'y', 0, 0, tiled=True)  7.1 us
    all_to_all x1, starting transfers between devices, local(): terms = lax.all_to_all(term, 'y', 0, 0, tiled=True)  6.94 us
  transfers between devices with their start and end apart: 8, of which 6 were waited for; matrix products, arithmetic and copies ran while one was open for 1% of the time, Pallas kernels for 3%

profile of v2, /device:TPU:6, one launch (start us, length us, event | category | flops | bytes accessed | tf_op | source)
XLA Modules:
  0.0 167.0 jit_solution(6373511076000401954)
XLA Ops:
  0.6 0.0 copy-start.3
  0.6 0.7 pad_add_fusion.place_ref
  1.3 34.6 %shard_map.68 = (bf16[256,256]{1,0:T(8,128)(2,1)}, bf16[256,2304]{1,0:T(8,128)(2,1)}) custom-call(s32[2]{0:T(128)} %pad_add_fusion.place_ref, s32[1,4]{1,0:T(1,128)} %counts_ref.1, s32[1,4]{1,0:T(1,128)} %offsets_ref.1, bf16[256,256]{1,0:T(8,128)(2,1)} %grad_ref.1, bf16[256,4096]{1,0:T(8,128)(2,1)} %inputs_ref.3), custom_call_target="tpu_custom_call" | custom-call | tf_op jit(solution)/shard_map/pallas_call | solution.py:123
  35.9 0.0 copy-done.3
  35.9 0.0 copy-start
  35.9 0.0 copy-start.1
  36.0 0.0 copy-start.2
  36.0 35.9 %all_to_all.20 = bf16[32,4,512]{2,1,0:T(4,128)(2,1)S(1)} all-to-all(bf16[32,4,512]{2,1,0:T(4,128)(2,1)S(1)} %bitcast.8), channel_id=1, replica_groups=mesh['z'=16,'xl'=2,'y'=8,'xh'=2,'c'=2] {'xl','z'}, dimensions={0} | all-to-all | bytes 262144 | tf_op jit(solution)/shard_map/all_to_all | solution.py:140
  71.9 1.1 broadcast_in_dim.10
  73.0 7.1 %all-to-all-start.1 = ((bf16[8,128,512]{2,1,0:T(8,128)(2,1)}), bf16[8,128,512]{2,1,0:T(8,128)(2,1)S(1)}, u32[]{:S(2)}, u32[]{:S(2)}) async-start(bf16[8,128,512]{2,1,0:T(8,128)(2,1)} %broadcast_in_dim.10), calls=%async_computation.1 | async-start | bytes 2097152 | tf_op jit(solution)/shard_map/all_to_all | solution.py:143
  80.1 3.4 %collective-permute-start = (bf16[256,2304]{1,0:T(8,128)(2,1)}, bf16[256,2304]{1,0:T(8,128)(2,1)S(1)}, u32[]{:S(2)}, u32[]{:S(2)}) collective-permute-start(bf16[256,2304]{1,0:T(8,128)(2,1)} %get-tuple-element.14), channel_id=1, source_target_pairs={{0,32},{32,0},{1,33},{33,1},{2,34},{34,2},{3,35},{35,3},{4,36},{36... | collective-permute-start | bytes 3538952 | tf_op jit(solution)/shard_map/ppermute | solution.py:135
  83.5 23.6 %collective-permute-done.received_ref = bf16[256,2304]{1,0:T(8,128)(2,1)S(1)} collective-permute-done((bf16[256,2304]{1,0:T(8,128)(2,1)}, bf16[256,2304]{1,0:T(8,128)(2,1)S(1)}, u32[]{:S(2)}, u32[]{:S(2)}) %collective-permute-start) | collective-permute-done | bytes 1179680 | tf_op jit(solution)/shard_map/ppermute | solution.py:135
  107.1 0.0 copy-done
  107.1 0.0 copy-done.1
  107.1 0.0 copy-done.2
  107.1 2.3 %shard_map.69 = bf16[8,256,256]{2,1,0:T(8,128)(2,1)} custom-call(s32[2]{0:T(128)S(1)} %copy-done.2, bf16[256,4096]{1,0:T(8,128)(2,1)S(1)} %copy-done, bf16[256,2304]{1,0:T(8,128)(2,1)S(1)} %collective-permute-done.received_ref, bf16[256,256]{1,0:T(8,128)(2,1)S(1)} %copy-done.1), custom_call_target="tpu_custom_call" | custom-call | tf_op jit(solution)/shard_map/pallas_call | solution.py:146
  109.5 0.0 all-to-all-done.1
  109.5 6.9 %all-to-all-start.2 = ((bf16[8,256,256]{2,1,0:T(8,128)(2,1)}), bf16[8,256,256]{2,1,0:T(8,128)(2,1)S(1)}, u32[]{:S(2)}, u32[]{:S(2)}) async-start(bf16[8,256,256]{2,1,0:T(8,128)(2,1)} %shard_map.69), calls=%async_computation.2 | async-start | bytes 2097152 | tf_op jit(solution)/shard_map/all_to_all | solution.py:155
  116.4 1.9 %collective-permute-start.3 = (bf16[512,256]{1,0:T(8,128)(2,1)S(1)}, bf16[512,256]{1,0:T(8,128)(2,1)S(1)}, u32[]{:S(2)}, u32[]{:S(2)}) collective-permute-start(bf16[512,256]{1,0:T(8,128)(2,1)S(1)} %pad_maximum_fusion.1.own_ref), channel_id=1, source_target_pairs={{0,3},{1,2},{2,1},{3,0},{4,7},{5,6},{6,5},{7,4},{8,11},{9,10},{10,... | collective-permute-start | bytes 786440 | tf_op jit(solution)/shard_map/ppermute | solution.py:158
  118.3 3.3 %collective-permute-start.2 = (bf16[512,256]{1,0:T(8,128)(2,1)S(1)}, bf16[512,256]{1,0:T(8,128)(2,1)S(1)}, u32[]{:S(2)}, u32[]{:S(2)}) collective-permute-start(bf16[512,256]{1,0:T(8,128)(2,1)S(1)} %pad_maximum_fusion.1.own_ref), channel_id=1, source_target_pairs={{0,2},{2,0},{1,3},{3,1},{4,6},{6,4},{5,7},{7,5},{8,10},{10,8},{9,1... | collective-permute-start | bytes 786440 | tf_op jit(solution)/shard_map/ppermute | solution.py:157
  121.6 3.9 %collective-permute-start.1 = (bf16[512,256]{1,0:T(8,128)(2,1)S(1)}, bf16[512,256]{1,0:T(8,128)(2,1)S(1)}, u32[]{:S(2)}, u32[]{:S(2)}) collective-permute-start(bf16[512,256]{1,0:T(8,128)(2,1)S(1)} %pad_maximum_fusion.1.own_ref), channel_id=1, source_target_pairs={{0,1},{1,0},{2,3},{3,2},{4,5},{5,4},{6,7},{7,6},{8,9},{9,8},{10,11... | collective-permute-start | bytes 786440 | tf_op jit(solution)/shard_map/ppermute | solution.py:156
  125.5 2.9 %collective-permute-done.3.both_ref = bf16[512,256]{1,0:T(8,128)(2,1)S(1)} collective-permute-done((bf16[512,256]{1,0:T(8,128)(2,1)S(1)}, bf16[512,256]{1,0:T(8,128)(2,1)S(1)}, u32[]{:S(2)}, u32[]{:S(2)}) %collective-permute-start.3) | collective-permute-done | bytes 262176 | tf_op jit(solution)/shard_map/ppermute | solution.py:158
  128.4 2.6 %collective-permute-done.2.far_ref = bf16[512,256]{1,0:T(8,128)(2,1)S(1)} collective-permute-done((bf16[512,256]{1,0:T(8,128)(2,1)S(1)}, bf16[512,256]{1,0:T(8,128)(2,1)S(1)}, u32[]{:S(2)}, u32[]{:S(2)}) %collective-permute-start.2) | collective-permute-done | bytes 262176 | tf_op jit(solution)/shard_map/ppermute | solution.py:157
  131.0 0.0 collective-permute-done.1.core_ref
  131.0 1.8 %shard_map.70.scaled_ref = bf16[512,1024]{1,0:T(8,128)(2,1)S(1)} custom-call(s32[2]{0:T(128)S(1)} %copy-done.2, bf16[512,256]{1,0:T(8,128)(2,1)S(1)} %pad_maximum_fusion.1.own_ref, bf16[512,256]{1,0:T(8,128)(2,1)S(1)} %collective-permute-done.1.core_ref, bf16[512,256]{1,0:T(8,128)(2,1)S(1)} %collective-permute-done.2.far_ref, ...), custom_call_target="tpu_custom_call" | custom-call | tf_op jit(solution)/shard_map/pallas_call | solution.py:159
  132.8 0.7 shard_map.71
  133.5 7.6 %all-to-all-done.2 = bf16[8,256,256]{2,1,0:T(8,128)(2,1)S(1)} async-done(((bf16[8,256,256]{2,1,0:T(8,128)(2,1)}), bf16[8,256,256]{2,1,0:T(8,128)(2,1)S(1)}, u32[]{:S(2)}, u32[]{:S(2)}) %all-to-all-start.2) | async-done | bytes 1048608 | tf_op jit(solution)/shard_map/all_to_all | solution.py:155
  141.1 0.8 convert_reduce_fusion
  142.0 7.1 %all-to-all-start.3 = ((f32[16,16,256]{2,1,0:T(8,128)}), f32[16,16,256]{2,1,0:T(8,128)S(1)}, u32[]{:S(2)}, u32[]{:S(2)}) async-start(f32[16,16,256]{2,1,0:T(8,128)} %bitcast.6), calls=%async_computation.3 | async-start | bytes 524288 | tf_op jit(solution)/shard_map/all_to_all | solution.py:176
  149.1 3.2 %collective-permute-start.4 = (bf16[256,512]{1,0:T(8,128)(2,1)S(1)}, bf16[256,512]{1,0:T(8,128)(2,1)S(1)}, u32[]{:S(2)}, u32[]{:S(2)}) collective-permute-start(bf16[256,512]{1,0:T(8,128)(2,1)S(1)} %get-tuple-element.22), channel_id=1, source_target_pairs={{0,32},{32,0},{1,33},{33,1},{2,34},{34,2},{3,35},{35,3},{4,36},{36... | collective-permute-start | bytes 786440 | tf_op jit(solution)/shard_map/ppermute | solution.py:179
  152.3 5.1 %collective-permute-done.4 = bf16[256,512]{1,0:T(8,128)(2,1)S(1)} collective-permute-done((bf16[256,512]{1,0:T(8,128)(2,1)S(1)}, bf16[256,512]{1,0:T(8,128)(2,1)S(1)}, u32[]{:S(2)}, u32[]{:S(2)}) %collective-permute-start.4) | collective-permute-done | bytes 262176 | tf_op jit(solution)/shard_map/ppermute | solution.py:179
  157.4 0.9 pad_maximum_fusion
  158.3 8.0 %all-to-all-done.3 = f32[16,16,256]{2,1,0:T(8,128)S(1)} async-done(((f32[16,16,256]{2,1,0:T(8,128)}), f32[16,16,256]{2,1,0:T(8,128)S(1)}, u32[]{:S(2)}, u32[]{:S(2)}) %all-to-all-start.3) | async-done | bytes 262176 | tf_op jit(solution)/shard_map/all_to_all | solution.py:176
  166.4 0.6 broadcast_multiply_fusion
  (8 shorter events, 0.2 us)
Async XLA Ops:
  0.6 35.3 %copy-start.3 = (bf16[1024,4]{0,1:T(4,128)(2,1)S(1)}, bf16[1024,4]{0,1:T(4,128)(2,1)}, u32[]{:S(2)}) copy-start(bf16[1024,4]{0,1:T(4,128)(2,1)} %param.7) | copy-start | bytes 24580
  35.9 71.2 %copy-start = (bf16[256,4096]{1,0:T(8,128)(2,1)S(1)}, bf16[256,4096]{1,0:T(8,128)(2,1)}, u32[]{:S(2)}) copy-start(bf16[256,4096]{1,0:T(8,128)(2,1)} %inputs_ref.3) | copy-start | bytes 6291460
  35.9 71.2 %copy-start.1 = (bf16[256,256]{1,0:T(8,128)(2,1)S(1)}, bf16[256,256]{1,0:T(8,128)(2,1)}, u32[]{:S(2)}) copy-start(bf16[256,256]{1,0:T(8,128)(2,1)} %get-tuple-element.15.own_ref) | copy-start | bytes 393220
  36.0 71.2 %copy-start.2 = (s32[2]{0:T(128)S(1)}, s32[2]{0:T(128)}, u32[]{:S(2)}) copy-start(s32[2]{0:T(128)} %pad_add_fusion.place_ref) | copy-start | bytes 28
  73.0 36.5 %all-to-all-start.1 = ((bf16[8,128,512]{2,1,0:T(8,128)(2,1)}), bf16[8,128,512]{2,1,0:T(8,128)(2,1)S(1)}, u32[]{:S(2)}, u32[]{:S(2)}) async-start(bf16[8,128,512]{2,1,0:T(8,128)(2,1)} %broadcast_in_dim.10), calls=%async_computation.1 | async-start | bytes 2097152 | tf_op jit(solution)/shard_map/all_to_all | solution.py:143
  80.1 27.0 %collective-permute-start = (bf16[256,2304]{1,0:T(8,128)(2,1)}, bf16[256,2304]{1,0:T(8,128)(2,1)S(1)}, u32[]{:S(2)}, u32[]{:S(2)}) collective-permute-start(bf16[256,2304]{1,0:T(8,128)(2,1)} %get-tuple-element.14), channel_id=1, source_target_pairs={{0,32},{32,0},{1,33},{33,1},{2,34},{34,2},{3,35},{35,3},{4,36},{36... | collective-permute-start | bytes 3538952 | tf_op jit(solution)/shard_map/ppermute | solution.py:135
  109.5 31.7 %all-to-all-start.2 = ((bf16[8,256,256]{2,1,0:T(8,128)(2,1)}), bf16[8,256,256]{2,1,0:T(8,128)(2,1)S(1)}, u32[]{:S(2)}, u32[]{:S(2)}) async-start(bf16[8,256,256]{2,1,0:T(8,128)(2,1)} %shard_map.69), calls=%async_computation.2 | async-start | bytes 2097152 | tf_op jit(solution)/shard_map/all_to_all | solution.py:155
  116.4 12.0 %collective-permute-start.3 = (bf16[512,256]{1,0:T(8,128)(2,1)S(1)}, bf16[512,256]{1,0:T(8,128)(2,1)S(1)}, u32[]{:S(2)}, u32[]{:S(2)}) collective-permute-start(bf16[512,256]{1,0:T(8,128)(2,1)S(1)} %pad_maximum_fusion.1.own_ref), channel_id=1, source_target_pairs={{0,3},{1,2},{2,1},{3,0},{4,7},{5,6},{6,5},{7,4},{8,11},{9,10},{10,... | collective-permute-start | bytes 786440 | tf_op jit(solution)/shard_map/ppermute | solution.py:158
  118.3 12.6 %collective-permute-start.2 = (bf16[512,256]{1,0:T(8,128)(2,1)S(1)}, bf16[512,256]{1,0:T(8,128)(2,1)S(1)}, u32[]{:S(2)}, u32[]{:S(2)}) collective-permute-start(bf16[512,256]{1,0:T(8,128)(2,1)S(1)} %pad_maximum_fusion.1.own_ref), channel_id=1, source_target_pairs={{0,2},{2,0},{1,3},{3,1},{4,6},{6,4},{5,7},{7,5},{8,10},{10,8},{9,1... | collective-permute-start | bytes 786440 | tf_op jit(solution)/shard_map/ppermute | solution.py:157
  121.6 9.3 %collective-permute-start.1 = (bf16[512,256]{1,0:T(8,128)(2,1)S(1)}, bf16[512,256]{1,0:T(8,128)(2,1)S(1)}, u32[]{:S(2)}, u32[]{:S(2)}) collective-permute-start(bf16[512,256]{1,0:T(8,128)(2,1)S(1)} %pad_maximum_fusion.1.own_ref), channel_id=1, source_target_pairs={{0,1},{1,0},{2,3},{3,2},{4,5},{5,4},{6,7},{7,6},{8,9},{9,8},{10,11... | collective-permute-start | bytes 786440 | tf_op jit(solution)/shard_map/ppermute | solution.py:156
  142.0 24.3 %all-to-all-start.3 = ((f32[16,16,256]{2,1,0:T(8,128)}), f32[16,16,256]{2,1,0:T(8,128)S(1)}, u32[]{:S(2)}, u32[]{:S(2)}) async-start(f32[16,16,256]{2,1,0:T(8,128)} %bitcast.6), calls=%async_computation.3 | async-start | bytes 524288 | tf_op jit(solution)/shard_map/all_to_all | solution.py:176
  149.1 8.3 %collective-permute-start.4 = (bf16[256,512]{1,0:T(8,128)(2,1)S(1)}, bf16[256,512]{1,0:T(8,128)(2,1)S(1)}, u32[]{:S(2)}, u32[]{:S(2)}) collective-permute-start(bf16[256,512]{1,0:T(8,128)(2,1)S(1)} %get-tuple-element.22), channel_id=1, source_target_pairs={{0,32},{32,0},{1,33},{33,1},{2,34},{34,2},{3,35},{35,3},{4,36},{36... | collective-permute-start | bytes 786440 | tf_op jit(solution)/shard_map/ppermute | solution.py:179

commit v3 on v0

v3 whole, which is shorter than its diff:
```python
import functools
import math

import jax
import jax.numpy as jnp
from jax import lax
from jax.experimental import pallas as pl
from jax.experimental.pallas import tpu as pltpu
from jax.sharding import Mesh
from jax.sharding import PartitionSpec as P

FSDP = ("zh", "zl", "xl", "y")
TP = ("xh", "c")
SWAP = [(0, 1), (1, 0)]
BOTH = [(i, i ^ 3) for i in range(4)]
MIB = 1024 * 1024


def prep_kernel(place_ref, counts_ref, offsets_ref, grad_ref, inputs_ref, *outs):
    q = place_ref[0]
    rows, columns = grad_ref.shape
    blocks = (outs[0].shape[1] - columns) // 128
    positions = lax.broadcasted_iota(jnp.int32, (rows, columns), 0)
    length = jnp.zeros((rows, columns), jnp.int32)
    for s in range(counts_ref.shape[1]):
        first = offsets_ref[0, s]
        count = counts_ref[0, s]
        length = jnp.where((positions >= first) & (positions < first + count), count, length)
    factor = jnp.where(length > 0, lax.rsqrt(jnp.maximum(length, 1).astype(jnp.float32)), 0.0)
    scaled = (grad_ref[...].astype(jnp.float32) * factor).astype(jnp.bfloat16)
    for m, out_ref in enumerate(outs):
        target = q ^ m
        for b in range(blocks):
            source = pl.ds(pl.multiple_of((4 * b + target) * 128, 128), 128)
            out_ref[:, b * 128 : (b + 1) * 128] = inputs_ref[:, source]
        out_ref[:, blocks * 128 :] = scaled


def weight_kernel(*refs):
    parts, out_ref = refs[:4], refs[4]
    peers, _, columns = out_ref.shape
    wide = parts[0].shape[1] - columns
    each = 128 // peers
    for b in range(wide // 128):
        term = None
        for part in parts:
            product = lax.dot_general(
                part[:, b * 128 : (b + 1) * 128],
                part[:, wide:],
                (((0,), (0,)), ((), ())),
                preferred_element_type=jnp.float32,
            )
            term = product if term is None else term + product
        out_ref[:, b * each : (b + 1) * each, :] = term.reshape(peers, each, -1).astype(jnp.bfloat16)


def order_kernel(sizes, place_ref, own_ref, core_ref, far_ref, both_ref, out_ref):
    tensor = place_ref[1]
    parts = [own_ref, core_ref, far_ref, both_ref]
    wide = own_ref.shape[1]
    n_z, n_y, n_j = sizes
    total = len(parts) * wide
    spot = lax.broadcasted_iota(jnp.int32, (1, total), 1)
    j = spot % n_j
    z = (spot // n_j) % n_z
    xl = (spot // (n_j * n_z)) % 2
    y = spot // (n_j * n_z * 2)
    source = ((z * 2 + xl) * n_y + y) * n_j + j
    for c in range(0, total, 256):
        moved = None
        for p, part in enumerate(parts):
            row = lax.broadcasted_iota(jnp.int32, (wide, 256), 0) + (tensor ^ p) * wide
            pick = (row == source[:, c : c + 256]).astype(jnp.float32).astype(jnp.bfloat16)
            term = jnp.dot(part[...], pick, preferred_element_type=jnp.float32)
            moved = term if moved is None else moved + term
        out_ref[:, c : c + 256] = moved.astype(jnp.bfloat16)


def input_kernel(scaled_ref, weight_ref, *outs):
    rows = outs[0].shape[0]
    for m, out_ref in enumerate(outs):
        out_ref[...] = jnp.dot(
            scaled_ref[m * rows : (m + 1) * rows, :],
            weight_ref[...],
            preferred_element_type=jnp.float32,
        ).astype(jnp.bfloat16)


def join_kernel(place_ref, *refs):
    parts, out_ref = refs[:4], refs[4]
    wide = parts[0].shape[1]
    for m, part in enumerate(parts):
        place = pl.multiple_of((place_ref[0] ^ m) * wide, 128)
        out_ref[:, pl.ds(place, wide)] = part[...]


def call(kernel, outs, n_smem, *args, vmem=24 * MIB):
    shapes = [jax.ShapeDtypeStruct(shape, jnp.bfloat16) for shape in outs]
    spaces = [pltpu.SMEM] * n_smem + [pltpu.VMEM] * (len(args) - n_smem)
    return pl.pallas_call(
        kernel,
        out_shape=shapes,
        in_specs=[pl.BlockSpec(memory_space=space) for space in spaces],
        out_specs=[pl.BlockSpec(memory_space=pltpu.VMEM)] * len(outs),
        compiler_params=pltpu.CompilerParams(vmem_limit_bytes=vmem),
    )(*args)


def from_group(blocks):
    return [
        blocks[0],
        lax.ppermute(blocks[1], "xl", SWAP),
        lax.ppermute(blocks[2], "zl", SWAP),
        lax.ppermute(blocks[3], ("zl", "xl"), BOTH),
    ]


def local(inputs, value_grad, value_weight, counts, offsets):
    rows, features = inputs.shape
    columns = value_grad.shape[1]
    quarter, own_columns = value_weight.shape
    n_tp, n_y, n_zh = (lax.axis_size(a) for a in (TP, "y", "zh"))
    wide = features // 4
    narrow = quarter // 4

    place = jnp.stack([lax.axis_index(("zl", "xl")), lax.axis_index(TP)]).astype(jnp.int32)
    args = (place, counts, offsets, value_grad, inputs)
    blocks = call(prep_kernel, [(rows, wide + columns)] * 4, 3, *args, vmem=60 * MIB)
    blocks, value_weight = lax.optimization_barrier((blocks, value_weight))
    received = from_group(blocks)

    mine = value_weight.T.reshape(own_columns, 2, 2, narrow).transpose(2, 1, 0, 3)
    mine = jnp.broadcast_to(mine[:, None], (2, n_zh, 2, own_columns, narrow))
    mine = mine.reshape(-1, own_columns, narrow)
    block = lax.all_to_all(mine, ("xl", "zh", "zl"), 0, 0, tiled=True)
    received, block = lax.optimization_barrier((received, block))
    block = block.reshape(-1, narrow)
    block = jnp.broadcast_to(block, (n_y, *block.shape))
    weight = lax.all_to_all(block, "y", 0, 0, tiled=True).reshape(-1, narrow)

    (term,) = call(weight_kernel, [(n_y, wide // n_y, columns)], 0, *received)
    own = jnp.concatenate([part[:, wide:] for part in received])
    gathered = [
        own,
        lax.ppermute(own, "c", SWAP),
        lax.ppermute(own, "xh", SWAP),
        lax.ppermute(own, TP, BOTH),
    ]
    term, weight, gathered = lax.optimization_barrier((term, weight, gathered))
    terms = lax.all_to_all(term, "y", 0, 0, tiled=True)

    sizes = (2 * n_zh, n_y, own_columns)
    kernel = functools.partial(order_kernel, sizes)
    (ordered,) = call(kernel, [(4 * rows, n_tp * columns)], 1, place, *gathered)
    outs = call(input_kernel, [(rows, narrow)] * 4, 0, ordered, weight)

    terms, outs = lax.optimization_barrier((terms, outs))
    summed = jnp.sum(terms.astype(jnp.float32), axis=0).reshape(n_zh, -1, columns)
    summed = lax.all_to_all(summed, "zh", 0, 0, tiled=True)
    normalizer = 1.0 / math.sqrt(counts.shape[1] * lax.axis_size(FSDP))
    weight_grad = jnp.sum(summed, axis=0) * normalizer

    (input_grad,) = call(join_kernel, [(rows, quarter)], 1, place, *from_group(outs))
    return (input_grad, weight_grad)


def solution(mesh):
    split = Mesh(mesh.devices.reshape(8, 2, 2, 8, 2, 2), (*FSDP, *TP))
    in_specs = (P(FSDP, None), P(FSDP, TP), P(TP, FSDP), P(FSDP, None), P(FSDP, None))
    out_specs = (P(FSDP, TP), P(FSDP, TP))
    return jax.shard_map(local, mesh=split, in_specs=in_specs, out_specs=out_specs, check_vma=False)
```

time: 202 us -> 150 us (0.74)
  waiting for transfers between devices: 95 us -> 32.8 us
  starting transfers between devices: 5.39 us -> 49.4 us
  local copies, waits for them, and re-layouts: 21.6 us -> 5.77 us
  between operations: 15.7 us -> 0.88 us
  Pallas kernels: 0 us -> 10.3 us
  matrix products: 5.79 us -> 0 us
  blocking collectives: 51.2 us -> 45.7 us
  other arithmetic: 4.54 us -> 1.99 us
    reduce_scatter x3 -> x0, waiting for transfers between devices: 95 us -> none  [own_block(): parts = lax.psum_scatter(parts, axes[k], scatter_dimension=0, tiled=True)]
    all_gather x2 -> x0, blocking collectives: 51.2 us -> none  [stacked_from(): parts = lax.all_gather(parts, axes[k], axis=0, tiled=True)]
    all_to_all x0 -> x1, blocking collectives: none -> 45.7 us  [local(): block = lax.all_to_all(mine, ('xl', 'zh', 'zl'), 0, 0, tiled=True)]
    ppermute x0 -> x9, starting transfers between devices: none -> 28 us  [the longest x2 7.16 us: from_group(): lax.ppermute(blocks[2], 'zl', SWAP)]
    ppermute x0 -> x9, waiting for transfers between devices: none -> 19.2 us  [the longest x1 8.03 us: local(): lax.ppermute(own, 'xh', SWAP)]
    all_to_all x1 -> x3, starting transfers between devices: 5.27 us -> 21.4 us  [the longest x1 7.2 us: local(): terms = lax.all_to_all(term, 'y', 0, 0, tiled=True)]
    all_to_all x1 -> x3, waiting for transfers between devices: 0.01 us -> 13.5 us  [the longest x1 13.2 us: local(): terms = lax.all_to_all(term, 'y', 0, 0, tiled=True)]
    transpose x3 -> x1, local copies, waits for them, and re-layouts: 10.5 us -> 0.01 us  [local(): value_weight.T.reshape(own_columns, 2, 2, narrow).transpose(2, 1, 0, 3)]
  transfers between devices with their start and end apart: 5 -> 12, of which waited for: 3 -> 6; matrix products, arithmetic and copies ran while one was open for 7% -> 0% of each run, Pallas kernels for 0% -> 4%
where the time goes in v3:
time: 150 us; the launch traced here: 147 us
  starting transfers between devices  49.4 us (33%)
  blocking collectives  45.7 us (30%)
  waiting for transfers between devices  32.8 us (22%)
  Pallas kernels  10.3 us (7%)
  local copies, waits for them, and re-layouts  5.77 us (4%)
  other arithmetic  1.99 us (1%)
    all_to_all x1, blocking collectives, local(): block = lax.all_to_all(mine, ('xl', 'zh', 'zl'), 0, 0, tiled=True)  45.7 us
    all_to_all x1, waiting for transfers between devices, local(): terms = lax.all_to_all(term, 'y', 0, 0, tiled=True)  13.2 us
    pallas_call x5, Pallas kernels, call(): pl.pallas_call(kernel, out_shape=shapes, in_specs=[pl.BlockSpec(memory_sp...  10.3 us
    ppermute x1, waiting for transfers between devices, local(): lax.ppermute(own, 'xh', SWAP)  8.03 us
    all_to_all x1, starting transfers between devices, local(): terms = lax.all_to_all(term, 'y', 0, 0, tiled=True)  7.2 us
    ppermute x2, starting transfers between devices, from_group(): lax.ppermute(blocks[2], 'zl', SWAP)  7.16 us
    all_to_all x1, starting transfers between devices, local(): weight = lax.all_to_all(block, 'y', 0, 0, tiled=True).reshape(-1, narrow)  7.1 us
    all_to_all x1, starting transfers between devices, local(): summed = lax.all_to_all(summed, 'zh', 0, 0, tiled=True)  7.1 us
  transfers between devices with their start and end apart: 12, of which 6 were waited for; matrix products, arithmetic and copies ran while one was open for 0% of the time, Pallas kernels for 4%

profile of v3, /device:TPU:6, one launch (start us, length us, event | category | flops | bytes accessed | tf_op | source)
XLA Modules:
  0.0 146.8 jit_solution(12865540685274428422)
XLA Ops:
  0.6 0.0 copy-start.8
  0.6 0.6 pad_add_fusion.place_ref
  1.3 3.7 %shard_map.68 = (bf16[256,1280]{1,0:T(8,128)(2,1)}, bf16[256,1280]{1,0:T(8,128)(2,1)}, bf16[256,1280]{1,0:T(8,128)(2,1)}, bf16[256,1280]{1,0:T(8,128)(2,1)}) custom-call(s32[2]{0:T(128)} %pad_add_fusion.place_ref, s32[1,4]{1,0:T(1,128)} %counts_ref.1, s32[1,4]{1,0:T(1,128)} %offsets_ref.1, bf16[256,256]{1,0:T(8,128)(2,1)} %grad_ref.1, ...), custom_call_target="tpu_custom_call" | custom-call | tf_op jit(solution)/shard_map/pallas_call | solution.py:100
  5.0 0.0 copy-start
  5.0 2.9 %collective-permute-start = (bf16[256,1280]{1,0:T(8,128)(2,1)}, bf16[256,1280]{1,0:T(8,128)(2,1)S(1)}, u32[]{:S(2)}, u32[]{:S(2)}) collective-permute-start(bf16[256,1280]{1,0:T(8,128)(2,1)} %get-tuple-element.36), channel_id=1, source_target_pairs={{0,32},{32,0},{1,33},{33,1},{2,34},{34,2},{3,35},{35,3},{4,36},{36... | collective-permute-start | bytes 1966088 | tf_op jit(solution)/shard_map/ppermute | solution.py:112
  7.9 4.3 %collective-permute-start.1 = (bf16[256,1280]{1,0:T(8,128)(2,1)}, bf16[256,1280]{1,0:T(8,128)(2,1)S(1)}, u32[]{:S(2)}, u32[]{:S(2)}) collective-permute-start(bf16[256,1280]{1,0:T(8,128)(2,1)} %get-tuple-element.37), channel_id=1, source_target_pairs={{0,64},{64,0},{1,65},{65,1},{2,66},{66,2},{3,67},{67,3},{4,68},{68... | collective-permute-start | bytes 1966088 | tf_op jit(solution)/shard_map/ppermute | solution.py:113
  12.2 2.6 %collective-permute-start.2 = (bf16[256,1280]{1,0:T(8,128)(2,1)}, bf16[256,1280]{1,0:T(8,128)(2,1)S(1)}, u32[]{:S(2)}, u32[]{:S(2)}) collective-permute-start(bf16[256,1280]{1,0:T(8,128)(2,1)} %get-tuple-element.38), channel_id=1, source_target_pairs={{0,96},{32,64},{64,32},{96,0},{1,97},{33,65},{65,33},{97,1},{2,98}... | collective-permute-start | bytes 1966088 | tf_op jit(solution)/shard_map/ppermute | solution.py:114
  14.7 0.0 copy-done.8
  14.8 45.7 %all_to_all.20 = bf16[32,4,256]{2,1,0:T(4,128)(2,1)S(1)} all-to-all(bf16[32,4,256]{2,1,0:T(4,128)(2,1)S(1)} %bitcast.8), channel_id=1, replica_groups=mesh['zh'=8,'zl'=2,'xl'=2,'y'=8,'xh'=2,'c'=2] {'xl','zh','zl'}, dimensions={0} | all-to-all | bytes 131072 | tf_op jit(solution)/shard_map/all_to_all | solution.py:135
  60.5 0.0 collective-permute-done.refs_1_
  60.5 0.0 collective-permute-done.1.refs_2_
  60.5 0.0 collective-permute-done.2.refs_3_
  60.5 0.0 copy-start.1
  60.6 0.9 broadcast_in_dim.10
  61.5 7.1 %all-to-all-start.1 = ((bf16[8,128,256]{2,1,0:T(8,128)(2,1)}), bf16[8,128,256]{2,1,0:T(8,128)(2,1)S(1)}, u32[]{:S(2)}, u32[]{:S(2)}) async-start(bf16[8,128,256]{2,1,0:T(8,128)(2,1)} %broadcast_in_dim.10), calls=%async_computation.1 | async-start | bytes 1048576 | tf_op jit(solution)/shard_map/all_to_all | solution.py:139
  68.6 0.0 copy-done
  68.6 0.0 copy-done.1
  68.7 0.0 copy-start.7
  68.7 1.9 %collective-permute-start.5 = (bf16[1024,256]{1,0:T(8,128)(2,1)S(1)}, bf16[1024,256]{1,0:T(8,128)(2,1)S(1)}, u32[]{:S(2)}, u32[]{:S(2)}) collective-permute-start(bf16[1024,256]{1,0:T(8,128)(2,1)S(1)} %pad_maximum_fusion.own_ref), channel_id=1, source_target_pairs={{0,3},{1,2},{2,1},{3,0},{4,7},{5,6},{6,5},{7,4},{8,11},{9,10},{10,... | collective-permute-start | bytes 1572872 | tf_op jit(solution)/shard_map/ppermute | solution.py:147
  70.7 3.3 %collective-permute-start.4 = (bf16[1024,256]{1,0:T(8,128)(2,1)S(1)}, bf16[1024,256]{1,0:T(8,128)(2,1)S(1)}, u32[]{:S(2)}, u32[]{:S(2)}) collective-permute-start(bf16[1024,256]{1,0:T(8,128)(2,1)S(1)} %pad_maximum_fusion.own_ref), channel_id=1, source_target_pairs={{0,2},{2,0},{1,3},{3,1},{4,6},{6,4},{5,7},{7,5},{8,10},{10,8},{9,1... | collective-permute-start | bytes 1572872 | tf_op jit(solution)/shard_map/ppermute | solution.py:146
  74.0 3.9 %collective-permute-start.3 = (bf16[1024,256]{1,0:T(8,128)(2,1)S(1)}, bf16[1024,256]{1,0:T(8,128)(2,1)S(1)}, u32[]{:S(2)}, u32[]{:S(2)}) collective-permute-start(bf16[1024,256]{1,0:T(8,128)(2,1)S(1)} %pad_maximum_fusion.own_ref), channel_id=1, source_target_pairs={{0,1},{1,0},{2,3},{3,2},{4,5},{5,4},{6,7},{7,6},{8,9},{9,8},{10,11... | collective-permute-start | bytes 1572872 | tf_op jit(solution)/shard_map/ppermute | solution.py:145
  77.8 0.0 copy-start.2
  77.8 1.1 copy-done.2
  78.9 1.6 %shard_map.69 = bf16[8,128,256]{2,1,0:T(8,128)(2,1)} custom-call(bf16[256,1280]{1,0:T(8,128)(2,1)S(1)} %copy-done, bf16[256,1280]{1,0:T(8,128)(2,1)S(1)} %collective-permute-done.refs_1_, bf16[256,1280]{1,0:T(8,128)(2,1)S(1)} %collective-permute-done.1.refs_2_, bf16[256,1280]{1,0:T(8,128)(2,1)S(1)} %copy-done.2), custom_call_target="tpu_custom_call" | custom-call | tf_op jit(solution)/shard_map/pallas_call | solution.py:100
  80.5 5.9 %collective-permute-done.5.both_ref = bf16[1024,256]{1,0:T(8,128)(2,1)S(1)} collective-permute-done((bf16[1024,256]{1,0:T(8,128)(2,1)S(1)}, bf16[1024,256]{1,0:T(8,128)(2,1)S(1)}, u32[]{:S(2)}, u32[]{:S(2)}) %collective-permute-start.5) | collective-permute-done | bytes 524320 | tf_op jit(solution)/shard_map/ppermute | solution.py:147
  86.4 8.0 %collective-permute-done.4.far_ref = bf16[1024,256]{1,0:T(8,128)(2,1)S(1)} collective-permute-done((bf16[1024,256]{1,0:T(8,128)(2,1)S(1)}, bf16[1024,256]{1,0:T(8,128)(2,1)S(1)}, u32[]{:S(2)}, u32[]{:S(2)}) %collective-permute-start.4) | collective-permute-done | bytes 524320 | tf_op jit(solution)/shard_map/ppermute | solution.py:146
  94.4 0.0 copy-start.3
  94.4 0.8 copy-done.3
  95.2 0.0 collective-permute-done.3.core_ref
  95.2 0.0 copy-start.5
  95.2 0.8 copy-done.5
  96.0 0.0 all-to-all-done.1
  96.0 7.2 %all-to-all-start.2 = ((bf16[8,128,256]{2,1,0:T(8,128)(2,1)}), bf16[8,128,256]{2,1,0:T(8,128)(2,1)S(1)}, u32[]{:S(2)}, u32[]{:S(2)}) async-start(bf16[8,128,256]{2,1,0:T(8,128)(2,1)} %shard_map.69), calls=%async_computation.2 | async-start | bytes 1048576 | tf_op jit(solution)/shard_map/all_to_all | solution.py:150
  103.2 0.0 copy-done.7
  103.2 0.0 copy-start.4
  103.2 1.0 copy-done.4
  104.3 0.0 copy-start.6
  104.3 1.0 copy-done.6
  105.3 2.9 %shard_map.70.scaled_ref = bf16[1024,1024]{1,0:T(8,128)(2,1)S(1)} custom-call(s32[2]{0:T(128)S(1)} %copy-done.7, bf16[1024,256]{1,0:T(8,128)(2,1)S(1)} %pad_maximum_fusion.own_ref, bf16[1024,256]{1,0:T(8,128)(2,1)S(1)} %copy-done.6, bf16[1024,256]{1,0:T(8,128)(2,1)S(1)} %copy-done.4, bf16[1024,256]{1,0:T(8,128)(2,1)S(1)} %collective-permute-done.5.both_ref), custom_call_target="tpu_custom_call" | custom-call | tf_op jit(solution)/shard_map/pallas_call | solution.py:100
  108.2 0.7 shard_map.71
  108.9 13.2 %all-to-all-done.2 = bf16[8,128,256]{2,1,0:T(8,128)(2,1)S(1)} async-done(((bf16[8,128,256]{2,1,0:T(8,128)(2,1)}), bf16[8,128,256]{2,1,0:T(8,128)(2,1)S(1)}, u32[]{:S(2)}, u32[]{:S(2)}) %all-to-all-start.2) | async-done | bytes 524320 | tf_op jit(solution)/shard_map/all_to_all | solution.py:150
  122.2 0.7 convert_reduce_fusion
  122.9 7.1 %all-to-all-start.3 = ((f32[8,16,256]{2,1,0:T(8,128)}), f32[8,16,256]{2,1,0:T(8,128)S(1)}, u32[]{:S(2)}, u32[]{:S(2)}) async-start(f32[8,16,256]{2,1,0:T(8,128)} %bitcast.6), calls=%async_computation.3 | async-start | bytes 262144 | tf_op jit(solution)/shard_map/all_to_all | solution.py:159
  130.0 2.2 %collective-permute-start.6 = (bf16[256,256]{1,0:T(8,128)(2,1)S(1)}, bf16[256,256]{1,0:T(8,128)(2,1)S(1)}, u32[]{:S(2)}, u32[]{:S(2)}) collective-permute-start(bf16[256,256]{1,0:T(8,128)(2,1)S(1)} %get-tuple-element.56), channel_id=1, source_target_pairs={{0,32},{32,0},{1,33},{33,1},{2,34},{34,2},{3,35},{35,3},{4,36},{36... | collective-permute-start | bytes 393224 | tf_op jit(solution)/shard_map/ppermute | solution.py:112
  132.2 2.9 %collective-permute-start.7 = (bf16[256,256]{1,0:T(8,128)(2,1)S(1)}, bf16[256,256]{1,0:T(8,128)(2,1)S(1)}, u32[]{:S(2)}, u32[]{:S(2)}) collective-permute-start(bf16[256,256]{1,0:T(8,128)(2,1)S(1)} %get-tuple-element.57), channel_id=1, source_target_pairs={{0,64},{64,0},{1,65},{65,1},{2,66},{66,2},{3,67},{67,3},{4,68},{68... | collective-permute-start | bytes 393224 | tf_op jit(solution)/shard_map/ppermute | solution.py:113
  135.1 4.1 %collective-permute-start.8 = (bf16[256,256]{1,0:T(8,128)(2,1)S(1)}, bf16[256,256]{1,0:T(8,128)(2,1)S(1)}, u32[]{:S(2)}, u32[]{:S(2)}) collective-permute-start(bf16[256,256]{1,0:T(8,128)(2,1)S(1)} %get-tuple-element.58), channel_id=1, source_target_pairs={{0,96},{32,64},{64,32},{96,0},{1,97},{33,65},{65,33},{97,1},{2,98}... | collective-permute-start | bytes 393224 | tf_op jit(solution)/shard_map/ppermute | solution.py:114
  139.2 0.0 collective-permute-done.6.refs_1_
  139.2 2.7 %collective-permute-done.7.refs_2_ = bf16[256,256]{1,0:T(8,128)(2,1)S(1)} collective-permute-done((bf16[256,256]{1,0:T(8,128)(2,1)S(1)}, bf16[256,256]{1,0:T(8,128)(2,1)S(1)}, u32[]{:S(2)}, u32[]{:S(2)}) %collective-permute-start.7) | collective-permute-done | bytes 131104 | tf_op jit(solution)/shard_map/ppermute | solution.py:113
  141.9 2.6 %collective-permute-done.8.refs_3_ = bf16[256,256]{1,0:T(8,128)(2,1)S(1)} collective-permute-done((bf16[256,256]{1,0:T(8,128)(2,1)S(1)}, bf16[256,256]{1,0:T(8,128)(2,1)S(1)}, u32[]{:S(2)}, u32[]{:S(2)}) %collective-permute-start.8) | collective-permute-done | bytes 131104 | tf_op jit(solution)/shard_map/ppermute | solution.py:114
  144.5 1.4 shard_map.72
  145.9 0.3 all-to-all-done.3
  146.2 0.6 broadcast_multiply_fusion
  (10 shorter events, 0.2 us)
Async XLA Ops:
  0.6 14.1 %copy-start.8 = (bf16[1024,4]{0,1:T(4,128)(2,1)S(1)}, bf16[1024,4]{0,1:T(4,128)(2,1)}, u32[]{:S(2)}) copy-start(bf16[1024,4]{0,1:T(4,128)(2,1)} %param.7) | copy-start | bytes 24580
  5.0 63.6 %copy-start = (bf16[256,1280]{1,0:T(8,128)(2,1)S(1)}, bf16[256,1280]{1,0:T(8,128)(2,1)}, u32[]{:S(2)}) copy-start(bf16[256,1280]{1,0:T(8,128)(2,1)} %get-tuple-element.40.refs_0_) | copy-start | bytes 1966084
  5.0 55.5 %collective-permute-start = (bf16[256,1280]{1,0:T(8,128)(2,1)}, bf16[256,1280]{1,0:T(8,128)(2,1)S(1)}, u32[]{:S(2)}, u32[]{:S(2)}) collective-permute-start(bf16[256,1280]{1,0:T(8,128)(2,1)} %get-tuple-element.36), channel_id=1, source_target_pairs={{0,32},{32,0},{1,33},{33,1},{2,34},{34,2},{3,35},{35,3},{4,36},{36... | collective-permute-start | bytes 1966088 | tf_op jit(solution)/shard_map/ppermute | solution.py:112
  7.9 52.7 %collective-permute-start.1 = (bf16[256,1280]{1,0:T(8,128)(2,1)}, bf16[256,1280]{1,0:T(8,128)(2,1)S(1)}, u32[]{:S(2)}, u32[]{:S(2)}) collective-permute-start(bf16[256,1280]{1,0:T(8,128)(2,1)} %get-tuple-element.37), channel_id=1, source_target_pairs={{0,64},{64,0},{1,65},{65,1},{2,66},{66,2},{3,67},{67,3},{4,68},{68... | collective-permute-start | bytes 1966088 | tf_op jit(solution)/shard_map/ppermute | solution.py:113
  12.2 48.4 %collective-permute-start.2 = (bf16[256,1280]{1,0:T(8,128)(2,1)}, bf16[256,1280]{1,0:T(8,128)(2,1)S(1)}, u32[]{:S(2)}, u32[]{:S(2)}) collective-permute-start(bf16[256,1280]{1,0:T(8,128)(2,1)} %get-tuple-element.38), channel_id=1, source_target_pairs={{0,96},{32,64},{64,32},{96,0},{1,97},{33,65},{65,33},{97,1},{2,98}... | collective-permute-start | bytes 1966088 | tf_op jit(solution)/shard_map/ppermute | solution.py:114
  60.5 8.1 %copy-start.1 = (bf16[256,1280]{1,0:T(8,128)(2,1)}, bf16[256,1280]{1,0:T(8,128)(2,1)S(1)}, u32[]{:S(2)}) copy-start(bf16[256,1280]{1,0:T(8,128)(2,1)S(1)} %collective-permute-done.2.refs_3_) | copy-start | bytes 1966084
  61.5 34.6 %all-to-all-start.1 = ((bf16[8,128,256]{2,1,0:T(8,128)(2,1)}), bf16[8,128,256]{2,1,0:T(8,128)(2,1)S(1)}, u32[]{:S(2)}, u32[]{:S(2)}) async-start(bf16[8,128,256]{2,1,0:T(8,128)(2,1)} %broadcast_in_dim.10), calls=%async_computation.1 | async-start | bytes 1048576 | tf_op jit(solution)/shard_map/all_to_all | solution.py:139
  68.7 34.6 %copy-start.7 = (s32[2]{0:T(128)S(1)}, s32[2]{0:T(128)}, u32[]{:S(2)}) copy-start(s32[2]{0:T(128)} %pad_add_fusion.place_ref) | copy-start | bytes 28
  68.7 17.7 %collective-permute-start.5 = (bf16[1024,256]{1,0:T(8,128)(2,1)S(1)}, bf16[1024,256]{1,0:T(8,128)(2,1)S(1)}, u32[]{:S(2)}, u32[]{:S(2)}) collective-permute-start(bf16[1024,256]{1,0:T(8,128)(2,1)S(1)} %pad_maximum_fusion.own_ref), channel_id=1, source_target_pairs={{0,3},{1,2},{2,1},{3,0},{4,7},{5,6},{6,5},{7,4},{8,11},{9,10},{10,... | collective-permute-start | bytes 1572872 | tf_op jit(solution)/shard_map/ppermute | solution.py:147
  70.7 23.8 %collective-permute-start.4 = (bf16[1024,256]{1,0:T(8,128)(2,1)S(1)}, bf16[1024,256]{1,0:T(8,128)(2,1)S(1)}, u32[]{:S(2)}, u32[]{:S(2)}) collective-permute-start(bf16[1024,256]{1,0:T(8,128)(2,1)S(1)} %pad_maximum_fusion.own_ref), channel_id=1, source_target_pairs={{0,2},{2,0},{1,3},{3,1},{4,6},{6,4},{5,7},{7,5},{8,10},{10,8},{9,1... | collective-permute-start | bytes 1572872 | tf_op jit(solution)/shard_map/ppermute | solution.py:146
  74.0 21.3 %collective-permute-start.3 = (bf16[1024,256]{1,0:T(8,128)(2,1)S(1)}, bf16[1024,256]{1,0:T(8,128)(2,1)S(1)}, u32[]{:S(2)}, u32[]{:S(2)}) collective-permute-start(bf16[1024,256]{1,0:T(8,128)(2,1)S(1)} %pad_maximum_fusion.own_ref), channel_id=1, source_target_pairs={{0,1},{1,0},{2,3},{3,2},{4,5},{5,4},{6,7},{7,6},{8,9},{9,8},{10,11... | collective-permute-start | bytes 1572872 | tf_op jit(solution)/shard_map/ppermute | solution.py:145
  77.8 1.1 copy-start.2
  94.4 0.8 copy-start.3
  95.2 0.8 copy-start.5
  96.0 26.1 %all-to-all-start.2 = ((bf16[8,128,256]{2,1,0:T(8,128)(2,1)}), bf16[8,128,256]{2,1,0:T(8,128)(2,1)S(1)}, u32[]{:S(2)}, u32[]{:S(2)}) async-start(bf16[8,128,256]{2,1,0:T(8,128)(2,1)} %shard_map.69), calls=%async_computation.2 | async-start | bytes 1048576 | tf_op jit(solution)/shard_map/all_to_all | solution.py:150
  103.2 1.0 copy-start.4
  104.3 1.0 copy-start.6
  122.9 23.3 %all-to-all-start.3 = ((f32[8,16,256]{2,1,0:T(8,128)}), f32[8,16,256]{2,1,0:T(8,128)S(1)}, u32[]{:S(2)}, u32[]{:S(2)}) async-start(f32[8,16,256]{2,1,0:T(8,128)} %bitcast.6), calls=%async_computation.3 | async-start | bytes 262144 | tf_op jit(solution)/shard_map/all_to_all | solution.py:159
  130.0 9.2 %collective-permute-start.6 = (bf16[256,256]{1,0:T(8,128)(2,1)S(1)}, bf16[256,256]{1,0:T(8,128)(2,1)S(1)}, u32[]{:S(2)}, u32[]{:S(2)}) collective-permute-start(bf16[256,256]{1,0:T(8,128)(2,1)S(1)} %get-tuple-element.56), channel_id=1, source_target_pairs={{0,32},{32,0},{1,33},{33,1},{2,34},{34,2},{3,35},{35,3},{4,36},{36... | collective-permute-start | bytes 393224 | tf_op jit(solution)/shard_map/ppermute | solution.py:112
  132.2 9.7 %collective-permute-start.7 = (bf16[256,256]{1,0:T(8,128)(2,1)S(1)}, bf16[256,256]{1,0:T(8,128)(2,1)S(1)}, u32[]{:S(2)}, u32[]{:S(2)}) collective-permute-start(bf16[256,256]{1,0:T(8,128)(2,1)S(1)} %get-tuple-element.57), channel_id=1, source_target_pairs={{0,64},{64,0},{1,65},{65,1},{2,66},{66,2},{3,67},{67,3},{4,68},{68... | collective-permute-start | bytes 393224 | tf_op jit(solution)/shard_map/ppermute | solution.py:113
  135.1 9.4 %collective-permute-start.8 = (bf16[256,256]{1,0:T(8,128)(2,1)S(1)}, bf16[256,256]{1,0:T(8,128)(2,1)S(1)}, u32[]{:S(2)}, u32[]{:S(2)}) collective-permute-start(bf16[256,256]{1,0:T(8,128)(2,1)S(1)} %get-tuple-element.58), channel_id=1, source_target_pairs={{0,96},{32,64},{64,32},{96,0},{1,97},{33,65},{65,33},{97,1},{2,98}... | collective-permute-start | bytes 393224 | tf_op jit(solution)/shard_map/ppermute | solution.py:114

commit v4 on v3

v4 whole, which is shorter than its diff:
```python
import math

import jax
import jax.numpy as jnp
from jax import lax
from jax.experimental import pallas as pl
from jax.experimental.pallas import tpu as pltpu
from jax.sharding import Mesh
from jax.sharding import PartitionSpec as P

FSDP = ("zh", "zl", "xl", "y")
TP = ("xh", "c")
SWAP = [(0, 1), (1, 0)]
BOTH = [(i, i ^ 3) for i in range(4)]
MIB = 1024 * 1024


def prep_kernel(place_ref, counts_ref, offsets_ref, grad_ref, inputs_ref, *outs):
    q = place_ref[0]
    rows, columns = grad_ref.shape
    blocks = (outs[0].shape[1] - columns) // 128
    positions = lax.broadcasted_iota(jnp.int32, (rows, columns), 0)
    length = jnp.zeros((rows, columns), jnp.int32)
    for s in range(counts_ref.shape[1]):
        first = offsets_ref[0, s]
        count = counts_ref[0, s]
        length = jnp.where((positions >= first) & (positions < first + count), count, length)
    factor = jnp.where(length > 0, lax.rsqrt(jnp.maximum(length, 1).astype(jnp.float32)), 0.0)
    scaled = (grad_ref[...].astype(jnp.float32) * factor).astype(jnp.bfloat16)
    for m, out_ref in enumerate(outs):
        target = q ^ m
        for b in range(blocks):
            source = pl.ds(pl.multiple_of((4 * b + target) * 128, 128), 128)
            out_ref[:, b * 128 : (b + 1) * 128] = inputs_ref[:, source]
        out_ref[:, blocks * 128 :] = scaled


def weight_kernel(place_ref, *refs):
    parts, outs, terms = refs[:4], refs[4:-1], refs[-1]
    peers, _, columns = terms.shape
    wide = parts[0].shape[1] - columns
    each = 128 // peers
    for b in range(wide // 128):
        term = None
        for part in parts:
            product = lax.dot_general(
                part[:, b * 128 : (b + 1) * 128],
                part[:, wide:],
                (((0,), (0,)), ((), ())),
                preferred_element_type=jnp.float32,
            )
            term = product if term is None else term + product
        terms[:, b * each : (b + 1) * each, :] = term.reshape(peers, each, -1).astype(jnp.bfloat16)
    for m, out_ref in enumerate(outs):
        out_ref[...] = terms[(place_ref[2] + m) % peers]


def sum_kernel(*refs):
    parts, out_ref = refs[:-1], refs[-1]
    total = parts[0][...].astype(jnp.float32)
    for part in parts[1:]:
        total += part[...].astype(jnp.float32)
    out_ref[...] = total


def input_kernel(place_ref, *refs):
    parts, weight_ref, outs = refs[:4], refs[4], refs[5:]
    rows, wide = outs[0].shape[0], parts[0].shape[1]
    for m, out_ref in enumerate(outs):
        total = None
        for p, part in enumerate(parts):
            place = pl.multiple_of((place_ref[1] ^ p) * wide, wide)
            term = jnp.dot(
                part[m * rows : (m + 1) * rows, :],
                weight_ref[pl.ds(place, wide), :],
                preferred_element_type=jnp.float32,
            )
            total = term if total is None else total + term
        out_ref[...] = total.astype(jnp.bfloat16)


def join_kernel(place_ref, *refs):
    parts, out_ref = refs[:4], refs[4]
    wide = parts[0].shape[1]
    for m, part in enumerate(parts):
        place = pl.multiple_of((place_ref[0] ^ m) * wide, 128)
        out_ref[:, pl.ds(place, wide)] = part[...]


def call(kernel, outs, n_smem, *args, vmem=24 * MIB, dtype=jnp.bfloat16, scratch=()):
    shapes = [jax.ShapeDtypeStruct(shape, dtype) for shape in outs]
    spaces = [pltpu.SMEM] * n_smem + [pltpu.VMEM] * (len(args) - n_smem)
    return pl.pallas_call(
        kernel,
        out_shape=shapes,
        in_specs=[pl.BlockSpec(memory_space=space) for space in spaces],
        out_specs=[pl.BlockSpec(memory_space=pltpu.VMEM)] * len(outs),
        scratch_shapes=scratch,
        compiler_params=pltpu.CompilerParams(vmem_limit_bytes=vmem),
    )(*args)


def from_group(blocks):
    return [
        blocks[0],
        lax.ppermute(blocks[1], "xl", SWAP),
        lax.ppermute(blocks[2], "zl", SWAP),
        lax.ppermute(blocks[3], ("zl", "xl"), BOTH),
    ]


def local(inputs, value_grad, value_weight, counts, offsets):
    rows, features = inputs.shape
    columns = value_grad.shape[1]
    quarter, own_columns = value_weight.shape
    n_y, n_zh = (lax.axis_size(a) for a in ("y", "zh"))
    wide = features // 4
    narrow = quarter // 4

    place = [lax.axis_index(a) for a in (("zl", "xl"), TP, "y")]
    place = jnp.stack(place).astype(jnp.int32)
    args = (place, counts, offsets, value_grad, inputs)
    blocks = call(prep_kernel, [(rows, wide + columns)] * 4, 3, *args, vmem=60 * MIB)
    blocks, value_weight = lax.optimization_barrier((blocks, value_weight))
    received = from_group(blocks)

    mine = value_weight.T.reshape(own_columns, 2, 2, narrow).transpose(1, 2, 0, 3)
    mine = jnp.broadcast_to(mine[None, :, :, None], (n_zh, 2, 2, n_y, own_columns, narrow))
    mine = mine.reshape(-1, own_columns, narrow)
    weight = lax.all_to_all(mine, FSDP, 0, 0, tiled=True).reshape(-1, narrow)

    chunk = (wide // n_y, columns)
    scratch = [pltpu.VMEM((n_y, *chunk), jnp.bfloat16)]
    terms = list(call(weight_kernel, [chunk] * n_y, 1, place, *received, scratch=scratch))
    for m in range(1, n_y):
        terms[m] = lax.ppermute(terms[m], "y", [(i, (i + m) % n_y) for i in range(n_y)])

    own = jnp.concatenate([part[:, wide:] for part in received])
    own, terms[1] = lax.optimization_barrier((own, terms[1]))
    gathered = [
        own,
        lax.ppermute(own, "c", SWAP),
        lax.ppermute(own, "xh", SWAP),
        lax.ppermute(own, TP, BOTH),
    ]

    (summed,) = call(sum_kernel, [chunk], 0, *terms, dtype=jnp.float32)
    summed, weight = lax.optimization_barrier((summed, weight))
    summed = lax.all_to_all(summed.reshape(n_zh, -1, columns), "zh", 0, 0, tiled=True)
    normalizer = 1.0 / math.sqrt(counts.shape[1] * lax.axis_size(FSDP))
    weight_grad = jnp.sum(summed, axis=0) * normalizer

    outs = call(input_kernel, [(rows, narrow)] * 4, 1, place, *gathered, weight)
    (input_grad,) = call(join_kernel, [(rows, quarter)], 1, place, *from_group(outs))
    return (input_grad, weight_grad)


def solution(mesh):
    split = Mesh(mesh.devices.reshape(8, 2, 2, 8, 2, 2), (*FSDP, *TP))
    in_specs = (P(FSDP, None), P(FSDP, TP), P(TP, FSDP), P(FSDP, None), P(FSDP, None))
    out_specs = (P(FSDP, TP), P(FSDP, TP))
    return jax.shard_map(local, mesh=split, in_specs=in_specs, out_specs=out_specs, check_vma=False)
```

time: 150 us -> 165 us (1.10)
  blocking collectives: 45.7 us -> 0 us
  starting transfers between devices: 49.4 us -> 92.9 us
  waiting for transfers between devices: 32.8 us -> 55.7 us
  local copies, waits for them, and re-layouts: 5.77 us -> 2.1 us
  Pallas kernels: 10.3 us -> 8.5 us
    all_to_all x1 -> x0, blocking collectives: 45.7 us -> none  [local(): block = lax.all_to_all(mine, ('xl', 'zh', 'zl'), 0, 0, tiled=True)]
    ppermute x0 -> x7, starting transfers between devices: none -> 25.6 us  [local(): lax.ppermute(terms[m], 'y', [(i, (i + m) % n_y) for i in range(n_y)])]
    all_to_all x3 -> x2, starting transfers between devices: 21.4 us -> 39.8 us  [the longest x1 28.3 us: local(): weight = lax.all_to_all(mine, FSDP, 0, 0, tiled=True).reshape(-1, narrow)]
    ppermute x2, waiting for transfers between devices: 2.71 us -> 18 us  [from_group(): lax.ppermute(blocks[2], 'zl', SWAP)]
    all_to_all x3 -> x2, waiting for transfers between devices: 13.5 us -> 0.01 us  [the longest x1 0.01 us: local(): lax.all_to_all(summed.reshape(n_zh, -1, columns), 'zh', 0, 0, tiled=True)]
    ppermute x2, waiting for transfers between devices: 2.58 us -> 15.1 us  [from_group(): lax.ppermute(blocks[3], ('zl', 'xl'), BOTH)]
    ppermute x2, waiting for transfers between devices: 0.01 us -> 12.2 us  [from_group(): lax.ppermute(blocks[1], 'xl', SWAP)]
    ppermute x0 -> x7, waiting for transfers between devices: none -> 10.4 us  [local(): lax.ppermute(terms[m], 'y', [(i, (i + m) % n_y) for i in range(n_y)])]
  transfers between devices with their start and end apart: 12 -> 18, of which waited for: 6 -> 9; matrix products, arithmetic and copies ran while one was open for 0% -> 1% of each run, Pallas kernels for 4% -> 3%
where the time goes in v4:
time: 165 us; the launch traced here: 161 us
  starting transfers between devices  92.9 us (56%)
  waiting for transfers between devices  55.7 us (34%)
  Pallas kernels  8.5 us (5%)
  local copies, waits for them, and re-layouts  2.1 us (1%)
    all_to_all x1, starting transfers between devices, local(): weight = lax.all_to_all(mine, FSDP, 0, 0, tiled=True).reshape(-1, narrow)  28.3 us
    ppermute x7, starting transfers between devices, local(): lax.ppermute(terms[m], 'y', [(i, (i + m) % n_y) for i in range(n_y)])  25.6 us
    ppermute x2, waiting for transfers between devices, from_group(): lax.ppermute(blocks[2], 'zl', SWAP)  18 us
    ppermute x2, waiting for transfers between devices, from_group(): lax.ppermute(blocks[3], ('zl', 'xl'), BOTH)  15.1 us
    ppermute x2, waiting for transfers between devices, from_group(): lax.ppermute(blocks[1], 'xl', SWAP)  12.2 us
    all_to_all x1, starting transfers between devices, local(): lax.all_to_all(summed.reshape(n_zh, -1, columns), 'zh', 0, 0, tiled=True)  11.4 us
    ppermute x7, waiting for transfers between devices, local(): lax.ppermute(terms[m], 'y', [(i, (i + m) % n_y) for i in range(n_y)])  10.4 us
    pallas_call x5, Pallas kernels, call(): pl.pallas_call(kernel, out_shape=shapes, in_specs=[pl.BlockSpec(memory_sp...  8.5 us
  transfers between devices with their start and end apart: 18, of which 9 were waited for; matrix products, arithmetic and copies ran while one was open for 1% of the time, Pallas kernels for 3%

profile of v4, /device:TPU:6, one launch (start us, length us, event | category | flops | bytes accessed | tf_op | source)
XLA Modules:
  0.0 161.5 jit_solution(12252413125878633353)
XLA Ops:
  0.6 0.0 copy-start.2
  0.6 0.6 pad_add_fusion.place_ref
  1.3 0.0 copy-start.1
  1.3 3.8 %shard_map.68 = (bf16[256,1280]{1,0:T(8,128)(2,1)}, bf16[256,1280]{1,0:T(8,128)(2,1)}, bf16[256,1280]{1,0:T(8,128)(2,1)}, bf16[256,1280]{1,0:T(8,128)(2,1)}) custom-call(s32[3]{0:T(128)} %pad_add_fusion.place_ref, s32[1,4]{1,0:T(1,128)} %counts_ref.1, s32[1,4]{1,0:T(1,128)} %offsets_ref.1, bf16[256,256]{1,0:T(8,128)(2,1)} %grad_ref.1, ...), custom_call_target="tpu_custom_call" | custom-call | tf_op jit(solution)/shard_map/pallas_call | solution.py:93
  5.1 0.0 copy-start
  5.1 0.0 copy-done.2
  5.1 1.0 broadcast_in_dim.2
  6.1 28.3 %all-to-all-start = ((bf16[256,4,256]{2,1,0:T(4,128)(2,1)}), bf16[256,4,256]{2,1,0:T(4,128)(2,1)S(1)}, u32[]{:S(2)}, u32[]{:S(2)}) async-start(bf16[256,4,256]{2,1,0:T(4,128)(2,1)} %bitcast.5), calls=%async_computation | async-start | bytes 1048576 | tf_op jit(solution)/shard_map/all_to_all | solution.py:130
  34.4 3.7 %collective-permute-start = (bf16[256,1280]{1,0:T(8,128)(2,1)}, bf16[256,1280]{1,0:T(8,128)(2,1)S(1)}, u32[]{:S(2)}, u32[]{:S(2)}) collective-permute-start(bf16[256,1280]{1,0:T(8,128)(2,1)} %get-tuple-element.32), channel_id=1, source_target_pairs={{0,32},{32,0},{1,33},{33,1},{2,34},{34,2},{3,35},{35,3},{4,36},{36... | collective-permute-start | bytes 1966088 | tf_op jit(solution)/shard_map/ppermute | solution.py:106
  38.1 2.2 %collective-permute-start.1 = (bf16[256,1280]{1,0:T(8,128)(2,1)}, bf16[256,1280]{1,0:T(8,128)(2,1)S(1)}, u32[]{:S(2)}, u32[]{:S(2)}) collective-permute-start(bf16[256,1280]{1,0:T(8,128)(2,1)} %get-tuple-element.33), channel_id=1, source_target_pairs={{0,64},{64,0},{1,65},{65,1},{2,66},{66,2},{3,67},{67,3},{4,68},{68... | collective-permute-start | bytes 1966088 | tf_op jit(solution)/shard_map/ppermute | solution.py:107
  40.3 3.4 %collective-permute-start.2 = (bf16[256,1280]{1,0:T(8,128)(2,1)}, bf16[256,1280]{1,0:T(8,128)(2,1)S(1)}, u32[]{:S(2)}, u32[]{:S(2)}) collective-permute-start(bf16[256,1280]{1,0:T(8,128)(2,1)} %get-tuple-element.34), channel_id=1, source_target_pairs={{0,96},{32,64},{64,32},{96,0},{1,97},{33,65},{65,33},{97,1},{2,98}... | collective-permute-start | bytes 1966088 | tf_op jit(solution)/shard_map/ppermute | solution.py:108
  43.7 0.9 slice.12
  44.6 12.2 %collective-permute-done.refs_1_ = bf16[256,1280]{1,0:T(8,128)(2,1)S(1)} collective-permute-done((bf16[256,1280]{1,0:T(8,128)(2,1)}, bf16[256,1280]{1,0:T(8,128)(2,1)S(1)}, u32[]{:S(2)}, u32[]{:S(2)}) %collective-permute-start) | collective-permute-done | bytes 655392 | tf_op jit(solution)/shard_map/ppermute | solution.py:106
  56.8 15.3 %collective-permute-done.1.refs_2_ = bf16[256,1280]{1,0:T(8,128)(2,1)S(1)} collective-permute-done((bf16[256,1280]{1,0:T(8,128)(2,1)}, bf16[256,1280]{1,0:T(8,128)(2,1)S(1)}, u32[]{:S(2)}, u32[]{:S(2)}) %collective-permute-start.1) | collective-permute-done | bytes 655392 | tf_op jit(solution)/shard_map/ppermute | solution.py:107
  72.1 12.8 %collective-permute-done.2.refs_3_ = bf16[256,1280]{1,0:T(8,128)(2,1)S(1)} collective-permute-done((bf16[256,1280]{1,0:T(8,128)(2,1)}, bf16[256,1280]{1,0:T(8,128)(2,1)S(1)}, u32[]{:S(2)}, u32[]{:S(2)}) %collective-permute-start.2) | collective-permute-done | bytes 655392 | tf_op jit(solution)/shard_map/ppermute | solution.py:108
  84.9 0.0 copy-done.1
  84.9 0.0 copy-done
  84.9 1.3 shard_map.69
  86.3 3.4 %collective-permute-start.3 = (bf16[128,256]{1,0:T(8,128)(2,1)S(1)}, bf16[128,256]{1,0:T(8,128)(2,1)S(1)}, u32[]{:S(2)}, u32[]{:S(2)}) collective-permute-start(bf16[128,256]{1,0:T(8,128)(2,1)S(1)} %get-tuple-element.35), channel_id=1, source_target_pairs={{0,4},{4,8},{8,12},{12,16},{16,20},{20,24},{24,28},{28,0},{1,5},{5... | collective-permute-start | bytes 196616 | tf_op jit(solution)/shard_map/ppermute | solution.py:136
  89.7 5.5 %collective-permute-start.10 = (bf16[128,256]{1,0:T(8,128)(2,1)S(1)}, bf16[128,256]{1,0:T(8,128)(2,1)S(1)}, u32[]{:S(2)}, u32[]{:S(2)}) collective-permute-start(bf16[128,256]{1,0:T(8,128)(2,1)S(1)} %get-tuple-element.42), channel_id=1, source_target_pairs={{0,20},{4,24},{8,28},{12,0},{16,4},{20,8},{24,12},{28,16},{1,21},{... | collective-permute-start | bytes 196616 | tf_op jit(solution)/shard_map/ppermute | solution.py:136
  95.2 5.5 %collective-permute-start.11 = (bf16[128,256]{1,0:T(8,128)(2,1)S(1)}, bf16[128,256]{1,0:T(8,128)(2,1)S(1)}, u32[]{:S(2)}, u32[]{:S(2)}) collective-permute-start(bf16[128,256]{1,0:T(8,128)(2,1)S(1)} %get-tuple-element.43), channel_id=1, source_target_pairs={{0,24},{4,28},{8,0},{12,4},{16,8},{20,12},{24,16},{28,20},{1,25},{... | collective-permute-start | bytes 196616 | tf_op jit(solution)/shard_map/ppermute | solution.py:136
  100.7 0.0 collective-permute-done.3.refs_1_
  100.8 1.9 %collective-permute-start.4 = (bf16[1024,256]{1,0:T(8,128)(2,1)S(1)}, bf16[1024,256]{1,0:T(8,128)(2,1)S(1)}, u32[]{:S(2)}, u32[]{:S(2)}) collective-permute-start(bf16[1024,256]{1,0:T(8,128)(2,1)S(1)} %pad_maximum_fusion.refs_0_), channel_id=1, source_target_pairs={{0,1},{1,0},{2,3},{3,2},{4,5},{5,4},{6,7},{7,6},{8,9},{9,8},{10,11... | collective-permute-start | bytes 1572872 | tf_op jit(solution)/shard_map/ppermute | solution.py:142
  102.7 3.3 %collective-permute-start.5 = (bf16[1024,256]{1,0:T(8,128)(2,1)S(1)}, bf16[1024,256]{1,0:T(8,128)(2,1)S(1)}, u32[]{:S(2)}, u32[]{:S(2)}) collective-permute-start(bf16[1024,256]{1,0:T(8,128)(2,1)S(1)} %pad_maximum_fusion.refs_0_), channel_id=1, source_target_pairs={{0,2},{2,0},{1,3},{3,1},{4,6},{6,4},{5,7},{7,5},{8,10},{10,8},{9,1... | collective-permute-start | bytes 1572872 | tf_op jit(solution)/shard_map/ppermute | solution.py:143
  106.0 3.9 %collective-permute-start.6 = (bf16[1024,256]{1,0:T(8,128)(2,1)S(1)}, bf16[1024,256]{1,0:T(8,128)(2,1)S(1)}, u32[]{:S(2)}, u32[]{:S(2)}) collective-permute-start(bf16[1024,256]{1,0:T(8,128)(2,1)S(1)} %pad_maximum_fusion.refs_0_), channel_id=1, source_target_pairs={{0,3},{1,2},{2,1},{3,0},{4,7},{5,6},{6,5},{7,4},{8,11},{9,10},{10,... | collective-permute-start | bytes 1572872 | tf_op jit(solution)/shard_map/ppermute | solution.py:144
  109.9 0.0 collective-permute-done.10.refs_5_
  109.9 1.9 %collective-permute-start.12 = (bf16[128,256]{1,0:T(8,128)(2,1)S(1)}, bf16[128,256]{1,0:T(8,128)(2,1)S(1)}, u32[]{:S(2)}, u32[]{:S(2)}) collective-permute-start(bf16[128,256]{1,0:T(8,128)(2,1)S(1)} %get-tuple-element.44), channel_id=1, source_target_pairs={{0,28},{4,0},{8,4},{12,8},{16,12},{20,16},{24,20},{28,24},{1,29},{... | collective-permute-start | bytes 196616 | tf_op jit(solution)/shard_map/ppermute | solution.py:136
  111.8 0.0 collective-permute-done.11.refs_6_
  111.8 2.7 %collective-permute-start.7 = (bf16[128,256]{1,0:T(8,128)(2,1)S(1)}, bf16[128,256]{1,0:T(8,128)(2,1)S(1)}, u32[]{:S(2)}, u32[]{:S(2)}) collective-permute-start(bf16[128,256]{1,0:T(8,128)(2,1)S(1)} %get-tuple-element.39), channel_id=1, source_target_pairs={{0,8},{4,12},{8,16},{12,20},{16,24},{20,28},{24,0},{28,4},{1,9},{5... | collective-permute-start | bytes 196616 | tf_op jit(solution)/shard_map/ppermute | solution.py:136
  114.5 1.5 collective-permute-done.12.refs_7_
  116.1 2.5 %collective-permute-start.8 = (bf16[128,256]{1,0:T(8,128)(2,1)S(1)}, bf16[128,256]{1,0:T(8,128)(2,1)S(1)}, u32[]{:S(2)}, u32[]{:S(2)}) collective-permute-start(bf16[128,256]{1,0:T(8,128)(2,1)S(1)} %get-tuple-element.40), channel_id=1, source_target_pairs={{0,12},{4,16},{8,20},{12,24},{16,28},{20,0},{24,4},{28,8},{1,13},{... | collective-permute-start | bytes 196616 | tf_op jit(solution)/shard_map/ppermute | solution.py:136
  118.6 2.8 %collective-permute-done.7.refs_2_ = bf16[128,256]{1,0:T(8,128)(2,1)S(1)} collective-permute-done((bf16[128,256]{1,0:T(8,128)(2,1)S(1)}, bf16[128,256]{1,0:T(8,128)(2,1)S(1)}, u32[]{:S(2)}, u32[]{:S(2)}) %collective-permute-start.7) | collective-permute-done | bytes 65568 | tf_op jit(solution)/shard_map/ppermute | solution.py:136
  121.4 4.2 %collective-permute-start.9 = (bf16[128,256]{1,0:T(8,128)(2,1)S(1)}, bf16[128,256]{1,0:T(8,128)(2,1)S(1)}, u32[]{:S(2)}, u32[]{:S(2)}) collective-permute-start(bf16[128,256]{1,0:T(8,128)(2,1)S(1)} %get-tuple-element.41), channel_id=1, source_target_pairs={{0,16},{4,20},{8,24},{12,28},{16,0},{20,4},{24,8},{28,12},{1,17},{... | collective-permute-start | bytes 196616 | tf_op jit(solution)/shard_map/ppermute | solution.py:136
  125.5 1.7 %collective-permute-done.8.refs_3_ = bf16[128,256]{1,0:T(8,128)(2,1)S(1)} collective-permute-done((bf16[128,256]{1,0:T(8,128)(2,1)S(1)}, bf16[128,256]{1,0:T(8,128)(2,1)S(1)}, u32[]{:S(2)}, u32[]{:S(2)}) %collective-permute-start.8) | collective-permute-done | bytes 65568 | tf_op jit(solution)/shard_map/ppermute | solution.py:136
  127.2 4.4 %collective-permute-done.9.refs_4_ = bf16[128,256]{1,0:T(8,128)(2,1)S(1)} collective-permute-done((bf16[128,256]{1,0:T(8,128)(2,1)S(1)}, bf16[128,256]{1,0:T(8,128)(2,1)S(1)}, u32[]{:S(2)}, u32[]{:S(2)}) %collective-permute-start.9) | collective-permute-done | bytes 65568 | tf_op jit(solution)/shard_map/ppermute | solution.py:136
  131.6 0.7 shard_map.70
  132.4 0.0 all-to-all-done
  132.4 0.1 reshape.19.refs_4_
  132.5 11.4 %all-to-all-start.1 = ((f32[8,16,256]{2,1,0:T(8,128)}), f32[8,16,256]{2,1,0:T(8,128)S(1)}, u32[]{:S(2)}, u32[]{:S(2)}) async-start(f32[8,16,256]{2,1,0:T(8,128)} %bitcast.6), calls=%async_computation.1 | async-start | bytes 262144 | tf_op jit(solution)/shard_map/all_to_all | solution.py:149
  143.9 0.0 collective-permute-done.4.refs_1_
  143.9 0.0 collective-permute-done.5.refs_2_
  144.0 0.0 collective-permute-done.6.refs_3_
  144.0 1.3 shard_map.71
  145.2 3.4 %collective-permute-start.13 = (bf16[256,256]{1,0:T(8,128)(2,1)S(1)}, bf16[256,256]{1,0:T(8,128)(2,1)S(1)}, u32[]{:S(2)}, u32[]{:S(2)}) collective-permute-start(bf16[256,256]{1,0:T(8,128)(2,1)S(1)} %get-tuple-element.48), channel_id=1, source_target_pairs={{0,32},{32,0},{1,33},{33,1},{2,34},{34,2},{3,35},{35,3},{4,36},{36... | collective-permute-start | bytes 393224 | tf_op jit(solution)/shard_map/ppermute | solution.py:106
  148.7 3.0 %collective-permute-start.14 = (bf16[256,256]{1,0:T(8,128)(2,1)S(1)}, bf16[256,256]{1,0:T(8,128)(2,1)S(1)}, u32[]{:S(2)}, u32[]{:S(2)}) collective-permute-start(bf16[256,256]{1,0:T(8,128)(2,1)S(1)} %get-tuple-element.49), channel_id=1, source_target_pairs={{0,64},{64,0},{1,65},{65,1},{2,66},{66,2},{3,67},{67,3},{4,68},{68... | collective-permute-start | bytes 393224 | tf_op jit(solution)/shard_map/ppermute | solution.py:107
  151.7 2.8 %collective-permute-start.15 = (bf16[256,256]{1,0:T(8,128)(2,1)S(1)}, bf16[256,256]{1,0:T(8,128)(2,1)S(1)}, u32[]{:S(2)}, u32[]{:S(2)}) collective-permute-start(bf16[256,256]{1,0:T(8,128)(2,1)S(1)} %get-tuple-element.50), channel_id=1, source_target_pairs={{0,96},{32,64},{64,32},{96,0},{1,97},{33,65},{65,33},{97,1},{2,98}... | collective-permute-start | bytes 393224 | tf_op jit(solution)/shard_map/ppermute | solution.py:108
  154.5 0.0 collective-permute-done.13.refs_1_
  154.5 2.7 %collective-permute-done.14.refs_2_ = bf16[256,256]{1,0:T(8,128)(2,1)S(1)} collective-permute-done((bf16[256,256]{1,0:T(8,128)(2,1)S(1)}, bf16[256,256]{1,0:T(8,128)(2,1)S(1)}, u32[]{:S(2)}, u32[]{:S(2)}) %collective-permute-start.14) | collective-permute-done | bytes 131104 | tf_op jit(solution)/shard_map/ppermute | solution.py:107
  157.2 2.3 %collective-permute-done.15.refs_3_ = bf16[256,256]{1,0:T(8,128)(2,1)S(1)} collective-permute-done((bf16[256,256]{1,0:T(8,128)(2,1)S(1)}, bf16[256,256]{1,0:T(8,128)(2,1)S(1)}, u32[]{:S(2)}, u32[]{:S(2)}) %collective-permute-start.15) | collective-permute-done | bytes 131104 | tf_op jit(solution)/shard_map/ppermute | solution.py:108
  159.4 1.4 shard_map.72
  160.8 0.0 all-to-all-done.1
  160.8 0.6 broadcast_multiply_fusion
  (7 shorter events, 0.1 us)
Async XLA Ops:
  0.6 4.5 %copy-start.2 = (bf16[1024,4]{0,1:T(4,128)(2,1)S(1)}, bf16[1024,4]{0,1:T(4,128)(2,1)}, u32[]{:S(2)}) copy-start(bf16[1024,4]{0,1:T(4,128)(2,1)} %param.7) | copy-start | bytes 24580
  1.3 83.6 %copy-start.1 = (s32[3]{0:T(128)S(1)}, s32[3]{0:T(128)}, u32[]{:S(2)}) copy-start(s32[3]{0:T(128)} %pad_add_fusion.place_ref) | copy-start | bytes 40
  5.1 79.8 %copy-start = (bf16[256,1280]{1,0:T(8,128)(2,1)S(1)}, bf16[256,1280]{1,0:T(8,128)(2,1)}, u32[]{:S(2)}) copy-start(bf16[256,1280]{1,0:T(8,128)(2,1)} %get-tuple-element.31.refs_0_) | copy-start | bytes 1966084
  6.1 126.3 %all-to-all-start = ((bf16[256,4,256]{2,1,0:T(4,128)(2,1)}), bf16[256,4,256]{2,1,0:T(4,128)(2,1)S(1)}, u32[]{:S(2)}, u32[]{:S(2)}) async-start(bf16[256,4,256]{2,1,0:T(4,128)(2,1)} %bitcast.5), calls=%async_computation | async-start | bytes 1048576 | tf_op jit(solution)/shard_map/all_to_all | solution.py:130
  34.4 22.3 %collective-permute-start = (bf16[256,1280]{1,0:T(8,128)(2,1)}, bf16[256,1280]{1,0:T(8,128)(2,1)S(1)}, u32[]{:S(2)}, u32[]{:S(2)}) collective-permute-start(bf16[256,1280]{1,0:T(8,128)(2,1)} %get-tuple-element.32), channel_id=1, source_target_pairs={{0,32},{32,0},{1,33},{33,1},{2,34},{34,2},{3,35},{35,3},{4,36},{36... | collective-permute-start | bytes 1966088 | tf_op jit(solution)/shard_map/ppermute | solution.py:106
  38.1 33.9 %collective-permute-start.1 = (bf16[256,1280]{1,0:T(8,128)(2,1)}, bf16[256,1280]{1,0:T(8,128)(2,1)S(1)}, u32[]{:S(2)}, u32[]{:S(2)}) collective-permute-start(bf16[256,1280]{1,0:T(8,128)(2,1)} %get-tuple-element.33), channel_id=1, source_target_pairs={{0,64},{64,0},{1,65},{65,1},{2,66},{66,2},{3,67},{67,3},{4,68},{68... | collective-permute-start | bytes 1966088 | tf_op jit(solution)/shard_map/ppermute | solution.py:107
  40.3 44.6 %collective-permute-start.2 = (bf16[256,1280]{1,0:T(8,128)(2,1)}, bf16[256,1280]{1,0:T(8,128)(2,1)S(1)}, u32[]{:S(2)}, u32[]{:S(2)}) collective-permute-start(bf16[256,1280]{1,0:T(8,128)(2,1)} %get-tuple-element.34), channel_id=1, source_target_pairs={{0,96},{32,64},{64,32},{96,0},{1,97},{33,65},{65,33},{97,1},{2,98}... | collective-permute-start | bytes 1966088 | tf_op jit(solution)/shard_map/ppermute | solution.py:108
  86.3 14.5 %collective-permute-start.3 = (bf16[128,256]{1,0:T(8,128)(2,1)S(1)}, bf16[128,256]{1,0:T(8,128)(2,1)S(1)}, u32[]{:S(2)}, u32[]{:S(2)}) collective-permute-start(bf16[128,256]{1,0:T(8,128)(2,1)S(1)} %get-tuple-element.35), channel_id=1, source_target_pairs={{0,4},{4,8},{8,12},{12,16},{16,20},{20,24},{24,28},{28,0},{1,5},{5... | collective-permute-start | bytes 196616 | tf_op jit(solution)/shard_map/ppermute | solution.py:136
  89.7 20.2 %collective-permute-start.10 = (bf16[128,256]{1,0:T(8,128)(2,1)S(1)}, bf16[128,256]{1,0:T(8,128)(2,1)S(1)}, u32[]{:S(2)}, u32[]{:S(2)}) collective-permute-start(bf16[128,256]{1,0:T(8,128)(2,1)S(1)} %get-tuple-element.42), channel_id=1, source_target_pairs={{0,20},{4,24},{8,28},{12,0},{16,4},{20,8},{24,12},{28,16},{1,21},{... | collective-permute-start | bytes 196616 | tf_op jit(solution)/shard_map/ppermute | solution.py:136
  95.2 16.6 %collective-permute-start.11 = (bf16[128,256]{1,0:T(8,128)(2,1)S(1)}, bf16[128,256]{1,0:T(8,128)(2,1)S(1)}, u32[]{:S(2)}, u32[]{:S(2)}) collective-permute-start(bf16[128,256]{1,0:T(8,128)(2,1)S(1)} %get-tuple-element.43), channel_id=1, source_target_pairs={{0,24},{4,28},{8,0},{12,4},{16,8},{20,12},{24,16},{28,20},{1,25},{... | collective-permute-start | bytes 196616 | tf_op jit(solution)/shard_map/ppermute | solution.py:136
  100.8 43.2 %collective-permute-start.4 = (bf16[1024,256]{1,0:T(8,128)(2,1)S(1)}, bf16[1024,256]{1,0:T(8,128)(2,1)S(1)}, u32[]{:S(2)}, u32[]{:S(2)}) collective-permute-start(bf16[1024,256]{1,0:T(8,128)(2,1)S(1)} %pad_maximum_fusion.refs_0_), channel_id=1, source_target_pairs={{0,1},{1,0},{2,3},{3,2},{4,5},{5,4},{6,7},{7,6},{8,9},{9,8},{10,11... | collective-permute-start | bytes 1572872 | tf_op jit(solution)/shard_map/ppermute | solution.py:142
  102.7 41.3 %collective-permute-start.5 = (bf16[1024,256]{1,0:T(8,128)(2,1)S(1)}, bf16[1024,256]{1,0:T(8,128)(2,1)S(1)}, u32[]{:S(2)}, u32[]{:S(2)}) collective-permute-start(bf16[1024,256]{1,0:T(8,128)(2,1)S(1)} %pad_maximum_fusion.refs_0_), channel_id=1, source_target_pairs={{0,2},{2,0},{1,3},{3,1},{4,6},{6,4},{5,7},{7,5},{8,10},{10,8},{9,1... | collective-permute-start | bytes 1572872 | tf_op jit(solution)/shard_map/ppermute | solution.py:143
  106.0 38.0 %collective-permute-start.6 = (bf16[1024,256]{1,0:T(8,128)(2,1)S(1)}, bf16[1024,256]{1,0:T(8,128)(2,1)S(1)}, u32[]{:S(2)}, u32[]{:S(2)}) collective-permute-start(bf16[1024,256]{1,0:T(8,128)(2,1)S(1)} %pad_maximum_fusion.refs_0_), channel_id=1, source_target_pairs={{0,3},{1,2},{2,1},{3,0},{4,7},{5,6},{6,5},{7,4},{8,11},{9,10},{10,... | collective-permute-start | bytes 1572872 | tf_op jit(solution)/shard_map/ppermute | solution.py:144
  109.9 6.2 %collective-permute-start.12 = (bf16[128,256]{1,0:T(8,128)(2,1)S(1)}, bf16[128,256]{1,0:T(8,128)(2,1)S(1)}, u32[]{:S(2)}, u32[]{:S(2)}) collective-permute-start(bf16[128,256]{1,0:T(8,128)(2,1)S(1)} %get-tuple-element.44), channel_id=1, source_target_pairs={{0,28},{4,0},{8,4},{12,8},{16,12},{20,16},{24,20},{28,24},{1,29},{... | collective-permute-start | bytes 196616 | tf_op jit(solution)/shard_map/ppermute | solution.py:136
  111.8 9.5 %collective-permute-start.7 = (bf16[128,256]{1,0:T(8,128)(2,1)S(1)}, bf16[128,256]{1,0:T(8,128)(2,1)S(1)}, u32[]{:S(2)}, u32[]{:S(2)}) collective-permute-start(bf16[128,256]{1,0:T(8,128)(2,1)S(1)} %get-tuple-element.39), channel_id=1, source_target_pairs={{0,8},{4,12},{8,16},{12,20},{16,24},{20,28},{24,0},{28,4},{1,9},{5... | collective-permute-start | bytes 196616 | tf_op jit(solution)/shard_map/ppermute | solution.py:136
  116.1 11.2 %collective-permute-start.8 = (bf16[128,256]{1,0:T(8,128)(2,1)S(1)}, bf16[128,256]{1,0:T(8,128)(2,1)S(1)}, u32[]{:S(2)}, u32[]{:S(2)}) collective-permute-start(bf16[128,256]{1,0:T(8,128)(2,1)S(1)} %get-tuple-element.40), channel_id=1, source_target_pairs={{0,12},{4,16},{8,20},{12,24},{16,28},{20,0},{24,4},{28,8},{1,13},{... | collective-permute-start | bytes 196616 | tf_op jit(solution)/shard_map/ppermute | solution.py:136
  121.4 10.3 %collective-permute-start.9 = (bf16[128,256]{1,0:T(8,128)(2,1)S(1)}, bf16[128,256]{1,0:T(8,128)(2,1)S(1)}, u32[]{:S(2)}, u32[]{:S(2)}) collective-permute-start(bf16[128,256]{1,0:T(8,128)(2,1)S(1)} %get-tuple-element.41), channel_id=1, source_target_pairs={{0,16},{4,20},{8,24},{12,28},{16,0},{20,4},{24,8},{28,12},{1,17},{... | collective-permute-start | bytes 196616 | tf_op jit(solution)/shard_map/ppermute | solution.py:136
  132.5 28.3 %all-to-all-start.1 = ((f32[8,16,256]{2,1,0:T(8,128)}), f32[8,16,256]{2,1,0:T(8,128)S(1)}, u32[]{:S(2)}, u32[]{:S(2)}) async-start(f32[8,16,256]{2,1,0:T(8,128)} %bitcast.6), calls=%async_computation.1 | async-start | bytes 262144 | tf_op jit(solution)/shard_map/all_to_all | solution.py:149
  145.2 9.2 %collective-permute-start.13 = (bf16[256,256]{1,0:T(8,128)(2,1)S(1)}, bf16[256,256]{1,0:T(8,128)(2,1)S(1)}, u32[]{:S(2)}, u32[]{:S(2)}) collective-permute-start(bf16[256,256]{1,0:T(8,128)(2,1)S(1)} %get-tuple-element.48), channel_id=1, source_target_pairs={{0,32},{32,0},{1,33},{33,1},{2,34},{34,2},{3,35},{35,3},{4,36},{36... | collective-permute-start | bytes 393224 | tf_op jit(solution)/shard_map/ppermute | solution.py:106
  148.7 8.5 %collective-permute-start.14 = (bf16[256,256]{1,0:T(8,128)(2,1)S(1)}, bf16[256,256]{1,0:T(8,128)(2,1)S(1)}, u32[]{:S(2)}, u32[]{:S(2)}) collective-permute-start(bf16[256,256]{1,0:T(8,128)(2,1)S(1)} %get-tuple-element.49), channel_id=1, source_target_pairs={{0,64},{64,0},{1,65},{65,1},{2,66},{66,2},{3,67},{67,3},{4,68},{68... | collective-permute-start | bytes 393224 | tf_op jit(solution)/shard_map/ppermute | solution.py:107
  151.7 7.8 %collective-permute-start.15 = (bf16[256,256]{1,0:T(8,128)(2,1)S(1)}, bf16[256,256]{1,0:T(8,128)(2,1)S(1)}, u32[]{:S(2)}, u32[]{:S(2)}) collective-permute-start(bf16[256,256]{1,0:T(8,128)(2,1)S(1)} %get-tuple-element.50), channel_id=1, source_target_pairs={{0,96},{32,64},{64,32},{96,0},{1,97},{33,65},{65,33},{97,1},{2,98}... | collective-permute-start | bytes 393224 | tf_op jit(solution)/shard_map/ppermute | solution.py:108

commit v5 on v3

--- a/solution.py
+++ b/solution.py
@@ -146,7 +146,7 @@
         lax.ppermute(own, "xh", SWAP),
         lax.ppermute(own, TP, BOTH),
     ]
-    term, weight, gathered = lax.optimization_barrier((term, weight, gathered))
+    term, weight, gathered[1] = lax.optimization_barrier((term, weight, gathered[1]))
     terms = lax.all_to_all(term, "y", 0, 0, tiled=True)
 
     sizes = (2 * n_zh, n_y, own_columns)
@@ -154,7 +154,6 @@
     (ordered,) = call(kernel, [(4 * rows, n_tp * columns)], 1, place, *gathered)
     outs = call(input_kernel, [(rows, narrow)] * 4, 0, ordered, weight)
 
-    terms, outs = lax.optimization_barrier((terms, outs))
     summed = jnp.sum(terms.astype(jnp.float32), axis=0).reshape(n_zh, -1, columns)
     summed = lax.all_to_all(summed, "zh", 0, 0, tiled=True)
     normalizer = 1.0 / math.sqrt(counts.shape[1] * lax.axis_size(FSDP))

time: 150 us -> 137 us (0.913)
  the two profiles are of different devices: /device:TPU:6 before, /device:TPU:1 now
where the time goes in v5:
time: 137 us; the launch traced here: 136 us
  starting transfers between devices  51.4 us (38%)
  blocking collectives  44.5 us (32%)
  waiting for transfers between devices  24.8 us (18%)
  Pallas kernels  10.3 us (8%)
  local copies, waits for them, and re-layouts  2.12 us (2%)
  other arithmetic  1.96 us (1%)
    all_to_all x1, blocking collectives, local(): block = lax.all_to_all(mine, ('xl', 'zh', 'zl'), 0, 0, tiled=True)  44.5 us
    pallas_call x5, Pallas kernels, call(): pl.pallas_call(kernel, out_shape=shapes, in_specs=[pl.BlockSpec(memory_sp...  10.3 us
    ppermute x1, waiting for transfers between devices, local(): lax.ppermute(own, 'xh', SWAP)  10.1 us
    ppermute x1, starting transfers between devices, local(): lax.ppermute(own, TP, BOTH)  8.36 us
    all_to_all x1, starting transfers between devices, local(): summed = lax.all_to_all(summed, 'zh', 0, 0, tiled=True)  7.59 us
    all_to_all x1, waiting for transfers between devices, local(): weight = lax.all_to_all(block, 'y', 0, 0, tiled=True).reshape(-1, narrow)  7.17 us
    all_to_all x1, starting transfers between devices, local(): weight = lax.all_to_all(block, 'y', 0, 0, tiled=True).reshape(-1, narrow)  6.82 us
    ppermute x2, starting transfers between devices, from_group(): lax.ppermute(blocks[2], 'zl', SWAP)  6.62 us
  transfers between devices with their start and end apart: 12, of which 5 were waited for; matrix products, arithmetic and copies ran while one was open for 1% of the time, Pallas kernels for 5%

profile of v5, /device:TPU:1, one launch (start us, length us, event | category | flops | bytes accessed | tf_op | source)
XLA Modules:
  0.0 136.0 jit_solution(9452725014536043577)
XLA Ops:
  0.6 0.0 copy-start.4
  0.6 0.6 pad_add_fusion.place_ref
  1.2 3.8 %shard_map.68 = (bf16[256,1280]{1,0:T(8,128)(2,1)}, bf16[256,1280]{1,0:T(8,128)(2,1)}, bf16[256,1280]{1,0:T(8,128)(2,1)}, bf16[256,1280]{1,0:T(8,128)(2,1)}) custom-call(s32[2]{0:T(128)} %pad_add_fusion.place_ref, s32[1,4]{1,0:T(1,128)} %counts_ref.1, s32[1,4]{1,0:T(1,128)} %offsets_ref.1, bf16[256,256]{1,0:T(8,128)(2,1)} %grad_ref.1, ...), custom_call_target="tpu_custom_call" | custom-call | tf_op jit(solution)/shard_map/pallas_call | solution.py:100
  5.0 0.0 copy-start
  5.0 4.1 %collective-permute-start = (bf16[256,1280]{1,0:T(8,128)(2,1)}, bf16[256,1280]{1,0:T(8,128)(2,1)S(1)}, u32[]{:S(2)}, u32[]{:S(2)}) collective-permute-start(bf16[256,1280]{1,0:T(8,128)(2,1)} %get-tuple-element.28), channel_id=1, source_target_pairs={{0,32},{32,0},{1,33},{33,1},{2,34},{34,2},{3,35},{35,3},{4,36},{36... | collective-permute-start | bytes 1966088 | tf_op jit(solution)/shard_map/ppermute | solution.py:112
  9.1 4.0 %collective-permute-start.1 = (bf16[256,1280]{1,0:T(8,128)(2,1)}, bf16[256,1280]{1,0:T(8,128)(2,1)S(1)}, u32[]{:S(2)}, u32[]{:S(2)}) collective-permute-start(bf16[256,1280]{1,0:T(8,128)(2,1)} %get-tuple-element.29), channel_id=1, source_target_pairs={{0,64},{64,0},{1,65},{65,1},{2,66},{66,2},{3,67},{67,3},{4,68},{68... | collective-permute-start | bytes 1966088 | tf_op jit(solution)/shard_map/ppermute | solution.py:113
  13.1 1.9 %collective-permute-start.2 = (bf16[256,1280]{1,0:T(8,128)(2,1)}, bf16[256,1280]{1,0:T(8,128)(2,1)S(1)}, u32[]{:S(2)}, u32[]{:S(2)}) collective-permute-start(bf16[256,1280]{1,0:T(8,128)(2,1)} %get-tuple-element.30), channel_id=1, source_target_pairs={{0,96},{32,64},{64,32},{96,0},{1,97},{33,65},{65,33},{97,1},{2,98}... | collective-permute-start | bytes 1966088 | tf_op jit(solution)/shard_map/ppermute | solution.py:114
  15.0 0.0 copy-done.4
  15.1 44.5 %all_to_all.20 = bf16[32,4,256]{2,1,0:T(4,128)(2,1)S(1)} all-to-all(bf16[32,4,256]{2,1,0:T(4,128)(2,1)S(1)} %bitcast.8), channel_id=1, replica_groups=mesh['zh'=8,'zl'=2,'xl'=2,'y'=8,'xh'=2,'c'=2] {'xl','zh','zl'}, dimensions={0} | all-to-all | bytes 131072 | tf_op jit(solution)/shard_map/all_to_all | solution.py:135
  59.5 0.0 collective-permute-done.refs_1_
  59.5 0.0 collective-permute-done.1.refs_2_
  59.5 0.0 collective-permute-done.2.refs_3_
  59.5 0.0 copy-start.1
  59.6 0.9 broadcast_in_dim.10
  60.5 6.8 %all-to-all-start.1 = ((bf16[8,128,256]{2,1,0:T(8,128)(2,1)}), bf16[8,128,256]{2,1,0:T(8,128)(2,1)S(1)}, u32[]{:S(2)}, u32[]{:S(2)}) async-start(bf16[8,128,256]{2,1,0:T(8,128)(2,1)} %broadcast_in_dim.10), calls=%async_computation.1 | async-start | bytes 1048576 | tf_op jit(solution)/shard_map/all_to_all | solution.py:139
  67.3 0.0 copy-done
  67.4 0.0 copy-done.1
  67.5 4.7 %collective-permute-start.3 = (bf16[1024,256]{1,0:T(8,128)(2,1)S(1)}, bf16[1024,256]{1,0:T(8,128)(2,1)S(1)}, u32[]{:S(2)}, u32[]{:S(2)}) collective-permute-start(bf16[1024,256]{1,0:T(8,128)(2,1)S(1)} %pad_maximum_fusion.own_ref), channel_id=1, source_target_pairs={{0,1},{1,0},{2,3},{3,2},{4,5},{5,4},{6,7},{7,6},{8,9},{9,8},{10,11... | collective-permute-start | bytes 1572872 | tf_op jit(solution)/shard_map/ppermute | solution.py:145
  72.1 0.0 copy-start.2
  72.1 1.1 copy-done.2
  73.2 0.0 copy-start.3
  73.2 1.6 %shard_map.69 = bf16[8,128,256]{2,1,0:T(8,128)(2,1)} custom-call(bf16[256,1280]{1,0:T(8,128)(2,1)S(1)} %copy-done, bf16[256,1280]{1,0:T(8,128)(2,1)S(1)} %collective-permute-done.refs_1_, bf16[256,1280]{1,0:T(8,128)(2,1)S(1)} %collective-permute-done.1.refs_2_, bf16[256,1280]{1,0:T(8,128)(2,1)S(1)} %copy-done.2), custom_call_target="tpu_custom_call" | custom-call | tf_op jit(solution)/shard_map/pallas_call | solution.py:100
  74.8 0.0 collective-permute-done.3.core_ref
  74.8 7.2 %all-to-all-done.1 = bf16[8,128,256]{2,1,0:T(8,128)(2,1)S(1)} async-done(((bf16[8,128,256]{2,1,0:T(8,128)(2,1)}), bf16[8,128,256]{2,1,0:T(8,128)(2,1)S(1)}, u32[]{:S(2)}, u32[]{:S(2)}) %all-to-all-start.1) | async-done | bytes 524320 | tf_op jit(solution)/shard_map/all_to_all | solution.py:139
  82.0 3.5 %all-to-all-start.2 = ((bf16[8,128,256]{2,1,0:T(8,128)(2,1)}), bf16[8,128,256]{2,1,0:T(8,128)(2,1)S(1)}, u32[]{:S(2)}, u32[]{:S(2)}) async-start(bf16[8,128,256]{2,1,0:T(8,128)(2,1)} %shard_map.69), calls=%async_computation.2 | async-start | bytes 1048576 | tf_op jit(solution)/shard_map/all_to_all | solution.py:150
  85.5 8.4 %collective-permute-start.5 = (bf16[1024,256]{1,0:T(8,128)(2,1)S(1)}, bf16[1024,256]{1,0:T(8,128)(2,1)S(1)}, u32[]{:S(2)}, u32[]{:S(2)}) collective-permute-start(bf16[1024,256]{1,0:T(8,128)(2,1)S(1)} %pad_maximum_fusion.own_ref), channel_id=1, source_target_pairs={{0,3},{1,2},{2,1},{3,0},{4,7},{5,6},{6,5},{7,4},{8,11},{9,10},{10,... | collective-permute-start | bytes 1572872 | tf_op jit(solution)/shard_map/ppermute | solution.py:147
  93.8 2.1 %collective-permute-start.4 = (bf16[1024,256]{1,0:T(8,128)(2,1)S(1)}, bf16[1024,256]{1,0:T(8,128)(2,1)S(1)}, u32[]{:S(2)}, u32[]{:S(2)}) collective-permute-start(bf16[1024,256]{1,0:T(8,128)(2,1)S(1)} %pad_maximum_fusion.own_ref), channel_id=1, source_target_pairs={{0,2},{2,0},{1,3},{3,1},{4,6},{6,4},{5,7},{7,5},{8,10},{10,8},{9,1... | collective-permute-start | bytes 1572872 | tf_op jit(solution)/shard_map/ppermute | solution.py:146
  96.0 3.2 %all-to-all-done.2 = bf16[8,128,256]{2,1,0:T(8,128)(2,1)S(1)} async-done(((bf16[8,128,256]{2,1,0:T(8,128)(2,1)}), bf16[8,128,256]{2,1,0:T(8,128)(2,1)S(1)}, u32[]{:S(2)}, u32[]{:S(2)}) %all-to-all-start.2) | async-done | bytes 524320 | tf_op jit(solution)/shard_map/all_to_all | solution.py:150
  99.2 0.7 convert_reduce_fusion
  99.9 7.6 %all-to-all-start.3 = ((f32[8,16,256]{2,1,0:T(8,128)}), f32[8,16,256]{2,1,0:T(8,128)S(1)}, u32[]{:S(2)}, u32[]{:S(2)}) async-start(f32[8,16,256]{2,1,0:T(8,128)} %bitcast.6), calls=%async_computation.3 | async-start | bytes 262144 | tf_op jit(solution)/shard_map/all_to_all | solution.py:158
  107.5 0.0 collective-permute-done.5.both_ref
  107.5 10.1 %collective-permute-done.4.far_ref = bf16[1024,256]{1,0:T(8,128)(2,1)S(1)} collective-permute-done((bf16[1024,256]{1,0:T(8,128)(2,1)S(1)}, bf16[1024,256]{1,0:T(8,128)(2,1)S(1)}, u32[]{:S(2)}, u32[]{:S(2)}) %collective-permute-start.4) | collective-permute-done | bytes 524320 | tf_op jit(solution)/shard_map/ppermute | solution.py:146
  117.7 0.0 copy-done.3
  117.7 2.9 %shard_map.70.scaled_ref = bf16[1024,1024]{1,0:T(8,128)(2,1)S(1)} custom-call(s32[2]{0:T(128)S(1)} %copy-done.3, bf16[1024,256]{1,0:T(8,128)(2,1)S(1)} %pad_maximum_fusion.own_ref, bf16[1024,256]{1,0:T(8,128)(2,1)S(1)} %collective-permute-done.3.core_ref, bf16[1024,256]{1,0:T(8,128)(2,1)S(1)} %collective-permute-done.4.far_ref, ...), custom_call_target="tpu_custom_call" | custom-call | tf_op jit(solution)/shard_map/pallas_call | solution.py:100
  120.6 0.7 shard_map.71
  121.3 2.1 %collective-permute-start.6 = (bf16[256,256]{1,0:T(8,128)(2,1)S(1)}, bf16[256,256]{1,0:T(8,128)(2,1)S(1)}, u32[]{:S(2)}, u32[]{:S(2)}) collective-permute-start(bf16[256,256]{1,0:T(8,128)(2,1)S(1)} %get-tuple-element.40), channel_id=1, source_target_pairs={{0,32},{32,0},{1,33},{33,1},{2,34},{34,2},{3,35},{35,3},{4,36},{36... | collective-permute-start | bytes 393224 | tf_op jit(solution)/shard_map/ppermute | solution.py:112
  123.4 2.6 %collective-permute-start.7 = (bf16[256,256]{1,0:T(8,128)(2,1)S(1)}, bf16[256,256]{1,0:T(8,128)(2,1)S(1)}, u32[]{:S(2)}, u32[]{:S(2)}) collective-permute-start(bf16[256,256]{1,0:T(8,128)(2,1)S(1)} %get-tuple-element.41), channel_id=1, source_target_pairs={{0,64},{64,0},{1,65},{65,1},{2,66},{66,2},{3,67},{67,3},{4,68},{68... | collective-permute-start | bytes 393224 | tf_op jit(solution)/shard_map/ppermute | solution.py:113
  126.0 3.7 %collective-permute-start.8 = (bf16[256,256]{1,0:T(8,128)(2,1)S(1)}, bf16[256,256]{1,0:T(8,128)(2,1)S(1)}, u32[]{:S(2)}, u32[]{:S(2)}) collective-permute-start(bf16[256,256]{1,0:T(8,128)(2,1)S(1)} %get-tuple-element.42), channel_id=1, source_target_pairs={{0,96},{32,64},{64,32},{96,0},{1,97},{33,65},{65,33},{97,1},{2,98}... | collective-permute-start | bytes 393224 | tf_op jit(solution)/shard_map/ppermute | solution.py:114
  129.7 0.0 collective-permute-done.6.refs_1_
  129.7 0.3 collective-permute-done.7.refs_2_
  130.0 3.9 %collective-permute-done.8.refs_3_ = bf16[256,256]{1,0:T(8,128)(2,1)S(1)} collective-permute-done((bf16[256,256]{1,0:T(8,128)(2,1)S(1)}, bf16[256,256]{1,0:T(8,128)(2,1)S(1)}, u32[]{:S(2)}, u32[]{:S(2)}) %collective-permute-start.8) | collective-permute-done | bytes 131104 | tf_op jit(solution)/shard_map/ppermute | solution.py:114
  133.9 1.4 %shard_map.72 = bf16[256,1024]{1,0:T(8,128)(2,1)} custom-call(s32[2]{0:T(128)S(1)} %copy-done.3, bf16[256,256]{1,0:T(8,128)(2,1)S(1)} %get-tuple-element.39.refs_0_, bf16[256,256]{1,0:T(8,128)(2,1)S(1)} %collective-permute-done.6.refs_1_, bf16[256,256]{1,0:T(8,128)(2,1)S(1)} %collective-permute-done.7.refs_2_, ...), custom_call_target="tpu_custom_call" | custom-call | tf_op jit(solution)/shard_map/pallas_call | solution.py:100
  135.3 0.0 all-to-all-done.3
  135.3 0.6 broadcast_multiply_fusion
  (10 shorter events, 0.2 us)
Async XLA Ops:
  0.6 14.4 %copy-start.4 = (bf16[1024,4]{0,1:T(4,128)(2,1)S(1)}, bf16[1024,4]{0,1:T(4,128)(2,1)}, u32[]{:S(2)}) copy-start(bf16[1024,4]{0,1:T(4,128)(2,1)} %param.7) | copy-start | bytes 24580
  5.0 62.3 %copy-start = (bf16[256,1280]{1,0:T(8,128)(2,1)S(1)}, bf16[256,1280]{1,0:T(8,128)(2,1)}, u32[]{:S(2)}) copy-start(bf16[256,1280]{1,0:T(8,128)(2,1)} %get-tuple-element.32.refs_0_) | copy-start | bytes 1966084
  5.0 54.6 %collective-permute-start = (bf16[256,1280]{1,0:T(8,128)(2,1)}, bf16[256,1280]{1,0:T(8,128)(2,1)S(1)}, u32[]{:S(2)}, u32[]{:S(2)}) collective-permute-start(bf16[256,1280]{1,0:T(8,128)(2,1)} %get-tuple-element.28), channel_id=1, source_target_pairs={{0,32},{32,0},{1,33},{33,1},{2,34},{34,2},{3,35},{35,3},{4,36},{36... | collective-permute-start | bytes 1966088 | tf_op jit(solution)/shard_map/ppermute | solution.py:112
  9.1 50.5 %collective-permute-start.1 = (bf16[256,1280]{1,0:T(8,128)(2,1)}, bf16[256,1280]{1,0:T(8,128)(2,1)S(1)}, u32[]{:S(2)}, u32[]{:S(2)}) collective-permute-start(bf16[256,1280]{1,0:T(8,128)(2,1)} %get-tuple-element.29), channel_id=1, source_target_pairs={{0,64},{64,0},{1,65},{65,1},{2,66},{66,2},{3,67},{67,3},{4,68},{68... | collective-permute-start | bytes 1966088 | tf_op jit(solution)/shard_map/ppermute | solution.py:113
  13.1 46.5 %collective-permute-start.2 = (bf16[256,1280]{1,0:T(8,128)(2,1)}, bf16[256,1280]{1,0:T(8,128)(2,1)S(1)}, u32[]{:S(2)}, u32[]{:S(2)}) collective-permute-start(bf16[256,1280]{1,0:T(8,128)(2,1)} %get-tuple-element.30), channel_id=1, source_target_pairs={{0,96},{32,64},{64,32},{96,0},{1,97},{33,65},{65,33},{97,1},{2,98}... | collective-permute-start | bytes 1966088 | tf_op jit(solution)/shard_map/ppermute | solution.py:114
  59.5 7.8 %copy-start.1 = (bf16[256,1280]{1,0:T(8,128)(2,1)}, bf16[256,1280]{1,0:T(8,128)(2,1)S(1)}, u32[]{:S(2)}) copy-start(bf16[256,1280]{1,0:T(8,128)(2,1)S(1)} %collective-permute-done.2.refs_3_) | copy-start | bytes 1966084
  60.5 21.5 %all-to-all-start.1 = ((bf16[8,128,256]{2,1,0:T(8,128)(2,1)}), bf16[8,128,256]{2,1,0:T(8,128)(2,1)S(1)}, u32[]{:S(2)}, u32[]{:S(2)}) async-start(bf16[8,128,256]{2,1,0:T(8,128)(2,1)} %broadcast_in_dim.10), calls=%async_computation.1 | async-start | bytes 1048576 | tf_op jit(solution)/shard_map/all_to_all | solution.py:139
  67.5 7.3 %collective-permute-start.3 = (bf16[1024,256]{1,0:T(8,128)(2,1)S(1)}, bf16[1024,256]{1,0:T(8,128)(2,1)S(1)}, u32[]{:S(2)}, u32[]{:S(2)}) collective-permute-start(bf16[1024,256]{1,0:T(8,128)(2,1)S(1)} %pad_maximum_fusion.own_ref), channel_id=1, source_target_pairs={{0,1},{1,0},{2,3},{3,2},{4,5},{5,4},{6,7},{7,6},{8,9},{9,8},{10,11... | collective-permute-start | bytes 1572872 | tf_op jit(solution)/shard_map/ppermute | solution.py:145
  72.1 1.1 copy-start.2
  73.2 44.4 %copy-start.3 = (s32[2]{0:T(128)S(1)}, s32[2]{0:T(128)}, u32[]{:S(2)}) copy-start(s32[2]{0:T(128)} %pad_add_fusion.place_ref) | copy-start | bytes 28
  82.0 17.2 %all-to-all-start.2 = ((bf16[8,128,256]{2,1,0:T(8,128)(2,1)}), bf16[8,128,256]{2,1,0:T(8,128)(2,1)S(1)}, u32[]{:S(2)}, u32[]{:S(2)}) async-start(bf16[8,128,256]{2,1,0:T(8,128)(2,1)} %shard_map.69), calls=%async_computation.2 | async-start | bytes 1048576 | tf_op jit(solution)/shard_map/all_to_all | solution.py:150
  85.5 22.0 %collective-permute-start.5 = (bf16[1024,256]{1,0:T(8,128)(2,1)S(1)}, bf16[1024,256]{1,0:T(8,128)(2,1)S(1)}, u32[]{:S(2)}, u32[]{:S(2)}) collective-permute-start(bf16[1024,256]{1,0:T(8,128)(2,1)S(1)} %pad_maximum_fusion.own_ref), channel_id=1, source_target_pairs={{0,3},{1,2},{2,1},{3,0},{4,7},{5,6},{6,5},{7,4},{8,11},{9,10},{10,... | collective-permute-start | bytes 1572872 | tf_op jit(solution)/shard_map/ppermute | solution.py:147
  93.8 23.8 %collective-permute-start.4 = (bf16[1024,256]{1,0:T(8,128)(2,1)S(1)}, bf16[1024,256]{1,0:T(8,128)(2,1)S(1)}, u32[]{:S(2)}, u32[]{:S(2)}) collective-permute-start(bf16[1024,256]{1,0:T(8,128)(2,1)S(1)} %pad_maximum_fusion.own_ref), channel_id=1, source_target_pairs={{0,2},{2,0},{1,3},{3,1},{4,6},{6,4},{5,7},{7,5},{8,10},{10,8},{9,1... | collective-permute-start | bytes 1572872 | tf_op jit(solution)/shard_map/ppermute | solution.py:146
  99.9 35.4 %all-to-all-start.3 = ((f32[8,16,256]{2,1,0:T(8,128)}), f32[8,16,256]{2,1,0:T(8,128)S(1)}, u32[]{:S(2)}, u32[]{:S(2)}) async-start(f32[8,16,256]{2,1,0:T(8,128)} %bitcast.6), calls=%async_computation.3 | async-start | bytes 262144 | tf_op jit(solution)/shard_map/all_to_all | solution.py:158
  121.3 8.4 %collective-permute-start.6 = (bf16[256,256]{1,0:T(8,128)(2,1)S(1)}, bf16[256,256]{1,0:T(8,128)(2,1)S(1)}, u32[]{:S(2)}, u32[]{:S(2)}) collective-permute-start(bf16[256,256]{1,0:T(8,128)(2,1)S(1)} %get-tuple-element.40), channel_id=1, source_target_pairs={{0,32},{32,0},{1,33},{33,1},{2,34},{34,2},{3,35},{35,3},{4,36},{36... | collective-permute-start | bytes 393224 | tf_op jit(solution)/shard_map/ppermute | solution.py:112
  123.4 6.7 %collective-permute-start.7 = (bf16[256,256]{1,0:T(8,128)(2,1)S(1)}, bf16[256,256]{1,0:T(8,128)(2,1)S(1)}, u32[]{:S(2)}, u32[]{:S(2)}) collective-permute-start(bf16[256,256]{1,0:T(8,128)(2,1)S(1)} %get-tuple-element.41), channel_id=1, source_target_pairs={{0,64},{64,0},{1,65},{65,1},{2,66},{66,2},{3,67},{67,3},{4,68},{68... | collective-permute-start | bytes 393224 | tf_op jit(solution)/shard_map/ppermute | solution.py:113
  126.0 7.9 %collective-permute-start.8 = (bf16[256,256]{1,0:T(8,128)(2,1)S(1)}, bf16[256,256]{1,0:T(8,128)(2,1)S(1)}, u32[]{:S(2)}, u32[]{:S(2)}) collective-permute-start(bf16[256,256]{1,0:T(8,128)(2,1)S(1)} %get-tuple-element.42), channel_id=1, source_target_pairs={{0,96},{32,64},{64,32},{96,0},{1,97},{33,65},{65,33},{97,1},{2,98}... | collective-permute-start | bytes 393224 | tf_op jit(solution)/shard_map/ppermute | solution.py:114

commit v6 on v3

--- a/solution.py
+++ b/solution.py
@@ -16,10 +16,11 @@
 MIB = 1024 * 1024
 
 
-def prep_kernel(place_ref, counts_ref, offsets_ref, grad_ref, inputs_ref, *outs):
-    q = place_ref[0]
+def prep_kernel(place_ref, counts_ref, offsets_ref, grad_ref, inputs_ref, own_ref, *outs):
+    q, core = place_ref[0], place_ref[2]
     rows, columns = grad_ref.shape
-    blocks = (outs[0].shape[1] - columns) // 128
+    wide = own_ref.shape[1] - columns
+    short = rows // 2
     positions = lax.broadcasted_iota(jnp.int32, (rows, columns), 0)
     length = jnp.zeros((rows, columns), jnp.int32)
     for s in range(counts_ref.shape[1]):
@@ -28,29 +29,51 @@
         length = jnp.where((positions >= first) & (positions < first + count), count, length)
     factor = jnp.where(length > 0, lax.rsqrt(jnp.maximum(length, 1).astype(jnp.float32)), 0.0)
     scaled = (grad_ref[...].astype(jnp.float32) * factor).astype(jnp.bfloat16)
-    for m, out_ref in enumerate(outs):
-        target = q ^ m
-        for b in range(blocks):
-            source = pl.ds(pl.multiple_of((4 * b + target) * 128, 128), 128)
-            out_ref[:, b * 128 : (b + 1) * 128] = inputs_ref[:, source]
-        out_ref[:, blocks * 128 :] = scaled
+    own_ref[:, wide:] = scaled
+    mine = pl.ds(pl.multiple_of(core * short, short), short)
+    other = pl.ds(pl.multiple_of((1 - core) * short, short), short)
+    for b in range(wide // 128):
+        source = pl.ds(pl.multiple_of((4 * b + q) * 128, 128), 128)
+        own_ref[:, b * 128 : (b + 1) * 128] = inputs_ref[:, source]
+    for m, out_ref in enumerate(outs, 1):
+        for b in range(wide // 128):
+            source = pl.ds(pl.multiple_of((4 * b + (q ^ m)) * 128, 128), 128)
+            out_ref[:, b * 128 : (b + 1) * 128] = inputs_ref[mine, source]
+        out_ref[:, wide : wide + columns] = own_ref[mine, wide:]
+        out_ref[:, wide + columns :] = own_ref[other, wide:]
 
 
-def weight_kernel(*refs):
-    parts, out_ref = refs[:4], refs[4]
+def split_kernel(place_ref, own_ref, *refs):
+    parts, half_ref, scaled_ref = refs[:3], refs[3], refs[4]
+    core = place_ref[2]
+    short, wide = parts[0].shape[0], half_ref.shape[1]
+    columns = scaled_ref.shape[1]
+    scaled_ref[: 2 * short, :] = own_ref[:, wide:]
+    for m, part in enumerate(parts, 1):
+        half_ref[(m - 1) * short : m * short, :] = part[:, :wide]
+        mine = pl.ds(pl.multiple_of((2 * m + core) * short, short), short)
+        other = pl.ds(pl.multiple_of((2 * m + 1 - core) * short, short), short)
+        scaled_ref[mine, :] = part[:, wide : wide + columns]
+        scaled_ref[other, :] = part[:, wide + columns :]
+
+
+def weight_kernel(own_ref, *refs):
+    parts, half_ref, out_ref = refs[:3], refs[3], refs[4]
     peers, _, columns = out_ref.shape
-    wide = parts[0].shape[1] - columns
+    wide = half_ref.shape[1]
+    short = parts[0].shape[0]
     each = 128 // peers
+
+    def product(left, right):
+        dims = (((0,), (0,)), ((), ()))
+        return lax.dot_general(left, right, dims, preferred_element_type=jnp.float32)
+
     for b in range(wide // 128):
-        term = None
-        for part in parts:
-            product = lax.dot_general(
-                part[:, b * 128 : (b + 1) * 128],
-                part[:, wide:],
-                (((0,), (0,)), ((), ())),
-                preferred_element_type=jnp.float32,
-            )
-            term = product if term is None else term + product
+        block = slice(b * 128, (b + 1) * 128)
+        term = product(own_ref[:, block], own_ref[:, wide:])
+        for m, part in enumerate(parts):
+            term += product(part[:, block], part[:, wide : wide + columns])
+            term += product(half_ref[m * short : (m + 1) * short, block], part[:, wide + columns :])
         out_ref[:, b * each : (b + 1) * each, :] = term.reshape(peers, each, -1).astype(jnp.bfloat16)
 
 
@@ -123,9 +146,10 @@
     wide = features // 4
     narrow = quarter // 4
 
-    place = jnp.stack([lax.axis_index(("zl", "xl")), lax.axis_index(TP)]).astype(jnp.int32)
+    place = jnp.stack([lax.axis_index(a) for a in (("zl", "xl"), TP, "c")]).astype(jnp.int32)
     args = (place, counts, offsets, value_grad, inputs)
-    blocks = call(prep_kernel, [(rows, wide + columns)] * 4, 3, *args, vmem=60 * MIB)
+    sizes = [(rows, wide + columns)] + [(rows // 2, wide + 2 * columns)] * 3
+    blocks = call(prep_kernel, sizes, 3, *args, vmem=60 * MIB)
     blocks, value_weight = lax.optimization_barrier((blocks, value_weight))
     received = from_group(blocks)
 
@@ -138,16 +162,16 @@
     block = jnp.broadcast_to(block, (n_y, *block.shape))
     weight = lax.all_to_all(block, "y", 0, 0, tiled=True).reshape(-1, narrow)
 
-    (term,) = call(weight_kernel, [(n_y, wide // n_y, columns)], 0, *received)
-    own = jnp.concatenate([part[:, wide:] for part in received])
-    gathered = [
-        own,
-        lax.ppermute(own, "c", SWAP),
-        lax.ppermute(own, "xh", SWAP),
-        lax.ppermute(own, TP, BOTH),
-    ]
-    term, weight, gathered = lax.optimization_barrier((term, weight, gathered))
+    sizes = [(3 * rows // 2, wide), (4 * rows, columns)]
+    half, own = call(split_kernel, sizes, 1, place, *received)
+    half = lax.ppermute(half, "c", SWAP)
+    from_far = lax.ppermute(own, "xh", SWAP)
+    from_core = lax.ppermute(own, "c", SWAP)
+    (term,) = call(weight_kernel, [(n_y, wide // n_y, columns)], 0, *received, half)
+    early = (term, weight, from_far, from_core)
+    term, weight, from_far, from_core = lax.optimization_barrier(early)
     terms = lax.all_to_all(term, "y", 0, 0, tiled=True)
+    gathered = [own, from_core, from_far, lax.ppermute(from_far, "c", SWAP)]
 
     sizes = (2 * n_zh, n_y, own_columns)
     kernel = functools.partial(order_kernel, sizes)

time: 150 us -> 128 us (0.85); the launches traced: 147 us -> 127 us
  blocking collectives: 45.7 us -> 34.5 us
  waiting for transfers between devices: 32.8 us -> 26.7 us
  local copies, waits for them, and re-layouts: 5.77 us -> 2.75 us
    all_to_all x1, blocking collectives: 45.7 us -> 34.5 us  [local(): block = lax.all_to_all(mine, ('xl', 'zh', 'zl'), 0, 0, tiled=True)]
    all_to_all x1, waiting for transfers between devices: 13.2 us -> 8.94 us  [local(): terms = lax.all_to_all(term, 'y', 0, 0, tiled=True)]
    unnamed x18 -> x10, local copies, waits for them, and re-layouts: 4.76 us -> 1.85 us
    ppermute x3 -> x4, waiting for transfers between devices: 14 us -> 12.2 us  [the longest x1 10.3 us: local(): from_far = lax.ppermute(own, 'xh', SWAP)]
    pallas_call x5 -> x6, Pallas kernels: 10.3 us -> 10.9 us  [call(): pl.pallas_call(kernel, out_shape=shapes, in_specs=[pl.BlockSpec(memory_sp...]
    ppermute x3 -> x4, starting transfers between devices: 9.09 us -> 9.27 us  [the longest x1 3.31 us: local(): from_far = lax.ppermute(own, 'xh', SWAP)]
  transfers between devices with their start and end apart: 12 -> 13, of which waited for: 6 -> 5; matrix products, arithmetic and copies ran while one was open for 0% -> 0% of each run, Pallas kernels for 4% -> 6%
where the time goes in v6:
time: 128 us; the launch traced here: 127 us
  starting transfers between devices  49.6 us (39%)
  blocking collectives  34.5 us (27%)
  waiting for transfers between devices  26.7 us (21%)
  Pallas kernels  10.9 us (9%)
  local copies, waits for them, and re-layouts  2.75 us (2%)
  other arithmetic  1.92 us (2%)
    all_to_all x1, blocking collectives, local(): block = lax.all_to_all(mine, ('xl', 'zh', 'zl'), 0, 0, tiled=True)  34.5 us
    pallas_call x6, Pallas kernels, call(): pl.pallas_call(kernel, out_shape=shapes, in_specs=[pl.BlockSpec(memory_sp...  10.9 us
    ppermute x1, waiting for transfers between devices, local(): from_far = lax.ppermute(own, 'xh', SWAP)  10.3 us
    all_to_all x1, waiting for transfers between devices, local(): terms = lax.all_to_all(term, 'y', 0, 0, tiled=True)  8.94 us
    all_to_all x1, starting transfers between devices, local(): terms = lax.all_to_all(term, 'y', 0, 0, tiled=True)  7.2 us
    all_to_all x1, starting transfers between devices, local(): weight = lax.all_to_all(block, 'y', 0, 0, tiled=True).reshape(-1, narrow)  7.1 us
    all_to_all x1, starting transfers between devices, local(): summed = lax.all_to_all(summed, 'zh', 0, 0, tiled=True)  7.09 us
    ppermute x2, starting transfers between devices, from_group(): lax.ppermute(blocks[2], 'zl', SWAP)  6.98 us
  transfers between devices with their start and end apart: 13, of which 5 were waited for; matrix products, arithmetic and copies ran while one was open for 0% of the time, Pallas kernels for 6%

profile of v6, /device:TPU:6, one launch (start us, length us, event | category | flops | bytes accessed | tf_op | source)
XLA Modules:
  0.0 127.2 jit_solution(3680755594112041560)
XLA Ops:
  0.6 0.0 copy-start.4
  0.6 0.6 pad_add_fusion.place_ref
  1.2 0.0 copy-start.3
  1.2 3.3 %shard_map.68 = (bf16[256,1280]{1,0:T(8,128)(2,1)}, bf16[128,1536]{1,0:T(8,128)(2,1)}, bf16[128,1536]{1,0:T(8,128)(2,1)}, bf16[128,1536]{1,0:T(8,128)(2,1)}) custom-call(s32[3]{0:T(128)} %pad_add_fusion.place_ref, s32[1,4]{1,0:T(1,128)} %counts_ref.1, s32[1,4]{1,0:T(1,128)} %offsets_ref.1, bf16[256,256]{1,0:T(8,128)(2,1)} %grad_ref.1, ...), custom_call_target="tpu_custom_call" | custom-call | tf_op jit(solution)/shard_map/pallas_call | solution.py:123
  4.5 0.0 copy-start
  4.5 2.9 %collective-permute-start = (bf16[128,1536]{1,0:T(8,128)(2,1)}, bf16[128,1536]{1,0:T(8,128)(2,1)S(1)}, u32[]{:S(2)}, u32[]{:S(2)}) collective-permute-start(bf16[128,1536]{1,0:T(8,128)(2,1)} %get-tuple-element.36), channel_id=1, source_target_pairs={{0,32},{32,0},{1,33},{33,1},{2,34},{34,2},{3,35},{35,3},{4,36},{36... | collective-permute-start | bytes 1179656 | tf_op jit(solution)/shard_map/ppermute | solution.py:135
  7.4 4.3 %collective-permute-start.1 = (bf16[128,1536]{1,0:T(8,128)(2,1)}, bf16[128,1536]{1,0:T(8,128)(2,1)S(1)}, u32[]{:S(2)}, u32[]{:S(2)}) collective-permute-start(bf16[128,1536]{1,0:T(8,128)(2,1)} %get-tuple-element.37), channel_id=1, source_target_pairs={{0,64},{64,0},{1,65},{65,1},{2,66},{66,2},{3,67},{67,3},{4,68},{68... | collective-permute-start | bytes 1179656 | tf_op jit(solution)/shard_map/ppermute | solution.py:136
  11.7 2.6 %collective-permute-start.2 = (bf16[128,1536]{1,0:T(8,128)(2,1)}, bf16[128,1536]{1,0:T(8,128)(2,1)S(1)}, u32[]{:S(2)}, u32[]{:S(2)}) collective-permute-start(bf16[128,1536]{1,0:T(8,128)(2,1)} %get-tuple-element.38), channel_id=1, source_target_pairs={{0,96},{32,64},{64,32},{96,0},{1,97},{33,65},{65,33},{97,1},{2,98}... | collective-permute-start | bytes 1179656 | tf_op jit(solution)/shard_map/ppermute | solution.py:137
  14.2 0.0 copy-done.4
  14.3 34.5 %all_to_all.20 = bf16[32,4,256]{2,1,0:T(4,128)(2,1)S(1)} all-to-all(bf16[32,4,256]{2,1,0:T(4,128)(2,1)S(1)} %bitcast.9), channel_id=1, replica_groups=mesh['zh'=8,'zl'=2,'xl'=2,'y'=8,'xh'=2,'c'=2] {'xl','zh','zl'}, dimensions={0} | all-to-all | bytes 131072 | tf_op jit(solution)/shard_map/all_to_all | solution.py:159
  48.8 0.0 collective-permute-done.refs_0_
  48.8 0.0 collective-permute-done.1.refs_1_
  48.8 0.0 collective-permute-done.2.refs_2_
  48.8 0.8 broadcast_in_dim.10
  49.7 7.1 %all-to-all-start.1 = ((bf16[8,128,256]{2,1,0:T(8,128)(2,1)}), bf16[8,128,256]{2,1,0:T(8,128)(2,1)S(1)}, u32[]{:S(2)}, u32[]{:S(2)}) async-start(bf16[8,128,256]{2,1,0:T(8,128)(2,1)} %broadcast_in_dim.10), calls=%async_computation.1 | async-start | bytes 1048576 | tf_op jit(solution)/shard_map/all_to_all | solution.py:163
  56.8 0.0 copy-done.3
  56.8 0.0 copy-done
  56.8 0.6 shard_map.69
  57.4 1.9 %collective-permute-start.3 = (bf16[384,1024]{1,0:T(8,128)(2,1)S(1)}, bf16[384,1024]{1,0:T(8,128)(2,1)S(1)}, u32[]{:S(2)}, u32[]{:S(2)}) collective-permute-start(bf16[384,1024]{1,0:T(8,128)(2,1)S(1)} %get-tuple-element.44), channel_id=1, source_target_pairs={{0,1},{1,0},{2,3},{3,2},{4,5},{5,4},{6,7},{7,6},{8,9},{9,8},{10,11... | collective-permute-start | bytes 2359304 | tf_op jit(solution)/shard_map/ppermute | solution.py:167
  59.3 3.3 %collective-permute-start.4 = (bf16[1024,256]{1,0:T(8,128)(2,1)S(1)}, bf16[1024,256]{1,0:T(8,128)(2,1)S(1)}, u32[]{:S(2)}, u32[]{:S(2)}) collective-permute-start(bf16[1024,256]{1,0:T(8,128)(2,1)S(1)} %get-tuple-element.46.own_ref), channel_id=1, source_target_pairs={{0,2},{2,0},{1,3},{3,1},{4,6},{6,4},{5,7},{7,5},{8,10},{10,8},{9,1... | collective-permute-start | bytes 1572872 | tf_op jit(solution)/shard_map/ppermute | solution.py:168
  62.7 2.1 %collective-permute-start.5 = (bf16[1024,256]{1,0:T(8,128)(2,1)S(1)}, bf16[1024,256]{1,0:T(8,128)(2,1)S(1)}, u32[]{:S(2)}, u32[]{:S(2)}) collective-permute-start(bf16[1024,256]{1,0:T(8,128)(2,1)S(1)} %get-tuple-element.46.own_ref), channel_id=1, source_target_pairs={{0,1},{1,0},{2,3},{3,2},{4,5},{5,4},{6,7},{7,6},{8,9},{9,8},{10,11... | collective-permute-start | bytes 1572872 | tf_op jit(solution)/shard_map/ppermute | solution.py:169
  64.8 0.0 collective-permute-done.3.refs_3_
  64.8 2.0 %shard_map.70 = bf16[8,128,256]{2,1,0:T(8,128)(2,1)} custom-call(bf16[256,1280]{1,0:T(8,128)(2,1)S(1)} %copy-done, bf16[128,1536]{1,0:T(8,128)(2,1)S(1)} %collective-permute-done.refs_0_, bf16[128,1536]{1,0:T(8,128)(2,1)S(1)} %collective-permute-done.1.refs_1_, bf16[128,1536]{1,0:T(8,128)(2,1)S(1)} %collective-permute-done.2.refs_2_, ...), custom_call_target="tpu_custom_call" | custom-call | tf_op jit(solution)/shard_map/pallas_call | solution.py:123
  66.8 10.3 %collective-permute-done.4.far_ref = bf16[1024,256]{1,0:T(8,128)(2,1)S(1)} collective-permute-done((bf16[1024,256]{1,0:T(8,128)(2,1)S(1)}, bf16[1024,256]{1,0:T(8,128)(2,1)S(1)}, u32[]{:S(2)}, u32[]{:S(2)}) %collective-permute-start.4) | collective-permute-done | bytes 524320 | tf_op jit(solution)/shard_map/ppermute | solution.py:168
  77.1 0.0 collective-permute-done.5.core_ref
  77.1 0.0 copy-start.1
  77.1 0.8 copy-done.1
  77.9 0.0 all-to-all-done.1
  77.9 7.2 %all-to-all-start.2 = ((bf16[8,128,256]{2,1,0:T(8,128)(2,1)}), bf16[8,128,256]{2,1,0:T(8,128)(2,1)S(1)}, u32[]{:S(2)}, u32[]{:S(2)}) async-start(bf16[8,128,256]{2,1,0:T(8,128)(2,1)} %shard_map.70), calls=%async_computation.2 | async-start | bytes 1048576 | tf_op jit(solution)/shard_map/all_to_all | solution.py:173
  85.1 1.9 %collective-permute-start.6 = (bf16[1024,256]{1,0:T(8,128)(2,1)S(1)}, bf16[1024,256]{1,0:T(8,128)(2,1)S(1)}, u32[]{:S(2)}, u32[]{:S(2)}) collective-permute-start(bf16[1024,256]{1,0:T(8,128)(2,1)S(1)} %collective-permute-done.4.far_ref), channel_id=1, source_target_pairs={{0,1},{1,0},{2,3},{3,2},{4,5},{5,4},{6,7},{7,6},{8,9},{9,8},{10,11... | collective-permute-start | bytes 1572872 | tf_op jit(solution)/shard_map/ppermute | solution.py:174
  87.0 1.9 %collective-permute-done.6.both_ref = bf16[1024,256]{1,0:T(8,128)(2,1)S(1)} collective-permute-done((bf16[1024,256]{1,0:T(8,128)(2,1)S(1)}, bf16[1024,256]{1,0:T(8,128)(2,1)S(1)}, u32[]{:S(2)}, u32[]{:S(2)}) %collective-permute-start.6) | collective-permute-done | bytes 524320 | tf_op jit(solution)/shard_map/ppermute | solution.py:174
  88.9 0.0 copy-start.2
  88.9 1.0 copy-done.2
  89.9 2.9 %shard_map.71.scaled_ref = bf16[1024,1024]{1,0:T(8,128)(2,1)S(1)} custom-call(s32[3]{0:T(128)S(1)} %copy-done.3, bf16[1024,256]{1,0:T(8,128)(2,1)S(1)} %get-tuple-element.46.own_ref, bf16[1024,256]{1,0:T(8,128)(2,1)S(1)} %copy-done.2, bf16[1024,256]{1,0:T(8,128)(2,1)S(1)} %collective-permute-done.4.far_ref, bf16[1024,256]{1,0:T(8,128)(2,1)S(1)} %collective-permute-done.6.both_ref), custom_call_target="tpu_custom_call" | custom-call | tf_op jit(solution)/shard_map/pallas_call | solution.py:123
  92.8 0.7 shard_map.72
  93.5 8.9 %all-to-all-done.2 = bf16[8,128,256]{2,1,0:T(8,128)(2,1)S(1)} async-done(((bf16[8,128,256]{2,1,0:T(8,128)(2,1)}), bf16[8,128,256]{2,1,0:T(8,128)(2,1)S(1)}, u32[]{:S(2)}, u32[]{:S(2)}) %all-to-all-start.2) | async-done | bytes 524320 | tf_op jit(solution)/shard_map/all_to_all | solution.py:173
  102.5 0.7 convert_reduce_fusion
  103.2 7.1 %all-to-all-start.3 = ((f32[8,16,256]{2,1,0:T(8,128)}), f32[8,16,256]{2,1,0:T(8,128)S(1)}, u32[]{:S(2)}, u32[]{:S(2)}) async-start(f32[8,16,256]{2,1,0:T(8,128)} %bitcast.7), calls=%async_computation.3 | async-start | bytes 262144 | tf_op jit(solution)/shard_map/all_to_all | solution.py:183
  110.3 2.7 %collective-permute-start.7 = (bf16[256,256]{1,0:T(8,128)(2,1)S(1)}, bf16[256,256]{1,0:T(8,128)(2,1)S(1)}, u32[]{:S(2)}, u32[]{:S(2)}) collective-permute-start(bf16[256,256]{1,0:T(8,128)(2,1)S(1)} %get-tuple-element.56), channel_id=1, source_target_pairs={{0,32},{32,0},{1,33},{33,1},{2,34},{34,2},{3,35},{35,3},{4,36},{36... | collective-permute-start | bytes 393224 | tf_op jit(solution)/shard_map/ppermute | solution.py:135
  113.0 2.7 %collective-permute-start.8 = (bf16[256,256]{1,0:T(8,128)(2,1)S(1)}, bf16[256,256]{1,0:T(8,128)(2,1)S(1)}, u32[]{:S(2)}, u32[]{:S(2)}) collective-permute-start(bf16[256,256]{1,0:T(8,128)(2,1)S(1)} %get-tuple-element.57), channel_id=1, source_target_pairs={{0,64},{64,0},{1,65},{65,1},{2,66},{66,2},{3,67},{67,3},{4,68},{68... | collective-permute-start | bytes 393224 | tf_op jit(solution)/shard_map/ppermute | solution.py:136
  115.7 3.8 %collective-permute-start.9 = (bf16[256,256]{1,0:T(8,128)(2,1)S(1)}, bf16[256,256]{1,0:T(8,128)(2,1)S(1)}, u32[]{:S(2)}, u32[]{:S(2)}) collective-permute-start(bf16[256,256]{1,0:T(8,128)(2,1)S(1)} %get-tuple-element.58), channel_id=1, source_target_pairs={{0,96},{32,64},{64,32},{96,0},{1,97},{33,65},{65,33},{97,1},{2,98}... | collective-permute-start | bytes 393224 | tf_op jit(solution)/shard_map/ppermute | solution.py:137
  119.5 0.0 collective-permute-done.7.refs_1_
  119.5 3.2 %collective-permute-done.8.refs_2_ = bf16[256,256]{1,0:T(8,128)(2,1)S(1)} collective-permute-done((bf16[256,256]{1,0:T(8,128)(2,1)S(1)}, bf16[256,256]{1,0:T(8,128)(2,1)S(1)}, u32[]{:S(2)}, u32[]{:S(2)}) %collective-permute-start.8) | collective-permute-done | bytes 131104 | tf_op jit(solution)/shard_map/ppermute | solution.py:136
  122.7 2.4 %collective-permute-done.9.refs_3_ = bf16[256,256]{1,0:T(8,128)(2,1)S(1)} collective-permute-done((bf16[256,256]{1,0:T(8,128)(2,1)S(1)}, bf16[256,256]{1,0:T(8,128)(2,1)S(1)}, u32[]{:S(2)}, u32[]{:S(2)}) %collective-permute-start.9) | collective-permute-done | bytes 131104 | tf_op jit(solution)/shard_map/ppermute | solution.py:137
  125.1 1.4 %shard_map.73 = bf16[256,1024]{1,0:T(8,128)(2,1)} custom-call(s32[3]{0:T(128)S(1)} %copy-done.3, bf16[256,256]{1,0:T(8,128)(2,1)S(1)} %get-tuple-element.55.refs_0_, bf16[256,256]{1,0:T(8,128)(2,1)S(1)} %collective-permute-done.7.refs_1_, bf16[256,256]{1,0:T(8,128)(2,1)S(1)} %collective-permute-done.8.refs_2_, ...), custom_call_target="tpu_custom_call" | custom-call | tf_op jit(solution)/shard_map/pallas_call | solution.py:123
  126.5 0.0 all-to-all-done.3
  126.5 0.6 broadcast_multiply_fusion
  (5 shorter events, 0.1 us)
Async XLA Ops:
  0.6 13.6 %copy-start.4 = (bf16[1024,4]{0,1:T(4,128)(2,1)S(1)}, bf16[1024,4]{0,1:T(4,128)(2,1)}, u32[]{:S(2)}) copy-start(bf16[1024,4]{0,1:T(4,128)(2,1)} %param.7) | copy-start | bytes 24580
  1.2 55.6 %copy-start.3 = (s32[3]{0:T(128)S(1)}, s32[3]{0:T(128)}, u32[]{:S(2)}) copy-start(s32[3]{0:T(128)} %pad_add_fusion.place_ref) | copy-start | bytes 40
  4.5 52.3 %copy-start = (bf16[256,1280]{1,0:T(8,128)(2,1)S(1)}, bf16[256,1280]{1,0:T(8,128)(2,1)}, u32[]{:S(2)}) copy-start(bf16[256,1280]{1,0:T(8,128)(2,1)} %get-tuple-element.40.own_ref) | copy-start | bytes 1966084
  4.5 44.3 %collective-permute-start = (bf16[128,1536]{1,0:T(8,128)(2,1)}, bf16[128,1536]{1,0:T(8,128)(2,1)S(1)}, u32[]{:S(2)}, u32[]{:S(2)}) collective-permute-start(bf16[128,1536]{1,0:T(8,128)(2,1)} %get-tuple-element.36), channel_id=1, source_target_pairs={{0,32},{32,0},{1,33},{33,1},{2,34},{34,2},{3,35},{35,3},{4,36},{36... | collective-permute-start | bytes 1179656 | tf_op jit(solution)/shard_map/ppermute | solution.py:135
  7.4 41.4 %collective-permute-start.1 = (bf16[128,1536]{1,0:T(8,128)(2,1)}, bf16[128,1536]{1,0:T(8,128)(2,1)S(1)}, u32[]{:S(2)}, u32[]{:S(2)}) collective-permute-start(bf16[128,1536]{1,0:T(8,128)(2,1)} %get-tuple-element.37), channel_id=1, source_target_pairs={{0,64},{64,0},{1,65},{65,1},{2,66},{66,2},{3,67},{67,3},{4,68},{68... | collective-permute-start | bytes 1179656 | tf_op jit(solution)/shard_map/ppermute | solution.py:136
  11.7 37.1 %collective-permute-start.2 = (bf16[128,1536]{1,0:T(8,128)(2,1)}, bf16[128,1536]{1,0:T(8,128)(2,1)S(1)}, u32[]{:S(2)}, u32[]{:S(2)}) collective-permute-start(bf16[128,1536]{1,0:T(8,128)(2,1)} %get-tuple-element.38), channel_id=1, source_target_pairs={{0,96},{32,64},{64,32},{96,0},{1,97},{33,65},{65,33},{97,1},{2,98}... | collective-permute-start | bytes 1179656 | tf_op jit(solution)/shard_map/ppermute | solution.py:137
  49.7 28.2 %all-to-all-start.1 = ((bf16[8,128,256]{2,1,0:T(8,128)(2,1)}), bf16[8,128,256]{2,1,0:T(8,128)(2,1)S(1)}, u32[]{:S(2)}, u32[]{:S(2)}) async-start(bf16[8,128,256]{2,1,0:T(8,128)(2,1)} %broadcast_in_dim.10), calls=%async_computation.1 | async-start | bytes 1048576 | tf_op jit(solution)/shard_map/all_to_all | solution.py:163
  57.4 7.4 %collective-permute-start.3 = (bf16[384,1024]{1,0:T(8,128)(2,1)S(1)}, bf16[384,1024]{1,0:T(8,128)(2,1)S(1)}, u32[]{:S(2)}, u32[]{:S(2)}) collective-permute-start(bf16[384,1024]{1,0:T(8,128)(2,1)S(1)} %get-tuple-element.44), channel_id=1, source_target_pairs={{0,1},{1,0},{2,3},{3,2},{4,5},{5,4},{6,7},{7,6},{8,9},{9,8},{10,11... | collective-permute-start | bytes 2359304 | tf_op jit(solution)/shard_map/ppermute | solution.py:167
  59.3 17.7 %collective-permute-start.4 = (bf16[1024,256]{1,0:T(8,128)(2,1)S(1)}, bf16[1024,256]{1,0:T(8,128)(2,1)S(1)}, u32[]{:S(2)}, u32[]{:S(2)}) collective-permute-start(bf16[1024,256]{1,0:T(8,128)(2,1)S(1)} %get-tuple-element.46.own_ref), channel_id=1, source_target_pairs={{0,2},{2,0},{1,3},{3,1},{4,6},{6,4},{5,7},{7,5},{8,10},{10,8},{9,1... | collective-permute-start | bytes 1572872 | tf_op jit(solution)/shard_map/ppermute | solution.py:168
  62.7 14.4 %collective-permute-start.5 = (bf16[1024,256]{1,0:T(8,128)(2,1)S(1)}, bf16[1024,256]{1,0:T(8,128)(2,1)S(1)}, u32[]{:S(2)}, u32[]{:S(2)}) collective-permute-start(bf16[1024,256]{1,0:T(8,128)(2,1)S(1)} %get-tuple-element.46.own_ref), channel_id=1, source_target_pairs={{0,1},{1,0},{2,3},{3,2},{4,5},{5,4},{6,7},{7,6},{8,9},{9,8},{10,11... | collective-permute-start | bytes 1572872 | tf_op jit(solution)/shard_map/ppermute | solution.py:169
  77.1 0.8 copy-start.1
  77.9 24.6 %all-to-all-start.2 = ((bf16[8,128,256]{2,1,0:T(8,128)(2,1)}), bf16[8,128,256]{2,1,0:T(8,128)(2,1)S(1)}, u32[]{:S(2)}, u32[]{:S(2)}) async-start(bf16[8,128,256]{2,1,0:T(8,128)(2,1)} %shard_map.70), calls=%async_computation.2 | async-start | bytes 1048576 | tf_op jit(solution)/shard_map/all_to_all | solution.py:173
  85.1 3.8 %collective-permute-start.6 = (bf16[1024,256]{1,0:T(8,128)(2,1)S(1)}, bf16[1024,256]{1,0:T(8,128)(2,1)S(1)}, u32[]{:S(2)}, u32[]{:S(2)}) collective-permute-start(bf16[1024,256]{1,0:T(8,128)(2,1)S(1)} %collective-permute-done.4.far_ref), channel_id=1, source_target_pairs={{0,1},{1,0},{2,3},{3,2},{4,5},{5,4},{6,7},{7,6},{8,9},{9,8},{10,11... | collective-permute-start | bytes 1572872 | tf_op jit(solution)/shard_map/ppermute | solution.py:174
  88.9 1.0 copy-start.2
  103.2 23.3 %all-to-all-start.3 = ((f32[8,16,256]{2,1,0:T(8,128)}), f32[8,16,256]{2,1,0:T(8,128)S(1)}, u32[]{:S(2)}, u32[]{:S(2)}) async-start(f32[8,16,256]{2,1,0:T(8,128)} %bitcast.7), calls=%async_computation.3 | async-start | bytes 262144 | tf_op jit(solution)/shard_map/all_to_all | solution.py:183
  110.3 9.2 %collective-permute-start.7 = (bf16[256,256]{1,0:T(8,128)(2,1)S(1)}, bf16[256,256]{1,0:T(8,128)(2,1)S(1)}, u32[]{:S(2)}, u32[]{:S(2)}) collective-permute-start(bf16[256,256]{1,0:T(8,128)(2,1)S(1)} %get-tuple-element.56), channel_id=1, source_target_pairs={{0,32},{32,0},{1,33},{33,1},{2,34},{34,2},{3,35},{35,3},{4,36},{36... | collective-permute-start | bytes 393224 | tf_op jit(solution)/shard_map/ppermute | solution.py:135
  113.0 9.7 %collective-permute-start.8 = (bf16[256,256]{1,0:T(8,128)(2,1)S(1)}, bf16[256,256]{1,0:T(8,128)(2,1)S(1)}, u32[]{:S(2)}, u32[]{:S(2)}) collective-permute-start(bf16[256,256]{1,0:T(8,128)(2,1)S(1)} %get-tuple-element.57), channel_id=1, source_target_pairs={{0,64},{64,0},{1,65},{65,1},{2,66},{66,2},{3,67},{67,3},{4,68},{68... | collective-permute-start | bytes 393224 | tf_op jit(solution)/shard_map/ppermute | solution.py:136
  115.7 9.4 %collective-permute-start.9 = (bf16[256,256]{1,0:T(8,128)(2,1)S(1)}, bf16[256,256]{1,0:T(8,128)(2,1)S(1)}, u32[]{:S(2)}, u32[]{:S(2)}) collective-permute-start(bf16[256,256]{1,0:T(8,128)(2,1)S(1)} %get-tuple-element.58), channel_id=1, source_target_pairs={{0,96},{32,64},{64,32},{96,0},{1,97},{33,65},{65,33},{97,1},{2,98}... | collective-permute-start | bytes 393224 | tf_op jit(solution)/shard_map/ppermute | solution.py:137

commit v7 on v6

--- a/solution.py
+++ b/solution.py
@@ -164,12 +164,12 @@
 
     sizes = [(3 * rows // 2, wide), (4 * rows, columns)]
     half, own = call(split_kernel, sizes, 1, place, *received)
+    from_far = lax.ppermute(own, "xh", SWAP)
     half = lax.ppermute(half, "c", SWAP)
-    from_far = lax.ppermute(own, "xh", SWAP)
+    half, from_far = lax.optimization_barrier((half, from_far))
     from_core = lax.ppermute(own, "c", SWAP)
     (term,) = call(weight_kernel, [(n_y, wide // n_y, columns)], 0, *received, half)
-    early = (term, weight, from_far, from_core)
-    term, weight, from_far, from_core = lax.optimization_barrier(early)
+    term, weight = lax.optimization_barrier((term, weight))
     terms = lax.all_to_all(term, "y", 0, 0, tiled=True)
     gathered = [own, from_core, from_far, lax.ppermute(from_far, "c", SWAP)]
 
@@ -178,13 +178,14 @@
     (ordered,) = call(kernel, [(4 * rows, n_tp * columns)], 1, place, *gathered)
     outs = call(input_kernel, [(rows, narrow)] * 4, 0, ordered, weight)
 
-    terms, outs = lax.optimization_barrier((terms, outs))
+    outs = from_group(outs)
+    terms, outs[1], outs[2] = lax.optimization_barrier((terms, outs[1], outs[2]))
     summed = jnp.sum(terms.astype(jnp.float32), axis=0).reshape(n_zh, -1, columns)
     summed = lax.all_to_all(summed, "zh", 0, 0, tiled=True)
     normalizer = 1.0 / math.sqrt(counts.shape[1] * lax.axis_size(FSDP))
     weight_grad = jnp.sum(summed, axis=0) * normalizer
 
-    (input_grad,) = call(join_kernel, [(rows, quarter)], 1, place, *from_group(outs))
+    (input_grad,) = call(join_kernel, [(rows, quarter)], 1, place, *outs)
     return (input_grad, weight_grad)
 
 

time: 128 us -> 132 us (1.031)
  waiting for transfers between devices: 26.7 us -> 31.3 us
  local copies, waits for them, and re-layouts: 2.75 us -> 0.9 us
    all_to_all x1, waiting for transfers between devices: 8.94 us -> 0.01 us  [local(): terms = lax.all_to_all(term, 'y', 0, 0, tiled=True)]
    ppermute x2, waiting for transfers between devices: 2.43 us -> 7.07 us  [from_group(): lax.ppermute(blocks[3], ('zl', 'xl'), BOTH)]
    ppermute x1, waiting for transfers between devices: 10.3 us -> 14.4 us  [local(): from_far = lax.ppermute(own, 'xh', SWAP)]
    all_to_all x1, waiting for transfers between devices: 0.01 us -> 3.92 us  [local(): summed = lax.all_to_all(summed, 'zh', 0, 0, tiled=True)]
    ppermute x2, waiting for transfers between devices: 0.01 us -> 1.89 us  [from_group(): lax.ppermute(blocks[1], 'xl', SWAP)]
    unnamed x10 -> x6, local copies, waits for them, and re-layouts: 1.85 us -> 0.01 us
  transfers between devices with their start and end apart: 13 -> 13, of which waited for: 5 -> 6; matrix products, arithmetic and copies ran while one was open for 0% -> 0% of each run, Pallas kernels for 6% -> 6%
where the time goes in v7:
time: 132 us; the launch traced here: 130 us
  starting transfers between devices  49.7 us (38%)
  blocking collectives  34.5 us (26%)
  waiting for transfers between devices  31.3 us (24%)
  Pallas kernels  10.8 us (8%)
  other arithmetic  2 us (2%)
    all_to_all x1, blocking collectives, local(): block = lax.all_to_all(mine, ('xl', 'zh', 'zl'), 0, 0, tiled=True)  34.5 us
    ppermute x1, waiting for transfers between devices, local(): from_far = lax.ppermute(own, 'xh', SWAP)  14.4 us
    pallas_call x6, Pallas kernels, call(): pl.pallas_call(kernel, out_shape=shapes, in_specs=[pl.BlockSpec(memory_sp...  10.8 us
    ppermute x2, starting transfers between devices, from_group(): lax.ppermute(blocks[2], 'zl', SWAP)  7.3 us
    all_to_all x1, starting transfers between devices, local(): terms = lax.all_to_all(term, 'y', 0, 0, tiled=True)  7.2 us
    all_to_all x1, starting transfers between devices, local(): weight = lax.all_to_all(block, 'y', 0, 0, tiled=True).reshape(-1, narrow)  7.1 us
    all_to_all x1, starting transfers between devices, local(): summed = lax.all_to_all(summed, 'zh', 0, 0, tiled=True)  7.09 us
    ppermute x2, waiting for transfers between devices, from_group(): lax.ppermute(blocks[3], ('zl', 'xl'), BOTH)  7.07 us
  transfers between devices with their start and end apart: 13, of which 6 were waited for; matrix products, arithmetic and copies ran while one was open for 0% of the time, Pallas kernels for 6%

profile of v7, /device:TPU:6, one launch (start us, length us, event | category | flops | bytes accessed | tf_op | source)
XLA Modules:
  0.0 130.0 jit_solution(11325164481232737759)
XLA Ops:
  0.6 0.0 copy-start.2
  0.6 0.7 pad_add_fusion.place_ref
  1.3 0.0 copy-start.1
  1.3 3.3 %shard_map.68 = (bf16[256,1280]{1,0:T(8,128)(2,1)}, bf16[128,1536]{1,0:T(8,128)(2,1)}, bf16[128,1536]{1,0:T(8,128)(2,1)}, bf16[128,1536]{1,0:T(8,128)(2,1)}) custom-call(s32[3]{0:T(128)} %pad_add_fusion.place_ref, s32[1,4]{1,0:T(1,128)} %counts_ref.1, s32[1,4]{1,0:T(1,128)} %offsets_ref.1, bf16[256,256]{1,0:T(8,128)(2,1)} %grad_ref.1, ...), custom_call_target="tpu_custom_call" | custom-call | tf_op jit(solution)/shard_map/pallas_call | solution.py:123
  4.6 0.0 copy-start
  4.6 2.9 %collective-permute-start = (bf16[128,1536]{1,0:T(8,128)(2,1)}, bf16[128,1536]{1,0:T(8,128)(2,1)S(1)}, u32[]{:S(2)}, u32[]{:S(2)}) collective-permute-start(bf16[128,1536]{1,0:T(8,128)(2,1)} %get-tuple-element.34), channel_id=1, source_target_pairs={{0,32},{32,0},{1,33},{33,1},{2,34},{34,2},{3,35},{35,3},{4,36},{36... | collective-permute-start | bytes 1179656 | tf_op jit(solution)/shard_map/ppermute | solution.py:135
  7.4 4.3 %collective-permute-start.1 = (bf16[128,1536]{1,0:T(8,128)(2,1)}, bf16[128,1536]{1,0:T(8,128)(2,1)S(1)}, u32[]{:S(2)}, u32[]{:S(2)}) collective-permute-start(bf16[128,1536]{1,0:T(8,128)(2,1)} %get-tuple-element.35), channel_id=1, source_target_pairs={{0,64},{64,0},{1,65},{65,1},{2,66},{66,2},{3,67},{67,3},{4,68},{68... | collective-permute-start | bytes 1179656 | tf_op jit(solution)/shard_map/ppermute | solution.py:136
  11.7 2.6 %collective-permute-start.2 = (bf16[128,1536]{1,0:T(8,128)(2,1)}, bf16[128,1536]{1,0:T(8,128)(2,1)S(1)}, u32[]{:S(2)}, u32[]{:S(2)}) collective-permute-start(bf16[128,1536]{1,0:T(8,128)(2,1)} %get-tuple-element.36), channel_id=1, source_target_pairs={{0,96},{32,64},{64,32},{96,0},{1,97},{33,65},{65,33},{97,1},{2,98}... | collective-permute-start | bytes 1179656 | tf_op jit(solution)/shard_map/ppermute | solution.py:137
  14.3 0.0 copy-done.2
  14.4 34.5 %all_to_all.20 = bf16[32,4,256]{2,1,0:T(4,128)(2,1)S(1)} all-to-all(bf16[32,4,256]{2,1,0:T(4,128)(2,1)S(1)} %bitcast.9), channel_id=1, replica_groups=mesh['zh'=8,'zl'=2,'xl'=2,'y'=8,'xh'=2,'c'=2] {'xl','zh','zl'}, dimensions={0} | all-to-all | bytes 131072 | tf_op jit(solution)/shard_map/all_to_all | solution.py:159
  48.9 0.0 collective-permute-done.refs_0_
  48.9 0.0 collective-permute-done.1.refs_1_
  48.9 0.0 collective-permute-done.2.refs_2_
  48.9 0.8 broadcast_in_dim.10
  49.7 7.1 %all-to-all-start.1 = ((bf16[8,128,256]{2,1,0:T(8,128)(2,1)}), bf16[8,128,256]{2,1,0:T(8,128)(2,1)S(1)}, u32[]{:S(2)}, u32[]{:S(2)}) async-start(bf16[8,128,256]{2,1,0:T(8,128)(2,1)} %broadcast_in_dim.10), calls=%async_computation.1 | async-start | bytes 1048576 | tf_op jit(solution)/shard_map/all_to_all | solution.py:163
  56.8 0.0 copy-done.1
  56.8 0.0 copy-done
  56.9 0.6 shard_map.69
  57.5 1.9 %collective-permute-start.4 = (bf16[384,1024]{1,0:T(8,128)(2,1)S(1)}, bf16[384,1024]{1,0:T(8,128)(2,1)S(1)}, u32[]{:S(2)}, u32[]{:S(2)}) collective-permute-start(bf16[384,1024]{1,0:T(8,128)(2,1)S(1)} %get-tuple-element.43), channel_id=1, source_target_pairs={{0,1},{1,0},{2,3},{3,2},{4,5},{5,4},{6,7},{7,6},{8,9},{9,8},{10,11... | collective-permute-start | bytes 2359304 | tf_op jit(solution)/shard_map/ppermute | solution.py:168
  59.4 3.3 %collective-permute-start.5 = (bf16[1024,256]{1,0:T(8,128)(2,1)S(1)}, bf16[1024,256]{1,0:T(8,128)(2,1)S(1)}, u32[]{:S(2)}, u32[]{:S(2)}) collective-permute-start(bf16[1024,256]{1,0:T(8,128)(2,1)S(1)} %get-tuple-element.42.own_ref), channel_id=1, source_target_pairs={{0,2},{2,0},{1,3},{3,1},{4,6},{6,4},{5,7},{7,5},{8,10},{10,8},{9,1... | collective-permute-start | bytes 1572872 | tf_op jit(solution)/shard_map/ppermute | solution.py:167
  62.7 14.4 %collective-permute-done.5.far_ref = bf16[1024,256]{1,0:T(8,128)(2,1)S(1)} collective-permute-done((bf16[1024,256]{1,0:T(8,128)(2,1)S(1)}, bf16[1024,256]{1,0:T(8,128)(2,1)S(1)}, u32[]{:S(2)}, u32[]{:S(2)}) %collective-permute-start.5) | collective-permute-done | bytes 524320 | tf_op jit(solution)/shard_map/ppermute | solution.py:167
  77.1 0.0 collective-permute-done.4.refs_3_
  77.1 1.9 %shard_map.71 = bf16[8,128,256]{2,1,0:T(8,128)(2,1)} custom-call(bf16[256,1280]{1,0:T(8,128)(2,1)S(1)} %copy-done, bf16[128,1536]{1,0:T(8,128)(2,1)S(1)} %collective-permute-done.refs_0_, bf16[128,1536]{1,0:T(8,128)(2,1)S(1)} %collective-permute-done.1.refs_1_, bf16[128,1536]{1,0:T(8,128)(2,1)S(1)} %collective-permute-done.2.refs_2_, ...), custom_call_target="tpu_custom_call" | custom-call | tf_op jit(solution)/shard_map/pallas_call | solution.py:123
  79.1 0.0 all-to-all-done.1
  79.1 7.2 %all-to-all-start.2 = ((bf16[8,128,256]{2,1,0:T(8,128)(2,1)}), bf16[8,128,256]{2,1,0:T(8,128)(2,1)S(1)}, u32[]{:S(2)}, u32[]{:S(2)}) async-start(bf16[8,128,256]{2,1,0:T(8,128)(2,1)} %shard_map.71), calls=%async_computation.2 | async-start | bytes 1048576 | tf_op jit(solution)/shard_map/all_to_all | solution.py:173
  86.3 1.9 %collective-permute-start.3 = (bf16[1024,256]{1,0:T(8,128)(2,1)S(1)}, bf16[1024,256]{1,0:T(8,128)(2,1)S(1)}, u32[]{:S(2)}, u32[]{:S(2)}) collective-permute-start(bf16[1024,256]{1,0:T(8,128)(2,1)S(1)} %get-tuple-element.42.own_ref), channel_id=1, source_target_pairs={{0,1},{1,0},{2,3},{3,2},{4,5},{5,4},{6,7},{7,6},{8,9},{9,8},{10,11... | collective-permute-start | bytes 1572872 | tf_op jit(solution)/shard_map/ppermute | solution.py:170
  88.2 2.4 %collective-permute-start.6 = (bf16[1024,256]{1,0:T(8,128)(2,1)S(1)}, bf16[1024,256]{1,0:T(8,128)(2,1)S(1)}, u32[]{:S(2)}, u32[]{:S(2)}) collective-permute-start(bf16[1024,256]{1,0:T(8,128)(2,1)S(1)} %collective-permute-done.5.far_ref), channel_id=1, source_target_pairs={{0,1},{1,0},{2,3},{3,2},{4,5},{5,4},{6,7},{7,6},{8,9},{9,8},{10,11... | collective-permute-start | bytes 1572872 | tf_op jit(solution)/shard_map/ppermute | solution.py:174
  90.6 0.0 collective-permute-done.3.core_ref
  90.6 1.5 %collective-permute-done.6.both_ref = bf16[1024,256]{1,0:T(8,128)(2,1)S(1)} collective-permute-done((bf16[1024,256]{1,0:T(8,128)(2,1)S(1)}, bf16[1024,256]{1,0:T(8,128)(2,1)S(1)}, u32[]{:S(2)}, u32[]{:S(2)}) %collective-permute-start.6) | collective-permute-done | bytes 524320 | tf_op jit(solution)/shard_map/ppermute | solution.py:174
  92.1 2.9 %shard_map.70.scaled_ref = bf16[1024,1024]{1,0:T(8,128)(2,1)S(1)} custom-call(s32[3]{0:T(128)S(1)} %copy-done.1, bf16[1024,256]{1,0:T(8,128)(2,1)S(1)} %get-tuple-element.42.own_ref, bf16[1024,256]{1,0:T(8,128)(2,1)S(1)} %collective-permute-done.3.core_ref, bf16[1024,256]{1,0:T(8,128)(2,1)S(1)} %collective-permute-done.5.far_ref, ...), custom_call_target="tpu_custom_call" | custom-call | tf_op jit(solution)/shard_map/pallas_call | solution.py:123
  95.0 0.7 shard_map.72
  95.7 2.8 %collective-permute-start.7 = (bf16[256,256]{1,0:T(8,128)(2,1)S(1)}, bf16[256,256]{1,0:T(8,128)(2,1)S(1)}, u32[]{:S(2)}, u32[]{:S(2)}) collective-permute-start(bf16[256,256]{1,0:T(8,128)(2,1)S(1)} %get-tuple-element.50), channel_id=1, source_target_pairs={{0,32},{32,0},{1,33},{33,1},{2,34},{34,2},{3,35},{35,3},{4,36},{36... | collective-permute-start | bytes 393224 | tf_op jit(solution)/shard_map/ppermute | solution.py:135
  98.5 3.0 %collective-permute-start.8 = (bf16[256,256]{1,0:T(8,128)(2,1)S(1)}, bf16[256,256]{1,0:T(8,128)(2,1)S(1)}, u32[]{:S(2)}, u32[]{:S(2)}) collective-permute-start(bf16[256,256]{1,0:T(8,128)(2,1)S(1)} %get-tuple-element.51), channel_id=1, source_target_pairs={{0,64},{64,0},{1,65},{65,1},{2,66},{66,2},{3,67},{67,3},{4,68},{68... | collective-permute-start | bytes 393224 | tf_op jit(solution)/shard_map/ppermute | solution.py:136
  101.5 1.9 %collective-permute-done.7.refs_1_ = bf16[256,256]{1,0:T(8,128)(2,1)S(1)} collective-permute-done((bf16[256,256]{1,0:T(8,128)(2,1)S(1)}, bf16[256,256]{1,0:T(8,128)(2,1)S(1)}, u32[]{:S(2)}, u32[]{:S(2)}) %collective-permute-start.7) | collective-permute-done | bytes 131104 | tf_op jit(solution)/shard_map/ppermute | solution.py:135
  103.4 2.5 %collective-permute-done.8.refs_2_ = bf16[256,256]{1,0:T(8,128)(2,1)S(1)} collective-permute-done((bf16[256,256]{1,0:T(8,128)(2,1)S(1)}, bf16[256,256]{1,0:T(8,128)(2,1)S(1)}, u32[]{:S(2)}, u32[]{:S(2)}) %collective-permute-start.8) | collective-permute-done | bytes 131104 | tf_op jit(solution)/shard_map/ppermute | solution.py:136
  105.9 0.0 all-to-all-done.2
  105.9 0.7 convert_reduce_fusion
  106.6 7.1 %all-to-all-start.3 = ((f32[8,16,256]{2,1,0:T(8,128)}), f32[8,16,256]{2,1,0:T(8,128)S(1)}, u32[]{:S(2)}, u32[]{:S(2)}) async-start(f32[8,16,256]{2,1,0:T(8,128)} %bitcast.7), calls=%async_computation.3 | async-start | bytes 262144 | tf_op jit(solution)/shard_map/all_to_all | solution.py:184
  113.7 3.3 %collective-permute-start.9 = (bf16[256,256]{1,0:T(8,128)(2,1)S(1)}, bf16[256,256]{1,0:T(8,128)(2,1)S(1)}, u32[]{:S(2)}, u32[]{:S(2)}) collective-permute-start(bf16[256,256]{1,0:T(8,128)(2,1)S(1)} %get-tuple-element.54), channel_id=1, source_target_pairs={{0,96},{32,64},{64,32},{96,0},{1,97},{33,65},{65,33},{97,1},{2,98}... | collective-permute-start | bytes 393224 | tf_op jit(solution)/shard_map/ppermute | solution.py:137
  117.0 7.1 %collective-permute-done.9.refs_3_ = bf16[256,256]{1,0:T(8,128)(2,1)S(1)} collective-permute-done((bf16[256,256]{1,0:T(8,128)(2,1)S(1)}, bf16[256,256]{1,0:T(8,128)(2,1)S(1)}, u32[]{:S(2)}, u32[]{:S(2)}) %collective-permute-start.9) | collective-permute-done | bytes 131104 | tf_op jit(solution)/shard_map/ppermute | solution.py:137
  124.1 1.4 %shard_map.73 = bf16[256,1024]{1,0:T(8,128)(2,1)} custom-call(s32[3]{0:T(128)S(1)} %copy-done.1, bf16[256,256]{1,0:T(8,128)(2,1)S(1)} %get-tuple-element.48.refs_0_, bf16[256,256]{1,0:T(8,128)(2,1)S(1)} %collective-permute-done.7.refs_1_, bf16[256,256]{1,0:T(8,128)(2,1)S(1)} %collective-permute-done.8.refs_2_, ...), custom_call_target="tpu_custom_call" | custom-call | tf_op jit(solution)/shard_map/pallas_call | solution.py:123
  125.5 3.9 %all-to-all-done.3 = f32[8,16,256]{2,1,0:T(8,128)S(1)} async-done(((f32[8,16,256]{2,1,0:T(8,128)}), f32[8,16,256]{2,1,0:T(8,128)S(1)}, u32[]{:S(2)}, u32[]{:S(2)}) %all-to-all-start.3) | async-done | bytes 131104 | tf_op jit(solution)/shard_map/all_to_all | solution.py:184
  129.4 0.6 broadcast_multiply_fusion
  (5 shorter events, 0.1 us)
Async XLA Ops:
  0.6 13.7 %copy-start.2 = (bf16[1024,4]{0,1:T(4,128)(2,1)S(1)}, bf16[1024,4]{0,1:T(4,128)(2,1)}, u32[]{:S(2)}) copy-start(bf16[1024,4]{0,1:T(4,128)(2,1)} %param.7) | copy-start | bytes 24580
  1.3 55.5 %copy-start.1 = (s32[3]{0:T(128)S(1)}, s32[3]{0:T(128)}, u32[]{:S(2)}) copy-start(s32[3]{0:T(128)} %pad_add_fusion.place_ref) | copy-start | bytes 40
  4.6 52.3 %copy-start = (bf16[256,1280]{1,0:T(8,128)(2,1)S(1)}, bf16[256,1280]{1,0:T(8,128)(2,1)}, u32[]{:S(2)}) copy-start(bf16[256,1280]{1,0:T(8,128)(2,1)} %get-tuple-element.38.own_ref) | copy-start | bytes 1966084
  4.6 44.3 %collective-permute-start = (bf16[128,1536]{1,0:T(8,128)(2,1)}, bf16[128,1536]{1,0:T(8,128)(2,1)S(1)}, u32[]{:S(2)}, u32[]{:S(2)}) collective-permute-start(bf16[128,1536]{1,0:T(8,128)(2,1)} %get-tuple-element.34), channel_id=1, source_target_pairs={{0,32},{32,0},{1,33},{33,1},{2,34},{34,2},{3,35},{35,3},{4,36},{36... | collective-permute-start | bytes 1179656 | tf_op jit(solution)/shard_map/ppermute | solution.py:135
  7.4 41.4 %collective-permute-start.1 = (bf16[128,1536]{1,0:T(8,128)(2,1)}, bf16[128,1536]{1,0:T(8,128)(2,1)S(1)}, u32[]{:S(2)}, u32[]{:S(2)}) collective-permute-start(bf16[128,1536]{1,0:T(8,128)(2,1)} %get-tuple-element.35), channel_id=1, source_target_pairs={{0,64},{64,0},{1,65},{65,1},{2,66},{66,2},{3,67},{67,3},{4,68},{68... | collective-permute-start | bytes 1179656 | tf_op jit(solution)/shard_map/ppermute | solution.py:136
  11.7 37.1 %collective-permute-start.2 = (bf16[128,1536]{1,0:T(8,128)(2,1)}, bf16[128,1536]{1,0:T(8,128)(2,1)S(1)}, u32[]{:S(2)}, u32[]{:S(2)}) collective-permute-start(bf16[128,1536]{1,0:T(8,128)(2,1)} %get-tuple-element.36), channel_id=1, source_target_pairs={{0,96},{32,64},{64,32},{96,0},{1,97},{33,65},{65,33},{97,1},{2,98}... | collective-permute-start | bytes 1179656 | tf_op jit(solution)/shard_map/ppermute | solution.py:137
  49.7 29.4 %all-to-all-start.1 = ((bf16[8,128,256]{2,1,0:T(8,128)(2,1)}), bf16[8,128,256]{2,1,0:T(8,128)(2,1)S(1)}, u32[]{:S(2)}, u32[]{:S(2)}) async-start(bf16[8,128,256]{2,1,0:T(8,128)(2,1)} %broadcast_in_dim.10), calls=%async_computation.1 | async-start | bytes 1048576 | tf_op jit(solution)/shard_map/all_to_all | solution.py:163
  57.5 19.7 %collective-permute-start.4 = (bf16[384,1024]{1,0:T(8,128)(2,1)S(1)}, bf16[384,1024]{1,0:T(8,128)(2,1)S(1)}, u32[]{:S(2)}, u32[]{:S(2)}) collective-permute-start(bf16[384,1024]{1,0:T(8,128)(2,1)S(1)} %get-tuple-element.43), channel_id=1, source_target_pairs={{0,1},{1,0},{2,3},{3,2},{4,5},{5,4},{6,7},{7,6},{8,9},{9,8},{10,11... | collective-permute-start | bytes 2359304 | tf_op jit(solution)/shard_map/ppermute | solution.py:168
  59.4 17.7 %collective-permute-start.5 = (bf16[1024,256]{1,0:T(8,128)(2,1)S(1)}, bf16[1024,256]{1,0:T(8,128)(2,1)S(1)}, u32[]{:S(2)}, u32[]{:S(2)}) collective-permute-start(bf16[1024,256]{1,0:T(8,128)(2,1)S(1)} %get-tuple-element.42.own_ref), channel_id=1, source_target_pairs={{0,2},{2,0},{1,3},{3,1},{4,6},{6,4},{5,7},{7,5},{8,10},{10,8},{9,1... | collective-permute-start | bytes 1572872 | tf_op jit(solution)/shard_map/ppermute | solution.py:167
  79.1 26.8 %all-to-all-start.2 = ((bf16[8,128,256]{2,1,0:T(8,128)(2,1)}), bf16[8,128,256]{2,1,0:T(8,128)(2,1)S(1)}, u32[]{:S(2)}, u32[]{:S(2)}) async-start(bf16[8,128,256]{2,1,0:T(8,128)(2,1)} %shard_map.71), calls=%async_computation.2 | async-start | bytes 1048576 | tf_op jit(solution)/shard_map/all_to_all | solution.py:173
  86.3 4.3 %collective-permute-start.3 = (bf16[1024,256]{1,0:T(8,128)(2,1)S(1)}, bf16[1024,256]{1,0:T(8,128)(2,1)S(1)}, u32[]{:S(2)}, u32[]{:S(2)}) collective-permute-start(bf16[1024,256]{1,0:T(8,128)(2,1)S(1)} %get-tuple-element.42.own_ref), channel_id=1, source_target_pairs={{0,1},{1,0},{2,3},{3,2},{4,5},{5,4},{6,7},{7,6},{8,9},{9,8},{10,11... | collective-permute-start | bytes 1572872 | tf_op jit(solution)/shard_map/ppermute | solution.py:170
  88.2 3.9 %collective-permute-start.6 = (bf16[1024,256]{1,0:T(8,128)(2,1)S(1)}, bf16[1024,256]{1,0:T(8,128)(2,1)S(1)}, u32[]{:S(2)}, u32[]{:S(2)}) collective-permute-start(bf16[1024,256]{1,0:T(8,128)(2,1)S(1)} %collective-permute-done.5.far_ref), channel_id=1, source_target_pairs={{0,1},{1,0},{2,3},{3,2},{4,5},{5,4},{6,7},{7,6},{8,9},{9,8},{10,11... | collective-permute-start | bytes 1572872 | tf_op jit(solution)/shard_map/ppermute | solution.py:174
  95.7 7.7 %collective-permute-start.7 = (bf16[256,256]{1,0:T(8,128)(2,1)S(1)}, bf16[256,256]{1,0:T(8,128)(2,1)S(1)}, u32[]{:S(2)}, u32[]{:S(2)}) collective-permute-start(bf16[256,256]{1,0:T(8,128)(2,1)S(1)} %get-tuple-element.50), channel_id=1, source_target_pairs={{0,32},{32,0},{1,33},{33,1},{2,34},{34,2},{3,35},{35,3},{4,36},{36... | collective-permute-start | bytes 393224 | tf_op jit(solution)/shard_map/ppermute | solution.py:135
  98.5 7.4 %collective-permute-start.8 = (bf16[256,256]{1,0:T(8,128)(2,1)S(1)}, bf16[256,256]{1,0:T(8,128)(2,1)S(1)}, u32[]{:S(2)}, u32[]{:S(2)}) collective-permute-start(bf16[256,256]{1,0:T(8,128)(2,1)S(1)} %get-tuple-element.51), channel_id=1, source_target_pairs={{0,64},{64,0},{1,65},{65,1},{2,66},{66,2},{3,67},{67,3},{4,68},{68... | collective-permute-start | bytes 393224 | tf_op jit(solution)/shard_map/ppermute | solution.py:136
  106.6 22.8 %all-to-all-start.3 = ((f32[8,16,256]{2,1,0:T(8,128)}), f32[8,16,256]{2,1,0:T(8,128)S(1)}, u32[]{:S(2)}, u32[]{:S(2)}) async-start(f32[8,16,256]{2,1,0:T(8,128)} %bitcast.7), calls=%async_computation.3 | async-start | bytes 262144 | tf_op jit(solution)/shard_map/all_to_all | solution.py:184
  113.7 10.4 %collective-permute-start.9 = (bf16[256,256]{1,0:T(8,128)(2,1)S(1)}, bf16[256,256]{1,0:T(8,128)(2,1)S(1)}, u32[]{:S(2)}, u32[]{:S(2)}) collective-permute-start(bf16[256,256]{1,0:T(8,128)(2,1)S(1)} %get-tuple-element.54), channel_id=1, source_target_pairs={{0,96},{32,64},{64,32},{96,0},{1,97},{33,65},{65,33},{97,1},{2,98}... | collective-permute-start | bytes 393224 | tf_op jit(solution)/shard_map/ppermute | solution.py:137

commit v8 on v6

--- a/solution.py
+++ b/solution.py
@@ -87,7 +87,8 @@
     j = spot % n_j
     z = (spot // n_j) % n_z
     xl = (spot // (n_j * n_z)) % 2
-    y = spot // (n_j * n_z * 2)
+    flip = spot // (n_j * n_z * 2)
+    y = place_ref[3] ^ ((flip % 2) * 4 + (flip // 2 % 2) * 2 + flip // 4)
     source = ((z * 2 + xl) * n_y + y) * n_j + j
     for c in range(0, total, 256):
         moved = None
@@ -99,14 +100,17 @@
         out_ref[:, c : c + 256] = moved.astype(jnp.bfloat16)
 
 
-def input_kernel(scaled_ref, weight_ref, *outs):
-    rows = outs[0].shape[0]
+def input_kernel(scaled_ref, near_ref, next_ref, *outs):
+    rows, deep = outs[0].shape[0], near_ref.shape[0]
     for m, out_ref in enumerate(outs):
-        out_ref[...] = jnp.dot(
-            scaled_ref[m * rows : (m + 1) * rows, :],
-            weight_ref[...],
-            preferred_element_type=jnp.float32,
-        ).astype(jnp.bfloat16)
+        block = slice(m * rows, (m + 1) * rows)
+        total = jnp.dot(
+            scaled_ref[block, :deep], near_ref[...], preferred_element_type=jnp.float32
+        )
+        total += jnp.dot(
+            scaled_ref[block, deep:], next_ref[...], preferred_element_type=jnp.float32
+        )
+        out_ref[...] = total.astype(jnp.bfloat16)
 
 
 def join_kernel(place_ref, *refs):
@@ -138,6 +142,10 @@
     ]
 
 
+def flipped(x, bits, n):
+    return lax.ppermute(x, "y", [(i, i ^ bits) for i in range(n)])
+
+
 def local(inputs, value_grad, value_weight, counts, offsets):
     rows, features = inputs.shape
     columns = value_grad.shape[1]
@@ -146,7 +154,7 @@
     wide = features // 4
     narrow = quarter // 4
 
-    place = jnp.stack([lax.axis_index(a) for a in (("zl", "xl"), TP, "c")]).astype(jnp.int32)
+    place = jnp.stack([lax.axis_index(a) for a in (("zl", "xl"), TP, "c", "y")]).astype(jnp.int32)
     args = (place, counts, offsets, value_grad, inputs)
     sizes = [(rows, wide + columns)] + [(rows // 2, wide + 2 * columns)] * 3
     blocks = call(prep_kernel, sizes, 3, *args, vmem=60 * MIB)
@@ -158,27 +166,28 @@
     mine = mine.reshape(-1, own_columns, narrow)
     block = lax.all_to_all(mine, ("xl", "zh", "zl"), 0, 0, tiled=True)
     received, block = lax.optimization_barrier((received, block))
-    block = block.reshape(-1, narrow)
-    block = jnp.broadcast_to(block, (n_y, *block.shape))
-    weight = lax.all_to_all(block, "y", 0, 0, tiled=True).reshape(-1, narrow)
+    near = block.reshape(-1, narrow)
+    first = flipped(near, 4, n_y)
 
     sizes = [(3 * rows // 2, wide), (4 * rows, columns)]
     half, own = call(split_kernel, sizes, 1, place, *received)
     half = lax.ppermute(half, "c", SWAP)
     from_far = lax.ppermute(own, "xh", SWAP)
     from_core = lax.ppermute(own, "c", SWAP)
+    half, first = lax.optimization_barrier((half, first))
     (term,) = call(weight_kernel, [(n_y, wide // n_y, columns)], 0, *received, half)
-    early = (term, weight, from_far, from_core)
-    term, weight, from_far, from_core = lax.optimization_barrier(early)
     terms = lax.all_to_all(term, "y", 0, 0, tiled=True)
+    near = jnp.concatenate([near, first])
+    near = jnp.concatenate([near, flipped(near, 2, n_y)])
+    last = flipped(near, 1, n_y)
+    terms, last = lax.optimization_barrier((terms, last))
     gathered = [own, from_core, from_far, lax.ppermute(from_far, "c", SWAP)]
 
     sizes = (2 * n_zh, n_y, own_columns)
     kernel = functools.partial(order_kernel, sizes)
     (ordered,) = call(kernel, [(4 * rows, n_tp * columns)], 1, place, *gathered)
-    outs = call(input_kernel, [(rows, narrow)] * 4, 0, ordered, weight)
-
-    terms, outs = lax.optimization_barrier((terms, outs))
+    outs = call(input_kernel, [(rows, narrow)] * 4, 0, ordered, near, last)
+
     summed = jnp.sum(terms.astype(jnp.float32), axis=0).reshape(n_zh, -1, columns)
     summed = lax.all_to_all(summed, "zh", 0, 0, tiled=True)
     normalizer = 1.0 / math.sqrt(counts.shape[1] * lax.axis_size(FSDP))

time: 128 us -> 130 us (1.016)
  starting transfers between devices: 49.6 us -> 58.1 us
  waiting for transfers between devices: 26.7 us -> 19.6 us
  local copies, waits for them, and re-layouts: 2.75 us -> 1.18 us
    ppermute x0 -> x3, waiting for transfers between devices: none -> 15.8 us  [flipped(): return lax.ppermute(x, 'y', [(i, i ^ bits) for i in range(n)])]
    ppermute x0 -> x3, starting transfers between devices: none -> 14.5 us  [flipped(): return lax.ppermute(x, 'y', [(i, i ^ bits) for i in range(n)])]
    ppermute x1, waiting for transfers between devices: 10.3 us -> 0.01 us  [local(): from_far = lax.ppermute(own, 'xh', SWAP)]
    all_to_all x1, waiting for transfers between devices: 8.94 us -> 0.01 us  [local(): terms = lax.all_to_all(term, 'y', 0, 0, tiled=True)]
    all_to_all x1 -> x0, starting transfers between devices: 7.1 us -> none  [local(): weight = lax.all_to_all(block, 'y', 0, 0, tiled=True).reshape(-1, narrow)]
    ppermute x2, waiting for transfers between devices: 3.19 us -> 1.28 us  [from_group(): lax.ppermute(blocks[2], 'zl', SWAP)]
    ppermute x1, waiting for transfers between devices: 1.88 us -> 0.01 us  [local(): gathered = [own, from_core, from_far, lax.ppermute(from_far, 'c', SWAP)]]
  transfers between devices with their start and end apart: 13 -> 15, of which waited for: 5 -> 5; matrix products, arithmetic and copies ran while one was open for 0% -> 1% of each run, Pallas kernels for 6% -> 4%
where the time goes in v8:
time: 130 us; the launch traced here: 128 us
  starting transfers between devices  58.1 us (45%)
  blocking collectives  34.5 us (27%)
  waiting for transfers between devices  19.6 us (15%)
  Pallas kernels  11.7 us (9%)
  other arithmetic  1.93 us (1%)
    all_to_all x1, blocking collectives, local(): block = lax.all_to_all(mine, ('xl', 'zh', 'zl'), 0, 0, tiled=True)  34.5 us
    ppermute x3, waiting for transfers between devices, flipped(): return lax.ppermute(x, 'y', [(i, i ^ bits) for i in range(n)])  15.8 us
    ppermute x3, starting transfers between devices, flipped(): return lax.ppermute(x, 'y', [(i, i ^ bits) for i in range(n)])  14.5 us
    pallas_call x6, Pallas kernels, call(): pl.pallas_call(kernel, out_shape=shapes, in_specs=[pl.BlockSpec(memory_sp...  11.7 us
    all_to_all x1, starting transfers between devices, local(): terms = lax.all_to_all(term, 'y', 0, 0, tiled=True)  8.2 us
    all_to_all x1, starting transfers between devices, local(): summed = lax.all_to_all(summed, 'zh', 0, 0, tiled=True)  7.09 us
    ppermute x2, starting transfers between devices, from_group(): lax.ppermute(blocks[2], 'zl', SWAP)  6.98 us
    ppermute x2, starting transfers between devices, from_group(): lax.ppermute(blocks[3], ('zl', 'xl'), BOTH)  6.55 us
  transfers between devices with their start and end apart: 15, of which 5 were waited for; matrix products, arithmetic and copies ran while one was open for 1% of the time, Pallas kernels for 4%

profile of v8, /device:TPU:6, one launch (start us, length us, event | category | flops | bytes accessed | tf_op | source)
XLA Modules:
  0.0 127.9 jit_solution(11654959973256024248)
XLA Ops:
  0.6 0.0 copy-start.3
  0.6 0.6 pad_add_fusion.place_ref
  1.2 0.0 copy-start.2
  1.2 3.3 %shard_map.68 = (bf16[256,1280]{1,0:T(8,128)(2,1)}, bf16[128,1536]{1,0:T(8,128)(2,1)}, bf16[128,1536]{1,0:T(8,128)(2,1)}, bf16[128,1536]{1,0:T(8,128)(2,1)}) custom-call(s32[4]{0:T(128)} %pad_add_fusion.place_ref, s32[1,4]{1,0:T(1,128)} %counts_ref.1, s32[1,4]{1,0:T(1,128)} %offsets_ref.1, bf16[256,256]{1,0:T(8,128)(2,1)} %grad_ref.1, ...), custom_call_target="tpu_custom_call" | custom-call | tf_op jit(solution)/shard_map/pallas_call | solution.py:127
  4.5 2.7 %collective-permute-start = (bf16[128,1536]{1,0:T(8,128)(2,1)}, bf16[128,1536]{1,0:T(8,128)(2,1)S(1)}, u32[]{:S(2)}, u32[]{:S(2)}) collective-permute-start(bf16[128,1536]{1,0:T(8,128)(2,1)} %get-tuple-element.31), channel_id=1, source_target_pairs={{0,32},{32,0},{1,33},{33,1},{2,34},{34,2},{3,35},{35,3},{4,36},{36... | collective-permute-start | bytes 1179656 | tf_op jit(solution)/shard_map/ppermute | solution.py:139
  7.2 4.3 %collective-permute-start.1 = (bf16[128,1536]{1,0:T(8,128)(2,1)}, bf16[128,1536]{1,0:T(8,128)(2,1)S(1)}, u32[]{:S(2)}, u32[]{:S(2)}) collective-permute-start(bf16[128,1536]{1,0:T(8,128)(2,1)} %get-tuple-element.32), channel_id=1, source_target_pairs={{0,64},{64,0},{1,65},{65,1},{2,66},{66,2},{3,67},{67,3},{4,68},{68... | collective-permute-start | bytes 1179656 | tf_op jit(solution)/shard_map/ppermute | solution.py:140
  11.5 2.6 %collective-permute-start.2 = (bf16[128,1536]{1,0:T(8,128)(2,1)}, bf16[128,1536]{1,0:T(8,128)(2,1)S(1)}, u32[]{:S(2)}, u32[]{:S(2)}) collective-permute-start(bf16[128,1536]{1,0:T(8,128)(2,1)} %get-tuple-element.33), channel_id=1, source_target_pairs={{0,96},{32,64},{64,32},{96,0},{1,97},{33,65},{65,33},{97,1},{2,98}... | collective-permute-start | bytes 1179656 | tf_op jit(solution)/shard_map/ppermute | solution.py:141
  14.1 0.0 copy-done.3
  14.1 34.5 %all_to_all.15 = bf16[32,4,256]{2,1,0:T(4,128)(2,1)S(1)} all-to-all(bf16[32,4,256]{2,1,0:T(4,128)(2,1)S(1)} %bitcast.8), channel_id=1, replica_groups=mesh['zh'=8,'zl'=2,'xl'=2,'y'=8,'xh'=2,'c'=2] {'xl','zh','zl'}, dimensions={0} | all-to-all | bytes 131072 | tf_op jit(solution)/shard_map/all_to_all | solution.py:167
  48.6 0.0 collective-permute-done.refs_0_
  48.6 0.0 collective-permute-done.1.refs_1_
  48.6 0.0 collective-permute-done.2.refs_2_
  48.6 0.0 copy-done.2
  48.6 0.0 copy-start
  48.7 1.1 copy-done
  49.7 0.0 copy-start.1
  49.7 1.5 %shard_map.69 = (bf16[384,1024]{1,0:T(8,128)(2,1)}, bf16[1024,256]{1,0:T(8,128)(2,1)S(1)}) custom-call(s32[4]{0:T(128)S(1)} %copy-done.2, bf16[256,1280]{1,0:T(8,128)(2,1)S(1)} %copy-done, bf16[128,1536]{1,0:T(8,128)(2,1)S(1)} %collective-permute-done.refs_0_, bf16[128,1536]{1,0:T(8,128)(2,1)S(1)} %collective-permute-done.1.refs_1_, ...), custom_call_target="tpu_custom_call" | custom-call | tf_op jit(solution)/shard_map/pallas_call | solution.py:127
  51.3 1.9 %collective-permute-start.6 = (bf16[384,1024]{1,0:T(8,128)(2,1)}, bf16[384,1024]{1,0:T(8,128)(2,1)S(1)}, u32[]{:S(2)}, u32[]{:S(2)}) collective-permute-start(bf16[384,1024]{1,0:T(8,128)(2,1)} %get-tuple-element.41), channel_id=1, source_target_pairs={{0,1},{1,0},{2,3},{3,2},{4,5},{5,4},{6,7},{7,6},{8,9},{9,8},{10,11... | collective-permute-start | bytes 2359304 | tf_op jit(solution)/shard_map/ppermute | solution.py:174
  53.2 7.7 %collective-permute-start.7 = (bf16[128,256]{1,0:T(8,128)(2,1)S(1)}, bf16[128,256]{1,0:T(8,128)(2,1)S(1)}, u32[]{:S(2)}, u32[]{:S(2)}) collective-permute-start(bf16[128,256]{1,0:T(8,128)(2,1)S(1)} %reshape.19), channel_id=1, source_target_pairs={{0,16},{4,20},{8,24},{12,28},{16,0},{20,4},{24,8},{28,12},{1,17},{... | collective-permute-start | bytes 196616 | tf_op jit(solution)/shard_map/ppermute | solution.py:146
  60.9 2.8 %collective-permute-done.7 = bf16[128,256]{1,0:T(8,128)(2,1)S(1)} collective-permute-done((bf16[128,256]{1,0:T(8,128)(2,1)S(1)}, bf16[128,256]{1,0:T(8,128)(2,1)S(1)}, u32[]{:S(2)}, u32[]{:S(2)}) %collective-permute-start.7) | collective-permute-done | bytes 65568 | tf_op jit(solution)/shard_map/ppermute | solution.py:146
  63.8 0.0 collective-permute-done.6.refs_3_
  63.8 0.0 copy-done.1
  63.8 1.9 %shard_map.71 = bf16[8,128,256]{2,1,0:T(8,128)(2,1)} custom-call(bf16[256,1280]{1,0:T(8,128)(2,1)S(1)} %copy-done.1, bf16[128,1536]{1,0:T(8,128)(2,1)S(1)} %collective-permute-done.refs_0_, bf16[128,1536]{1,0:T(8,128)(2,1)S(1)} %collective-permute-done.1.refs_1_, bf16[128,1536]{1,0:T(8,128)(2,1)S(1)} %collective-permute-done.2.refs_2_, ...), custom_call_target="tpu_custom_call" | custom-call | tf_op jit(solution)/shard_map/pallas_call | solution.py:127
  65.7 8.2 %all-to-all-start.1 = ((bf16[8,128,256]{2,1,0:T(8,128)(2,1)}), bf16[8,128,256]{2,1,0:T(8,128)(2,1)S(1)}, u32[]{:S(2)}, u32[]{:S(2)}) async-start(bf16[8,128,256]{2,1,0:T(8,128)(2,1)} %shard_map.71), calls=%async_computation.1 | async-start | bytes 1048576 | tf_op jit(solution)/shard_map/all_to_all | solution.py:179
  73.9 3.3 %collective-permute-start.4 = (bf16[1024,256]{1,0:T(8,128)(2,1)S(1)}, bf16[1024,256]{1,0:T(8,128)(2,1)S(1)}, u32[]{:S(2)}, u32[]{:S(2)}) collective-permute-start(bf16[1024,256]{1,0:T(8,128)(2,1)S(1)} %get-tuple-element.39.own_ref), channel_id=1, source_target_pairs={{0,2},{2,0},{1,3},{3,1},{4,6},{6,4},{5,7},{7,5},{8,10},{10,8},{9,1... | collective-permute-start | bytes 1572872 | tf_op jit(solution)/shard_map/ppermute | solution.py:175
  77.3 4.8 %collective-permute-start.8 = (bf16[256,256]{1,0:T(8,128)(2,1)S(1)}, bf16[256,256]{1,0:T(8,128)(2,1)S(1)}, u32[]{:S(2)}, u32[]{:S(2)}) collective-permute-start(bf16[256,256]{1,0:T(8,128)(2,1)S(1)} %pad_maximum_fusion), channel_id=1, source_target_pairs={{0,8},{4,12},{8,0},{12,4},{16,24},{20,28},{24,16},{28,20},{1,9},{5... | collective-permute-start | bytes 393224 | tf_op jit(solution)/shard_map/ppermute | solution.py:146
  82.1 10.6 %collective-permute-done.8 = bf16[256,256]{1,0:T(8,128)(2,1)S(1)} collective-permute-done((bf16[256,256]{1,0:T(8,128)(2,1)S(1)}, bf16[256,256]{1,0:T(8,128)(2,1)S(1)}, u32[]{:S(2)}, u32[]{:S(2)}) %collective-permute-start.8) | collective-permute-done | bytes 131104 | tf_op jit(solution)/shard_map/ppermute | solution.py:146
  92.7 1.9 %collective-permute-start.9 = (bf16[512,256]{1,0:T(8,128)(2,1)S(1)}, bf16[512,256]{1,0:T(8,128)(2,1)S(1)}, u32[]{:S(2)}, u32[]{:S(2)}) collective-permute-start(bf16[512,256]{1,0:T(8,128)(2,1)S(1)} %constant_dynamic-update-slice_fusion.near_ref), channel_id=1, source_target_pairs={{0,4},{4,0},{8,12},{12,8},{16,20},{20,16},{24,28},{28,24},{1,5},{5... | collective-permute-start | bytes 786440 | tf_op jit(solution)/shard_map/ppermute | solution.py:146
  94.6 1.9 %collective-permute-start.3 = (bf16[1024,256]{1,0:T(8,128)(2,1)S(1)}, bf16[1024,256]{1,0:T(8,128)(2,1)S(1)}, u32[]{:S(2)}, u32[]{:S(2)}) collective-permute-start(bf16[1024,256]{1,0:T(8,128)(2,1)S(1)} %get-tuple-element.39.own_ref), channel_id=1, source_target_pairs={{0,1},{1,0},{2,3},{3,2},{4,5},{5,4},{6,7},{7,6},{8,9},{9,8},{10,11... | collective-permute-start | bytes 1572872 | tf_op jit(solution)/shard_map/ppermute | solution.py:176
  96.6 0.0 collective-permute-done.4.far_ref
  96.6 2.4 %collective-permute-start.5 = (bf16[1024,256]{1,0:T(8,128)(2,1)S(1)}, bf16[1024,256]{1,0:T(8,128)(2,1)S(1)}, u32[]{:S(2)}, u32[]{:S(2)}) collective-permute-start(bf16[1024,256]{1,0:T(8,128)(2,1)S(1)} %collective-permute-done.4.far_ref), channel_id=1, source_target_pairs={{0,1},{1,0},{2,3},{3,2},{4,5},{5,4},{6,7},{7,6},{8,9},{9,8},{10,11... | collective-permute-start | bytes 1572872 | tf_op jit(solution)/shard_map/ppermute | solution.py:184
  99.0 2.4 %collective-permute-done.9.next_ref = bf16[512,256]{1,0:T(8,128)(2,1)S(1)} collective-permute-done((bf16[512,256]{1,0:T(8,128)(2,1)S(1)}, bf16[512,256]{1,0:T(8,128)(2,1)S(1)}, u32[]{:S(2)}, u32[]{:S(2)}) %collective-permute-start.9) | collective-permute-done | bytes 262176 | tf_op jit(solution)/shard_map/ppermute | solution.py:146
  101.4 0.0 all-to-all-done.1
  101.4 0.7 convert_reduce_fusion
  102.1 7.1 %all-to-all-start.2 = ((f32[8,16,256]{2,1,0:T(8,128)}), f32[8,16,256]{2,1,0:T(8,128)S(1)}, u32[]{:S(2)}, u32[]{:S(2)}) async-start(f32[8,16,256]{2,1,0:T(8,128)} %bitcast.7), calls=%async_computation.2 | async-start | bytes 262144 | tf_op jit(solution)/shard_map/all_to_all | solution.py:192
  109.2 0.0 collective-permute-done.3.core_ref
  109.2 0.0 collective-permute-done.5.both_ref
  109.2 2.9 %shard_map.70.scaled_ref = bf16[1024,1024]{1,0:T(8,128)(2,1)S(1)} custom-call(s32[4]{0:T(128)S(1)} %copy-done.2, bf16[1024,256]{1,0:T(8,128)(2,1)S(1)} %get-tuple-element.39.own_ref, bf16[1024,256]{1,0:T(8,128)(2,1)S(1)} %collective-permute-done.3.core_ref, bf16[1024,256]{1,0:T(8,128)(2,1)S(1)} %collective-permute-done.4.far_ref, ...), custom_call_target="tpu_custom_call" | custom-call | tf_op jit(solution)/shard_map/pallas_call | solution.py:127
  112.1 0.7 shard_map.72
  112.8 2.5 %collective-permute-start.10 = (bf16[256,256]{1,0:T(8,128)(2,1)S(1)}, bf16[256,256]{1,0:T(8,128)(2,1)S(1)}, u32[]{:S(2)}, u32[]{:S(2)}) collective-permute-start(bf16[256,256]{1,0:T(8,128)(2,1)S(1)} %get-tuple-element.46), channel_id=1, source_target_pairs={{0,32},{32,0},{1,33},{33,1},{2,34},{34,2},{3,35},{35,3},{4,36},{36... | collective-permute-start | bytes 393224 | tf_op jit(solution)/shard_map/ppermute | solution.py:139
  115.4 2.7 %collective-permute-start.11 = (bf16[256,256]{1,0:T(8,128)(2,1)S(1)}, bf16[256,256]{1,0:T(8,128)(2,1)S(1)}, u32[]{:S(2)}, u32[]{:S(2)}) collective-permute-start(bf16[256,256]{1,0:T(8,128)(2,1)S(1)} %get-tuple-element.47), channel_id=1, source_target_pairs={{0,64},{64,0},{1,65},{65,1},{2,66},{66,2},{3,67},{67,3},{4,68},{68... | collective-permute-start | bytes 393224 | tf_op jit(solution)/shard_map/ppermute | solution.py:140
  118.1 4.0 %collective-permute-start.12 = (bf16[256,256]{1,0:T(8,128)(2,1)S(1)}, bf16[256,256]{1,0:T(8,128)(2,1)S(1)}, u32[]{:S(2)}, u32[]{:S(2)}) collective-permute-start(bf16[256,256]{1,0:T(8,128)(2,1)S(1)} %get-tuple-element.48), channel_id=1, source_target_pairs={{0,96},{32,64},{64,32},{96,0},{1,97},{33,65},{65,33},{97,1},{2,98}... | collective-permute-start | bytes 393224 | tf_op jit(solution)/shard_map/ppermute | solution.py:141
  122.1 0.0 collective-permute-done.10.refs_1_
  122.1 1.3 %collective-permute-done.11.refs_2_ = bf16[256,256]{1,0:T(8,128)(2,1)S(1)} collective-permute-done((bf16[256,256]{1,0:T(8,128)(2,1)S(1)}, bf16[256,256]{1,0:T(8,128)(2,1)S(1)}, u32[]{:S(2)}, u32[]{:S(2)}) %collective-permute-start.11) | collective-permute-done | bytes 131104 | tf_op jit(solution)/shard_map/ppermute | solution.py:140
  123.4 2.5 %collective-permute-done.12.refs_3_ = bf16[256,256]{1,0:T(8,128)(2,1)S(1)} collective-permute-done((bf16[256,256]{1,0:T(8,128)(2,1)S(1)}, bf16[256,256]{1,0:T(8,128)(2,1)S(1)}, u32[]{:S(2)}, u32[]{:S(2)}) %collective-permute-start.12) | collective-permute-done | bytes 131104 | tf_op jit(solution)/shard_map/ppermute | solution.py:141
  125.8 1.4 %shard_map.73 = bf16[256,1024]{1,0:T(8,128)(2,1)} custom-call(s32[4]{0:T(128)S(1)} %copy-done.2, bf16[256,256]{1,0:T(8,128)(2,1)S(1)} %get-tuple-element.45.refs_0_, bf16[256,256]{1,0:T(8,128)(2,1)S(1)} %collective-permute-done.10.refs_1_, bf16[256,256]{1,0:T(8,128)(2,1)S(1)} %collective-permute-done.11.refs_2_, ...), custom_call_target="tpu_custom_call" | custom-call | tf_op jit(solution)/shard_map/pallas_call | solution.py:127
  127.2 0.0 all-to-all-done.2
  127.3 0.6 broadcast_multiply_fusion
  (9 shorter events, 0.1 us)
Async XLA Ops:
  0.6 13.4 %copy-start.3 = (bf16[1024,4]{0,1:T(4,128)(2,1)S(1)}, bf16[1024,4]{0,1:T(4,128)(2,1)}, u32[]{:S(2)}) copy-start(bf16[1024,4]{0,1:T(4,128)(2,1)} %param.7) | copy-start | bytes 24580
  1.2 47.4 %copy-start.2 = (s32[4]{0:T(128)S(1)}, s32[4]{0:T(128)}, u32[]{:S(2)}) copy-start(s32[4]{0:T(128)} %pad_add_fusion.place_ref) | copy-start | bytes 52
  4.5 44.2 %collective-permute-start = (bf16[128,1536]{1,0:T(8,128)(2,1)}, bf16[128,1536]{1,0:T(8,128)(2,1)S(1)}, u32[]{:S(2)}, u32[]{:S(2)}) collective-permute-start(bf16[128,1536]{1,0:T(8,128)(2,1)} %get-tuple-element.31), channel_id=1, source_target_pairs={{0,32},{32,0},{1,33},{33,1},{2,34},{34,2},{3,35},{35,3},{4,36},{36... | collective-permute-start | bytes 1179656 | tf_op jit(solution)/shard_map/ppermute | solution.py:139
  7.2 41.4 %collective-permute-start.1 = (bf16[128,1536]{1,0:T(8,128)(2,1)}, bf16[128,1536]{1,0:T(8,128)(2,1)S(1)}, u32[]{:S(2)}, u32[]{:S(2)}) collective-permute-start(bf16[128,1536]{1,0:T(8,128)(2,1)} %get-tuple-element.32), channel_id=1, source_target_pairs={{0,64},{64,0},{1,65},{65,1},{2,66},{66,2},{3,67},{67,3},{4,68},{68... | collective-permute-start | bytes 1179656 | tf_op jit(solution)/shard_map/ppermute | solution.py:140
  11.5 37.1 %collective-permute-start.2 = (bf16[128,1536]{1,0:T(8,128)(2,1)}, bf16[128,1536]{1,0:T(8,128)(2,1)S(1)}, u32[]{:S(2)}, u32[]{:S(2)}) collective-permute-start(bf16[128,1536]{1,0:T(8,128)(2,1)} %get-tuple-element.33), channel_id=1, source_target_pairs={{0,96},{32,64},{64,32},{96,0},{1,97},{33,65},{65,33},{97,1},{2,98}... | collective-permute-start | bytes 1179656 | tf_op jit(solution)/shard_map/ppermute | solution.py:141
  48.6 1.1 copy-start
  49.7 14.0 %copy-start.1 = (bf16[256,1280]{1,0:T(8,128)(2,1)S(1)}, bf16[256,1280]{1,0:T(8,128)(2,1)}, u32[]{:S(2)}) copy-start(bf16[256,1280]{1,0:T(8,128)(2,1)} %get-tuple-element.35.own_ref) | copy-start | bytes 1966084
  51.3 12.5 %collective-permute-start.6 = (bf16[384,1024]{1,0:T(8,128)(2,1)}, bf16[384,1024]{1,0:T(8,128)(2,1)S(1)}, u32[]{:S(2)}, u32[]{:S(2)}) collective-permute-start(bf16[384,1024]{1,0:T(8,128)(2,1)} %get-tuple-element.41), channel_id=1, source_target_pairs={{0,1},{1,0},{2,3},{3,2},{4,5},{5,4},{6,7},{7,6},{8,9},{9,8},{10,11... | collective-permute-start | bytes 2359304 | tf_op jit(solution)/shard_map/ppermute | solution.py:174
  53.2 10.6 %collective-permute-start.7 = (bf16[128,256]{1,0:T(8,128)(2,1)S(1)}, bf16[128,256]{1,0:T(8,128)(2,1)S(1)}, u32[]{:S(2)}, u32[]{:S(2)}) collective-permute-start(bf16[128,256]{1,0:T(8,128)(2,1)S(1)} %reshape.19), channel_id=1, source_target_pairs={{0,16},{4,20},{8,24},{12,28},{16,0},{20,4},{24,8},{28,12},{1,17},{... | collective-permute-start | bytes 196616 | tf_op jit(solution)/shard_map/ppermute | solution.py:146
  65.7 35.6 %all-to-all-start.1 = ((bf16[8,128,256]{2,1,0:T(8,128)(2,1)}), bf16[8,128,256]{2,1,0:T(8,128)(2,1)S(1)}, u32[]{:S(2)}, u32[]{:S(2)}) async-start(bf16[8,128,256]{2,1,0:T(8,128)(2,1)} %shard_map.71), calls=%async_computation.1 | async-start | bytes 1048576 | tf_op jit(solution)/shard_map/all_to_all | solution.py:179
  73.9 22.6 %collective-permute-start.4 = (bf16[1024,256]{1,0:T(8,128)(2,1)S(1)}, bf16[1024,256]{1,0:T(8,128)(2,1)S(1)}, u32[]{:S(2)}, u32[]{:S(2)}) collective-permute-start(bf16[1024,256]{1,0:T(8,128)(2,1)S(1)} %get-tuple-element.39.own_ref), channel_id=1, source_target_pairs={{0,2},{2,0},{1,3},{3,1},{4,6},{6,4},{5,7},{7,5},{8,10},{10,8},{9,1... | collective-permute-start | bytes 1572872 | tf_op jit(solution)/shard_map/ppermute | solution.py:175
  77.3 15.4 %collective-permute-start.8 = (bf16[256,256]{1,0:T(8,128)(2,1)S(1)}, bf16[256,256]{1,0:T(8,128)(2,1)S(1)}, u32[]{:S(2)}, u32[]{:S(2)}) collective-permute-start(bf16[256,256]{1,0:T(8,128)(2,1)S(1)} %pad_maximum_fusion), channel_id=1, source_target_pairs={{0,8},{4,12},{8,0},{12,4},{16,24},{20,28},{24,16},{28,20},{1,9},{5... | collective-permute-start | bytes 393224 | tf_op jit(solution)/shard_map/ppermute | solution.py:146
  92.7 8.7 %collective-permute-start.9 = (bf16[512,256]{1,0:T(8,128)(2,1)S(1)}, bf16[512,256]{1,0:T(8,128)(2,1)S(1)}, u32[]{:S(2)}, u32[]{:S(2)}) collective-permute-start(bf16[512,256]{1,0:T(8,128)(2,1)S(1)} %constant_dynamic-update-slice_fusion.near_ref), channel_id=1, source_target_pairs={{0,4},{4,0},{8,12},{12,8},{16,20},{20,16},{24,28},{28,24},{1,5},{5... | collective-permute-start | bytes 786440 | tf_op jit(solution)/shard_map/ppermute | solution.py:146
  94.6 14.6 %collective-permute-start.3 = (bf16[1024,256]{1,0:T(8,128)(2,1)S(1)}, bf16[1024,256]{1,0:T(8,128)(2,1)S(1)}, u32[]{:S(2)}, u32[]{:S(2)}) collective-permute-start(bf16[1024,256]{1,0:T(8,128)(2,1)S(1)} %get-tuple-element.39.own_ref), channel_id=1, source_target_pairs={{0,1},{1,0},{2,3},{3,2},{4,5},{5,4},{6,7},{7,6},{8,9},{9,8},{10,11... | collective-permute-start | bytes 1572872 | tf_op jit(solution)/shard_map/ppermute | solution.py:176
  96.6 12.6 %collective-permute-start.5 = (bf16[1024,256]{1,0:T(8,128)(2,1)S(1)}, bf16[1024,256]{1,0:T(8,128)(2,1)S(1)}, u32[]{:S(2)}, u32[]{:S(2)}) collective-permute-start(bf16[1024,256]{1,0:T(8,128)(2,1)S(1)} %collective-permute-done.4.far_ref), channel_id=1, source_target_pairs={{0,1},{1,0},{2,3},{3,2},{4,5},{5,4},{6,7},{7,6},{8,9},{9,8},{10,11... | collective-permute-start | bytes 1572872 | tf_op jit(solution)/shard_map/ppermute | solution.py:184
  102.1 25.1 %all-to-all-start.2 = ((f32[8,16,256]{2,1,0:T(8,128)}), f32[8,16,256]{2,1,0:T(8,128)S(1)}, u32[]{:S(2)}, u32[]{:S(2)}) async-start(f32[8,16,256]{2,1,0:T(8,128)} %bitcast.7), calls=%async_computation.2 | async-start | bytes 262144 | tf_op jit(solution)/shard_map/all_to_all | solution.py:192
  112.8 9.2 %collective-permute-start.10 = (bf16[256,256]{1,0:T(8,128)(2,1)S(1)}, bf16[256,256]{1,0:T(8,128)(2,1)S(1)}, u32[]{:S(2)}, u32[]{:S(2)}) collective-permute-start(bf16[256,256]{1,0:T(8,128)(2,1)S(1)} %get-tuple-element.46), channel_id=1, source_target_pairs={{0,32},{32,0},{1,33},{33,1},{2,34},{34,2},{3,35},{35,3},{4,36},{36... | collective-permute-start | bytes 393224 | tf_op jit(solution)/shard_map/ppermute | solution.py:139
  115.4 8.0 %collective-permute-start.11 = (bf16[256,256]{1,0:T(8,128)(2,1)S(1)}, bf16[256,256]{1,0:T(8,128)(2,1)S(1)}, u32[]{:S(2)}, u32[]{:S(2)}) collective-permute-start(bf16[256,256]{1,0:T(8,128)(2,1)S(1)} %get-tuple-element.47), channel_id=1, source_target_pairs={{0,64},{64,0},{1,65},{65,1},{2,66},{66,2},{3,67},{67,3},{4,68},{68... | collective-permute-start | bytes 393224 | tf_op jit(solution)/shard_map/ppermute | solution.py:140
  118.1 7.8 %collective-permute-start.12 = (bf16[256,256]{1,0:T(8,128)(2,1)S(1)}, bf16[256,256]{1,0:T(8,128)(2,1)S(1)}, u32[]{:S(2)}, u32[]{:S(2)}) collective-permute-start(bf16[256,256]{1,0:T(8,128)(2,1)S(1)} %get-tuple-element.48), channel_id=1, source_target_pairs={{0,96},{32,64},{64,32},{96,0},{1,97},{33,65},{65,33},{97,1},{2,98}... | collective-permute-start | bytes 393224 | tf_op jit(solution)/shard_map/ppermute | solution.py:141

commit v9 on v6

--- a/solution.py
+++ b/solution.py
@@ -85,9 +85,10 @@
     total = len(parts) * wide
     spot = lax.broadcasted_iota(jnp.int32, (1, total), 1)
     j = spot % n_j
-    z = (spot // n_j) % n_z
-    xl = (spot // (n_j * n_z)) % 2
-    y = spot // (n_j * n_z * 2)
+    low = spot // n_j % 2
+    z = spot // (n_j * 2) % n_z
+    xl = spot // (n_j * 2 * n_z) % 2
+    y = place_ref[3] ^ (spot // (n_j * 4 * n_z) * 2 + low)
     source = ((z * 2 + xl) * n_y + y) * n_j + j
     for c in range(0, total, 256):
         moved = None
@@ -99,14 +100,16 @@
         out_ref[:, c : c + 256] = moved.astype(jnp.bfloat16)
 
 
-def input_kernel(scaled_ref, weight_ref, *outs):
-    rows = outs[0].shape[0]
+def input_kernel(scaled_ref, *refs):
+    weights, outs = refs[:-4], refs[-4:]
+    rows, deep = outs[0].shape[0], weights[0].shape[0]
     for m, out_ref in enumerate(outs):
-        out_ref[...] = jnp.dot(
-            scaled_ref[m * rows : (m + 1) * rows, :],
-            weight_ref[...],
-            preferred_element_type=jnp.float32,
-        ).astype(jnp.bfloat16)
+        total = None
+        for f, weight in enumerate(weights):
+            block = scaled_ref[m * rows : (m + 1) * rows, f * deep : (f + 1) * deep]
+            term = jnp.dot(block, weight[...], preferred_element_type=jnp.float32)
+            total = term if total is None else total + term
+        out_ref[...] = total.astype(jnp.bfloat16)
 
 
 def join_kernel(place_ref, *refs):
@@ -138,6 +141,10 @@
     ]
 
 
+def flipped(x, bits, n):
+    return lax.ppermute(x, "y", [(i, i ^ bits) for i in range(n)])
+
+
 def local(inputs, value_grad, value_weight, counts, offsets):
     rows, features = inputs.shape
     columns = value_grad.shape[1]
@@ -146,21 +153,20 @@
     wide = features // 4
     narrow = quarter // 4
 
-    place = jnp.stack([lax.axis_index(a) for a in (("zl", "xl"), TP, "c")]).astype(jnp.int32)
+    place = jnp.stack([lax.axis_index(a) for a in (("zl", "xl"), TP, "c", "y")]).astype(jnp.int32)
     args = (place, counts, offsets, value_grad, inputs)
     sizes = [(rows, wide + columns)] + [(rows // 2, wide + 2 * columns)] * 3
     blocks = call(prep_kernel, sizes, 3, *args, vmem=60 * MIB)
-    blocks, value_weight = lax.optimization_barrier((blocks, value_weight))
+    turned = value_weight.T
+    pair = jnp.concatenate([turned, flipped(turned, 1, n_y)])
     received = from_group(blocks)
-
-    mine = value_weight.T.reshape(own_columns, 2, 2, narrow).transpose(2, 1, 0, 3)
-    mine = jnp.broadcast_to(mine[:, None], (2, n_zh, 2, own_columns, narrow))
-    mine = mine.reshape(-1, own_columns, narrow)
+    received[1], pair = lax.optimization_barrier((received[1], pair))
+
+    mine = pair.reshape(2 * own_columns, 2, 2, narrow).transpose(2, 1, 0, 3)
+    mine = jnp.broadcast_to(mine[:, None], (2, n_zh, 2, 2 * own_columns, narrow))
+    mine = mine.reshape(-1, 2 * own_columns, narrow)
     block = lax.all_to_all(mine, ("xl", "zh", "zl"), 0, 0, tiled=True)
-    received, block = lax.optimization_barrier((received, block))
     block = block.reshape(-1, narrow)
-    block = jnp.broadcast_to(block, (n_y, *block.shape))
-    weight = lax.all_to_all(block, "y", 0, 0, tiled=True).reshape(-1, narrow)
 
     sizes = [(3 * rows // 2, wide), (4 * rows, columns)]
     half, own = call(split_kernel, sizes, 1, place, *received)
@@ -168,23 +174,24 @@
     from_far = lax.ppermute(own, "xh", SWAP)
     from_core = lax.ppermute(own, "c", SWAP)
     (term,) = call(weight_kernel, [(n_y, wide // n_y, columns)], 0, *received, half)
-    early = (term, weight, from_far, from_core)
-    term, weight, from_far, from_core = lax.optimization_barrier(early)
     terms = lax.all_to_all(term, "y", 0, 0, tiled=True)
+    weights = [block] + [flipped(block, bits, n_y) for bits in range(2, n_y, 2)]
+    terms, weights, from_far = lax.optimization_barrier((terms, weights, from_far))
     gathered = [own, from_core, from_far, lax.ppermute(from_far, "c", SWAP)]
 
     sizes = (2 * n_zh, n_y, own_columns)
     kernel = functools.partial(order_kernel, sizes)
     (ordered,) = call(kernel, [(4 * rows, n_tp * columns)], 1, place, *gathered)
-    outs = call(input_kernel, [(rows, narrow)] * 4, 0, ordered, weight)
-
-    terms, outs = lax.optimization_barrier((terms, outs))
+    outs = call(input_kernel, [(rows, narrow)] * 4, 0, ordered, *weights)
+
     summed = jnp.sum(terms.astype(jnp.float32), axis=0).reshape(n_zh, -1, columns)
     summed = lax.all_to_all(summed, "zh", 0, 0, tiled=True)
+    outs = from_group(outs)
+    summed, outs = lax.optimization_barrier((summed, outs))
     normalizer = 1.0 / math.sqrt(counts.shape[1] * lax.axis_size(FSDP))
     weight_grad = jnp.sum(summed, axis=0) * normalizer
 
-    (input_grad,) = call(join_kernel, [(rows, quarter)], 1, place, *from_group(outs))
+    (input_grad,) = call(join_kernel, [(rows, quarter)], 1, place, *outs)
     return (input_grad, weight_grad)
 
 

time: 128 us -> 133 us (1.039)
  blocking collectives: 34.5 us -> 0 us
  starting transfers between devices: 49.6 us -> 76.3 us
  waiting for transfers between devices: 26.7 us -> 38.9 us
    all_to_all x1 -> x0, blocking collectives: 34.5 us -> none  [local(): block = lax.all_to_all(mine, ('xl', 'zh', 'zl'), 0, 0, tiled=True)]
    ppermute x0 -> x4, starting transfers between devices: none -> 15.7 us  [flipped(): return lax.ppermute(x, 'y', [(i, i ^ bits) for i in range(n)])]
    all_to_all x1, waiting for transfers between devices: 0.01 us -> 14.3 us  [local(): block = lax.all_to_all(mine, ('xl', 'zh', 'zl'), 0, 0, tiled=True)]
    all_to_all x1, starting transfers between devices: 7.1 us -> 19.7 us  [local(): block = lax.all_to_all(mine, ('xl', 'zh', 'zl'), 0, 0, tiled=True)]
    ppermute x1, waiting for transfers between devices: 10.3 us -> 0.01 us  [local(): from_far = lax.ppermute(own, 'xh', SWAP)]
    ppermute x0 -> x4, waiting for transfers between devices: none -> 9.48 us  [flipped(): return lax.ppermute(x, 'y', [(i, i ^ bits) for i in range(n)])]
    all_to_all x1, waiting for transfers between devices: 8.94 us -> 0.01 us  [local(): terms = lax.all_to_all(term, 'y', 0, 0, tiled=True)]
    ppermute x2, waiting for transfers between devices: 2.43 us -> 9.6 us  [from_group(): lax.ppermute(blocks[3], ('zl', 'xl'), BOTH)]
  transfers between devices with their start and end apart: 13 -> 17, of which waited for: 5 -> 8; matrix products, arithmetic and copies ran while one was open for 0% -> 1% of each run, Pallas kernels for 6% -> 4%
where the time goes in v9:
time: 133 us; the launch traced here: 132 us
  starting transfers between devices  76.3 us (57%)
  waiting for transfers between devices  38.9 us (29%)
  Pallas kernels  11.7 us (9%)
  other arithmetic  2.03 us (2%)
  local copies, waits for them, and re-layouts  1.76 us (1%)
    all_to_all x1, starting transfers between devices, local(): block = lax.all_to_all(mine, ('xl', 'zh', 'zl'), 0, 0, tiled=True)  19.7 us
    ppermute x4, starting transfers between devices, flipped(): return lax.ppermute(x, 'y', [(i, i ^ bits) for i in range(n)])  15.7 us
    all_to_all x1, waiting for transfers between devices, local(): block = lax.all_to_all(mine, ('xl', 'zh', 'zl'), 0, 0, tiled=True)  14.3 us
    pallas_call x6, Pallas kernels, call(): pl.pallas_call(kernel, out_shape=shapes, in_specs=[pl.BlockSpec(memory_sp...  11.7 us
    ppermute x2, waiting for transfers between devices, from_group(): lax.ppermute(blocks[3], ('zl', 'xl'), BOTH)  9.6 us
    ppermute x4, waiting for transfers between devices, flipped(): return lax.ppermute(x, 'y', [(i, i ^ bits) for i in range(n)])  9.48 us
    ppermute x2, starting transfers between devices, from_group(): lax.ppermute(blocks[2], 'zl', SWAP)  7.86 us
    all_to_all x1, starting transfers between devices, local(): terms = lax.all_to_all(term, 'y', 0, 0, tiled=True)  7.1 us
  transfers between devices with their start and end apart: 17, of which 8 were waited for; matrix products, arithmetic and copies ran while one was open for 1% of the time, Pallas kernels for 4%

profile of v9, /device:TPU:6, one launch (start us, length us, event | category | flops | bytes accessed | tf_op | source)
XLA Modules:
  0.0 131.5 jit_solution(8305796272421871065)
XLA Ops:
  0.6 0.0 copy-start.3
  0.6 0.7 pad_add_fusion.place_ref
  1.3 0.0 copy-start.2
  1.3 3.2 %shard_map.68 = (bf16[256,1280]{1,0:T(8,128)(2,1)}, bf16[128,1536]{1,0:T(8,128)(2,1)}, bf16[128,1536]{1,0:T(8,128)(2,1)}, bf16[128,1536]{1,0:T(8,128)(2,1)}) custom-call(s32[4]{0:T(128)} %pad_add_fusion.place_ref, s32[1,4]{1,0:T(1,128)} %counts_ref.1, s32[1,4]{1,0:T(1,128)} %offsets_ref.1, bf16[256,256]{1,0:T(8,128)(2,1)} %grad_ref.1, ...), custom_call_target="tpu_custom_call" | custom-call | tf_op jit(solution)/shard_map/pallas_call | solution.py:126
  4.6 2.7 %collective-permute-start = (bf16[128,1536]{1,0:T(8,128)(2,1)}, bf16[128,1536]{1,0:T(8,128)(2,1)S(1)}, u32[]{:S(2)}, u32[]{:S(2)}) collective-permute-start(bf16[128,1536]{1,0:T(8,128)(2,1)} %get-tuple-element.26), channel_id=1, source_target_pairs={{0,32},{32,0},{1,33},{33,1},{2,34},{34,2},{3,35},{35,3},{4,36},{36... | collective-permute-start | bytes 1179656 | tf_op jit(solution)/shard_map/ppermute | solution.py:138
  7.3 4.3 %collective-permute-start.2 = (bf16[128,1536]{1,0:T(8,128)(2,1)}, bf16[128,1536]{1,0:T(8,128)(2,1)S(1)}, u32[]{:S(2)}, u32[]{:S(2)}) collective-permute-start(bf16[128,1536]{1,0:T(8,128)(2,1)} %get-tuple-element.28), channel_id=1, source_target_pairs={{0,64},{64,0},{1,65},{65,1},{2,66},{66,2},{3,67},{67,3},{4,68},{68... | collective-permute-start | bytes 1179656 | tf_op jit(solution)/shard_map/ppermute | solution.py:139
  11.6 2.6 %collective-permute-start.3 = (bf16[128,1536]{1,0:T(8,128)(2,1)}, bf16[128,1536]{1,0:T(8,128)(2,1)S(1)}, u32[]{:S(2)}, u32[]{:S(2)}) collective-permute-start(bf16[128,1536]{1,0:T(8,128)(2,1)} %get-tuple-element.29), channel_id=1, source_target_pairs={{0,96},{32,64},{64,32},{96,0},{1,97},{33,65},{65,33},{97,1},{2,98}... | collective-permute-start | bytes 1179656 | tf_op jit(solution)/shard_map/ppermute | solution.py:140
  14.2 0.0 copy-done.3
  14.2 3.5 %collective-permute-start.1 = (bf16[4,1024]{1,0:T(4,128)(2,1)S(1)}, bf16[4,1024]{1,0:T(4,128)(2,1)S(1)}, u32[]{:S(2)}, u32[]{:S(2)}) collective-permute-start(bf16[4,1024]{1,0:T(4,128)(2,1)S(1)} %bitcast.16), channel_id=1, source_target_pairs={{0,4},{4,0},{8,12},{12,8},{16,20},{20,16},{24,28},{28,24},{1,5},{5... | collective-permute-start | bytes 24584 | tf_op jit(solution)/shard_map/ppermute | solution.py:145
  17.7 2.1 %collective-permute-done.1 = bf16[4,1024]{1,0:T(4,128)(2,1)S(1)} collective-permute-done((bf16[4,1024]{1,0:T(4,128)(2,1)S(1)}, bf16[4,1024]{1,0:T(4,128)(2,1)S(1)}, u32[]{:S(2)}, u32[]{:S(2)}) %collective-permute-start.1) | collective-permute-done | bytes 8224 | tf_op jit(solution)/shard_map/ppermute | solution.py:145
  19.7 0.0 collective-permute-done.refs_0_
  19.7 2.0 %collective-permute-done.2.refs_1_ = bf16[128,1536]{1,0:T(8,128)(2,1)S(1)} collective-permute-done((bf16[128,1536]{1,0:T(8,128)(2,1)}, bf16[128,1536]{1,0:T(8,128)(2,1)S(1)}, u32[]{:S(2)}, u32[]{:S(2)}) %collective-permute-start.2) | collective-permute-done | bytes 393248 | tf_op jit(solution)/shard_map/ppermute | solution.py:139
  21.8 7.9 %collective-permute-done.3.refs_2_ = bf16[128,1536]{1,0:T(8,128)(2,1)S(1)} collective-permute-done((bf16[128,1536]{1,0:T(8,128)(2,1)}, bf16[128,1536]{1,0:T(8,128)(2,1)S(1)}, u32[]{:S(2)}, u32[]{:S(2)}) %collective-permute-start.3) | collective-permute-done | bytes 393248 | tf_op jit(solution)/shard_map/ppermute | solution.py:140
  29.7 0.0 copy-done.2
  29.7 0.0 copy-start
  29.7 1.1 copy-done
  30.8 0.0 copy-start.1
  30.8 1.5 %shard_map.69 = (bf16[384,1024]{1,0:T(8,128)(2,1)}, bf16[1024,256]{1,0:T(8,128)(2,1)S(1)}) custom-call(s32[4]{0:T(128)S(1)} %copy-done.2, bf16[256,1280]{1,0:T(8,128)(2,1)S(1)} %copy-done, bf16[128,1536]{1,0:T(8,128)(2,1)S(1)} %collective-permute-done.refs_0_, bf16[128,1536]{1,0:T(8,128)(2,1)S(1)} %collective-permute-done.2.refs_1_, ...), custom_call_target="tpu_custom_call" | custom-call | tf_op jit(solution)/shard_map/pallas_call | solution.py:126
  32.3 1.9 %collective-permute-start.4 = (bf16[384,1024]{1,0:T(8,128)(2,1)}, bf16[384,1024]{1,0:T(8,128)(2,1)S(1)}, u32[]{:S(2)}, u32[]{:S(2)}) collective-permute-start(bf16[384,1024]{1,0:T(8,128)(2,1)} %get-tuple-element.30), channel_id=1, source_target_pairs={{0,1},{1,0},{2,3},{3,2},{4,5},{5,4},{6,7},{7,6},{8,9},{9,8},{10,11... | collective-permute-start | bytes 2359304 | tf_op jit(solution)/shard_map/ppermute | solution.py:173
  34.2 0.7 broadcast_in_dim.2
  34.9 19.7 %all-to-all-start.1 = ((bf16[32,8,256]{2,1,0:T(8,128)(2,1)}), bf16[32,8,256]{2,1,0:T(8,128)(2,1)S(1)}, u32[]{:S(2)}, u32[]{:S(2)}) async-start(bf16[32,8,256]{2,1,0:T(8,128)(2,1)} %bitcast.7), calls=%async_computation.1 | async-start | bytes 262144 | tf_op jit(solution)/shard_map/all_to_all | solution.py:168
  54.6 0.0 collective-permute-done.4.refs_3_
  54.6 0.0 copy-done.1
  54.6 1.9 %shard_map.70 = bf16[8,128,256]{2,1,0:T(8,128)(2,1)} custom-call(bf16[256,1280]{1,0:T(8,128)(2,1)S(1)} %copy-done.1, bf16[128,1536]{1,0:T(8,128)(2,1)S(1)} %collective-permute-done.refs_0_, bf16[128,1536]{1,0:T(8,128)(2,1)S(1)} %collective-permute-done.2.refs_1_, bf16[128,1536]{1,0:T(8,128)(2,1)S(1)} %collective-permute-done.3.refs_2_, ...), custom_call_target="tpu_custom_call" | custom-call | tf_op jit(solution)/shard_map/pallas_call | solution.py:126
  56.6 14.3 %all-to-all-done.1 = bf16[32,8,256]{2,1,0:T(8,128)(2,1)S(1)} async-done(((bf16[32,8,256]{2,1,0:T(8,128)(2,1)}), bf16[32,8,256]{2,1,0:T(8,128)(2,1)S(1)}, u32[]{:S(2)}, u32[]{:S(2)}) %all-to-all-start.1) | async-done | bytes 131104 | tf_op jit(solution)/shard_map/all_to_all | solution.py:168
  70.9 7.1 %all-to-all-start = ((bf16[8,128,256]{2,1,0:T(8,128)(2,1)}), bf16[8,128,256]{2,1,0:T(8,128)(2,1)S(1)}, u32[]{:S(2)}, u32[]{:S(2)}) async-start(bf16[8,128,256]{2,1,0:T(8,128)(2,1)} %shard_map.70), calls=%async_computation | async-start | bytes 1048576 | tf_op jit(solution)/shard_map/all_to_all | solution.py:177
  78.0 3.3 %collective-permute-start.8 = (bf16[1024,256]{1,0:T(8,128)(2,1)S(1)}, bf16[1024,256]{1,0:T(8,128)(2,1)S(1)}, u32[]{:S(2)}, u32[]{:S(2)}) collective-permute-start(bf16[1024,256]{1,0:T(8,128)(2,1)S(1)} %get-tuple-element.32.own_ref), channel_id=1, source_target_pairs={{0,2},{2,0},{1,3},{3,1},{4,6},{6,4},{5,7},{7,5},{8,10},{10,8},{9,1... | collective-permute-start | bytes 1572872 | tf_op jit(solution)/shard_map/ppermute | solution.py:174
  81.3 4.8 %collective-permute-start.5 = (bf16[256,256]{1,0:T(8,128)(2,1)S(1)}, bf16[256,256]{1,0:T(8,128)(2,1)S(1)}, u32[]{:S(2)}, u32[]{:S(2)}) collective-permute-start(bf16[256,256]{1,0:T(8,128)(2,1)S(1)} %bitcast.11), channel_id=1, source_target_pairs={{0,8},{4,12},{8,0},{12,4},{16,24},{20,28},{24,16},{28,20},{1,9},{5... | collective-permute-start | bytes 393224 | tf_op jit(solution)/shard_map/ppermute | solution.py:145
  86.1 5.5 %collective-permute-start.6 = (bf16[256,256]{1,0:T(8,128)(2,1)S(1)}, bf16[256,256]{1,0:T(8,128)(2,1)S(1)}, u32[]{:S(2)}, u32[]{:S(2)}) collective-permute-start(bf16[256,256]{1,0:T(8,128)(2,1)S(1)} %bitcast.12), channel_id=1, source_target_pairs={{0,16},{4,20},{8,24},{12,28},{16,0},{20,4},{24,8},{28,12},{1,17},{... | collective-permute-start | bytes 393224 | tf_op jit(solution)/shard_map/ppermute | solution.py:145
  91.6 1.9 %collective-permute-start.7 = (bf16[256,256]{1,0:T(8,128)(2,1)S(1)}, bf16[256,256]{1,0:T(8,128)(2,1)S(1)}, u32[]{:S(2)}, u32[]{:S(2)}) collective-permute-start(bf16[256,256]{1,0:T(8,128)(2,1)S(1)} %bitcast.13), channel_id=1, source_target_pairs={{0,24},{4,28},{8,16},{12,20},{16,8},{20,12},{24,0},{28,4},{1,25},{... | collective-permute-start | bytes 393224 | tf_op jit(solution)/shard_map/ppermute | solution.py:145
  93.5 1.9 %collective-permute-start.9 = (bf16[1024,256]{1,0:T(8,128)(2,1)S(1)}, bf16[1024,256]{1,0:T(8,128)(2,1)S(1)}, u32[]{:S(2)}, u32[]{:S(2)}) collective-permute-start(bf16[1024,256]{1,0:T(8,128)(2,1)S(1)} %get-tuple-element.32.own_ref), channel_id=1, source_target_pairs={{0,1},{1,0},{2,3},{3,2},{4,5},{5,4},{6,7},{7,6},{8,9},{9,8},{10,11... | collective-permute-start | bytes 1572872 | tf_op jit(solution)/shard_map/ppermute | solution.py:175
  95.5 0.0 collective-permute-done.8.far_ref
  95.5 7.1 %collective-permute-done.5.refs_1_ = bf16[256,256]{1,0:T(8,128)(2,1)S(1)} collective-permute-done((bf16[256,256]{1,0:T(8,128)(2,1)S(1)}, bf16[256,256]{1,0:T(8,128)(2,1)S(1)}, u32[]{:S(2)}, u32[]{:S(2)}) %collective-permute-start.5) | collective-permute-done | bytes 131104 | tf_op jit(solution)/shard_map/ppermute | solution.py:145
  102.5 0.4 collective-permute-done.6.refs_2_
  102.9 0.0 collective-permute-done.7.refs_3_
  102.9 0.0 all-to-all-done
  102.9 1.9 %collective-permute-start.10 = (bf16[1024,256]{1,0:T(8,128)(2,1)S(1)}, bf16[1024,256]{1,0:T(8,128)(2,1)S(1)}, u32[]{:S(2)}, u32[]{:S(2)}) collective-permute-start(bf16[1024,256]{1,0:T(8,128)(2,1)S(1)} %collective-permute-done.8.far_ref), channel_id=1, source_target_pairs={{0,1},{1,0},{2,3},{3,2},{4,5},{5,4},{6,7},{7,6},{8,9},{9,8},{10,11... | collective-permute-start | bytes 1572872 | tf_op jit(solution)/shard_map/ppermute | solution.py:180
  104.8 0.7 convert_reduce_fusion
  105.5 5.9 %all-to-all-start.2 = ((f32[8,16,256]{2,1,0:T(8,128)}), f32[8,16,256]{2,1,0:T(8,128)S(1)}, u32[]{:S(2)}, u32[]{:S(2)}) async-start(f32[8,16,256]{2,1,0:T(8,128)} %bitcast.9), calls=%async_computation.2 | async-start | bytes 262144 | tf_op jit(solution)/shard_map/all_to_all | solution.py:188
  111.4 0.0 collective-permute-done.9.core_ref
  111.4 0.0 collective-permute-done.10.both_ref
  111.4 2.9 %shard_map.71.scaled_ref = bf16[1024,1024]{1,0:T(8,128)(2,1)S(1)} custom-call(s32[4]{0:T(128)S(1)} %copy-done.2, bf16[1024,256]{1,0:T(8,128)(2,1)S(1)} %get-tuple-element.32.own_ref, bf16[1024,256]{1,0:T(8,128)(2,1)S(1)} %collective-permute-done.9.core_ref, bf16[1024,256]{1,0:T(8,128)(2,1)S(1)} %collective-permute-done.8.far_ref, ...), custom_call_target="tpu_custom_call" | custom-call | tf_op jit(solution)/shard_map/pallas_call | solution.py:126
  114.3 0.7 shard_map.72
  115.1 3.0 %collective-permute-start.11 = (bf16[256,256]{1,0:T(8,128)(2,1)S(1)}, bf16[256,256]{1,0:T(8,128)(2,1)S(1)}, u32[]{:S(2)}, u32[]{:S(2)}) collective-permute-start(bf16[256,256]{1,0:T(8,128)(2,1)S(1)} %get-tuple-element.40), channel_id=1, source_target_pairs={{0,32},{32,0},{1,33},{33,1},{2,34},{34,2},{3,35},{35,3},{4,36},{36... | collective-permute-start | bytes 393224 | tf_op jit(solution)/shard_map/ppermute | solution.py:138
  118.1 3.6 %collective-permute-start.12 = (bf16[256,256]{1,0:T(8,128)(2,1)S(1)}, bf16[256,256]{1,0:T(8,128)(2,1)S(1)}, u32[]{:S(2)}, u32[]{:S(2)}) collective-permute-start(bf16[256,256]{1,0:T(8,128)(2,1)S(1)} %get-tuple-element.41), channel_id=1, source_target_pairs={{0,64},{64,0},{1,65},{65,1},{2,66},{66,2},{3,67},{67,3},{4,68},{68... | collective-permute-start | bytes 393224 | tf_op jit(solution)/shard_map/ppermute | solution.py:139
  121.6 2.6 %collective-permute-start.13 = (bf16[256,256]{1,0:T(8,128)(2,1)S(1)}, bf16[256,256]{1,0:T(8,128)(2,1)S(1)}, u32[]{:S(2)}, u32[]{:S(2)}) collective-permute-start(bf16[256,256]{1,0:T(8,128)(2,1)S(1)} %get-tuple-element.42), channel_id=1, source_target_pairs={{0,96},{32,64},{64,32},{96,0},{1,97},{33,65},{65,33},{97,1},{2,98}... | collective-permute-start | bytes 393224 | tf_op jit(solution)/shard_map/ppermute | solution.py:140
  124.3 3.5 %all-to-all-done.2 = f32[8,16,256]{2,1,0:T(8,128)S(1)} async-done(((f32[8,16,256]{2,1,0:T(8,128)}), f32[8,16,256]{2,1,0:T(8,128)S(1)}, u32[]{:S(2)}, u32[]{:S(2)}) %all-to-all-start.2) | async-done | bytes 131104 | tf_op jit(solution)/shard_map/all_to_all | solution.py:188
  127.8 0.0 collective-permute-done.11.refs_1_
  127.8 0.0 collective-permute-done.12.refs_2_
  127.8 1.7 %collective-permute-done.13.refs_3_ = bf16[256,256]{1,0:T(8,128)(2,1)S(1)} collective-permute-done((bf16[256,256]{1,0:T(8,128)(2,1)S(1)}, bf16[256,256]{1,0:T(8,128)(2,1)S(1)}, u32[]{:S(2)}, u32[]{:S(2)}) %collective-permute-start.13) | collective-permute-done | bytes 131104 | tf_op jit(solution)/shard_map/ppermute | solution.py:140
  129.5 0.6 broadcast_multiply_fusion
  130.1 1.4 %shard_map.73 = bf16[256,1024]{1,0:T(8,128)(2,1)} custom-call(s32[4]{0:T(128)S(1)} %copy-done.2, bf16[256,256]{1,0:T(8,128)(2,1)S(1)} %get-tuple-element.43.refs_0_, bf16[256,256]{1,0:T(8,128)(2,1)S(1)} %collective-permute-done.11.refs_1_, bf16[256,256]{1,0:T(8,128)(2,1)S(1)} %collective-permute-done.12.refs_2_, ...), custom_call_target="tpu_custom_call" | custom-call | tf_op jit(solution)/shard_map/pallas_call | solution.py:126
  (3 shorter events, 0.0 us)
Async XLA Ops:
  0.6 13.5 %copy-start.3 = (bf16[1024,4]{0,1:T(4,128)(2,1)S(1)}, bf16[1024,4]{0,1:T(4,128)(2,1)}, u32[]{:S(2)}) copy-start(bf16[1024,4]{0,1:T(4,128)(2,1)} %param.7) | copy-start | bytes 24580
  1.3 28.4 %copy-start.2 = (s32[4]{0:T(128)S(1)}, s32[4]{0:T(128)}, u32[]{:S(2)}) copy-start(s32[4]{0:T(128)} %pad_add_fusion.place_ref) | copy-start | bytes 52
  4.6 15.2 %collective-permute-start = (bf16[128,1536]{1,0:T(8,128)(2,1)}, bf16[128,1536]{1,0:T(8,128)(2,1)S(1)}, u32[]{:S(2)}, u32[]{:S(2)}) collective-permute-start(bf16[128,1536]{1,0:T(8,128)(2,1)} %get-tuple-element.26), channel_id=1, source_target_pairs={{0,32},{32,0},{1,33},{33,1},{2,34},{34,2},{3,35},{35,3},{4,36},{36... | collective-permute-start | bytes 1179656 | tf_op jit(solution)/shard_map/ppermute | solution.py:138
  7.3 14.5 %collective-permute-start.2 = (bf16[128,1536]{1,0:T(8,128)(2,1)}, bf16[128,1536]{1,0:T(8,128)(2,1)S(1)}, u32[]{:S(2)}, u32[]{:S(2)}) collective-permute-start(bf16[128,1536]{1,0:T(8,128)(2,1)} %get-tuple-element.28), channel_id=1, source_target_pairs={{0,64},{64,0},{1,65},{65,1},{2,66},{66,2},{3,67},{67,3},{4,68},{68... | collective-permute-start | bytes 1179656 | tf_op jit(solution)/shard_map/ppermute | solution.py:139
  11.6 18.1 %collective-permute-start.3 = (bf16[128,1536]{1,0:T(8,128)(2,1)}, bf16[128,1536]{1,0:T(8,128)(2,1)S(1)}, u32[]{:S(2)}, u32[]{:S(2)}) collective-permute-start(bf16[128,1536]{1,0:T(8,128)(2,1)} %get-tuple-element.29), channel_id=1, source_target_pairs={{0,96},{32,64},{64,32},{96,0},{1,97},{33,65},{65,33},{97,1},{2,98}... | collective-permute-start | bytes 1179656 | tf_op jit(solution)/shard_map/ppermute | solution.py:140
  14.2 5.5 %collective-permute-start.1 = (bf16[4,1024]{1,0:T(4,128)(2,1)S(1)}, bf16[4,1024]{1,0:T(4,128)(2,1)S(1)}, u32[]{:S(2)}, u32[]{:S(2)}) collective-permute-start(bf16[4,1024]{1,0:T(4,128)(2,1)S(1)} %bitcast.16), channel_id=1, source_target_pairs={{0,4},{4,0},{8,12},{12,8},{16,20},{20,16},{24,28},{28,24},{1,5},{5... | collective-permute-start | bytes 24584 | tf_op jit(solution)/shard_map/ppermute | solution.py:145
  29.7 1.1 copy-start
  30.8 23.9 %copy-start.1 = (bf16[256,1280]{1,0:T(8,128)(2,1)S(1)}, bf16[256,1280]{1,0:T(8,128)(2,1)}, u32[]{:S(2)}) copy-start(bf16[256,1280]{1,0:T(8,128)(2,1)} %get-tuple-element.25.own_ref) | copy-start | bytes 1966084
  32.3 22.3 %collective-permute-start.4 = (bf16[384,1024]{1,0:T(8,128)(2,1)}, bf16[384,1024]{1,0:T(8,128)(2,1)S(1)}, u32[]{:S(2)}, u32[]{:S(2)}) collective-permute-start(bf16[384,1024]{1,0:T(8,128)(2,1)} %get-tuple-element.30), channel_id=1, source_target_pairs={{0,1},{1,0},{2,3},{3,2},{4,5},{5,4},{6,7},{7,6},{8,9},{9,8},{10,11... | collective-permute-start | bytes 2359304 | tf_op jit(solution)/shard_map/ppermute | solution.py:173
  34.9 36.0 %all-to-all-start.1 = ((bf16[32,8,256]{2,1,0:T(8,128)(2,1)}), bf16[32,8,256]{2,1,0:T(8,128)(2,1)S(1)}, u32[]{:S(2)}, u32[]{:S(2)}) async-start(bf16[32,8,256]{2,1,0:T(8,128)(2,1)} %bitcast.7), calls=%async_computation.1 | async-start | bytes 262144 | tf_op jit(solution)/shard_map/all_to_all | solution.py:168
  70.9 32.0 %all-to-all-start = ((bf16[8,128,256]{2,1,0:T(8,128)(2,1)}), bf16[8,128,256]{2,1,0:T(8,128)(2,1)S(1)}, u32[]{:S(2)}, u32[]{:S(2)}) async-start(bf16[8,128,256]{2,1,0:T(8,128)(2,1)} %shard_map.70), calls=%async_computation | async-start | bytes 1048576 | tf_op jit(solution)/shard_map/all_to_all | solution.py:177
  78.0 17.5 %collective-permute-start.8 = (bf16[1024,256]{1,0:T(8,128)(2,1)S(1)}, bf16[1024,256]{1,0:T(8,128)(2,1)S(1)}, u32[]{:S(2)}, u32[]{:S(2)}) collective-permute-start(bf16[1024,256]{1,0:T(8,128)(2,1)S(1)} %get-tuple-element.32.own_ref), channel_id=1, source_target_pairs={{0,2},{2,0},{1,3},{3,1},{4,6},{6,4},{5,7},{7,5},{8,10},{10,8},{9,1... | collective-permute-start | bytes 1572872 | tf_op jit(solution)/shard_map/ppermute | solution.py:174
  81.3 21.2 %collective-permute-start.5 = (bf16[256,256]{1,0:T(8,128)(2,1)S(1)}, bf16[256,256]{1,0:T(8,128)(2,1)S(1)}, u32[]{:S(2)}, u32[]{:S(2)}) collective-permute-start(bf16[256,256]{1,0:T(8,128)(2,1)S(1)} %bitcast.11), channel_id=1, source_target_pairs={{0,8},{4,12},{8,0},{12,4},{16,24},{20,28},{24,16},{28,20},{1,9},{5... | collective-permute-start | bytes 393224 | tf_op jit(solution)/shard_map/ppermute | solution.py:145
  86.1 16.8 %collective-permute-start.6 = (bf16[256,256]{1,0:T(8,128)(2,1)S(1)}, bf16[256,256]{1,0:T(8,128)(2,1)S(1)}, u32[]{:S(2)}, u32[]{:S(2)}) collective-permute-start(bf16[256,256]{1,0:T(8,128)(2,1)S(1)} %bitcast.12), channel_id=1, source_target_pairs={{0,16},{4,20},{8,24},{12,28},{16,0},{20,4},{24,8},{28,12},{1,17},{... | collective-permute-start | bytes 393224 | tf_op jit(solution)/shard_map/ppermute | solution.py:145
  91.6 11.3 %collective-permute-start.7 = (bf16[256,256]{1,0:T(8,128)(2,1)S(1)}, bf16[256,256]{1,0:T(8,128)(2,1)S(1)}, u32[]{:S(2)}, u32[]{:S(2)}) collective-permute-start(bf16[256,256]{1,0:T(8,128)(2,1)S(1)} %bitcast.13), channel_id=1, source_target_pairs={{0,24},{4,28},{8,16},{12,20},{16,8},{20,12},{24,0},{28,4},{1,25},{... | collective-permute-start | bytes 393224 | tf_op jit(solution)/shard_map/ppermute | solution.py:145
  93.5 17.9 %collective-permute-start.9 = (bf16[1024,256]{1,0:T(8,128)(2,1)S(1)}, bf16[1024,256]{1,0:T(8,128)(2,1)S(1)}, u32[]{:S(2)}, u32[]{:S(2)}) collective-permute-start(bf16[1024,256]{1,0:T(8,128)(2,1)S(1)} %get-tuple-element.32.own_ref), channel_id=1, source_target_pairs={{0,1},{1,0},{2,3},{3,2},{4,5},{5,4},{6,7},{7,6},{8,9},{9,8},{10,11... | collective-permute-start | bytes 1572872 | tf_op jit(solution)/shard_map/ppermute | solution.py:175
  102.9 8.5 %collective-permute-start.10 = (bf16[1024,256]{1,0:T(8,128)(2,1)S(1)}, bf16[1024,256]{1,0:T(8,128)(2,1)S(1)}, u32[]{:S(2)}, u32[]{:S(2)}) collective-permute-start(bf16[1024,256]{1,0:T(8,128)(2,1)S(1)} %collective-permute-done.8.far_ref), channel_id=1, source_target_pairs={{0,1},{1,0},{2,3},{3,2},{4,5},{5,4},{6,7},{7,6},{8,9},{9,8},{10,11... | collective-permute-start | bytes 1572872 | tf_op jit(solution)/shard_map/ppermute | solution.py:180
  105.5 22.3 %all-to-all-start.2 = ((f32[8,16,256]{2,1,0:T(8,128)}), f32[8,16,256]{2,1,0:T(8,128)S(1)}, u32[]{:S(2)}, u32[]{:S(2)}) async-start(f32[8,16,256]{2,1,0:T(8,128)} %bitcast.9), calls=%async_computation.2 | async-start | bytes 262144 | tf_op jit(solution)/shard_map/all_to_all | solution.py:188
  115.1 12.7 %collective-permute-start.11 = (bf16[256,256]{1,0:T(8,128)(2,1)S(1)}, bf16[256,256]{1,0:T(8,128)(2,1)S(1)}, u32[]{:S(2)}, u32[]{:S(2)}) collective-permute-start(bf16[256,256]{1,0:T(8,128)(2,1)S(1)} %get-tuple-element.40), channel_id=1, source_target_pairs={{0,32},{32,0},{1,33},{33,1},{2,34},{34,2},{3,35},{35,3},{4,36},{36... | collective-permute-start | bytes 393224 | tf_op jit(solution)/shard_map/ppermute | solution.py:138
  118.1 9.8 %collective-permute-start.12 = (bf16[256,256]{1,0:T(8,128)(2,1)S(1)}, bf16[256,256]{1,0:T(8,128)(2,1)S(1)}, u32[]{:S(2)}, u32[]{:S(2)}) collective-permute-start(bf16[256,256]{1,0:T(8,128)(2,1)S(1)} %get-tuple-element.41), channel_id=1, source_target_pairs={{0,64},{64,0},{1,65},{65,1},{2,66},{66,2},{3,67},{67,3},{4,68},{68... | collective-permute-start | bytes 393224 | tf_op jit(solution)/shard_map/ppermute | solution.py:139
  121.6 7.9 %collective-permute-start.13 = (bf16[256,256]{1,0:T(8,128)(2,1)S(1)}, bf16[256,256]{1,0:T(8,128)(2,1)S(1)}, u32[]{:S(2)}, u32[]{:S(2)}) collective-permute-start(bf16[256,256]{1,0:T(8,128)(2,1)S(1)} %get-tuple-element.42), channel_id=1, source_target_pairs={{0,96},{32,64},{64,32},{96,0},{1,97},{33,65},{65,33},{97,1},{2,98}... | collective-permute-start | bytes 393224 | tf_op jit(solution)/shard_map/ppermute | solution.py:140

commit v10 on v9

--- a/solution.py
+++ b/solution.py
@@ -78,18 +78,20 @@
 
 
 def order_kernel(sizes, place_ref, own_ref, core_ref, far_ref, both_ref, out_ref):
-    tensor = place_ref[1]
+    q, tensor, y, zh = (place_ref[i] for i in (0, 1, 3, 4))
     parts = [own_ref, core_ref, far_ref, both_ref]
     wide = own_ref.shape[1]
-    n_z, n_y, n_j = sizes
+    n_y, n_j = sizes
     total = len(parts) * wide
     spot = lax.broadcasted_iota(jnp.int32, (1, total), 1)
     j = spot % n_j
-    low = spot // n_j % 2
-    z = spot // (n_j * 2) % n_z
-    xl = spot // (n_j * 2 * n_z) % 2
-    y = place_ref[3] ^ (spot // (n_j * 4 * n_z) * 2 + low)
-    source = ((z * 2 + xl) * n_y + y) * n_j + j
+    y_low = spot // n_j % 2
+    group = q ^ (spot // (2 * n_j) % 4)
+    zh_high = spot // (8 * n_j) % 4
+    zh_low = spot // (32 * n_j) % 2
+    y_high = spot // (64 * n_j)
+    fsdp = ((zh ^ (2 * zh_high + zh_low)) * 4 + group) * n_y + (y ^ (2 * y_high + y_low))
+    source = fsdp * n_j + j
     for c in range(0, total, 256):
         moved = None
         for p, part in enumerate(parts):
@@ -141,8 +143,8 @@
     ]
 
 
-def flipped(x, bits, n):
-    return lax.ppermute(x, "y", [(i, i ^ bits) for i in range(n)])
+def flipped(x, axis, bits):
+    return lax.ppermute(x, axis, [(i, i ^ bits) for i in range(lax.axis_size(axis))])
 
 
 def local(inputs, value_grad, value_weight, counts, offsets):
@@ -153,33 +155,35 @@
     wide = features // 4
     narrow = quarter // 4
 
-    place = jnp.stack([lax.axis_index(a) for a in (("zl", "xl"), TP, "c", "y")]).astype(jnp.int32)
+    place = jnp.stack([lax.axis_index(a) for a in (("zl", "xl"), TP, "c", "y", "zh")]).astype(jnp.int32)
     args = (place, counts, offsets, value_grad, inputs)
     sizes = [(rows, wide + columns)] + [(rows // 2, wide + 2 * columns)] * 3
     blocks = call(prep_kernel, sizes, 3, *args, vmem=60 * MIB)
     turned = value_weight.T
-    pair = jnp.concatenate([turned, flipped(turned, 1, n_y)])
+    pair = jnp.concatenate([turned, flipped(turned, "y", 1)])
+    blocks, pair = lax.optimization_barrier((blocks, pair))
     received = from_group(blocks)
-    received[1], pair = lax.optimization_barrier((received[1], pair))
-
-    mine = pair.reshape(2 * own_columns, 2, 2, narrow).transpose(2, 1, 0, 3)
-    mine = jnp.broadcast_to(mine[:, None], (2, n_zh, 2, 2 * own_columns, narrow))
-    mine = mine.reshape(-1, 2 * own_columns, narrow)
-    block = lax.all_to_all(mine, ("xl", "zh", "zl"), 0, 0, tiled=True)
-    block = block.reshape(-1, narrow)
+    starts = [(place[0] ^ m) * narrow for m in range(4)]
+    quarters = [lax.dynamic_slice_in_dim(pair, start, narrow, 1) for start in starts]
+    received, quarters = lax.optimization_barrier((received, from_group(quarters)))
+    block = jnp.concatenate(quarters)
+    far_z = [flipped(block, "zh", bits) for bits in (2, 4, 6)]
 
     sizes = [(3 * rows // 2, wide), (4 * rows, columns)]
     half, own = call(split_kernel, sizes, 1, place, *received)
     half = lax.ppermute(half, "c", SWAP)
     from_far = lax.ppermute(own, "xh", SWAP)
     from_core = lax.ppermute(own, "c", SWAP)
+    half, far_z = lax.optimization_barrier((half, far_z))
     (term,) = call(weight_kernel, [(n_y, wide // n_y, columns)], 0, *received, half)
     terms = lax.all_to_all(term, "y", 0, 0, tiled=True)
-    weights = [block] + [flipped(block, bits, n_y) for bits in range(2, n_y, 2)]
+    block = jnp.concatenate([block] + far_z)
+    block = jnp.concatenate([block, flipped(block, "zh", 1)])
+    weights = [block] + [flipped(block, "y", bits) for bits in (2, 4, 6)]
     terms, weights, from_far = lax.optimization_barrier((terms, weights, from_far))
     gathered = [own, from_core, from_far, lax.ppermute(from_far, "c", SWAP)]
 
-    sizes = (2 * n_zh, n_y, own_columns)
+    sizes = (n_y, own_columns)
     kernel = functools.partial(order_kernel, sizes)
     (ordered,) = call(kernel, [(4 * rows, n_tp * columns)], 1, place, *gathered)
     outs = call(input_kernel, [(rows, narrow)] * 4, 0, ordered, *weights)

time: 133 us -> 141 us (1.060)
  the two profiles are of different devices: /device:TPU:6 before, /device:TPU:16 now
where the time goes in v10:
time: 141 us
  starting transfers between devices  98.3 us (70%)
  waiting for transfers between devices  27.1 us (19%)
  Pallas kernels  10.9 us (8%)
  local copies, waits for them, and re-layouts  1.82 us (1%)
    ppermute x8, starting transfers between devices, flipped(): lax.ppermute(x, axis, [(i, i ^ bits) for i in range(lax.axis_size(axis))])  47 us
    ppermute x8, waiting for transfers between devices, flipped(): lax.ppermute(x, axis, [(i, i ^ bits) for i in range(lax.axis_size(axis))])  17.1 us
    ppermute x3, starting transfers between devices, from_group(): lax.ppermute(blocks[2], 'zl', SWAP)  12.1 us
    pallas_call x6, Pallas kernels, call(): pl.pallas_call(kernel, out_shape=shapes, in_specs=[pl.BlockSpec(memory_sp...  10.9 us
    ppermute x3, starting transfers between devices, from_group(): lax.ppermute(blocks[1], 'xl', SWAP)  9.27 us
    ppermute x3, starting transfers between devices, from_group(): lax.ppermute(blocks[3], ('zl', 'xl'), BOTH)  7.74 us
    all_to_all x1, starting transfers between devices, local(): terms = lax.all_to_all(term, 'y', 0, 0, tiled=True)  6.53 us
    ppermute x3, waiting for transfers between devices, from_group(): lax.ppermute(blocks[2], 'zl', SWAP)  4.98 us
  transfers between devices with their start and end apart: 23, of which 7 were waited for; matrix products, arithmetic and copies ran while one was open for 1% of the time, Pallas kernels for 5%

profile of v10, /device:TPU:16, one launch (start us, length us, event | category | flops | bytes accessed | tf_op | source)
XLA Modules:
  0.0 140.5 jit_solution(9212253687278859677)
XLA Ops:
  0.6 0.0 copy-start.3
  0.6 3.5 %collective-permute-start = (bf16[4,1024]{1,0:T(4,128)(2,1)}, bf16[4,1024]{1,0:T(4,128)(2,1)S(1)}, u32[]{:S(2)}, u32[]{:S(2)}) collective-permute-start(bf16[4,1024]{1,0:T(4,128)(2,1)} %bitcast.7), channel_id=1, source_target_pairs={{0,4},{4,0},{8,12},{12,8},{16,20},{20,16},{24,28},{28,24},{1,5},{5... | collective-permute-start | bytes 24584 | tf_op jit(solution)/shard_map/ppermute | solution.py:147
  4.1 0.7 stack.23.place_ref
  4.8 0.0 copy-start.2
  4.8 3.3 %shard_map.68 = (bf16[256,1280]{1,0:T(8,128)(2,1)}, bf16[128,1536]{1,0:T(8,128)(2,1)}, bf16[128,1536]{1,0:T(8,128)(2,1)}, bf16[128,1536]{1,0:T(8,128)(2,1)}) custom-call(s32[5]{0:T(128)} %stack.23.place_ref, s32[1,4]{1,0:T(1,128)} %counts_ref.1, s32[1,4]{1,0:T(1,128)} %offsets_ref.1, bf16[256,256]{1,0:T(8,128)(2,1)} %grad_ref.1, bf16[256,4096]{1,0:T(8,128)(2,1)} %inputs_ref.1), custom_call_target="tpu_custom_call" | custom-call | tf_op jit(solution)/shard_map/pallas_call | solution.py:128
  8.1 0.0 collective-permute-done
  8.1 0.0 copy-done.3
  8.1 3.4 %collective-permute-start.1 = (bf16[128,1536]{1,0:T(8,128)(2,1)}, bf16[128,1536]{1,0:T(8,128)(2,1)S(1)}, u32[]{:S(2)}, u32[]{:S(2)}) collective-permute-start(bf16[128,1536]{1,0:T(8,128)(2,1)} %get-tuple-element.45), channel_id=1, source_target_pairs={{0,32},{32,0},{1,33},{33,1},{2,34},{34,2},{3,35},{35,3},{4,36},{36... | collective-permute-start | bytes 1179656 | tf_op jit(solution)/shard_map/ppermute | solution.py:140
  11.5 4.3 %collective-permute-start.2 = (bf16[128,1536]{1,0:T(8,128)(2,1)}, bf16[128,1536]{1,0:T(8,128)(2,1)S(1)}, u32[]{:S(2)}, u32[]{:S(2)}) collective-permute-start(bf16[128,1536]{1,0:T(8,128)(2,1)} %get-tuple-element.46), channel_id=1, source_target_pairs={{0,64},{64,0},{1,65},{65,1},{2,66},{66,2},{3,67},{67,3},{4,68},{68... | collective-permute-start | bytes 1179656 | tf_op jit(solution)/shard_map/ppermute | solution.py:141
  15.8 1.9 %collective-permute-start.3 = (bf16[128,1536]{1,0:T(8,128)(2,1)}, bf16[128,1536]{1,0:T(8,128)(2,1)S(1)}, u32[]{:S(2)}, u32[]{:S(2)}) collective-permute-start(bf16[128,1536]{1,0:T(8,128)(2,1)} %get-tuple-element.47), channel_id=1, source_target_pairs={{0,96},{32,64},{64,32},{96,0},{1,97},{33,65},{65,33},{97,1},{2,98}... | collective-permute-start | bytes 1179656 | tf_op jit(solution)/shard_map/ppermute | solution.py:142
  17.8 3.4 %collective-permute-start.4 = (bf16[8,256]{1,0:T(8,128)(2,1)S(1)}, bf16[8,256]{1,0:T(8,128)(2,1)S(1)}, u32[]{:S(2)}, u32[]{:S(2)}) collective-permute-start(bf16[8,256]{1,0:T(8,128)(2,1)S(1)} %get-tuple-element.86), channel_id=1, source_target_pairs={{0,32},{32,0},{1,33},{33,1},{2,34},{34,2},{3,35},{35,3},{4,36},{36... | collective-permute-start | bytes 12296 | tf_op jit(solution)/shard_map/ppermute | solution.py:140
  21.2 3.9 %collective-permute-start.5 = (bf16[8,256]{1,0:T(8,128)(2,1)S(1)}, bf16[8,256]{1,0:T(8,128)(2,1)S(1)}, u32[]{:S(2)}, u32[]{:S(2)}) collective-permute-start(bf16[8,256]{1,0:T(8,128)(2,1)S(1)} %get-tuple-element.85), channel_id=1, source_target_pairs={{0,64},{64,0},{1,65},{65,1},{2,66},{66,2},{3,67},{67,3},{4,68},{68... | collective-permute-start | bytes 12296 | tf_op jit(solution)/shard_map/ppermute | solution.py:141
  25.1 0.0 collective-permute-done.4
  25.1 3.0 %collective-permute-start.6 = (bf16[8,256]{1,0:T(8,128)(2,1)S(1)}, bf16[8,256]{1,0:T(8,128)(2,1)S(1)}, u32[]{:S(2)}, u32[]{:S(2)}) collective-permute-start(bf16[8,256]{1,0:T(8,128)(2,1)S(1)} %get-tuple-element.84), channel_id=1, source_target_pairs={{0,96},{32,64},{64,32},{96,0},{1,97},{33,65},{65,33},{97,1},{2,98}... | collective-permute-start | bytes 12296 | tf_op jit(solution)/shard_map/ppermute | solution.py:142
  28.1 5.0 %collective-permute-done.5 = bf16[8,256]{1,0:T(8,128)(2,1)S(1)} collective-permute-done((bf16[8,256]{1,0:T(8,128)(2,1)S(1)}, bf16[8,256]{1,0:T(8,128)(2,1)S(1)}, u32[]{:S(2)}, u32[]{:S(2)}) %collective-permute-start.5) | collective-permute-done | bytes 4128 | tf_op jit(solution)/shard_map/ppermute | solution.py:141
  33.1 0.0 collective-permute-done.6
  33.1 0.0 collective-permute-done.1.refs_0_
  33.1 0.0 collective-permute-done.2.refs_1_
  33.1 0.0 collective-permute-done.3.refs_2_
  33.2 0.0 copy-done.2
  33.2 0.0 copy-start
  33.2 1.1 copy-done
  34.3 0.0 copy-start.1
  34.3 0.6 shard_map.69
  34.9 1.9 %collective-permute-start.7 = (bf16[384,1024]{1,0:T(8,128)(2,1)S(1)}, bf16[384,1024]{1,0:T(8,128)(2,1)S(1)}, u32[]{:S(2)}, u32[]{:S(2)}) collective-permute-start(bf16[384,1024]{1,0:T(8,128)(2,1)S(1)} %get-tuple-element.53), channel_id=1, source_target_pairs={{0,1},{1,0},{2,3},{3,2},{4,5},{5,4},{6,7},{7,6},{8,9},{9,8},{10,11... | collective-permute-start | bytes 2359304 | tf_op jit(solution)/shard_map/ppermute | solution.py:174
  36.9 10.9 %collective-permute-start.8 = (bf16[32,256]{1,0:T(8,128)(2,1)S(1)}, bf16[32,256]{1,0:T(8,128)(2,1)S(1)}, u32[]{:S(2)}, u32[]{:S(2)}) collective-permute-start(bf16[32,256]{1,0:T(8,128)(2,1)S(1)} %get-tuple-element.90), channel_id=1, source_target_pairs={{0,256},{128,384},{256,0},{384,128},{512,768},{640,896},{768,512},... | collective-permute-start | bytes 49160 | tf_op jit(solution)/shard_map/ppermute | solution.py:147
  47.8 13.9 %collective-permute-start.9 = (bf16[32,256]{1,0:T(8,128)(2,1)S(1)}, bf16[32,256]{1,0:T(8,128)(2,1)S(1)}, u32[]{:S(2)}, u32[]{:S(2)}) collective-permute-start(bf16[32,256]{1,0:T(8,128)(2,1)S(1)} %get-tuple-element.90), channel_id=1, source_target_pairs={{0,512},{128,640},{256,768},{384,896},{512,0},{640,128},{768,256},... | collective-permute-start | bytes 49160 | tf_op jit(solution)/shard_map/ppermute | solution.py:147
  61.7 1.9 %collective-permute-start.10 = (bf16[32,256]{1,0:T(8,128)(2,1)S(1)}, bf16[32,256]{1,0:T(8,128)(2,1)S(1)}, u32[]{:S(2)}, u32[]{:S(2)}) collective-permute-start(bf16[32,256]{1,0:T(8,128)(2,1)S(1)} %get-tuple-element.90), channel_id=1, source_target_pairs={{0,768},{128,896},{256,512},{384,640},{512,256},{640,384},{768,0},... | collective-permute-start | bytes 49160 | tf_op jit(solution)/shard_map/ppermute | solution.py:147
  63.6 0.0 collective-permute-done.8
  63.6 0.0 collective-permute-done.9
  63.7 7.6 %collective-permute-done.10 = bf16[32,256]{1,0:T(8,128)(2,1)S(1)} collective-permute-done((bf16[32,256]{1,0:T(8,128)(2,1)S(1)}, bf16[32,256]{1,0:T(8,128)(2,1)S(1)}, u32[]{:S(2)}, u32[]{:S(2)}) %collective-permute-start.10) | collective-permute-done | bytes 16416 | tf_op jit(solution)/shard_map/ppermute | solution.py:147
  71.3 0.0 collective-permute-done.7.refs_3_
  71.3 0.0 copy-done.1
  71.3 1.9 %shard_map.70 = bf16[8,128,256]{2,1,0:T(8,128)(2,1)} custom-call(bf16[256,1280]{1,0:T(8,128)(2,1)S(1)} %copy-done.1, bf16[128,1536]{1,0:T(8,128)(2,1)S(1)} %collective-permute-done.1.refs_0_, bf16[128,1536]{1,0:T(8,128)(2,1)S(1)} %collective-permute-done.2.refs_1_, bf16[128,1536]{1,0:T(8,128)(2,1)S(1)} %collective-permute-done.3.refs_2_, ...), custom_call_target="tpu_custom_call" | custom-call | tf_op jit(solution)/shard_map/pallas_call | solution.py:128
  73.2 6.5 %all-to-all-start = ((bf16[8,128,256]{2,1,0:T(8,128)(2,1)}), bf16[8,128,256]{2,1,0:T(8,128)(2,1)S(1)}, u32[]{:S(2)}, u32[]{:S(2)}) async-start(bf16[8,128,256]{2,1,0:T(8,128)(2,1)} %shard_map.70), calls=%async_computation | async-start | bytes 1048576 | tf_op jit(solution)/shard_map/all_to_all | solution.py:179
  79.8 4.9 %collective-permute-start.15 = (bf16[1024,256]{1,0:T(8,128)(2,1)S(1)}, bf16[1024,256]{1,0:T(8,128)(2,1)S(1)}, u32[]{:S(2)}, u32[]{:S(2)}) collective-permute-start(bf16[1024,256]{1,0:T(8,128)(2,1)S(1)} %get-tuple-element.62.own_ref), channel_id=1, source_target_pairs={{0,2},{2,0},{1,3},{3,1},{4,6},{6,4},{5,7},{7,5},{8,10},{10,8},{9,1... | collective-permute-start | bytes 1572872 | tf_op jit(solution)/shard_map/ppermute | solution.py:175
  84.7 4.6 %collective-permute-start.11 = (bf16[128,256]{1,0:T(8,128)(2,1)S(1)}, bf16[128,256]{1,0:T(8,128)(2,1)S(1)}, u32[]{:S(2)}, u32[]{:S(2)}) collective-permute-start(bf16[128,256]{1,0:T(8,128)(2,1)S(1)} %get-tuple-element.78), channel_id=1, source_target_pairs={{0,128},{128,0},{256,384},{384,256},{512,640},{640,512},{768,896},... | collective-permute-start | bytes 196616 | tf_op jit(solution)/shard_map/ppermute | solution.py:147
  89.3 2.5 %collective-permute-done.11 = bf16[128,256]{1,0:T(8,128)(2,1)S(1)} collective-permute-done((bf16[128,256]{1,0:T(8,128)(2,1)S(1)}, bf16[128,256]{1,0:T(8,128)(2,1)S(1)}, u32[]{:S(2)}, u32[]{:S(2)}) %collective-permute-start.11) | collective-permute-done | bytes 65568 | tf_op jit(solution)/shard_map/ppermute | solution.py:147
  91.8 1.9 %collective-permute-start.12 = (bf16[256,256]{1,0:T(8,128)(2,1)S(1)}, bf16[256,256]{1,0:T(8,128)(2,1)S(1)}, u32[]{:S(2)}, u32[]{:S(2)}) collective-permute-start(bf16[256,256]{1,0:T(8,128)(2,1)S(1)} %constant_dynamic-update-slice_fusion.11.refs_0_), channel_id=1, source_target_pairs={{0,8},{4,12},{8,0},{12,4},{16,24},{20,28},{24,16},{28,20},{1,9},{5... | collective-permute-start | bytes 393224 | tf_op jit(solution)/shard_map/ppermute | solution.py:147
  93.7 7.8 %collective-permute-start.13 = (bf16[256,256]{1,0:T(8,128)(2,1)S(1)}, bf16[256,256]{1,0:T(8,128)(2,1)S(1)}, u32[]{:S(2)}, u32[]{:S(2)}) collective-permute-start(bf16[256,256]{1,0:T(8,128)(2,1)S(1)} %constant_dynamic-update-slice_fusion.11.refs_0_), channel_id=1, source_target_pairs={{0,16},{4,20},{8,24},{12,28},{16,0},{20,4},{24,8},{28,12},{1,17},{... | collective-permute-start | bytes 393224 | tf_op jit(solution)/shard_map/ppermute | solution.py:147
  101.5 2.5 %collective-permute-start.14 = (bf16[256,256]{1,0:T(8,128)(2,1)S(1)}, bf16[256,256]{1,0:T(8,128)(2,1)S(1)}, u32[]{:S(2)}, u32[]{:S(2)}) collective-permute-start(bf16[256,256]{1,0:T(8,128)(2,1)S(1)} %constant_dynamic-update-slice_fusion.11.refs_0_), channel_id=1, source_target_pairs={{0,24},{4,28},{8,16},{12,20},{16,8},{20,12},{24,0},{28,4},{1,25},{... | collective-permute-start | bytes 393224 | tf_op jit(solution)/shard_map/ppermute | solution.py:147
  104.0 1.9 %collective-permute-start.16 = (bf16[1024,256]{1,0:T(8,128)(2,1)S(1)}, bf16[1024,256]{1,0:T(8,128)(2,1)S(1)}, u32[]{:S(2)}, u32[]{:S(2)}) collective-permute-start(bf16[1024,256]{1,0:T(8,128)(2,1)S(1)} %get-tuple-element.62.own_ref), channel_id=1, source_target_pairs={{0,1},{1,0},{2,3},{3,2},{4,5},{5,4},{6,7},{7,6},{8,9},{9,8},{10,11... | collective-permute-start | bytes 1572872 | tf_op jit(solution)/shard_map/ppermute | solution.py:176
  106.0 0.0 collective-permute-done.15.far_ref
  106.0 0.0 collective-permute-done.12.refs_1_
  106.0 1.5 %collective-permute-done.13.refs_2_ = bf16[256,256]{1,0:T(8,128)(2,1)S(1)} collective-permute-done((bf16[256,256]{1,0:T(8,128)(2,1)S(1)}, bf16[256,256]{1,0:T(8,128)(2,1)S(1)}, u32[]{:S(2)}, u32[]{:S(2)}) %collective-permute-start.13) | collective-permute-done | bytes 131104 | tf_op jit(solution)/shard_map/ppermute | solution.py:147
  107.5 5.4 %collective-permute-done.14.refs_3_ = bf16[256,256]{1,0:T(8,128)(2,1)S(1)} collective-permute-done((bf16[256,256]{1,0:T(8,128)(2,1)S(1)}, bf16[256,256]{1,0:T(8,128)(2,1)S(1)}, u32[]{:S(2)}, u32[]{:S(2)}) %collective-permute-start.14) | collective-permute-done | bytes 131104 | tf_op jit(solution)/shard_map/ppermute | solution.py:147
  113.0 0.0 all-to-all-done
  113.0 1.9 %collective-permute-start.17 = (bf16[1024,256]{1,0:T(8,128)(2,1)S(1)}, bf16[1024,256]{1,0:T(8,128)(2,1)S(1)}, u32[]{:S(2)}, u32[]{:S(2)}) collective-permute-start(bf16[1024,256]{1,0:T(8,128)(2,1)S(1)} %collective-permute-done.15.far_ref), channel_id=1, source_target_pairs={{0,1},{1,0},{2,3},{3,2},{4,5},{5,4},{6,7},{7,6},{8,9},{9,8},{10,11... | collective-permute-start | bytes 1572872 | tf_op jit(solution)/shard_map/ppermute | solution.py:184
  114.9 0.7 convert_reduce_fusion
  115.6 4.9 %all-to-all-start.1 = ((f32[8,16,256]{2,1,0:T(8,128)}), f32[8,16,256]{2,1,0:T(8,128)S(1)}, u32[]{:S(2)}, u32[]{:S(2)}) async-start(f32[8,16,256]{2,1,0:T(8,128)} %bitcast.6), calls=%async_computation.1 | async-start | bytes 262144 | tf_op jit(solution)/shard_map/all_to_all | solution.py:192
  120.5 0.0 collective-permute-done.16.core_ref
  120.5 0.0 collective-permute-done.17.both_ref
  120.6 2.9 %shard_map.71.scaled_ref = bf16[1024,1024]{1,0:T(8,128)(2,1)S(1)} custom-call(s32[5]{0:T(128)S(1)} %copy-done.2, bf16[1024,256]{1,0:T(8,128)(2,1)S(1)} %get-tuple-element.62.own_ref, bf16[1024,256]{1,0:T(8,128)(2,1)S(1)} %collective-permute-done.16.core_ref, bf16[1024,256]{1,0:T(8,128)(2,1)S(1)} %collective-permute-done.15.far_ref, ...), custom_call_target="tpu_custom_call" | custom-call | tf_op jit(solution)/shard_map/pallas_call | solution.py:128
  123.5 0.7 shard_map.72
  124.2 2.5 %collective-permute-start.18 = (bf16[256,256]{1,0:T(8,128)(2,1)S(1)}, bf16[256,256]{1,0:T(8,128)(2,1)S(1)}, u32[]{:S(2)}, u32[]{:S(2)}) collective-permute-start(bf16[256,256]{1,0:T(8,128)(2,1)S(1)} %get-tuple-element.70), channel_id=1, source_target_pairs={{0,32},{32,0},{1,33},{33,1},{2,34},{34,2},{3,35},{35,3},{4,36},{36... | collective-permute-start | bytes 393224 | tf_op jit(solution)/shard_map/ppermute | solution.py:140
  126.7 3.9 %collective-permute-start.19 = (bf16[256,256]{1,0:T(8,128)(2,1)S(1)}, bf16[256,256]{1,0:T(8,128)(2,1)S(1)}, u32[]{:S(2)}, u32[]{:S(2)}) collective-permute-start(bf16[256,256]{1,0:T(8,128)(2,1)S(1)} %get-tuple-element.71), channel_id=1, source_target_pairs={{0,64},{64,0},{1,65},{65,1},{2,66},{66,2},{3,67},{67,3},{4,68},{68... | collective-permute-start | bytes 393224 | tf_op jit(solution)/shard_map/ppermute | solution.py:141
  130.6 2.8 %collective-permute-start.20 = (bf16[256,256]{1,0:T(8,128)(2,1)S(1)}, bf16[256,256]{1,0:T(8,128)(2,1)S(1)}, u32[]{:S(2)}, u32[]{:S(2)}) collective-permute-start(bf16[256,256]{1,0:T(8,128)(2,1)S(1)} %get-tuple-element.72), channel_id=1, source_target_pairs={{0,96},{32,64},{64,32},{96,0},{1,97},{33,65},{65,33},{97,1},{2,98}... | collective-permute-start | bytes 393224 | tf_op jit(solution)/shard_map/ppermute | solution.py:142
  133.4 4.0 %all-to-all-done.1 = f32[8,16,256]{2,1,0:T(8,128)S(1)} async-done(((f32[8,16,256]{2,1,0:T(8,128)}), f32[8,16,256]{2,1,0:T(8,128)S(1)}, u32[]{:S(2)}, u32[]{:S(2)}) %all-to-all-start.1) | async-done | bytes 131104 | tf_op jit(solution)/shard_map/all_to_all | solution.py:192
  137.5 0.0 collective-permute-done.18.refs_1_
  137.5 0.0 collective-permute-done.19.refs_2_
  137.5 1.0 collective-permute-done.20.refs_3_
  138.5 0.6 broadcast_multiply_fusion
  139.1 1.4 shard_map.73
  (11 shorter events, 0.1 us)
Async XLA Ops:
  0.6 7.5 %copy-start.3 = (bf16[1024,4]{0,1:T(4,128)(2,1)S(1)}, bf16[1024,4]{0,1:T(4,128)(2,1)}, u32[]{:S(2)}) copy-start(bf16[1024,4]{0,1:T(4,128)(2,1)} %param.7) | copy-start | bytes 24580
  0.6 7.5 %collective-permute-start = (bf16[4,1024]{1,0:T(4,128)(2,1)}, bf16[4,1024]{1,0:T(4,128)(2,1)S(1)}, u32[]{:S(2)}, u32[]{:S(2)}) collective-permute-start(bf16[4,1024]{1,0:T(4,128)(2,1)} %bitcast.7), channel_id=1, source_target_pairs={{0,4},{4,0},{8,12},{12,8},{16,20},{20,16},{24,28},{28,24},{1,5},{5... | collective-permute-start | bytes 24584 | tf_op jit(solution)/shard_map/ppermute | solution.py:147
  4.8 28.3 %copy-start.2 = (s32[5]{0:T(128)S(1)}, s32[5]{0:T(128)}, u32[]{:S(2)}) copy-start(s32[5]{0:T(128)} %stack.23.place_ref) | copy-start | bytes 64
  8.1 25.0 %collective-permute-start.1 = (bf16[128,1536]{1,0:T(8,128)(2,1)}, bf16[128,1536]{1,0:T(8,128)(2,1)S(1)}, u32[]{:S(2)}, u32[]{:S(2)}) collective-permute-start(bf16[128,1536]{1,0:T(8,128)(2,1)} %get-tuple-element.45), channel_id=1, source_target_pairs={{0,32},{32,0},{1,33},{33,1},{2,34},{34,2},{3,35},{35,3},{4,36},{36... | collective-permute-start | bytes 1179656 | tf_op jit(solution)/shard_map/ppermute | solution.py:140
  11.5 21.6 %collective-permute-start.2 = (bf16[128,1536]{1,0:T(8,128)(2,1)}, bf16[128,1536]{1,0:T(8,128)(2,1)S(1)}, u32[]{:S(2)}, u32[]{:S(2)}) collective-permute-start(bf16[128,1536]{1,0:T(8,128)(2,1)} %get-tuple-element.46), channel_id=1, source_target_pairs={{0,64},{64,0},{1,65},{65,1},{2,66},{66,2},{3,67},{67,3},{4,68},{68... | collective-permute-start | bytes 1179656 | tf_op jit(solution)/shard_map/ppermute | solution.py:141
  15.8 17.3 %collective-permute-start.3 = (bf16[128,1536]{1,0:T(8,128)(2,1)}, bf16[128,1536]{1,0:T(8,128)(2,1)S(1)}, u32[]{:S(2)}, u32[]{:S(2)}) collective-permute-start(bf16[128,1536]{1,0:T(8,128)(2,1)} %get-tuple-element.47), channel_id=1, source_target_pairs={{0,96},{32,64},{64,32},{96,0},{1,97},{33,65},{65,33},{97,1},{2,98}... | collective-permute-start | bytes 1179656 | tf_op jit(solution)/shard_map/ppermute | solution.py:142
  17.8 7.3 %collective-permute-start.4 = (bf16[8,256]{1,0:T(8,128)(2,1)S(1)}, bf16[8,256]{1,0:T(8,128)(2,1)S(1)}, u32[]{:S(2)}, u32[]{:S(2)}) collective-permute-start(bf16[8,256]{1,0:T(8,128)(2,1)S(1)} %get-tuple-element.86), channel_id=1, source_target_pairs={{0,32},{32,0},{1,33},{33,1},{2,34},{34,2},{3,35},{35,3},{4,36},{36... | collective-permute-start | bytes 12296 | tf_op jit(solution)/shard_map/ppermute | solution.py:140
  21.2 12.0 %collective-permute-start.5 = (bf16[8,256]{1,0:T(8,128)(2,1)S(1)}, bf16[8,256]{1,0:T(8,128)(2,1)S(1)}, u32[]{:S(2)}, u32[]{:S(2)}) collective-permute-start(bf16[8,256]{1,0:T(8,128)(2,1)S(1)} %get-tuple-element.85), channel_id=1, source_target_pairs={{0,64},{64,0},{1,65},{65,1},{2,66},{66,2},{3,67},{67,3},{4,68},{68... | collective-permute-start | bytes 12296 | tf_op jit(solution)/shard_map/ppermute | solution.py:141
  25.1 8.0 %collective-permute-start.6 = (bf16[8,256]{1,0:T(8,128)(2,1)S(1)}, bf16[8,256]{1,0:T(8,128)(2,1)S(1)}, u32[]{:S(2)}, u32[]{:S(2)}) collective-permute-start(bf16[8,256]{1,0:T(8,128)(2,1)S(1)} %get-tuple-element.84), channel_id=1, source_target_pairs={{0,96},{32,64},{64,32},{96,0},{1,97},{33,65},{65,33},{97,1},{2,98}... | collective-permute-start | bytes 12296 | tf_op jit(solution)/shard_map/ppermute | solution.py:142
  33.2 1.1 copy-start
  34.3 37.0 %copy-start.1 = (bf16[256,1280]{1,0:T(8,128)(2,1)S(1)}, bf16[256,1280]{1,0:T(8,128)(2,1)}, u32[]{:S(2)}) copy-start(bf16[256,1280]{1,0:T(8,128)(2,1)} %get-tuple-element.49.own_ref) | copy-start | bytes 1966084
  34.9 36.4 %collective-permute-start.7 = (bf16[384,1024]{1,0:T(8,128)(2,1)S(1)}, bf16[384,1024]{1,0:T(8,128)(2,1)S(1)}, u32[]{:S(2)}, u32[]{:S(2)}) collective-permute-start(bf16[384,1024]{1,0:T(8,128)(2,1)S(1)} %get-tuple-element.53), channel_id=1, source_target_pairs={{0,1},{1,0},{2,3},{3,2},{4,5},{5,4},{6,7},{7,6},{8,9},{9,8},{10,11... | collective-permute-start | bytes 2359304 | tf_op jit(solution)/shard_map/ppermute | solution.py:174
  36.9 26.8 %collective-permute-start.8 = (bf16[32,256]{1,0:T(8,128)(2,1)S(1)}, bf16[32,256]{1,0:T(8,128)(2,1)S(1)}, u32[]{:S(2)}, u32[]{:S(2)}) collective-permute-start(bf16[32,256]{1,0:T(8,128)(2,1)S(1)} %get-tuple-element.90), channel_id=1, source_target_pairs={{0,256},{128,384},{256,0},{384,128},{512,768},{640,896},{768,512},... | collective-permute-start | bytes 49160 | tf_op jit(solution)/shard_map/ppermute | solution.py:147
  47.8 15.9 %collective-permute-start.9 = (bf16[32,256]{1,0:T(8,128)(2,1)S(1)}, bf16[32,256]{1,0:T(8,128)(2,1)S(1)}, u32[]{:S(2)}, u32[]{:S(2)}) collective-permute-start(bf16[32,256]{1,0:T(8,128)(2,1)S(1)} %get-tuple-element.90), channel_id=1, source_target_pairs={{0,512},{128,640},{256,768},{384,896},{512,0},{640,128},{768,256},... | collective-permute-start | bytes 49160 | tf_op jit(solution)/shard_map/ppermute | solution.py:147
  61.7 9.6 %collective-permute-start.10 = (bf16[32,256]{1,0:T(8,128)(2,1)S(1)}, bf16[32,256]{1,0:T(8,128)(2,1)S(1)}, u32[]{:S(2)}, u32[]{:S(2)}) collective-permute-start(bf16[32,256]{1,0:T(8,128)(2,1)S(1)} %get-tuple-element.90), channel_id=1, source_target_pairs={{0,768},{128,896},{256,512},{384,640},{512,256},{640,384},{768,0},... | collective-permute-start | bytes 49160 | tf_op jit(solution)/shard_map/ppermute | solution.py:147
  73.2 39.7 %all-to-all-start = ((bf16[8,128,256]{2,1,0:T(8,128)(2,1)}), bf16[8,128,256]{2,1,0:T(8,128)(2,1)S(1)}, u32[]{:S(2)}, u32[]{:S(2)}) async-start(bf16[8,128,256]{2,1,0:T(8,128)(2,1)} %shard_map.70), calls=%async_computation | async-start | bytes 1048576 | tf_op jit(solution)/shard_map/all_to_all | solution.py:179
  79.8 26.2 %collective-permute-start.15 = (bf16[1024,256]{1,0:T(8,128)(2,1)S(1)}, bf16[1024,256]{1,0:T(8,128)(2,1)S(1)}, u32[]{:S(2)}, u32[]{:S(2)}) collective-permute-start(bf16[1024,256]{1,0:T(8,128)(2,1)S(1)} %get-tuple-element.62.own_ref), channel_id=1, source_target_pairs={{0,2},{2,0},{1,3},{3,1},{4,6},{6,4},{5,7},{7,5},{8,10},{10,8},{9,1... | collective-permute-start | bytes 1572872 | tf_op jit(solution)/shard_map/ppermute | solution.py:175
  84.7 7.1 %collective-permute-start.11 = (bf16[128,256]{1,0:T(8,128)(2,1)S(1)}, bf16[128,256]{1,0:T(8,128)(2,1)S(1)}, u32[]{:S(2)}, u32[]{:S(2)}) collective-permute-start(bf16[128,256]{1,0:T(8,128)(2,1)S(1)} %get-tuple-element.78), channel_id=1, source_target_pairs={{0,128},{128,0},{256,384},{384,256},{512,640},{640,512},{768,896},... | collective-permute-start | bytes 196616 | tf_op jit(solution)/shard_map/ppermute | solution.py:147
  91.8 14.2 %collective-permute-start.12 = (bf16[256,256]{1,0:T(8,128)(2,1)S(1)}, bf16[256,256]{1,0:T(8,128)(2,1)S(1)}, u32[]{:S(2)}, u32[]{:S(2)}) collective-permute-start(bf16[256,256]{1,0:T(8,128)(2,1)S(1)} %constant_dynamic-update-slice_fusion.11.refs_0_), channel_id=1, source_target_pairs={{0,8},{4,12},{8,0},{12,4},{16,24},{20,28},{24,16},{28,20},{1,9},{5... | collective-permute-start | bytes 393224 | tf_op jit(solution)/shard_map/ppermute | solution.py:147
  93.7 13.8 %collective-permute-start.13 = (bf16[256,256]{1,0:T(8,128)(2,1)S(1)}, bf16[256,256]{1,0:T(8,128)(2,1)S(1)}, u32[]{:S(2)}, u32[]{:S(2)}) collective-permute-start(bf16[256,256]{1,0:T(8,128)(2,1)S(1)} %constant_dynamic-update-slice_fusion.11.refs_0_), channel_id=1, source_target_pairs={{0,16},{4,20},{8,24},{12,28},{16,0},{20,4},{24,8},{28,12},{1,17},{... | collective-permute-start | bytes 393224 | tf_op jit(solution)/shard_map/ppermute | solution.py:147
  101.5 11.4 %collective-permute-start.14 = (bf16[256,256]{1,0:T(8,128)(2,1)S(1)}, bf16[256,256]{1,0:T(8,128)(2,1)S(1)}, u32[]{:S(2)}, u32[]{:S(2)}) collective-permute-start(bf16[256,256]{1,0:T(8,128)(2,1)S(1)} %constant_dynamic-update-slice_fusion.11.refs_0_), channel_id=1, source_target_pairs={{0,24},{4,28},{8,16},{12,20},{16,8},{20,12},{24,0},{28,4},{1,25},{... | collective-permute-start | bytes 393224 | tf_op jit(solution)/shard_map/ppermute | solution.py:147
  104.0 16.5 %collective-permute-start.16 = (bf16[1024,256]{1,0:T(8,128)(2,1)S(1)}, bf16[1024,256]{1,0:T(8,128)(2,1)S(1)}, u32[]{:S(2)}, u32[]{:S(2)}) collective-permute-start(bf16[1024,256]{1,0:T(8,128)(2,1)S(1)} %get-tuple-element.62.own_ref), channel_id=1, source_target_pairs={{0,1},{1,0},{2,3},{3,2},{4,5},{5,4},{6,7},{7,6},{8,9},{9,8},{10,11... | collective-permute-start | bytes 1572872 | tf_op jit(solution)/shard_map/ppermute | solution.py:176
  113.0 7.6 %collective-permute-start.17 = (bf16[1024,256]{1,0:T(8,128)(2,1)S(1)}, bf16[1024,256]{1,0:T(8,128)(2,1)S(1)}, u32[]{:S(2)}, u32[]{:S(2)}) collective-permute-start(bf16[1024,256]{1,0:T(8,128)(2,1)S(1)} %collective-permute-done.15.far_ref), channel_id=1, source_target_pairs={{0,1},{1,0},{2,3},{3,2},{4,5},{5,4},{6,7},{7,6},{8,9},{9,8},{10,11... | collective-permute-start | bytes 1572872 | tf_op jit(solution)/shard_map/ppermute | solution.py:184
  115.6 21.9 %all-to-all-start.1 = ((f32[8,16,256]{2,1,0:T(8,128)}), f32[8,16,256]{2,1,0:T(8,128)S(1)}, u32[]{:S(2)}, u32[]{:S(2)}) async-start(f32[8,16,256]{2,1,0:T(8,128)} %bitcast.6), calls=%async_computation.1 | async-start | bytes 262144 | tf_op jit(solution)/shard_map/all_to_all | solution.py:192
  124.2 13.3 %collective-permute-start.18 = (bf16[256,256]{1,0:T(8,128)(2,1)S(1)}, bf16[256,256]{1,0:T(8,128)(2,1)S(1)}, u32[]{:S(2)}, u32[]{:S(2)}) collective-permute-start(bf16[256,256]{1,0:T(8,128)(2,1)S(1)} %get-tuple-element.70), channel_id=1, source_target_pairs={{0,32},{32,0},{1,33},{33,1},{2,34},{34,2},{3,35},{35,3},{4,36},{36... | collective-permute-start | bytes 393224 | tf_op jit(solution)/shard_map/ppermute | solution.py:140
  126.7 10.8 %collective-permute-start.19 = (bf16[256,256]{1,0:T(8,128)(2,1)S(1)}, bf16[256,256]{1,0:T(8,128)(2,1)S(1)}, u32[]{:S(2)}, u32[]{:S(2)}) collective-permute-start(bf16[256,256]{1,0:T(8,128)(2,1)S(1)} %get-tuple-element.71), channel_id=1, source_target_pairs={{0,64},{64,0},{1,65},{65,1},{2,66},{66,2},{3,67},{67,3},{4,68},{68... | collective-permute-start | bytes 393224 | tf_op jit(solution)/shard_map/ppermute | solution.py:141
  130.6 7.8 %collective-permute-start.20 = (bf16[256,256]{1,0:T(8,128)(2,1)S(1)}, bf16[256,256]{1,0:T(8,128)(2,1)S(1)}, u32[]{:S(2)}, u32[]{:S(2)}) collective-permute-start(bf16[256,256]{1,0:T(8,128)(2,1)S(1)} %get-tuple-element.72), channel_id=1, source_target_pairs={{0,96},{32,64},{64,32},{96,0},{1,97},{33,65},{65,33},{97,1},{2,98}... | collective-permute-start | bytes 393224 | tf_op jit(solution)/shard_map/ppermute | solution.py:142

commit v11 on v9

--- a/solution.py
+++ b/solution.py
@@ -159,13 +159,14 @@
     blocks = call(prep_kernel, sizes, 3, *args, vmem=60 * MIB)
     turned = value_weight.T
     pair = jnp.concatenate([turned, flipped(turned, 1, n_y)])
+    blocks, pair = lax.optimization_barrier((blocks, pair))
     received = from_group(blocks)
-    received[1], pair = lax.optimization_barrier((received[1], pair))
 
     mine = pair.reshape(2 * own_columns, 2, 2, narrow).transpose(2, 1, 0, 3)
     mine = jnp.broadcast_to(mine[:, None], (2, n_zh, 2, 2 * own_columns, narrow))
     mine = mine.reshape(-1, 2 * own_columns, narrow)
     block = lax.all_to_all(mine, ("xl", "zh", "zl"), 0, 0, tiled=True)
+    received, block = lax.optimization_barrier((received, block))
     block = block.reshape(-1, narrow)
 
     sizes = [(3 * rows // 2, wide), (4 * rows, columns)]

time: 133 us -> 130 us (0.977)
  waiting for transfers between devices: 38.9 us -> 34.4 us
  starting transfers between devices: 76.3 us -> 79.8 us
    all_to_all x1, waiting for transfers between devices: 14.3 us -> 0.01 us  [local(): block = lax.all_to_all(mine, ('xl', 'zh', 'zl'), 0, 0, tiled=True)]
    all_to_all x1, starting transfers between devices: 5.87 us -> 10 us  [local(): summed = lax.all_to_all(summed, 'zh', 0, 0, tiled=True)]
    ppermute x2, waiting for transfers between devices: 0.01 us -> 4.03 us  [from_group(): lax.ppermute(blocks[1], 'xl', SWAP)]
    ppermute x1, waiting for transfers between devices: 0.01 us -> 2.25 us  [local(): half = lax.ppermute(half, 'c', SWAP)]
    ppermute x4, waiting for transfers between devices: 9.48 us -> 11.6 us  [flipped(): return lax.ppermute(x, 'y', [(i, i ^ bits) for i in range(n)])]
    ppermute x2, waiting for transfers between devices: 2.03 us -> 4.05 us  [from_group(): lax.ppermute(blocks[2], 'zl', SWAP)]
  transfers between devices with their start and end apart: 17 -> 17, of which waited for: 8 -> 8; matrix products, arithmetic and copies ran while one was open for 1% -> 1% of each run, Pallas kernels for 4% -> 5%
where the time goes in v11:
time: 130 us
  starting transfers between devices  79.8 us (61%)
  waiting for transfers between devices  34.4 us (26%)
  Pallas kernels  10.8 us (8%)
  other arithmetic  1.96 us (2%)
  local copies, waits for them, and re-layouts  1.75 us (1%)
    all_to_all x1, starting transfers between devices, local(): block = lax.all_to_all(mine, ('xl', 'zh', 'zl'), 0, 0, tiled=True)  20.4 us
    ppermute x4, starting transfers between devices, flipped(): return lax.ppermute(x, 'y', [(i, i ^ bits) for i in range(n)])  15.7 us
    ppermute x4, waiting for transfers between devices, flipped(): return lax.ppermute(x, 'y', [(i, i ^ bits) for i in range(n)])  11.6 us
    pallas_call x6, Pallas kernels, call(): pl.pallas_call(kernel, out_shape=shapes, in_specs=[pl.BlockSpec(memory_sp...  10.8 us
    all_to_all x1, starting transfers between devices, local(): summed = lax.all_to_all(summed, 'zh', 0, 0, tiled=True)  10 us
    ppermute x2, waiting for transfers between devices, from_group(): lax.ppermute(blocks[3], ('zl', 'xl'), BOTH)  8.92 us
    ppermute x2, starting transfers between devices, from_group(): lax.ppermute(blocks[2], 'zl', SWAP)  7.06 us
    ppermute x2, starting transfers between devices, from_group(): lax.ppermute(blocks[3], ('zl', 'xl'), BOTH)  6.52 us
  transfers between devices with their start and end apart: 17, of which 8 were waited for; matrix products, arithmetic and copies ran while one was open for 1% of the time, Pallas kernels for 5%

profile of v11, /device:TPU:6, one launch (start us, length us, event | category | flops | bytes accessed | tf_op | source)
XLA Modules:
  0.0 129.6 jit_solution(11475881932427228579)
XLA Ops:
  0.6 0.0 copy-start.3
  0.6 3.5 %collective-permute-start = (bf16[4,1024]{1,0:T(4,128)(2,1)}, bf16[4,1024]{1,0:T(4,128)(2,1)S(1)}, u32[]{:S(2)}, u32[]{:S(2)}) collective-permute-start(bf16[4,1024]{1,0:T(4,128)(2,1)} %bitcast.16), channel_id=1, source_target_pairs={{0,4},{4,0},{8,12},{12,8},{16,20},{20,16},{24,28},{28,24},{1,5},{5... | collective-permute-start | bytes 24584 | tf_op jit(solution)/shard_map/ppermute | solution.py:145
  4.1 0.6 pad_add_fusion.place_ref
  4.7 0.0 copy-start.2
  4.7 3.3 %shard_map.68 = (bf16[256,1280]{1,0:T(8,128)(2,1)}, bf16[128,1536]{1,0:T(8,128)(2,1)}, bf16[128,1536]{1,0:T(8,128)(2,1)}, bf16[128,1536]{1,0:T(8,128)(2,1)}) custom-call(s32[4]{0:T(128)} %pad_add_fusion.place_ref, s32[1,4]{1,0:T(1,128)} %counts_ref.1, s32[1,4]{1,0:T(1,128)} %offsets_ref.1, bf16[256,256]{1,0:T(8,128)(2,1)} %grad_ref.1, ...), custom_call_target="tpu_custom_call" | custom-call | tf_op jit(solution)/shard_map/pallas_call | solution.py:126
  8.0 0.0 collective-permute-done
  8.0 0.0 copy-done.3
  8.1 0.7 broadcast_in_dim.2
  8.7 20.4 %all-to-all-start = ((bf16[32,8,256]{2,1,0:T(8,128)(2,1)}), bf16[32,8,256]{2,1,0:T(8,128)(2,1)S(1)}, u32[]{:S(2)}, u32[]{:S(2)}) async-start(bf16[32,8,256]{2,1,0:T(8,128)(2,1)} %bitcast.7), calls=%async_computation | async-start | bytes 262144 | tf_op jit(solution)/shard_map/all_to_all | solution.py:168
  29.1 2.1 %collective-permute-start.1 = (bf16[128,1536]{1,0:T(8,128)(2,1)}, bf16[128,1536]{1,0:T(8,128)(2,1)S(1)}, u32[]{:S(2)}, u32[]{:S(2)}) collective-permute-start(bf16[128,1536]{1,0:T(8,128)(2,1)} %get-tuple-element.38), channel_id=1, source_target_pairs={{0,32},{32,0},{1,33},{33,1},{2,34},{34,2},{3,35},{35,3},{4,36},{36... | collective-permute-start | bytes 1179656 | tf_op jit(solution)/shard_map/ppermute | solution.py:138
  31.2 3.7 %collective-permute-start.2 = (bf16[128,1536]{1,0:T(8,128)(2,1)}, bf16[128,1536]{1,0:T(8,128)(2,1)S(1)}, u32[]{:S(2)}, u32[]{:S(2)}) collective-permute-start(bf16[128,1536]{1,0:T(8,128)(2,1)} %get-tuple-element.39), channel_id=1, source_target_pairs={{0,64},{64,0},{1,65},{65,1},{2,66},{66,2},{3,67},{67,3},{4,68},{68... | collective-permute-start | bytes 1179656 | tf_op jit(solution)/shard_map/ppermute | solution.py:139
  35.0 3.4 %collective-permute-start.3 = (bf16[128,1536]{1,0:T(8,128)(2,1)}, bf16[128,1536]{1,0:T(8,128)(2,1)S(1)}, u32[]{:S(2)}, u32[]{:S(2)}) collective-permute-start(bf16[128,1536]{1,0:T(8,128)(2,1)} %get-tuple-element.40), channel_id=1, source_target_pairs={{0,96},{32,64},{64,32},{96,0},{1,97},{33,65},{65,33},{97,1},{2,98}... | collective-permute-start | bytes 1179656 | tf_op jit(solution)/shard_map/ppermute | solution.py:140
  38.3 4.0 %collective-permute-done.1.refs_0_ = bf16[128,1536]{1,0:T(8,128)(2,1)S(1)} collective-permute-done((bf16[128,1536]{1,0:T(8,128)(2,1)}, bf16[128,1536]{1,0:T(8,128)(2,1)S(1)}, u32[]{:S(2)}, u32[]{:S(2)}) %collective-permute-start.1) | collective-permute-done | bytes 393248 | tf_op jit(solution)/shard_map/ppermute | solution.py:138
  42.4 4.1 %collective-permute-done.2.refs_1_ = bf16[128,1536]{1,0:T(8,128)(2,1)S(1)} collective-permute-done((bf16[128,1536]{1,0:T(8,128)(2,1)}, bf16[128,1536]{1,0:T(8,128)(2,1)S(1)}, u32[]{:S(2)}, u32[]{:S(2)}) %collective-permute-start.2) | collective-permute-done | bytes 393248 | tf_op jit(solution)/shard_map/ppermute | solution.py:139
  46.4 7.8 %collective-permute-done.3.refs_2_ = bf16[128,1536]{1,0:T(8,128)(2,1)S(1)} collective-permute-done((bf16[128,1536]{1,0:T(8,128)(2,1)}, bf16[128,1536]{1,0:T(8,128)(2,1)S(1)}, u32[]{:S(2)}, u32[]{:S(2)}) %collective-permute-start.3) | collective-permute-done | bytes 393248 | tf_op jit(solution)/shard_map/ppermute | solution.py:140
  54.2 0.0 all-to-all-done
  54.2 0.0 copy-done.2
  54.2 0.0 copy-start
  54.3 1.1 copy-done
  55.3 0.0 copy-start.1
  55.3 0.6 shard_map.69
  56.0 1.9 %collective-permute-start.4 = (bf16[384,1024]{1,0:T(8,128)(2,1)S(1)}, bf16[384,1024]{1,0:T(8,128)(2,1)S(1)}, u32[]{:S(2)}, u32[]{:S(2)}) collective-permute-start(bf16[384,1024]{1,0:T(8,128)(2,1)S(1)} %get-tuple-element.46), channel_id=1, source_target_pairs={{0,1},{1,0},{2,3},{3,2},{4,5},{5,4},{6,7},{7,6},{8,9},{9,8},{10,11... | collective-permute-start | bytes 2359304 | tf_op jit(solution)/shard_map/ppermute | solution.py:174
  57.9 2.3 %collective-permute-done.4.refs_3_ = bf16[384,1024]{1,0:T(8,128)(2,1)S(1)} collective-permute-done((bf16[384,1024]{1,0:T(8,128)(2,1)S(1)}, bf16[384,1024]{1,0:T(8,128)(2,1)S(1)}, u32[]{:S(2)}, u32[]{:S(2)}) %collective-permute-start.4) | collective-permute-done | bytes 786464 | tf_op jit(solution)/shard_map/ppermute | solution.py:174
  60.1 0.0 copy-done.1
  60.2 1.9 %shard_map.70 = bf16[8,128,256]{2,1,0:T(8,128)(2,1)} custom-call(bf16[256,1280]{1,0:T(8,128)(2,1)S(1)} %copy-done.1, bf16[128,1536]{1,0:T(8,128)(2,1)S(1)} %collective-permute-done.1.refs_0_, bf16[128,1536]{1,0:T(8,128)(2,1)S(1)} %collective-permute-done.2.refs_1_, bf16[128,1536]{1,0:T(8,128)(2,1)S(1)} %collective-permute-done.3.refs_2_, ...), custom_call_target="tpu_custom_call" | custom-call | tf_op jit(solution)/shard_map/pallas_call | solution.py:126
  62.1 6.2 %all-to-all-start.1 = ((bf16[8,128,256]{2,1,0:T(8,128)(2,1)}), bf16[8,128,256]{2,1,0:T(8,128)(2,1)S(1)}, u32[]{:S(2)}, u32[]{:S(2)}) async-start(bf16[8,128,256]{2,1,0:T(8,128)(2,1)} %shard_map.70), calls=%async_computation.1 | async-start | bytes 1048576 | tf_op jit(solution)/shard_map/all_to_all | solution.py:178
  68.3 3.3 %collective-permute-start.8 = (bf16[1024,256]{1,0:T(8,128)(2,1)S(1)}, bf16[1024,256]{1,0:T(8,128)(2,1)S(1)}, u32[]{:S(2)}, u32[]{:S(2)}) collective-permute-start(bf16[1024,256]{1,0:T(8,128)(2,1)S(1)} %get-tuple-element.48.own_ref), channel_id=1, source_target_pairs={{0,2},{2,0},{1,3},{3,1},{4,6},{6,4},{5,7},{7,5},{8,10},{10,8},{9,1... | collective-permute-start | bytes 1572872 | tf_op jit(solution)/shard_map/ppermute | solution.py:175
  71.6 4.8 %collective-permute-start.5 = (bf16[256,256]{1,0:T(8,128)(2,1)S(1)}, bf16[256,256]{1,0:T(8,128)(2,1)S(1)}, u32[]{:S(2)}, u32[]{:S(2)}) collective-permute-start(bf16[256,256]{1,0:T(8,128)(2,1)S(1)} %bitcast.11), channel_id=1, source_target_pairs={{0,8},{4,12},{8,0},{12,4},{16,24},{20,28},{24,16},{28,20},{1,9},{5... | collective-permute-start | bytes 393224 | tf_op jit(solution)/shard_map/ppermute | solution.py:145
  76.4 5.5 %collective-permute-start.6 = (bf16[256,256]{1,0:T(8,128)(2,1)S(1)}, bf16[256,256]{1,0:T(8,128)(2,1)S(1)}, u32[]{:S(2)}, u32[]{:S(2)}) collective-permute-start(bf16[256,256]{1,0:T(8,128)(2,1)S(1)} %bitcast.12), channel_id=1, source_target_pairs={{0,16},{4,20},{8,24},{12,28},{16,0},{20,4},{24,8},{28,12},{1,17},{... | collective-permute-start | bytes 393224 | tf_op jit(solution)/shard_map/ppermute | solution.py:145
  81.9 1.9 %collective-permute-start.7 = (bf16[256,256]{1,0:T(8,128)(2,1)S(1)}, bf16[256,256]{1,0:T(8,128)(2,1)S(1)}, u32[]{:S(2)}, u32[]{:S(2)}) collective-permute-start(bf16[256,256]{1,0:T(8,128)(2,1)S(1)} %bitcast.13), channel_id=1, source_target_pairs={{0,24},{4,28},{8,16},{12,20},{16,8},{20,12},{24,0},{28,4},{1,25},{... | collective-permute-start | bytes 393224 | tf_op jit(solution)/shard_map/ppermute | solution.py:145
  83.9 1.9 %collective-permute-start.9 = (bf16[1024,256]{1,0:T(8,128)(2,1)S(1)}, bf16[1024,256]{1,0:T(8,128)(2,1)S(1)}, u32[]{:S(2)}, u32[]{:S(2)}) collective-permute-start(bf16[1024,256]{1,0:T(8,128)(2,1)S(1)} %get-tuple-element.48.own_ref), channel_id=1, source_target_pairs={{0,1},{1,0},{2,3},{3,2},{4,5},{5,4},{6,7},{7,6},{8,9},{9,8},{10,11... | collective-permute-start | bytes 1572872 | tf_op jit(solution)/shard_map/ppermute | solution.py:176
  85.8 8.5 %collective-permute-done.5.refs_1_ = bf16[256,256]{1,0:T(8,128)(2,1)S(1)} collective-permute-done((bf16[256,256]{1,0:T(8,128)(2,1)S(1)}, bf16[256,256]{1,0:T(8,128)(2,1)S(1)}, u32[]{:S(2)}, u32[]{:S(2)}) %collective-permute-start.5) | collective-permute-done | bytes 131104 | tf_op jit(solution)/shard_map/ppermute | solution.py:145
  94.3 3.1 %collective-permute-done.6.refs_2_ = bf16[256,256]{1,0:T(8,128)(2,1)S(1)} collective-permute-done((bf16[256,256]{1,0:T(8,128)(2,1)S(1)}, bf16[256,256]{1,0:T(8,128)(2,1)S(1)}, u32[]{:S(2)}, u32[]{:S(2)}) %collective-permute-start.6) | collective-permute-done | bytes 131104 | tf_op jit(solution)/shard_map/ppermute | solution.py:145
  97.4 0.0 collective-permute-done.7.refs_3_
  97.4 0.0 collective-permute-done.8.far_ref
  97.4 0.0 all-to-all-done.1
  97.4 1.9 %collective-permute-start.10 = (bf16[1024,256]{1,0:T(8,128)(2,1)S(1)}, bf16[1024,256]{1,0:T(8,128)(2,1)S(1)}, u32[]{:S(2)}, u32[]{:S(2)}) collective-permute-start(bf16[1024,256]{1,0:T(8,128)(2,1)S(1)} %collective-permute-done.8.far_ref), channel_id=1, source_target_pairs={{0,1},{1,0},{2,3},{3,2},{4,5},{5,4},{6,7},{7,6},{8,9},{9,8},{10,11... | collective-permute-start | bytes 1572872 | tf_op jit(solution)/shard_map/ppermute | solution.py:181
  99.3 0.7 convert_reduce_fusion
  100.0 10.0 %all-to-all-start.2 = ((f32[8,16,256]{2,1,0:T(8,128)}), f32[8,16,256]{2,1,0:T(8,128)S(1)}, u32[]{:S(2)}, u32[]{:S(2)}) async-start(f32[8,16,256]{2,1,0:T(8,128)} %bitcast.9), calls=%async_computation.2 | async-start | bytes 262144 | tf_op jit(solution)/shard_map/all_to_all | solution.py:189
  110.0 0.0 collective-permute-done.9.core_ref
  110.0 0.0 collective-permute-done.10.both_ref
  110.1 2.9 %shard_map.71.scaled_ref = bf16[1024,1024]{1,0:T(8,128)(2,1)S(1)} custom-call(s32[4]{0:T(128)S(1)} %copy-done.2, bf16[1024,256]{1,0:T(8,128)(2,1)S(1)} %get-tuple-element.48.own_ref, bf16[1024,256]{1,0:T(8,128)(2,1)S(1)} %collective-permute-done.9.core_ref, bf16[1024,256]{1,0:T(8,128)(2,1)S(1)} %collective-permute-done.8.far_ref, ...), custom_call_target="tpu_custom_call" | custom-call | tf_op jit(solution)/shard_map/pallas_call | solution.py:126
  113.0 0.7 shard_map.72
  113.7 2.7 %collective-permute-start.11 = (bf16[256,256]{1,0:T(8,128)(2,1)S(1)}, bf16[256,256]{1,0:T(8,128)(2,1)S(1)}, u32[]{:S(2)}, u32[]{:S(2)}) collective-permute-start(bf16[256,256]{1,0:T(8,128)(2,1)S(1)} %get-tuple-element.56), channel_id=1, source_target_pairs={{0,32},{32,0},{1,33},{33,1},{2,34},{34,2},{3,35},{35,3},{4,36},{36... | collective-permute-start | bytes 393224 | tf_op jit(solution)/shard_map/ppermute | solution.py:138
  116.4 3.4 %collective-permute-start.12 = (bf16[256,256]{1,0:T(8,128)(2,1)S(1)}, bf16[256,256]{1,0:T(8,128)(2,1)S(1)}, u32[]{:S(2)}, u32[]{:S(2)}) collective-permute-start(bf16[256,256]{1,0:T(8,128)(2,1)S(1)} %get-tuple-element.57), channel_id=1, source_target_pairs={{0,64},{64,0},{1,65},{65,1},{2,66},{66,2},{3,67},{67,3},{4,68},{68... | collective-permute-start | bytes 393224 | tf_op jit(solution)/shard_map/ppermute | solution.py:139
  119.8 3.1 %collective-permute-start.13 = (bf16[256,256]{1,0:T(8,128)(2,1)S(1)}, bf16[256,256]{1,0:T(8,128)(2,1)S(1)}, u32[]{:S(2)}, u32[]{:S(2)}) collective-permute-start(bf16[256,256]{1,0:T(8,128)(2,1)S(1)} %get-tuple-element.58), channel_id=1, source_target_pairs={{0,96},{32,64},{64,32},{96,0},{1,97},{33,65},{65,33},{97,1},{2,98}... | collective-permute-start | bytes 393224 | tf_op jit(solution)/shard_map/ppermute | solution.py:140
  122.9 3.6 %all-to-all-done.2 = f32[8,16,256]{2,1,0:T(8,128)S(1)} async-done(((f32[8,16,256]{2,1,0:T(8,128)}), f32[8,16,256]{2,1,0:T(8,128)S(1)}, u32[]{:S(2)}, u32[]{:S(2)}) %all-to-all-start.2) | async-done | bytes 131104 | tf_op jit(solution)/shard_map/all_to_all | solution.py:189
  126.5 0.0 collective-permute-done.11.refs_1_
  126.5 0.0 collective-permute-done.12.refs_2_
  126.5 1.1 collective-permute-done.13.refs_3_
  127.6 0.6 broadcast_multiply_fusion
  128.2 1.4 %shard_map.73 = bf16[256,1024]{1,0:T(8,128)(2,1)} custom-call(s32[4]{0:T(128)S(1)} %copy-done.2, bf16[256,256]{1,0:T(8,128)(2,1)S(1)} %get-tuple-element.59.refs_0_, bf16[256,256]{1,0:T(8,128)(2,1)S(1)} %collective-permute-done.11.refs_1_, bf16[256,256]{1,0:T(8,128)(2,1)S(1)} %collective-permute-done.12.refs_2_, ...), custom_call_target="tpu_custom_call" | custom-call | tf_op jit(solution)/shard_map/pallas_call | solution.py:126
  (3 shorter events, 0.0 us)
Async XLA Ops:
  0.6 7.4 %copy-start.3 = (bf16[1024,4]{0,1:T(4,128)(2,1)S(1)}, bf16[1024,4]{0,1:T(4,128)(2,1)}, u32[]{:S(2)}) copy-start(bf16[1024,4]{0,1:T(4,128)(2,1)} %param.7) | copy-start | bytes 24580
  0.6 7.4 %collective-permute-start = (bf16[4,1024]{1,0:T(4,128)(2,1)}, bf16[4,1024]{1,0:T(4,128)(2,1)S(1)}, u32[]{:S(2)}, u32[]{:S(2)}) collective-permute-start(bf16[4,1024]{1,0:T(4,128)(2,1)} %bitcast.16), channel_id=1, source_target_pairs={{0,4},{4,0},{8,12},{12,8},{16,20},{20,16},{24,28},{28,24},{1,5},{5... | collective-permute-start | bytes 24584 | tf_op jit(solution)/shard_map/ppermute | solution.py:145
  4.7 49.5 %copy-start.2 = (s32[4]{0:T(128)S(1)}, s32[4]{0:T(128)}, u32[]{:S(2)}) copy-start(s32[4]{0:T(128)} %pad_add_fusion.place_ref) | copy-start | bytes 52
  8.7 45.5 %all-to-all-start = ((bf16[32,8,256]{2,1,0:T(8,128)(2,1)}), bf16[32,8,256]{2,1,0:T(8,128)(2,1)S(1)}, u32[]{:S(2)}, u32[]{:S(2)}) async-start(bf16[32,8,256]{2,1,0:T(8,128)(2,1)} %bitcast.7), calls=%async_computation | async-start | bytes 262144 | tf_op jit(solution)/shard_map/all_to_all | solution.py:168
  29.1 13.3 %collective-permute-start.1 = (bf16[128,1536]{1,0:T(8,128)(2,1)}, bf16[128,1536]{1,0:T(8,128)(2,1)S(1)}, u32[]{:S(2)}, u32[]{:S(2)}) collective-permute-start(bf16[128,1536]{1,0:T(8,128)(2,1)} %get-tuple-element.38), channel_id=1, source_target_pairs={{0,32},{32,0},{1,33},{33,1},{2,34},{34,2},{3,35},{35,3},{4,36},{36... | collective-permute-start | bytes 1179656 | tf_op jit(solution)/shard_map/ppermute | solution.py:138
  31.2 15.2 %collective-permute-start.2 = (bf16[128,1536]{1,0:T(8,128)(2,1)}, bf16[128,1536]{1,0:T(8,128)(2,1)S(1)}, u32[]{:S(2)}, u32[]{:S(2)}) collective-permute-start(bf16[128,1536]{1,0:T(8,128)(2,1)} %get-tuple-element.39), channel_id=1, source_target_pairs={{0,64},{64,0},{1,65},{65,1},{2,66},{66,2},{3,67},{67,3},{4,68},{68... | collective-permute-start | bytes 1179656 | tf_op jit(solution)/shard_map/ppermute | solution.py:139
  35.0 19.3 %collective-permute-start.3 = (bf16[128,1536]{1,0:T(8,128)(2,1)}, bf16[128,1536]{1,0:T(8,128)(2,1)S(1)}, u32[]{:S(2)}, u32[]{:S(2)}) collective-permute-start(bf16[128,1536]{1,0:T(8,128)(2,1)} %get-tuple-element.40), channel_id=1, source_target_pairs={{0,96},{32,64},{64,32},{96,0},{1,97},{33,65},{65,33},{97,1},{2,98}... | collective-permute-start | bytes 1179656 | tf_op jit(solution)/shard_map/ppermute | solution.py:140
  54.2 1.1 copy-start
  55.3 4.8 %copy-start.1 = (bf16[256,1280]{1,0:T(8,128)(2,1)S(1)}, bf16[256,1280]{1,0:T(8,128)(2,1)}, u32[]{:S(2)}) copy-start(bf16[256,1280]{1,0:T(8,128)(2,1)} %get-tuple-element.42.own_ref) | copy-start | bytes 1966084
  56.0 4.2 %collective-permute-start.4 = (bf16[384,1024]{1,0:T(8,128)(2,1)S(1)}, bf16[384,1024]{1,0:T(8,128)(2,1)S(1)}, u32[]{:S(2)}, u32[]{:S(2)}) collective-permute-start(bf16[384,1024]{1,0:T(8,128)(2,1)S(1)} %get-tuple-element.46), channel_id=1, source_target_pairs={{0,1},{1,0},{2,3},{3,2},{4,5},{5,4},{6,7},{7,6},{8,9},{9,8},{10,11... | collective-permute-start | bytes 2359304 | tf_op jit(solution)/shard_map/ppermute | solution.py:174
  62.1 35.3 %all-to-all-start.1 = ((bf16[8,128,256]{2,1,0:T(8,128)(2,1)}), bf16[8,128,256]{2,1,0:T(8,128)(2,1)S(1)}, u32[]{:S(2)}, u32[]{:S(2)}) async-start(bf16[8,128,256]{2,1,0:T(8,128)(2,1)} %shard_map.70), calls=%async_computation.1 | async-start | bytes 1048576 | tf_op jit(solution)/shard_map/all_to_all | solution.py:178
  68.3 29.1 %collective-permute-start.8 = (bf16[1024,256]{1,0:T(8,128)(2,1)S(1)}, bf16[1024,256]{1,0:T(8,128)(2,1)S(1)}, u32[]{:S(2)}, u32[]{:S(2)}) collective-permute-start(bf16[1024,256]{1,0:T(8,128)(2,1)S(1)} %get-tuple-element.48.own_ref), channel_id=1, source_target_pairs={{0,2},{2,0},{1,3},{3,1},{4,6},{6,4},{5,7},{7,5},{8,10},{10,8},{9,1... | collective-permute-start | bytes 1572872 | tf_op jit(solution)/shard_map/ppermute | solution.py:175
  71.6 22.7 %collective-permute-start.5 = (bf16[256,256]{1,0:T(8,128)(2,1)S(1)}, bf16[256,256]{1,0:T(8,128)(2,1)S(1)}, u32[]{:S(2)}, u32[]{:S(2)}) collective-permute-start(bf16[256,256]{1,0:T(8,128)(2,1)S(1)} %bitcast.11), channel_id=1, source_target_pairs={{0,8},{4,12},{8,0},{12,4},{16,24},{20,28},{24,16},{28,20},{1,9},{5... | collective-permute-start | bytes 393224 | tf_op jit(solution)/shard_map/ppermute | solution.py:145
  76.4 20.9 %collective-permute-start.6 = (bf16[256,256]{1,0:T(8,128)(2,1)S(1)}, bf16[256,256]{1,0:T(8,128)(2,1)S(1)}, u32[]{:S(2)}, u32[]{:S(2)}) collective-permute-start(bf16[256,256]{1,0:T(8,128)(2,1)S(1)} %bitcast.12), channel_id=1, source_target_pairs={{0,16},{4,20},{8,24},{12,28},{16,0},{20,4},{24,8},{28,12},{1,17},{... | collective-permute-start | bytes 393224 | tf_op jit(solution)/shard_map/ppermute | solution.py:145
  81.9 15.4 %collective-permute-start.7 = (bf16[256,256]{1,0:T(8,128)(2,1)S(1)}, bf16[256,256]{1,0:T(8,128)(2,1)S(1)}, u32[]{:S(2)}, u32[]{:S(2)}) collective-permute-start(bf16[256,256]{1,0:T(8,128)(2,1)S(1)} %bitcast.13), channel_id=1, source_target_pairs={{0,24},{4,28},{8,16},{12,20},{16,8},{20,12},{24,0},{28,4},{1,25},{... | collective-permute-start | bytes 393224 | tf_op jit(solution)/shard_map/ppermute | solution.py:145
  83.9 26.2 %collective-permute-start.9 = (bf16[1024,256]{1,0:T(8,128)(2,1)S(1)}, bf16[1024,256]{1,0:T(8,128)(2,1)S(1)}, u32[]{:S(2)}, u32[]{:S(2)}) collective-permute-start(bf16[1024,256]{1,0:T(8,128)(2,1)S(1)} %get-tuple-element.48.own_ref), channel_id=1, source_target_pairs={{0,1},{1,0},{2,3},{3,2},{4,5},{5,4},{6,7},{7,6},{8,9},{9,8},{10,11... | collective-permute-start | bytes 1572872 | tf_op jit(solution)/shard_map/ppermute | solution.py:176
  97.4 12.7 %collective-permute-start.10 = (bf16[1024,256]{1,0:T(8,128)(2,1)S(1)}, bf16[1024,256]{1,0:T(8,128)(2,1)S(1)}, u32[]{:S(2)}, u32[]{:S(2)}) collective-permute-start(bf16[1024,256]{1,0:T(8,128)(2,1)S(1)} %collective-permute-done.8.far_ref), channel_id=1, source_target_pairs={{0,1},{1,0},{2,3},{3,2},{4,5},{5,4},{6,7},{7,6},{8,9},{9,8},{10,11... | collective-permute-start | bytes 1572872 | tf_op jit(solution)/shard_map/ppermute | solution.py:181
  100.0 26.5 %all-to-all-start.2 = ((f32[8,16,256]{2,1,0:T(8,128)}), f32[8,16,256]{2,1,0:T(8,128)S(1)}, u32[]{:S(2)}, u32[]{:S(2)}) async-start(f32[8,16,256]{2,1,0:T(8,128)} %bitcast.9), calls=%async_computation.2 | async-start | bytes 262144 | tf_op jit(solution)/shard_map/all_to_all | solution.py:189
  113.7 12.8 %collective-permute-start.11 = (bf16[256,256]{1,0:T(8,128)(2,1)S(1)}, bf16[256,256]{1,0:T(8,128)(2,1)S(1)}, u32[]{:S(2)}, u32[]{:S(2)}) collective-permute-start(bf16[256,256]{1,0:T(8,128)(2,1)S(1)} %get-tuple-element.56), channel_id=1, source_target_pairs={{0,32},{32,0},{1,33},{33,1},{2,34},{34,2},{3,35},{35,3},{4,36},{36... | collective-permute-start | bytes 393224 | tf_op jit(solution)/shard_map/ppermute | solution.py:138
  116.4 10.1 %collective-permute-start.12 = (bf16[256,256]{1,0:T(8,128)(2,1)S(1)}, bf16[256,256]{1,0:T(8,128)(2,1)S(1)}, u32[]{:S(2)}, u32[]{:S(2)}) collective-permute-start(bf16[256,256]{1,0:T(8,128)(2,1)S(1)} %get-tuple-element.57), channel_id=1, source_target_pairs={{0,64},{64,0},{1,65},{65,1},{2,66},{66,2},{3,67},{67,3},{4,68},{68... | collective-permute-start | bytes 393224 | tf_op jit(solution)/shard_map/ppermute | solution.py:139
  119.8 7.9 %collective-permute-start.13 = (bf16[256,256]{1,0:T(8,128)(2,1)S(1)}, bf16[256,256]{1,0:T(8,128)(2,1)S(1)}, u32[]{:S(2)}, u32[]{:S(2)}) collective-permute-start(bf16[256,256]{1,0:T(8,128)(2,1)S(1)} %get-tuple-element.58), channel_id=1, source_target_pairs={{0,96},{32,64},{64,32},{96,0},{1,97},{33,65},{65,33},{97,1},{2,98}... | collective-permute-start | bytes 393224 | tf_op jit(solution)/shard_map/ppermute | solution.py:140

commit v12 on v8

--- a/solution.py
+++ b/solution.py
@@ -179,8 +179,8 @@
     terms = lax.all_to_all(term, "y", 0, 0, tiled=True)
     near = jnp.concatenate([near, first])
     near = jnp.concatenate([near, flipped(near, 2, n_y)])
+    terms, near = lax.optimization_barrier((terms, near))
     last = flipped(near, 1, n_y)
-    terms, last = lax.optimization_barrier((terms, last))
     gathered = [own, from_core, from_far, lax.ppermute(from_far, "c", SWAP)]
 
     sizes = (2 * n_zh, n_y, own_columns)

time: 130 us -> 127 us (0.977)
  waiting for transfers between devices: 19.6 us -> 17.3 us
    ppermute x3, waiting for transfers between devices: 15.8 us -> 8.03 us  [flipped(): return lax.ppermute(x, 'y', [(i, i ^ bits) for i in range(n)])]
    ppermute x1, waiting for transfers between devices: 0.01 us -> 5.29 us  [local(): from_far = lax.ppermute(own, 'xh', SWAP)]
  transfers between devices with their start and end apart: 15 -> 15, of which waited for: 5 -> 6; matrix products, arithmetic and copies ran while one was open for 1% -> 1% of each run, Pallas kernels for 4% -> 4%
where the time goes in v12:
time: 127 us; the launch traced here: 125 us
  starting transfers between devices  57.9 us (46%)
  blocking collectives  34.5 us (27%)
  waiting for transfers between devices  17.3 us (14%)
  Pallas kernels  11.7 us (9%)
  other arithmetic  1.95 us (2%)
    all_to_all x1, blocking collectives, local(): block = lax.all_to_all(mine, ('xl', 'zh', 'zl'), 0, 0, tiled=True)  34.5 us
    ppermute x3, starting transfers between devices, flipped(): return lax.ppermute(x, 'y', [(i, i ^ bits) for i in range(n)])  14.8 us
    pallas_call x6, Pallas kernels, call(): pl.pallas_call(kernel, out_shape=shapes, in_specs=[pl.BlockSpec(memory_sp...  11.7 us
    all_to_all x1, starting transfers between devices, local(): terms = lax.all_to_all(term, 'y', 0, 0, tiled=True)  8.2 us
    ppermute x3, waiting for transfers between devices, flipped(): return lax.ppermute(x, 'y', [(i, i ^ bits) for i in range(n)])  8.03 us
    all_to_all x1, starting transfers between devices, local(): summed = lax.all_to_all(summed, 'zh', 0, 0, tiled=True)  7.09 us
    ppermute x2, starting transfers between devices, from_group(): lax.ppermute(blocks[2], 'zl', SWAP)  6.98 us
    ppermute x2, starting transfers between devices, from_group(): lax.ppermute(blocks[3], ('zl', 'xl'), BOTH)  6.34 us
  transfers between devices with their start and end apart: 15, of which 6 were waited for; matrix products, arithmetic and copies ran while one was open for 1% of the time, Pallas kernels for 4%

profile of v12, /device:TPU:6, one launch (start us, length us, event | category | flops | bytes accessed | tf_op | source)
XLA Modules:
  0.0 125.4 jit_solution(2631537692495165376)
XLA Ops:
  0.6 0.0 copy-start.3
  0.6 0.6 pad_add_fusion.place_ref
  1.2 0.0 copy-start.2
  1.2 3.3 %shard_map.68 = (bf16[256,1280]{1,0:T(8,128)(2,1)}, bf16[128,1536]{1,0:T(8,128)(2,1)}, bf16[128,1536]{1,0:T(8,128)(2,1)}, bf16[128,1536]{1,0:T(8,128)(2,1)}) custom-call(s32[4]{0:T(128)} %pad_add_fusion.place_ref, s32[1,4]{1,0:T(1,128)} %counts_ref.1, s32[1,4]{1,0:T(1,128)} %offsets_ref.1, bf16[256,256]{1,0:T(8,128)(2,1)} %grad_ref.1, ...), custom_call_target="tpu_custom_call" | custom-call | tf_op jit(solution)/shard_map/pallas_call | solution.py:127
  4.5 2.7 %collective-permute-start = (bf16[128,1536]{1,0:T(8,128)(2,1)}, bf16[128,1536]{1,0:T(8,128)(2,1)S(1)}, u32[]{:S(2)}, u32[]{:S(2)}) collective-permute-start(bf16[128,1536]{1,0:T(8,128)(2,1)} %get-tuple-element.31), channel_id=1, source_target_pairs={{0,32},{32,0},{1,33},{33,1},{2,34},{34,2},{3,35},{35,3},{4,36},{36... | collective-permute-start | bytes 1179656 | tf_op jit(solution)/shard_map/ppermute | solution.py:139
  7.2 4.3 %collective-permute-start.1 = (bf16[128,1536]{1,0:T(8,128)(2,1)}, bf16[128,1536]{1,0:T(8,128)(2,1)S(1)}, u32[]{:S(2)}, u32[]{:S(2)}) collective-permute-start(bf16[128,1536]{1,0:T(8,128)(2,1)} %get-tuple-element.32), channel_id=1, source_target_pairs={{0,64},{64,0},{1,65},{65,1},{2,66},{66,2},{3,67},{67,3},{4,68},{68... | collective-permute-start | bytes 1179656 | tf_op jit(solution)/shard_map/ppermute | solution.py:140
  11.5 2.6 %collective-permute-start.2 = (bf16[128,1536]{1,0:T(8,128)(2,1)}, bf16[128,1536]{1,0:T(8,128)(2,1)S(1)}, u32[]{:S(2)}, u32[]{:S(2)}) collective-permute-start(bf16[128,1536]{1,0:T(8,128)(2,1)} %get-tuple-element.33), channel_id=1, source_target_pairs={{0,96},{32,64},{64,32},{96,0},{1,97},{33,65},{65,33},{97,1},{2,98}... | collective-permute-start | bytes 1179656 | tf_op jit(solution)/shard_map/ppermute | solution.py:141
  14.1 0.0 copy-done.3
  14.1 34.5 %all_to_all.15 = bf16[32,4,256]{2,1,0:T(4,128)(2,1)S(1)} all-to-all(bf16[32,4,256]{2,1,0:T(4,128)(2,1)S(1)} %bitcast.8), channel_id=1, replica_groups=mesh['zh'=8,'zl'=2,'xl'=2,'y'=8,'xh'=2,'c'=2] {'xl','zh','zl'}, dimensions={0} | all-to-all | bytes 131072 | tf_op jit(solution)/shard_map/all_to_all | solution.py:167
  48.6 0.0 collective-permute-done.refs_0_
  48.6 0.0 collective-permute-done.1.refs_1_
  48.6 0.0 collective-permute-done.2.refs_2_
  48.6 0.0 copy-done.2
  48.6 0.0 copy-start
  48.7 1.1 copy-done
  49.7 0.0 copy-start.1
  49.7 1.5 %shard_map.69 = (bf16[384,1024]{1,0:T(8,128)(2,1)}, bf16[1024,256]{1,0:T(8,128)(2,1)S(1)}) custom-call(s32[4]{0:T(128)S(1)} %copy-done.2, bf16[256,1280]{1,0:T(8,128)(2,1)S(1)} %copy-done, bf16[128,1536]{1,0:T(8,128)(2,1)S(1)} %collective-permute-done.refs_0_, bf16[128,1536]{1,0:T(8,128)(2,1)S(1)} %collective-permute-done.1.refs_1_, ...), custom_call_target="tpu_custom_call" | custom-call | tf_op jit(solution)/shard_map/pallas_call | solution.py:127
  51.3 1.9 %collective-permute-start.6 = (bf16[384,1024]{1,0:T(8,128)(2,1)}, bf16[384,1024]{1,0:T(8,128)(2,1)S(1)}, u32[]{:S(2)}, u32[]{:S(2)}) collective-permute-start(bf16[384,1024]{1,0:T(8,128)(2,1)} %get-tuple-element.40), channel_id=1, source_target_pairs={{0,1},{1,0},{2,3},{3,2},{4,5},{5,4},{6,7},{7,6},{8,9},{9,8},{10,11... | collective-permute-start | bytes 2359304 | tf_op jit(solution)/shard_map/ppermute | solution.py:174
  53.2 7.7 %collective-permute-start.7 = (bf16[128,256]{1,0:T(8,128)(2,1)S(1)}, bf16[128,256]{1,0:T(8,128)(2,1)S(1)}, u32[]{:S(2)}, u32[]{:S(2)}) collective-permute-start(bf16[128,256]{1,0:T(8,128)(2,1)S(1)} %reshape.19), channel_id=1, source_target_pairs={{0,16},{4,20},{8,24},{12,28},{16,0},{20,4},{24,8},{28,12},{1,17},{... | collective-permute-start | bytes 196616 | tf_op jit(solution)/shard_map/ppermute | solution.py:146
  60.9 2.8 %collective-permute-done.7 = bf16[128,256]{1,0:T(8,128)(2,1)S(1)} collective-permute-done((bf16[128,256]{1,0:T(8,128)(2,1)S(1)}, bf16[128,256]{1,0:T(8,128)(2,1)S(1)}, u32[]{:S(2)}, u32[]{:S(2)}) %collective-permute-start.7) | collective-permute-done | bytes 65568 | tf_op jit(solution)/shard_map/ppermute | solution.py:146
  63.8 0.0 collective-permute-done.6.refs_3_
  63.8 0.0 copy-done.1
  63.8 1.9 %shard_map.71 = bf16[8,128,256]{2,1,0:T(8,128)(2,1)} custom-call(bf16[256,1280]{1,0:T(8,128)(2,1)S(1)} %copy-done.1, bf16[128,1536]{1,0:T(8,128)(2,1)S(1)} %collective-permute-done.refs_0_, bf16[128,1536]{1,0:T(8,128)(2,1)S(1)} %collective-permute-done.1.refs_1_, bf16[128,1536]{1,0:T(8,128)(2,1)S(1)} %collective-permute-done.2.refs_2_, ...), custom_call_target="tpu_custom_call" | custom-call | tf_op jit(solution)/shard_map/pallas_call | solution.py:127
  65.7 8.2 %all-to-all-start.1 = ((bf16[8,128,256]{2,1,0:T(8,128)(2,1)}), bf16[8,128,256]{2,1,0:T(8,128)(2,1)S(1)}, u32[]{:S(2)}, u32[]{:S(2)}) async-start(bf16[8,128,256]{2,1,0:T(8,128)(2,1)} %shard_map.71), calls=%async_computation.1 | async-start | bytes 1048576 | tf_op jit(solution)/shard_map/all_to_all | solution.py:179
  73.9 3.3 %collective-permute-start.4 = (bf16[1024,256]{1,0:T(8,128)(2,1)S(1)}, bf16[1024,256]{1,0:T(8,128)(2,1)S(1)}, u32[]{:S(2)}, u32[]{:S(2)}) collective-permute-start(bf16[1024,256]{1,0:T(8,128)(2,1)S(1)} %get-tuple-element.39.own_ref), channel_id=1, source_target_pairs={{0,2},{2,0},{1,3},{3,1},{4,6},{6,4},{5,7},{7,5},{8,10},{10,8},{9,1... | collective-permute-start | bytes 1572872 | tf_op jit(solution)/shard_map/ppermute | solution.py:175
  77.3 4.8 %collective-permute-start.8 = (bf16[256,256]{1,0:T(8,128)(2,1)S(1)}, bf16[256,256]{1,0:T(8,128)(2,1)S(1)}, u32[]{:S(2)}, u32[]{:S(2)}) collective-permute-start(bf16[256,256]{1,0:T(8,128)(2,1)S(1)} %pad_maximum_fusion.1), channel_id=1, source_target_pairs={{0,8},{4,12},{8,0},{12,4},{16,24},{20,28},{24,16},{28,20},{1,9},{5... | collective-permute-start | bytes 393224 | tf_op jit(solution)/shard_map/ppermute | solution.py:146
  82.1 1.9 %collective-permute-start.3 = (bf16[1024,256]{1,0:T(8,128)(2,1)S(1)}, bf16[1024,256]{1,0:T(8,128)(2,1)S(1)}, u32[]{:S(2)}, u32[]{:S(2)}) collective-permute-start(bf16[1024,256]{1,0:T(8,128)(2,1)S(1)} %get-tuple-element.39.own_ref), channel_id=1, source_target_pairs={{0,1},{1,0},{2,3},{3,2},{4,5},{5,4},{6,7},{7,6},{8,9},{9,8},{10,11... | collective-permute-start | bytes 1572872 | tf_op jit(solution)/shard_map/ppermute | solution.py:176
  84.0 5.3 %collective-permute-done.4.far_ref = bf16[1024,256]{1,0:T(8,128)(2,1)S(1)} collective-permute-done((bf16[1024,256]{1,0:T(8,128)(2,1)S(1)}, bf16[1024,256]{1,0:T(8,128)(2,1)S(1)}, u32[]{:S(2)}, u32[]{:S(2)}) %collective-permute-start.4) | collective-permute-done | bytes 524320 | tf_op jit(solution)/shard_map/ppermute | solution.py:175
  89.3 1.9 %collective-permute-start.5 = (bf16[1024,256]{1,0:T(8,128)(2,1)S(1)}, bf16[1024,256]{1,0:T(8,128)(2,1)S(1)}, u32[]{:S(2)}, u32[]{:S(2)}) collective-permute-start(bf16[1024,256]{1,0:T(8,128)(2,1)S(1)} %collective-permute-done.4.far_ref), channel_id=1, source_target_pairs={{0,1},{1,0},{2,3},{3,2},{4,5},{5,4},{6,7},{7,6},{8,9},{9,8},{10,11... | collective-permute-start | bytes 1572872 | tf_op jit(solution)/shard_map/ppermute | solution.py:184
  91.2 1.5 %collective-permute-done.8 = bf16[256,256]{1,0:T(8,128)(2,1)S(1)} collective-permute-done((bf16[256,256]{1,0:T(8,128)(2,1)S(1)}, bf16[256,256]{1,0:T(8,128)(2,1)S(1)}, u32[]{:S(2)}, u32[]{:S(2)}) %collective-permute-start.8) | collective-permute-done | bytes 131104 | tf_op jit(solution)/shard_map/ppermute | solution.py:146
  92.7 0.0 all-to-all-done.1
  92.7 0.7 convert_reduce_fusion
  93.5 7.1 %all-to-all-start.2 = ((f32[8,16,256]{2,1,0:T(8,128)}), f32[8,16,256]{2,1,0:T(8,128)S(1)}, u32[]{:S(2)}, u32[]{:S(2)}) async-start(f32[8,16,256]{2,1,0:T(8,128)} %bitcast.7), calls=%async_computation.2 | async-start | bytes 262144 | tf_op jit(solution)/shard_map/all_to_all | solution.py:192
  100.5 2.2 %collective-permute-start.9 = (bf16[512,256]{1,0:T(8,128)(2,1)S(1)}, bf16[512,256]{1,0:T(8,128)(2,1)S(1)}, u32[]{:S(2)}, u32[]{:S(2)}) collective-permute-start(bf16[512,256]{1,0:T(8,128)(2,1)S(1)} %pad_maximum_fusion.near_ref), channel_id=1, source_target_pairs={{0,4},{4,0},{8,12},{12,8},{16,20},{20,16},{24,28},{28,24},{1,5},{5... | collective-permute-start | bytes 786440 | tf_op jit(solution)/shard_map/ppermute | solution.py:146
  102.8 0.0 collective-permute-done.3.core_ref
  102.8 0.0 collective-permute-done.5.both_ref
  102.8 2.9 %shard_map.70.scaled_ref = bf16[1024,1024]{1,0:T(8,128)(2,1)S(1)} custom-call(s32[4]{0:T(128)S(1)} %copy-done.2, bf16[1024,256]{1,0:T(8,128)(2,1)S(1)} %get-tuple-element.39.own_ref, bf16[1024,256]{1,0:T(8,128)(2,1)S(1)} %collective-permute-done.3.core_ref, bf16[1024,256]{1,0:T(8,128)(2,1)S(1)} %collective-permute-done.4.far_ref, ...), custom_call_target="tpu_custom_call" | custom-call | tf_op jit(solution)/shard_map/pallas_call | solution.py:127
  105.7 3.7 %collective-permute-done.9.next_ref = bf16[512,256]{1,0:T(8,128)(2,1)S(1)} collective-permute-done((bf16[512,256]{1,0:T(8,128)(2,1)S(1)}, bf16[512,256]{1,0:T(8,128)(2,1)S(1)}, u32[]{:S(2)}, u32[]{:S(2)}) %collective-permute-start.9) | collective-permute-done | bytes 262176 | tf_op jit(solution)/shard_map/ppermute | solution.py:146
  109.4 0.7 shard_map.72
  110.1 2.7 %collective-permute-start.10 = (bf16[256,256]{1,0:T(8,128)(2,1)S(1)}, bf16[256,256]{1,0:T(8,128)(2,1)S(1)}, u32[]{:S(2)}, u32[]{:S(2)}) collective-permute-start(bf16[256,256]{1,0:T(8,128)(2,1)S(1)} %get-tuple-element.46), channel_id=1, source_target_pairs={{0,32},{32,0},{1,33},{33,1},{2,34},{34,2},{3,35},{35,3},{4,36},{36... | collective-permute-start | bytes 393224 | tf_op jit(solution)/shard_map/ppermute | solution.py:139
  112.9 2.7 %collective-permute-start.11 = (bf16[256,256]{1,0:T(8,128)(2,1)S(1)}, bf16[256,256]{1,0:T(8,128)(2,1)S(1)}, u32[]{:S(2)}, u32[]{:S(2)}) collective-permute-start(bf16[256,256]{1,0:T(8,128)(2,1)S(1)} %get-tuple-element.47), channel_id=1, source_target_pairs={{0,64},{64,0},{1,65},{65,1},{2,66},{66,2},{3,67},{67,3},{4,68},{68... | collective-permute-start | bytes 393224 | tf_op jit(solution)/shard_map/ppermute | solution.py:140
  115.6 3.8 %collective-permute-start.12 = (bf16[256,256]{1,0:T(8,128)(2,1)S(1)}, bf16[256,256]{1,0:T(8,128)(2,1)S(1)}, u32[]{:S(2)}, u32[]{:S(2)}) collective-permute-start(bf16[256,256]{1,0:T(8,128)(2,1)S(1)} %get-tuple-element.48), channel_id=1, source_target_pairs={{0,96},{32,64},{64,32},{96,0},{1,97},{33,65},{65,33},{97,1},{2,98}... | collective-permute-start | bytes 393224 | tf_op jit(solution)/shard_map/ppermute | solution.py:141
  119.4 0.0 collective-permute-done.10.refs_1_
  119.4 1.4 %collective-permute-done.11.refs_2_ = bf16[256,256]{1,0:T(8,128)(2,1)S(1)} collective-permute-done((bf16[256,256]{1,0:T(8,128)(2,1)S(1)}, bf16[256,256]{1,0:T(8,128)(2,1)S(1)}, u32[]{:S(2)}, u32[]{:S(2)}) %collective-permute-start.11) | collective-permute-done | bytes 131104 | tf_op jit(solution)/shard_map/ppermute | solution.py:140
  120.8 2.6 %collective-permute-done.12.refs_3_ = bf16[256,256]{1,0:T(8,128)(2,1)S(1)} collective-permute-done((bf16[256,256]{1,0:T(8,128)(2,1)S(1)}, bf16[256,256]{1,0:T(8,128)(2,1)S(1)}, u32[]{:S(2)}, u32[]{:S(2)}) %collective-permute-start.12) | collective-permute-done | bytes 131104 | tf_op jit(solution)/shard_map/ppermute | solution.py:141
  123.3 1.4 %shard_map.73 = bf16[256,1024]{1,0:T(8,128)(2,1)} custom-call(s32[4]{0:T(128)S(1)} %copy-done.2, bf16[256,256]{1,0:T(8,128)(2,1)S(1)} %get-tuple-element.45.refs_0_, bf16[256,256]{1,0:T(8,128)(2,1)S(1)} %collective-permute-done.10.refs_1_, bf16[256,256]{1,0:T(8,128)(2,1)S(1)} %collective-permute-done.11.refs_2_, ...), custom_call_target="tpu_custom_call" | custom-call | tf_op jit(solution)/shard_map/pallas_call | solution.py:127
  124.7 0.0 all-to-all-done.2
  124.8 0.6 broadcast_multiply_fusion
  (7 shorter events, 0.1 us)
Async XLA Ops:
  0.6 13.4 %copy-start.3 = (bf16[1024,4]{0,1:T(4,128)(2,1)S(1)}, bf16[1024,4]{0,1:T(4,128)(2,1)}, u32[]{:S(2)}) copy-start(bf16[1024,4]{0,1:T(4,128)(2,1)} %param.7) | copy-start | bytes 24580
  1.2 47.4 %copy-start.2 = (s32[4]{0:T(128)S(1)}, s32[4]{0:T(128)}, u32[]{:S(2)}) copy-start(s32[4]{0:T(128)} %pad_add_fusion.place_ref) | copy-start | bytes 52
  4.5 44.2 %collective-permute-start = (bf16[128,1536]{1,0:T(8,128)(2,1)}, bf16[128,1536]{1,0:T(8,128)(2,1)S(1)}, u32[]{:S(2)}, u32[]{:S(2)}) collective-permute-start(bf16[128,1536]{1,0:T(8,128)(2,1)} %get-tuple-element.31), channel_id=1, source_target_pairs={{0,32},{32,0},{1,33},{33,1},{2,34},{34,2},{3,35},{35,3},{4,36},{36... | collective-permute-start | bytes 1179656 | tf_op jit(solution)/shard_map/ppermute | solution.py:139
  7.2 41.4 %collective-permute-start.1 = (bf16[128,1536]{1,0:T(8,128)(2,1)}, bf16[128,1536]{1,0:T(8,128)(2,1)S(1)}, u32[]{:S(2)}, u32[]{:S(2)}) collective-permute-start(bf16[128,1536]{1,0:T(8,128)(2,1)} %get-tuple-element.32), channel_id=1, source_target_pairs={{0,64},{64,0},{1,65},{65,1},{2,66},{66,2},{3,67},{67,3},{4,68},{68... | collective-permute-start | bytes 1179656 | tf_op jit(solution)/shard_map/ppermute | solution.py:140
  11.5 37.1 %collective-permute-start.2 = (bf16[128,1536]{1,0:T(8,128)(2,1)}, bf16[128,1536]{1,0:T(8,128)(2,1)S(1)}, u32[]{:S(2)}, u32[]{:S(2)}) collective-permute-start(bf16[128,1536]{1,0:T(8,128)(2,1)} %get-tuple-element.33), channel_id=1, source_target_pairs={{0,96},{32,64},{64,32},{96,0},{1,97},{33,65},{65,33},{97,1},{2,98}... | collective-permute-start | bytes 1179656 | tf_op jit(solution)/shard_map/ppermute | solution.py:141
  48.6 1.1 copy-start
  49.7 14.0 %copy-start.1 = (bf16[256,1280]{1,0:T(8,128)(2,1)S(1)}, bf16[256,1280]{1,0:T(8,128)(2,1)}, u32[]{:S(2)}) copy-start(bf16[256,1280]{1,0:T(8,128)(2,1)} %get-tuple-element.35.own_ref) | copy-start | bytes 1966084
  51.3 12.5 %collective-permute-start.6 = (bf16[384,1024]{1,0:T(8,128)(2,1)}, bf16[384,1024]{1,0:T(8,128)(2,1)S(1)}, u32[]{:S(2)}, u32[]{:S(2)}) collective-permute-start(bf16[384,1024]{1,0:T(8,128)(2,1)} %get-tuple-element.40), channel_id=1, source_target_pairs={{0,1},{1,0},{2,3},{3,2},{4,5},{5,4},{6,7},{7,6},{8,9},{9,8},{10,11... | collective-permute-start | bytes 2359304 | tf_op jit(solution)/shard_map/ppermute | solution.py:174
  53.2 10.6 %collective-permute-start.7 = (bf16[128,256]{1,0:T(8,128)(2,1)S(1)}, bf16[128,256]{1,0:T(8,128)(2,1)S(1)}, u32[]{:S(2)}, u32[]{:S(2)}) collective-permute-start(bf16[128,256]{1,0:T(8,128)(2,1)S(1)} %reshape.19), channel_id=1, source_target_pairs={{0,16},{4,20},{8,24},{12,28},{16,0},{20,4},{24,8},{28,12},{1,17},{... | collective-permute-start | bytes 196616 | tf_op jit(solution)/shard_map/ppermute | solution.py:146
  65.7 27.0 %all-to-all-start.1 = ((bf16[8,128,256]{2,1,0:T(8,128)(2,1)}), bf16[8,128,256]{2,1,0:T(8,128)(2,1)S(1)}, u32[]{:S(2)}, u32[]{:S(2)}) async-start(bf16[8,128,256]{2,1,0:T(8,128)(2,1)} %shard_map.71), calls=%async_computation.1 | async-start | bytes 1048576 | tf_op jit(solution)/shard_map/all_to_all | solution.py:179
  73.9 15.4 %collective-permute-start.4 = (bf16[1024,256]{1,0:T(8,128)(2,1)S(1)}, bf16[1024,256]{1,0:T(8,128)(2,1)S(1)}, u32[]{:S(2)}, u32[]{:S(2)}) collective-permute-start(bf16[1024,256]{1,0:T(8,128)(2,1)S(1)} %get-tuple-element.39.own_ref), channel_id=1, source_target_pairs={{0,2},{2,0},{1,3},{3,1},{4,6},{6,4},{5,7},{7,5},{8,10},{10,8},{9,1... | collective-permute-start | bytes 1572872 | tf_op jit(solution)/shard_map/ppermute | solution.py:175
  77.3 15.4 %collective-permute-start.8 = (bf16[256,256]{1,0:T(8,128)(2,1)S(1)}, bf16[256,256]{1,0:T(8,128)(2,1)S(1)}, u32[]{:S(2)}, u32[]{:S(2)}) collective-permute-start(bf16[256,256]{1,0:T(8,128)(2,1)S(1)} %pad_maximum_fusion.1), channel_id=1, source_target_pairs={{0,8},{4,12},{8,0},{12,4},{16,24},{20,28},{24,16},{28,20},{1,9},{5... | collective-permute-start | bytes 393224 | tf_op jit(solution)/shard_map/ppermute | solution.py:146
  82.1 20.7 %collective-permute-start.3 = (bf16[1024,256]{1,0:T(8,128)(2,1)S(1)}, bf16[1024,256]{1,0:T(8,128)(2,1)S(1)}, u32[]{:S(2)}, u32[]{:S(2)}) collective-permute-start(bf16[1024,256]{1,0:T(8,128)(2,1)S(1)} %get-tuple-element.39.own_ref), channel_id=1, source_target_pairs={{0,1},{1,0},{2,3},{3,2},{4,5},{5,4},{6,7},{7,6},{8,9},{9,8},{10,11... | collective-permute-start | bytes 1572872 | tf_op jit(solution)/shard_map/ppermute | solution.py:176
  89.3 13.5 %collective-permute-start.5 = (bf16[1024,256]{1,0:T(8,128)(2,1)S(1)}, bf16[1024,256]{1,0:T(8,128)(2,1)S(1)}, u32[]{:S(2)}, u32[]{:S(2)}) collective-permute-start(bf16[1024,256]{1,0:T(8,128)(2,1)S(1)} %collective-permute-done.4.far_ref), channel_id=1, source_target_pairs={{0,1},{1,0},{2,3},{3,2},{4,5},{5,4},{6,7},{7,6},{8,9},{9,8},{10,11... | collective-permute-start | bytes 1572872 | tf_op jit(solution)/shard_map/ppermute | solution.py:184
  93.5 31.3 %all-to-all-start.2 = ((f32[8,16,256]{2,1,0:T(8,128)}), f32[8,16,256]{2,1,0:T(8,128)S(1)}, u32[]{:S(2)}, u32[]{:S(2)}) async-start(f32[8,16,256]{2,1,0:T(8,128)} %bitcast.7), calls=%async_computation.2 | async-start | bytes 262144 | tf_op jit(solution)/shard_map/all_to_all | solution.py:192
  100.5 8.9 %collective-permute-start.9 = (bf16[512,256]{1,0:T(8,128)(2,1)S(1)}, bf16[512,256]{1,0:T(8,128)(2,1)S(1)}, u32[]{:S(2)}, u32[]{:S(2)}) collective-permute-start(bf16[512,256]{1,0:T(8,128)(2,1)S(1)} %pad_maximum_fusion.near_ref), channel_id=1, source_target_pairs={{0,4},{4,0},{8,12},{12,8},{16,20},{20,16},{24,28},{28,24},{1,5},{5... | collective-permute-start | bytes 786440 | tf_op jit(solution)/shard_map/ppermute | solution.py:146
  110.1 9.2 %collective-permute-start.10 = (bf16[256,256]{1,0:T(8,128)(2,1)S(1)}, bf16[256,256]{1,0:T(8,128)(2,1)S(1)}, u32[]{:S(2)}, u32[]{:S(2)}) collective-permute-start(bf16[256,256]{1,0:T(8,128)(2,1)S(1)} %get-tuple-element.46), channel_id=1, source_target_pairs={{0,32},{32,0},{1,33},{33,1},{2,34},{34,2},{3,35},{35,3},{4,36},{36... | collective-permute-start | bytes 393224 | tf_op jit(solution)/shard_map/ppermute | solution.py:139
  112.9 7.9 %collective-permute-start.11 = (bf16[256,256]{1,0:T(8,128)(2,1)S(1)}, bf16[256,256]{1,0:T(8,128)(2,1)S(1)}, u32[]{:S(2)}, u32[]{:S(2)}) collective-permute-start(bf16[256,256]{1,0:T(8,128)(2,1)S(1)} %get-tuple-element.47), channel_id=1, source_target_pairs={{0,64},{64,0},{1,65},{65,1},{2,66},{66,2},{3,67},{67,3},{4,68},{68... | collective-permute-start | bytes 393224 | tf_op jit(solution)/shard_map/ppermute | solution.py:140
  115.6 7.8 %collective-permute-start.12 = (bf16[256,256]{1,0:T(8,128)(2,1)S(1)}, bf16[256,256]{1,0:T(8,128)(2,1)S(1)}, u32[]{:S(2)}, u32[]{:S(2)}) collective-permute-start(bf16[256,256]{1,0:T(8,128)(2,1)S(1)} %get-tuple-element.48), channel_id=1, source_target_pairs={{0,96},{32,64},{64,32},{96,0},{1,97},{33,65},{65,33},{97,1},{2,98}... | collective-permute-start | bytes 393224 | tf_op jit(solution)/shard_map/ppermute | solution.py:141
